TPU v7x, 32 devices: a whole 2x2x4 slice. The times are simulated.
32 devices in a mesh: gx: 4 (over x, core), gy: 8 (over z, y).
Axes of the slice: x: 2, y: 2, z: 4, core: 2. Of those that a mesh axis runs over, the one named last changes fastest.
Arguments:
- samples: float32 [4096, 2, 128], P(('gx', 'gy')), may hold values from -6 to 6
- kernel: float32 [4096, 3, 4, 128], P(('gx', 'gy')), may hold values from 0.1 to 1
- offsets: int32 [4096, 3, 128], P(('gx', 'gy')), may hold values from 0 to 4
- owners: int32 [4096, 1], P(('gx', 'gy')), may hold values from 0 to 31; in each aligned block of 128 rows (0 to 127, 128 to 255, ...) at most 8 rows name the same one
- tile_ids: int32 [4096], P(('gx', 'gy')), may hold values from 0 to 3455
- deapod_first: float32 [192], replicated, may hold values from 1 to 3
- deapod_second: float32 [192], P('gx'), may hold values from 1 to 3
- deapod_third: float32 [192], P('gy'), may hold values from 1 to 3
Outputs:
- image: float32 [2, 192, 192, 192], P(None, 'gy', 'gx')
Inputs may be any that keep to these rules, and one draw needn't show every extreme that they name: `owners`: among the 128 blocks of one device no owner is named more than 8 times, and in some device one owner is named exactly 8 times. `tile_ids`: tiles are numbered row, column, depth over the owner's 12 x 6 x 48 tiles. `offsets`: each sample's kernel lies inside its block's tile.
All inputs are finite; a program needn't handle non-finite values.
Results may differ from a plain program's by a relative error of at most 0.0003.
Values sent between devices are 32-bit elements; how exact they have to be, the bound alone decides.
No kernel may reach another device: no remote copies, remote signals or barrier semaphores. Data moves between devices by JAX's collectives and lax.ppermute only.
A program may use at most 256 MiB of HBM per device.

v0:
```python
import math

import jax
import jax.numpy as jnp
from jax import lax
from jax.sharding import PartitionSpec as P

NX = 384
NY = 384
NZ = 384
TILE = 8


def fourier_table(length, outputs):
    freq = jnp.arange(length, dtype=jnp.int32) - length // 2
    image_pos = jnp.arange(outputs, dtype=jnp.int32) - outputs // 2
    phase_steps = jnp.mod(freq[:, None] * image_pos[None, :], length)
    phases = phase_steps.astype(jnp.float32) * (2.0 * math.pi / length)
    norming = 1.0 / math.sqrt(length)
    return (jnp.cos(phases) * norming, jnp.sin(phases) * norming)


def complex_apply(real_part, imag_part, cos_table, sin_table, pattern):
    highest = lax.Precision.HIGHEST
    real_cos = jnp.einsum(pattern, real_part, cos_table, precision=highest)
    real_sin = jnp.einsum(pattern, real_part, sin_table, precision=highest)
    imag_cos = jnp.einsum(pattern, imag_part, cos_table, precision=highest)
    imag_sin = jnp.einsum(pattern, imag_part, sin_table, precision=highest)
    return jnp.stack((real_cos - imag_sin, real_sin + imag_cos))


def spread(values, kernel, starts, tile_width):
    kernel_taps = jnp.arange(kernel.shape[2], dtype=jnp.float32)
    cell_axis = jnp.arange(tile_width, dtype=jnp.float32)
    matches = (
        cell_axis[None, None, :, None, None]
        == starts[:, :, None, None, :] + kernel_taps[None, None, None, :, None]
    ).astype(jnp.float32)
    placed = jnp.sum(matches * kernel[:, :, None, :, :], axis=3)
    plane_weight = placed[:, 0][:, :, None, :] * placed[:, 1][:, None, :, :]
    depth_weight = values[:, :, None, :] * placed[:, 2][:, None, :, :]
    return jnp.einsum(
        "nijs,ncls->ncijl", plane_weight, depth_weight, precision=lax.Precision.HIGHEST
    )


def on_device(
    samples, kernel, offsets, owners, tile_ids, deapod_first, deapod_second, deapod_third
):
    devices = lax.axis_size(("gx", "gy"))
    grid_rows = lax.axis_size("gx")
    grid_cols = lax.axis_size("gy")
    blocks = samples.shape[0]
    block_width = samples.shape[2]
    kernel_taps = kernel.shape[2]
    capacity = max(2, 2 * blocks // devices)
    tile_rows = NX // (TILE * grid_rows)
    tile_cols = NY // (TILE * grid_cols)
    tile_depth = NZ // TILE
    tile_count = tile_rows * tile_cols * tile_depth
    starts = offsets.astype(jnp.float32)
    target = owners[:, 0]
    onehot = (target[:, None] == jnp.arange(devices, dtype=jnp.int32)[None, :]).astype(jnp.float32)
    earlier = (jnp.arange(blocks)[:, None] > jnp.arange(blocks)[None, :]).astype(jnp.float32)
    counted = jnp.dot(earlier, onehot, precision=lax.Precision.HIGHEST)
    position = jnp.sum(counted * onehot, axis=1).astype(jnp.int32)
    marker = jnp.broadcast_to(tile_ids.astype(jnp.float32)[:, None, None], (blocks, 1, block_width))
    payload = jnp.concatenate(
        (samples, kernel.reshape(blocks, 3 * kernel_taps, block_width), starts, marker), axis=1
    )
    payload_rows = payload.shape[1]
    outbox = jnp.zeros((devices, capacity, payload_rows, block_width), jnp.float32)
    outbox = outbox.at[:, :, payload_rows - 1, :].set(float(tile_count))
    outbox = outbox.at[target, position].set(payload)
    arrived = lax.all_to_all(outbox, ("gx", "gy"), split_axis=0, concat_axis=0, tiled=True)
    arrived = arrived.reshape(devices * capacity, payload_rows, block_width)
    tile_index = arrived[:, payload_rows - 1, 0].astype(jnp.int32)
    pieces = spread(
        arrived[:, 0:2],
        arrived[:, 2 : 2 + 3 * kernel_taps].reshape(-1, 3, kernel_taps, block_width),
        arrived[:, 2 + 3 * kernel_taps : 5 + 3 * kernel_taps],
        TILE,
    )
    cos_z, sin_z = fourier_table(NZ, NZ // 2)
    tile_cells = 2 * TILE * TILE * TILE
    flat_pieces = pieces.reshape(-1, tile_cells)
    spread_grid = (
        jnp.zeros((tile_count, tile_cells), jnp.float32)
        .at[tile_index]
        .add(flat_pieces, mode="drop")
    )
    spread_grid = (
        spread_grid.reshape(tile_rows, tile_cols, tile_depth, 2, TILE, TILE, TILE)
        .transpose(3, 0, 4, 1, 5, 2, 6)
        .reshape(2, tile_rows * TILE, tile_cols * TILE, NZ)
    )
    along_z = complex_apply(spread_grid[0], spread_grid[1], cos_z, sin_z, "xyk,km->mxy")
    cos_y, sin_y = fourier_table(NY, NY // 2)
    slab = lax.all_to_all(along_z, "gy", split_axis=1, concat_axis=3, tiled=True)
    along_y = complex_apply(slab[0], slab[1], cos_y, sin_y, "zxy,yq->zqx")
    cos_x, sin_x = fourier_table(NX, NX // 2)
    slab = lax.all_to_all(along_y, "gx", split_axis=2, concat_axis=3, tiled=True)
    along_x = complex_apply(slab[0], slab[1], cos_x, sin_x, "zyx,xp->zyp")
    return (
        along_x
        * deapod_third[None, :, None, None]
        * deapod_second[None, None, :, None]
        * deapod_first[None, None, None, :]
    )


def solution(mesh):
    in_specs = (
        P(("gx", "gy"), None, None),
        P(("gx", "gy"), None, None, None),
        P(("gx", "gy"), None, None),
        P(("gx", "gy"), None),
        P(("gx", "gy")),
        P(),
        P("gx"),
        P("gy"),
    )
    out_specs = P(None, "gy", "gx", None)
    return jax.shard_map(
        on_device, mesh=mesh, in_specs=in_specs, out_specs=out_specs, check_vma=False
    )
```

profile of v0, /device:TPU:16, one launch (start us, length us, event | category | flops | bytes accessed | tf_op | source)
XLA Modules:
  0.0 973.6 jit_solution(9148142012049549325)
XLA Ops:
  7.7 13.1 %scatter_fusion = f32[32,8,18,128]{3,2,1,0:T(8,128)S(1)} fusion(f32[32,8,18,128]{3,2,1,0:T(8,128)S(1)} %copy-done.3, s32[128]{0:T(128)S(1)} %fusion.101, f32[128,18,128]{2,1,0:T(8,128)} %copy.82), kind=kCustom, calls=%fused_computation | custom fusion | bytes 3539968 | tf_op jit(solution)/shard_map/scatter | solution.py:74
  22.6 5.9 all-to-all-start
  29.7 50.2 %all-to-all-done = f32[32,8,18,128]{3,1,2,0:T(8,128)S(1)} async-done(((f32[32,8,18,128]{3,1,2,0:T(8,128)}), f32[32,8,18,128]{3,1,2,0:T(8,128)S(1)}, u32[]{:S(2)}, u32[]{:S(2)}) %all-to-all-start) | async-done | bytes 2359328 | tf_op jit(solution)/shard_map/all_to_all | solution.py:75
  85.1 125.2 %convolution_bitcast_fusion = f32[256,2,8,8,8]{3,4,2,1,0:T(8,128)} fusion(f32[256,8,128]{2,1,0:T(8,128)S(1)} %get-tuple-element.24, f32[256,8,128]{2,1,0:T(8,128)S(1)} %get-tuple-element.25, f32[256,8,128]{2,1,0:T(8,128)S(1)} %get-tuple-element.23, f32[256,2,128]{2,1,0:T(2,128)S(1)} %copy.85), kind=kOutput, calls=%fused_computation.6 | convolution fusion | flops 405274624 | bytes 4456448 | tf_op jit(solution)/shard_map/nijs,ncls->ncijl/dot_general | solution.py:42
  210.4 11.9 %copy.88 = f32[256,2,8,8,8]{0,4,3,2,1:T(8,128)S(1)} copy(f32[256,2,8,8,8]{3,4,2,1,0:T(8,128)} %convolution_bitcast_fusion) | data formatting | bytes 2097152 | tf_op jit(solution)/shard_map/nijs,ncls->ncijl/transpose | solution.py:42
  222.7 8.5 scatter_custom_fusion.1
  231.2 15.2 %copy.90 = f32[3456,1024]{0,1:T(8,128)} copy(f32[3456,1024]{1,0:T(8,128)} %scatter_custom_fusion.1) | data formatting | bytes 28311552 | tf_op jit(solution)/shard_map/scatter-add | solution.py:90
  246.4 35.1 %reshape.122 = f32[12,6,48,2,8,8,8]{2,1,0,6,5,4,3:T(8,128)} reshape(f32[3456,1024]{0,1:T(8,128)} %copy.90) | data formatting | bytes 28311552 | tf_op jit(solution)/shard_map/reshape | solution.py:93
  281.5 33.5 %fusion.150 = (f32[1,12,8,6,8,48,8]{5,3,1,6,4,2,0:T(8,128)}, f32[1,12,8,6,8,48,8]{5,3,1,6,4,2,0:T(8,128)}) fusion(f32[2,12,8,6,8,48,8]{5,3,1,6,4,2,0:T(8,128)} %bitcast.108), kind=kLoop, calls=%fused_computation.176 | loop fusion | bytes 28311552 | tf_op jit(solution)/shard_map/slice | solution.py:97
  315.1 59.5 %copy.111 = f32[1,12,8,6,8,48,8]{6,5,2,1,4,3,0:T(8,128)} copy(f32[1,12,8,6,8,48,8]{5,3,1,6,4,2,0:T(8,128)} %get-tuple-element.18) | data formatting | bytes 14155776 | tf_op jit(solution)/shard_map/squeeze | solution.py:97
  374.5 75.4 %reshape.141 = f32[96,48,384]{2,0,1:T(8,128)} reshape(f32[1,12,8,6,8,48,8]{6,5,2,1,4,3,0:T(8,128)} %copy.111) | data formatting | bytes 14155776 | tf_op jit(solution)/shard_map/squeeze | solution.py:97
  449.9 16.3 %fusion.33 = f32[192,96,48]{1,0,2:T(8,128)} fusion(f32[96,48,384]{2,0,1:T(8,128)} %reshape.141, s32[192]{0:T(256)S(1)} %copy-done.5, s32[384]{0:T(512)S(1)} %copy-done.4), kind=kOutput, calls=%fused_computation.57 | convolution fusion | flops 4077600768 | bytes 10619136 | tf_op jit(solution)/shard_map/xyk,km->mxy/dot_general | solution.py:25
  466.2 14.4 %fusion.23 = f32[192,96,48]{1,0,2:T(8,128)} fusion(f32[96,48,384]{2,0,1:T(8,128)S(1)} %copy-done.1, s32[192]{0:T(256)S(1)} %copy-done.5, s32[384]{0:T(512)S(1)} %copy-done.4), kind=kOutput, calls=%fused_computation.47 | convolution fusion | flops 4077600768 | bytes 10619136 | tf_op jit(solution)/shard_map/xyk,km->mxy/dot_general | solution.py:26
  480.6 59.5 %copy.112 = f32[1,12,8,6,8,48,8]{6,5,2,1,4,3,0:T(8,128)} copy(f32[1,12,8,6,8,48,8]{5,3,1,6,4,2,0:T(8,128)} %get-tuple-element.17) | data formatting | bytes 14155776 | tf_op jit(solution)/shard_map/squeeze | solution.py:97
  540.1 75.4 %reshape.142 = f32[96,48,384]{2,0,1:T(8,128)} reshape(f32[1,12,8,6,8,48,8]{6,5,2,1,4,3,0:T(8,128)} %copy.112) | data formatting | bytes 14155776 | tf_op jit(solution)/shard_map/squeeze | solution.py:97
  615.5 15.6 %subtract_bitcast_fusion = f32[1,192,96,48]{2,1,3,0:T(8,128)S(1)} fusion(f32[192,96,48]{1,0,2:T(8,128)} %fusion.33, f32[96,48,384]{2,0,1:T(8,128)} %reshape.142, s32[192]{0:T(256)S(1)} %copy-done.5, s32[384]{0:T(512)S(1)} %copy-done.4), kind=kOutput, calls=%fused_computation.14 | convolution fusion | flops 4078485504 | bytes 14158080 | tf_op jit(solution)/shard_map/xyk,km->mxy/dot_general | solution.py:28
  631.1 11.5 %add_bitcast_fusion = f32[1,192,96,48]{2,1,3,0:T(8,128)S(1)} fusion(f32[192,96,48]{1,0,2:T(8,128)S(1)} %copy-done.2, f32[96,48,384]{2,0,1:T(8,128)S(1)} %copy-done, s32[192]{0:T(256)S(1)} %copy-done.5, s32[384]{0:T(512)S(1)} %copy-done.4), kind=kOutput, calls=%fused_computation.13 | convolution fusion | flops 4078485504 | bytes 14158080 | tf_op jit(solution)/shard_map/xyk,km->mxy/dot_general | solution.py:27
  644.2 5.9 copy.97
  650.1 211.2 %all_to_all.35 = f32[2,192,96,48]{2,3,0,1:T(8,128)S(1)} all-to-all(f32[2,192,96,48]{2,3,0,1:T(8,128)S(1)} %copy.97), channel_id=1, replica_groups=mesh['gx'=4,'gy'=8] {'gy'}, dimensions={1} | all-to-all | bytes 14155776 | tf_op jit(solution)/shard_map/all_to_all | solution.py:99
  863.7 5.5 fusion.30
  869.2 5.4 fusion.20
  874.6 5.6 subtract_bitcast_fusion.1
  880.2 5.5 add_bitcast_fusion.1
  889.2 56.4 %all_to_all.36 = f32[2,24,192,96]{3,1,0,2:T(8,128)S(1)} all-to-all(f32[2,24,192,96]{3,1,0,2:T(8,128)S(1)} %copy.103), channel_id=1, replica_groups=mesh['gx'=4,'gy'=8] {'gx'}, dimensions={2} | all-to-all | bytes 7077888 | tf_op jit(solution)/shard_map/all_to_all | solution.py:102
  (59 shorter events, 51.2 us)
Async XLA Ops:
  5.8 0.7 copy-start.9
  5.8 1.9 copy-start.3
  22.6 57.2 %all-to-all-start = ((f32[32,8,18,128]{3,1,2,0:T(8,128)}), f32[32,8,18,128]{3,1,2,0:T(8,128)S(1)}, u32[]{:S(2)}, u32[]{:S(2)}) async-start(f32[32,8,18,128]{3,1,2,0:T(8,128)} %copy.83), calls=%async_computation | async-start | bytes 4718592 | tf_op jit(solution)/shard_map/all_to_all | solution.py:75
  374.5 75.4 %copy-start.4 = (s32[384]{0:T(512)S(1)}, s32[384]{0:T(512)}, u32[]{:S(2)}) copy-start(s32[384]{0:T(512)} %iota_add_fusion.1) | copy-start | bytes 4612
  374.5 75.4 %copy-start.5 = (s32[192]{0:T(256)S(1)}, s32[192]{0:T(256)}, u32[]{:S(2)}) copy-start(s32[192]{0:T(256)} %iota_add_fusion.2) | copy-start | bytes 2308
  449.9 16.3 %copy-start.1 = (f32[96,48,384]{2,0,1:T(8,128)S(1)}, f32[96,48,384]{2,0,1:T(8,128)}, u32[]{:S(2)}) copy-start(f32[96,48,384]{2,0,1:T(8,128)} %reshape.141) | copy-start | bytes 21233668
  615.5 15.6 %copy-start = (f32[96,48,384]{2,0,1:T(8,128)S(1)}, f32[96,48,384]{2,0,1:T(8,128)}, u32[]{:S(2)}) copy-start(f32[96,48,384]{2,0,1:T(8,128)} %reshape.142) | copy-start | bytes 21233668
  615.5 15.6 %copy-start.2 = (f32[192,96,48]{1,0,2:T(8,128)S(1)}, f32[192,96,48]{1,0,2:T(8,128)}, u32[]{:S(2)}) copy-start(f32[192,96,48]{1,0,2:T(8,128)} %fusion.23) | copy-start | bytes 10616836
  963.6 7.7 copy-start.6
  963.6 7.7 copy-start.7
  963.6 7.7 copy-start.8
where the time goes:
time: 989 us; the launch traced here: 974 us
  local copies, waits for them, and re-layouts  411 us (42%)
  blocking collectives  268 us (27%)
  matrix products  220 us (22%)
  waiting for transfers between devices  50.2 us (5%)
  other arithmetic  18.6 us (2%)
    all_to_all x1, blocking collectives, on_device(): lax.all_to_all(along_z, 'gy', split_axis=1, concat_axis=3, tiled=True)  211 us
    squeeze x2, local copies, waits for them, and re-layouts, on_device(): spread_grid[1]  135 us
    squeeze x2, local copies, waits for them, and re-layouts, on_device(): spread_grid[0]  135 us
    dot_general x1, matrix products, spread(): jnp.einsum('nijs,ncls->ncijl', plane_weight, depth_weight, precision=lax....  125 us
    all_to_all x1, blocking collectives, on_device(): lax.all_to_all(along_y, 'gx', split_axis=2, concat_axis=3, tiled=True)  56.4 us
    all_to_all x1, waiting for transfers between devices, on_device(): lax.all_to_all(outbox, ('gx', 'gy'), split_axis=0, concat_axis=0, tiled=T...  50.2 us
    reshape x1, local copies, waits for them, and re-layouts, on_device(): spread_grid.reshape(tile_rows, tile_cols, tile_depth, 2, TILE, TILE, TILE)  35.1 us
    slice x1, local copies, waits for them, and re-layouts, on_device(): spread_grid[1]  33.5 us
  transfers between devices with their start and end apart: 1, of which 1 were waited for; matrix products, arithmetic and copies ran while one was open for 0% of the time, Pallas kernels for 0%

commit v1 on v0

v1 whole, which is shorter than its diff:
```python
import functools
import math

import jax
import jax.numpy as jnp
import ml_dtypes
import numpy as np
from jax import lax
from jax.experimental import pallas as pl
from jax.experimental.pallas import tpu as pltpu
from jax.sharding import PartitionSpec as P

NX = 384
NY = 384
NZ = 384
TILE = 8
LANES = 128
PLANES = 32
PHASES = 128
BF16 = jnp.bfloat16
F32 = jnp.float32
VMEM_LIMIT = 60 * 1024 * 1024


def halves(array):
    high = array.astype(ml_dtypes.bfloat16)
    low = (array - high.astype(np.float64)).astype(ml_dtypes.bfloat16)
    return high, low


def split(value):
    high = value.astype(BF16)
    return high, (value - high.astype(F32)).astype(BF16)


def waves(freq, position, length):
    steps = np.mod(freq[:, None] * position[None, :], length)
    phase = 2.0 * math.pi * steps / length
    return np.cos(phase), np.sin(phase)


def depth_tables(planes):
    matrices, phases = [], []
    lane_part = np.arange(LANES) // 64
    lane_odd = np.arange(LANES) // 32 % 2
    lane_plane = np.arange(LANES) % 32
    used = (lane_plane < planes).astype(np.float64)
    for index in range(NZ // 2 // planes):
        position = index * planes + lane_plane - NZ // 4
        cos, sin = waves(np.arange(TILE) - NZ // 2, position, NZ)
        cos, sin = cos * used / math.sqrt(NZ), sin * used / math.sqrt(NZ)
        real = np.where(lane_part == 0, cos, sin)
        imag = np.where(lane_part == 0, -sin, cos)
        plain = np.concatenate((real, imag))
        turned = np.concatenate((-np.where(lane_part == 0, sin, -cos), -np.where(lane_part == 0, cos, sin)))
        high, low = halves(np.concatenate((plain, turned), axis=1))
        matrices.append(np.concatenate((high, high, low), axis=0))
        cos, sin = waves(np.arange(NZ // TILE), position, NZ // TILE)
        sign = np.where(lane_odd == 1, -1.0, 1.0)[None, :]
        phases.append(np.stack((np.concatenate((cos, cos * sign)), np.concatenate((sin, sin * sign)))))
    return np.stack(matrices), np.stack(phases).astype(np.float32)


def column_tables(chunks):
    half = NY // 2
    out = []
    for chunk in range(chunks):
        rows = half // chunks
        parts = []
        for parity in range(2):
            position = chunk * rows + 2 * np.arange(rows // 2) + parity - NY // 4
            cos, sin = waves(position, np.arange(half) - half, NY)
            high, low = halves(np.concatenate((cos, sin)) / math.sqrt(NY))
            parts.append(np.concatenate((high, high, low), axis=1))
        out.append(np.stack(parts))
    return np.stack(out)


def row_tables():
    half = NX // 2
    quarter = NX // 4
    out = []
    for parity in range(2):
        position = 2 * np.arange(quarter) + parity - NX // 4
        cos, sin = waves(np.arange(half) - half, position, NX)
        table = np.zeros((half, 2 * LANES))
        lanes = (np.arange(quarter) + parity * quarter) % LANES
        table[:, lanes] = cos / math.sqrt(NX)
        table[:, LANES + lanes] = sin / math.sqrt(NX)
        out.append(np.stack(halves(table)))
    return np.stack(out)


def order_tables():
    first = np.zeros((LANES, NX // 2))
    second = np.zeros((LANES, NX // 2))
    quarter = NX // 4
    for m1 in range(NX // 2):
        place = m1 // 2 + m1 % 2 * quarter
        if place < LANES:
            first[place, m1] = 1.0
        else:
            second[place - LANES, m1] = 1.0
    return np.concatenate((first, first, second, second)).astype(ml_dtypes.bfloat16)


def spread_kernel(samples_ref, kernel_ref, offsets_ref, codes_ref, out_ref):
    blocks = samples_ref.shape[0]
    taps = kernel_ref.shape[2]
    cell = lax.broadcasted_iota(jnp.int32, (TILE, LANES), 0)
    left = lax.broadcasted_iota(jnp.int32, (2 * TILE, LANES), 1) < LANES // 2

    def weights(block):
        placed = []
        for dim in range(3):
            shifted = cell - offsets_ref[block, pl.ds(dim, 1), :]
            value = jnp.zeros((TILE, LANES), F32)
            for tap in range(taps):
                value = jnp.where(shifted == tap, kernel_ref[block, dim, pl.ds(tap, 1), :], value)
            placed.append(value)
        plane = jnp.concatenate([placed[0][i : i + 1] * placed[1] for i in range(TILE)], axis=0)
        depth = jnp.concatenate([samples_ref[block, pl.ds(c, 1), :] * placed[2] for c in range(2)], axis=0)
        return depth, plane

    def pair_body(pair, carry):
        depth_a, plane_a = weights(2 * pair)
        depth_b, plane_b = weights(2 * pair + 1)
        depth_high, depth_low = split(jnp.concatenate((depth_a, depth_b), axis=0))
        plane_high, plane_low = split(jnp.concatenate((plane_a, plane_b), axis=0))
        piece = lax.dot_general(
            jnp.concatenate((depth_high, depth_low, depth_high), axis=1),
            jnp.concatenate((plane_high, plane_high, plane_low), axis=1),
            (((1,), (1,)), ((), ())),
            preferred_element_type=F32,
        )
        out_ref[pair] = jnp.where(left, piece[: 2 * TILE], piece[2 * TILE :])
        return carry

    lax.fori_loop(0, blocks // 2, pair_body, 0, unroll=2)
    out_ref[blocks // 2] = jnp.broadcast_to(codes_ref[...], (2 * TILE, LANES))


def transform_kernel(
    group, planes_padded, place_ref, codes_ref, tiles_ref, depth_ref, phases_ref, column_ref, row_ref, keep_ref, send_ref, acc_ref
):
    half = NX // 2
    stride = NY
    sources = tiles_ref.shape[0]
    pairs = tiles_ref.shape[1] - 1
    kept = column_ref.shape[1]
    per_device = kept // group
    slots = per_device // 2

    def clear(step, carry):
        acc_ref[pl.ds(pl.multiple_of(step * stride, stride), stride), :] = jnp.zeros((stride, LANES), F32)
        return carry

    lax.fori_loop(0, half, clear, 0)

    def add_source(source, carry):
        def add_pair(pair, inner):
            high, low = split(tiles_ref[source, pair])
            spectrum = lax.dot_general(
                jnp.concatenate((high, low, high), axis=0),
                depth_ref[...],
                (((0,), (0,)), ((), ())),
                preferred_element_type=F32,
            )
            for side in range(2):
                code = codes_ref[source * 2 * pairs + 2 * pair + side]
                base = lax.shift_right_logical(code, 7)
                phase = jnp.bitwise_and(code, PHASES - 1)
                cos = phases_ref[0, pl.ds(phase, 1), :]
                sin = phases_ref[1, pl.ds(phase, 1), :]
                for i in range(TILE):
                    row = side * TILE * TILE + i * TILE
                    value = spectrum[row : row + TILE, :LANES] * cos + spectrum[row : row + TILE, LANES:] * sin
                    at = pl.ds(pl.multiple_of(base * TILE + i * stride, TILE), TILE)
                    acc_ref[at, :] = acc_ref[at, :] + value
            return inner

        lax.fori_loop(0, pairs, add_pair, 0, unroll=2)
        return carry

    lax.fori_loop(0, sources, add_source, 0)

    turn = jnp.where(lax.broadcasted_iota(jnp.int32, (kept // 2, LANES), 1) < LANES // 2, -1.0, 1.0)

    def columns(step, carry):
        folded = ([], [])
        for side in range(2):
            start = pl.multiple_of((2 * step + side) * stride, stride)
            lower = acc_ref[pl.ds(start, NY // 2), :]
            upper = acc_ref[pl.ds(start + NY // 2, NY // 2), :]
            folded[0].append(lower + upper)
            folded[1].append(lower - upper)
        for parity in range(2):
            high, low = split(jnp.concatenate(folded[parity], axis=1))
            product = jnp.dot(
                column_ref[parity], jnp.concatenate((high, low, high), axis=0), preferred_element_type=F32
            )
            for side in range(2):
                start = pl.multiple_of((2 * step + side) * stride, stride)
                lanes = slice(side * LANES, (side + 1) * LANES)
                acc_ref[pl.ds(start + parity * (kept // 2), kept // 2), :] = (
                    product[: kept // 2, lanes] + pltpu.roll(product[kept // 2 :, lanes], LANES // 2, 1) * turn
                )
        return carry

    lax.fori_loop(0, half // 2, columns, 0)

    member = jnp.bitwise_and(place_ref[0], group - 1)
    lane = lax.broadcasted_iota(jnp.int32, (PLANES, LANES), 1)

    for relative in range(group):
        target = send_ref if relative % 2 else keep_ref
        first = jnp.bitwise_xor(member, relative) * per_device

        def rows(slot, carry):
            turned = []
            for side in range(2):
                m2 = first + slot + side * slots
                row = jnp.bitwise_and(m2, 1) * (kept // 2) + lax.shift_right_logical(m2, 1)
                turned.append(acc_ref[pl.ds(row, half, stride=stride), :].T)
            parts = []
            for parity in range(2):
                at = parity * PLANES
                stacked = [
                    value[part * 64 + at : part * 64 + at + PLANES] for value in turned for part in range(2)
                ]
                high, low = split(jnp.concatenate(stacked, axis=0))
                both = jnp.dot(
                    jnp.concatenate((high, low), axis=0), row_ref[parity, 0], preferred_element_type=F32
                )
                product = (
                    both[: 4 * PLANES]
                    + both[4 * PLANES :]
                    + jnp.dot(high, row_ref[parity, 1], preferred_element_type=F32)
                )
                sides = []
                for side in range(2):
                    real = product[2 * side * PLANES : (2 * side + 1) * PLANES]
                    imag = product[(2 * side + 1) * PLANES : (2 * side + 2) * PLANES]
                    sides.append(
                        (real[:, :LANES] - imag[:, LANES:], real[:, LANES:] + imag[:, :LANES])
                    )
                parts.append(sides)
            for part in range(2):
                even = [parts[0][side][part] for side in range(2)]
                odd = [parts[1][side][part] for side in range(2)]
                values = [jnp.where(lane < NX // 4, even[side], odd[side]) for side in range(2)]
                values.append(jnp.where(lane < LANES // 2, odd[0], pltpu.roll(odd[1], LANES // 2, 1)))
                for number, value in enumerate(values):
                    target[relative // 2, slot, number, pl.ds(part * planes_padded, planes_padded), :] = value[
                        :planes_padded
                    ]
            return carry

        lax.fori_loop(0, slots, rows, 0)


def finish_kernel(slots, planes, planes_padded, parts, refs):
    part_refs = refs[:parts]
    order_ref, first_ref, second_ref, third_ref, out_ref = refs[parts:]
    first = first_ref[...]
    second = second_ref[...]

    def plane_body(plane, carry):
        for part in range(2):
            values = []
            for number in range(3):
                at = pl.ds(number * 2 * planes_padded + part * planes_padded + plane, slots, stride=6 * planes_padded)
                total = part_refs[0][at, :]
                for ref in part_refs[1:]:
                    total = total + ref[at, :]
                values.append(total)
            main = jnp.concatenate(values[:2], axis=0)
            rest = jnp.concatenate((values[2], pltpu.roll(values[2], LANES // 2, 1)), axis=0)
            ordered = jnp.dot(
                jnp.concatenate(split(main) + split(rest), axis=1), order_ref[...], preferred_element_type=F32
            )
            out_ref[part, plane] = ordered * (second * third_ref[plane]) * first
        return carry

    lax.fori_loop(0, planes, plane_body, 0)


def on_device(samples, kernel, offsets, owners, tile_ids, deapod_first, deapod_second, deapod_third):
    grid_rows = lax.axis_size("gx")
    grid_cols = lax.axis_size("gy")
    blocks = samples.shape[0]
    block_width = samples.shape[2]
    assert block_width == LANES and blocks <= LANES
    tile_rows = NX // (TILE * grid_rows)
    tile_cols = NY // (TILE * grid_cols)
    tile_depth = NZ // TILE
    planes = deapod_third.shape[0]
    per_device = deapod_second.shape[0]
    slots = per_device // 2
    planes_padded = -(-planes // 8) * 8
    vmem = pl.BlockSpec(memory_space=pltpu.VMEM)
    smem = pl.BlockSpec(memory_space=pltpu.SMEM)
    params = pltpu.CompilerParams(vmem_limit_bytes=VMEM_LIMIT)

    owner = owners[:, 0]
    row = owner // grid_cols * tile_rows + tile_ids // (tile_cols * tile_depth)
    col = owner % grid_cols * tile_cols + tile_ids // tile_depth % tile_cols
    folds = NX // TILE // 2
    base = row % folds * (TILE * NY // TILE) + col
    phase = tile_ids % tile_depth + row // folds * tile_depth
    codes = (base * PHASES + phase).astype(F32)
    codes = jnp.pad(codes, (0, LANES - blocks))[None, :]

    tiles = pl.pallas_call(
        spread_kernel,
        out_shape=jax.ShapeDtypeStruct((blocks // 2 + 1, 2 * TILE, LANES), F32),
        in_specs=[vmem] * 4,
        out_specs=vmem,
        compiler_params=params,
        name="spread",
    )(samples, kernel, offsets, codes)

    gathered = lax.all_gather(tiles, "gy", axis=0, tiled=False)
    tile_codes = gathered[:, blocks // 2, 0, :blocks].astype(jnp.int32).reshape(-1)

    gx = lax.axis_index("gx").astype(jnp.int32)
    gy = lax.axis_index("gy")
    group = grid_rows
    matrices, phases = depth_tables(planes)
    matrix = lax.dynamic_index_in_dim(jnp.asarray(matrices), gy, 0, keepdims=False)
    phase_rows = lax.dynamic_index_in_dim(jnp.asarray(phases), gy, 0, keepdims=False)
    column = jnp.asarray(column_tables(grid_rows // group)[0])
    shape = jax.ShapeDtypeStruct((group // 2, slots, 3, 2 * planes_padded, LANES), F32)
    keep, send = pl.pallas_call(
        functools.partial(transform_kernel, group, planes_padded),
        out_shape=(shape, shape),
        in_specs=[smem, smem] + [vmem] * 5,
        out_specs=(vmem, vmem),
        scratch_shapes=[pltpu.VMEM((NX // 2 * NY, LANES), F32)],
        compiler_params=params,
        name="transform",
    )(gx.reshape(1), tile_codes, gathered, matrix, phase_rows, column, jnp.asarray(row_tables()))

    parts = [[keep[index] for index in range(group // 2)]]
    sent = [send[index] for index in range(group // 2)]
    bit = 1
    while True:
        swap = [(index, index ^ bit) for index in range(grid_rows)]
        arrived = [lax.ppermute(value, "gx", swap) for value in sent]
        parts.append(arrived)
        bit *= 2
        if bit == group:
            break
        width = len(parts[0])
        sent = [sum(layer[index] for layer in parts) for index in range(1, width, 2)]
        parts = [[layer[index] for index in range(0, width, 2)] for layer in parts]
    finals = [layer[0].reshape(slots * 6 * planes_padded, LANES) for layer in parts]

    def finish(*refs):
        finish_kernel(slots, planes, planes_padded, len(finals), refs)

    return pl.pallas_call(
        finish,
        out_shape=jax.ShapeDtypeStruct((2, planes, per_device, NX // 2), F32),
        in_specs=[vmem] * (len(finals) + 3) + [smem],
        out_specs=vmem,
        compiler_params=params,
        name="finish",
    )(*finals, jnp.asarray(order_tables()), deapod_first[None, :], deapod_second[:, None], deapod_third)


def solution(mesh):
    in_specs = (
        P(("gx", "gy"), None, None),
        P(("gx", "gy"), None, None, None),
        P(("gx", "gy"), None, None),
        P(("gx", "gy"), None),
        P(("gx", "gy")),
        P(),
        P("gx"),
        P("gy"),
    )
    out_specs = P(None, "gy", "gx", None)
    return jax.shard_map(
        on_device, mesh=mesh, in_specs=in_specs, out_specs=out_specs, check_vma=False
    )
```

time: 989 us -> 326 us (0.33); the launches traced: 974 us -> 323 us
  local copies, waits for them, and re-layouts: 411 us -> 10.2 us
  blocking collectives: 268 us -> 0 us
  matrix products: 220 us -> 0 us
  Pallas kernels: 0 us -> 178 us
  waiting for transfers between devices: 50.2 us -> 115 us
  other arithmetic: 18.6 us -> 4.24 us
  between operations: 0.81 us -> 13.4 us
    squeeze x6 -> x3, local copies, waits for them, and re-layouts: 275 us -> 6.46 us  [the longest x1 3.59 us: on_device(): sent = [send[index] for index in range(group // 2)]]
    all_to_all x2 -> x0, blocking collectives: 268 us -> none  [the longest x1 211 us: on_device(): lax.all_to_all(along_z, 'gy', split_axis=1, concat_axis=3, tiled=True)]
    dot_general x14 -> x0, matrix products: 220 us -> none  [the longest x1 125 us: spread(): jnp.einsum('nijs,ncls->ncijl', plane_weight, depth_weight, precision=lax....]
    pallas_call x0 -> x3, Pallas kernels: none -> 178 us  [the longest x1 160 us: on_device(): pl.pallas_call(functools.partial(transform_kernel, group, planes_padded),...]
    all_gather x0 -> x1, waiting for transfers between devices: none -> 71.7 us  [on_device(): gathered = lax.all_gather(tiles, 'gy', axis=0, tiled=False)]
    all_to_all x1 -> x0, waiting for transfers between devices: 50.2 us -> none  [on_device(): lax.all_to_all(outbox, ('gx', 'gy'), split_axis=0, concat_axis=0, tiled=T...]
    ppermute x0 -> x3, waiting for transfers between devices: none -> 43.2 us  [on_device(): arrived = [lax.ppermute(value, 'gx', swap) for value in sent]]
    slice x8 -> x1, local copies, waits for them, and re-layouts: 37.7 us -> 1.31 us  [on_device(): parts = [[keep[index] for index in range(group // 2)]]]
  transfers between devices with their start and end apart: 1 -> 4, of which waited for: 1 -> 3; matrix products, arithmetic and copies ran while one was open for 0% -> 2% of each run, Pallas kernels for 0% -> 0%
where the time goes in v1:
time: 326 us; the launch traced here: 323 us
  Pallas kernels  178 us (55%)
  waiting for transfers between devices  115 us (35%)
  between operations  13.4 us (4%)
  local copies, waits for them, and re-layouts  10.2 us (3%)
  other arithmetic  4.24 us (1%)
    pallas_call x1, Pallas kernels, on_device(): pl.pallas_call(functools.partial(transform_kernel, group, planes_padded),...  160 us
    all_gather x1, waiting for transfers between devices, on_device(): gathered = lax.all_gather(tiles, 'gy', axis=0, tiled=False)  71.7 us
    ppermute x3, waiting for transfers between devices, on_device(): arrived = [lax.ppermute(value, 'gx', swap) for value in sent]  43.2 us
    pallas_call x1, Pallas kernels, on_device(): pl.pallas_call(finish, out_shape=jax.ShapeDtypeStruct((2, planes, per_dev...  9.41 us
    pallas_call x1, Pallas kernels, on_device(): pl.pallas_call(spread_kernel, out_shape=jax.ShapeDtypeStruct((blocks // 2...  8.27 us
  transfers between devices with their start and end apart: 4, of which 3 were waited for; matrix products, arithmetic and copies ran while one was open for 2% of the time, Pallas kernels for 0%

profile of v1, /device:TPU:16, one launch (start us, length us, event | category | flops | bytes accessed | tf_op | source)
XLA Modules:
  0.0 322.9 jit_solution(6351747134112827500)
XLA Ops:
  6.5 0.0 all-gather.3.cloned.1.call-start
  6.5 1.8 copy.16.offsets_ref
  8.3 1.3 convert_bitcast_fusion.codes_ref
  9.6 8.3 %spread.1 = f32[65,16,128]{2,1,0:T(8,128)} custom-call(f32[128,2,128]{2,1,0:T(2,128)} %samples_ref.1, f32[128,3,4,128]{3,2,1,0:T(4,128)} %kernel_ref.1, s32[128,3,128]{2,1,0:T(4,128)} %copy.16.offsets_ref, f32[1,128]{1,0:T(1,128)} %convert_bitcast_fusion.codes_ref), custom_call_target="tpu_custom_call" | custom-call | tf_op jit(solution)/shard_map/spread/pallas_call | solution.py:314
  17.9 0.0 all-gather.3.cloned.1.call-update
  17.9 1.3 dynamic-slice_bitcast_fusion.1.depth_ref
  19.2 1.5 dynamic-slice_bitcast_fusion.phases_ref
  20.8 71.7 %all-gather.3.cloned.1.call-done = f32[520,16,128]{2,1,0:T(8,128)} async-done(((f32[65,16,128]{2,1,0:T(8,128)}), f32[520,16,128]{2,1,0:T(8,128)}) %all-gather.3.cloned.1.call-update) | async-done | bytes 4259856 | tf_op jit(solution)/shard_map/all_gather | solution.py:323
  92.5 1.4 slice_convert_fusion
  93.8 160.4 %transform.1 = (f32[2,24,3,48,128]{4,3,2,1,0:T(8,128)}, f32[2,24,3,48,128]{4,3,2,1,0:T(8,128)}) custom-call(s32[1]{0:T(128)} %bitcast.place_ref, s32[1024]{0:T(1024)} %bitcast.38, f32[8,65,16,128]{3,2,1,0:T(8,128)} %bitcast.37, bf16[48,256]{1,0:T(8,128)(2,1)} %dynamic-slice_bitcast_fusion.1.depth_ref, f32[2,96,128]{2,1,0:T(8,128)} %dynamic-slice_bitcast_fusion.phases_ref, ...), custom_call_target="tpu_custom_call" | custom-call | tf_op jit(solution)/shard_map/transform/pallas_call | solution.py:334
  254.2 0.0 copy-start
  254.2 3.6 %slice_bitcast_fusion = (f32[24,3,48,128]{3,2,1,0:T(8,128)S(1)}, f32[24,3,48,128]{3,2,1,0:T(8,128)}) fusion(f32[2,24,3,48,128]{4,3,2,1,0:T(8,128)} %get-tuple-element.8), kind=kLoop, calls=%fused_computation.1 | loop fusion | bytes 7077888 | tf_op jit(solution)/shard_map/squeeze | solution.py:345
  257.8 0.0 collective-permute-start.1
  257.8 0.5 collective-permute-start
  258.4 5.7 %collective-permute-done.1 = f32[24,3,48,128]{3,2,1,0:T(8,128)S(1)} collective-permute-done((f32[24,3,48,128]{3,2,1,0:T(8,128)S(1)}, f32[24,3,48,128]{3,2,1,0:T(8,128)S(1)}, u32[]{:S(2)}, u32[]{:S(2)}) %collective-permute-start.1) | collective-permute-done | bytes 1769504 | tf_op jit(solution)/shard_map/ppermute | solution.py:349
  264.0 0.0 copy-done
  264.0 1.6 bitcast_add_fusion
  265.6 1.5 collective-permute-start.2
  267.1 0.0 copy-done.1
  267.1 0.7 copy.17.refs_5_
  267.8 1.3 slice.16
  269.1 0.0 collective-permute-done
  269.1 37.5 %collective-permute-done.2 = f32[24,3,48,128]{3,2,1,0:T(8,128)} collective-permute-done((f32[24,3,48,128]{3,2,1,0:T(8,128)}, f32[24,3,48,128]{3,2,1,0:T(8,128)}, u32[]{:S(2)}, u32[]{:S(2)}) %collective-permute-start.2) | collective-permute-done | bytes 1769504 | tf_op jit(solution)/shard_map/ppermute | solution.py:349
  306.6 9.4 %finish.1 = f32[2,24,48,192]{3,2,1,0:T(8,128)} custom-call(f32[3456,128]{1,0:T(8,128)} %bitcast.35, f32[3456,128]{1,0:T(8,128)} %bitcast.9.refs_1_, f32[3456,128]{1,0:T(8,128)} %bitcast.12.refs_2_, bf16[512,192]{1,0:T(8,128)(2,1)} %constant.105.clone.refs_3_, f32[1,192]{1,0:T(1,128)} %bitcast.39, f32[48,1]{1,0:T(8,128)} %copy.17.refs_5_, f32[24]{0:T(128)} %refs_6_.1), custom_call_target="tpu_custom_call" | custom-call | tf_op jit(solution)/shard_map/finish/pallas_call | solution.py:362
  (1 shorter events, 0.0 us)
Async XLA Ops:
  6.5 85.9 %all-gather.3.cloned.1.call-start = ((), (), s32[]{:S(2)}) async-start(), calls=%async_computation | async-start | bytes 4792320 | tf_op jit(solution)/shard_map/all_gather | solution.py:323
  254.2 9.8 %copy-start = (f32[2,24,3,48,128]{4,3,2,1,0:T(8,128)S(1)}, f32[2,24,3,48,128]{4,3,2,1,0:T(8,128)}, u32[]{:S(2)}) copy-start(f32[2,24,3,48,128]{4,3,2,1,0:T(8,128)} %get-tuple-element.7) | copy-start | bytes 10616836
  257.8 6.2 %collective-permute-start.1 = (f32[24,3,48,128]{3,2,1,0:T(8,128)S(1)}, f32[24,3,48,128]{3,2,1,0:T(8,128)S(1)}, u32[]{:S(2)}, u32[]{:S(2)}) collective-permute-start(f32[24,3,48,128]{3,2,1,0:T(8,128)S(1)} %get-tuple-element.9), channel_id=1, source_target_pairs={{0,8},{8,0},{16,24},{24,16},{1,9},{9,1},{17,25},{25,17},{2,10},{10... | collective-permute-start | bytes 5308424 | tf_op jit(solution)/shard_map/ppermute | solution.py:349
  257.8 11.3 %collective-permute-start = (f32[24,3,48,128]{3,2,1,0:T(8,128)}, f32[24,3,48,128]{3,2,1,0:T(8,128)}, u32[]{:S(2)}, u32[]{:S(2)}) collective-permute-start(f32[24,3,48,128]{3,2,1,0:T(8,128)} %get-tuple-element.10), channel_id=1, source_target_pairs={{0,8},{8,0},{16,24},{24,16},{1,9},{9,1},{17,25},{25,17},{2,10},{10... | collective-permute-start | bytes 5308424 | tf_op jit(solution)/shard_map/ppermute | solution.py:349
  264.0 3.1 copy-start.1
  265.6 41.0 %collective-permute-start.2 = (f32[24,3,48,128]{3,2,1,0:T(8,128)}, f32[24,3,48,128]{3,2,1,0:T(8,128)}, u32[]{:S(2)}, u32[]{:S(2)}) collective-permute-start(f32[24,3,48,128]{3,2,1,0:T(8,128)} %bitcast_add_fusion), channel_id=1, source_target_pairs={{0,16},{8,24},{16,0},{24,8},{1,17},{9,25},{17,1},{25,9},{2,18},{10... | collective-permute-start | bytes 5308424 | tf_op jit(solution)/shard_map/ppermute | solution.py:349
Sparse Core Ops, SparseCore 0:
  18.0 74.4 all-gather.2

commit v2 on v1

v2 whole, which is shorter than its diff:
```python
import functools
import math

import jax
import jax.numpy as jnp
import ml_dtypes
import numpy as np
from jax import lax
from jax.experimental import pallas as pl
from jax.experimental.pallas import tpu as pltpu
from jax.sharding import PartitionSpec as P

NX = 384
NY = 384
NZ = 384
TILE = 8
LANES = 128
PLANES = 32
PHASES = 128
BF16 = jnp.bfloat16
F32 = jnp.float32
VMEM_LIMIT = 60 * 1024 * 1024


def halves(array):
    high = array.astype(ml_dtypes.bfloat16)
    low = (array - high.astype(np.float64)).astype(ml_dtypes.bfloat16)
    return high, low


def split(value):
    high = value.astype(BF16)
    return high, (value - high.astype(F32)).astype(BF16)


def waves(freq, position, length):
    steps = np.mod(freq[:, None] * position[None, :], length)
    phase = 2.0 * math.pi * steps / length
    return np.cos(phase), np.sin(phase)


def depth_tables(planes):
    matrices, phases = [], []
    lane_part = np.arange(LANES) // 64
    lane_odd = np.arange(LANES) // 32 % 2
    lane_plane = np.arange(LANES) % 32
    used = (lane_plane < planes).astype(np.float64)
    for index in range(NZ // 2 // planes):
        position = index * planes + lane_plane - NZ // 4
        cos, sin = waves(np.arange(TILE) - NZ // 2, position, NZ)
        cos, sin = cos * used / math.sqrt(NZ), sin * used / math.sqrt(NZ)
        real = np.where(lane_part == 0, cos, sin)
        imag = np.where(lane_part == 0, -sin, cos)
        plain = np.concatenate((real, imag))
        turned = np.concatenate((-np.where(lane_part == 0, sin, -cos), -np.where(lane_part == 0, cos, sin)))
        high, low = halves(np.concatenate((plain, turned), axis=1))
        matrices.append(np.concatenate((high, high, low), axis=0))
        cos, sin = waves(np.arange(NZ // TILE), position, NZ // TILE)
        sign = np.where(lane_odd == 1, -1.0, 1.0)[None, :]
        phases.append(np.stack((np.concatenate((cos, cos * sign)), np.concatenate((sin, sin * sign)))))
    return np.stack(matrices), np.stack(phases).astype(np.float32)


def padded_rows(per_device):
    return -(-(per_device // 2) // TILE) * TILE


def column_tables(devices, per_device):
    half = NY // 2
    rows = padded_rows(per_device)
    place = np.arange(rows)
    slot = place // 8 * 4 + place % 4
    local = 2 * slot + place % 8 // 4 * (per_device // 2)
    used = (slot < per_device // 4).astype(np.float64)[:, None]
    out = []
    for parity in range(2):
        cos_parts, sin_parts = [], []
        for device in range(devices):
            cos, sin = waves(device * per_device + local + parity - NY // 4, np.arange(half) - half, NY)
            cos_parts.append(cos * used)
            sin_parts.append(sin * used)
        out.append(np.concatenate(halves(np.concatenate(cos_parts + sin_parts) / math.sqrt(NY))))
    return np.stack(out)


def row_tables():
    half = NX // 2
    quarter = NX // 4
    out = []
    for parity in range(2):
        position = 2 * np.arange(quarter) + parity - NX // 4
        cos, sin = waves(np.arange(half) - half, position, NX)
        table = np.zeros((half, 2 * LANES))
        lanes = (np.arange(quarter) + parity * quarter) % LANES
        table[:, lanes] = cos / math.sqrt(NX)
        table[:, LANES + lanes] = sin / math.sqrt(NX)
        out.append(np.stack(halves(table)))
    return np.stack(out)


def order_tables():
    first = np.zeros((LANES, NX // 2))
    second = np.zeros((LANES, NX // 2))
    quarter = NX // 4
    for m1 in range(NX // 2):
        place = m1 // 2 + m1 % 2 * quarter
        if place < LANES:
            first[place, m1] = 1.0
        else:
            second[place - LANES, m1] = 1.0
    return np.concatenate((first, first, second, second)).astype(ml_dtypes.bfloat16)


def spread_kernel(samples_ref, kernel_ref, offsets_ref, codes_ref, out_ref):
    blocks = samples_ref.shape[0]
    taps = kernel_ref.shape[2]
    cell = lax.broadcasted_iota(jnp.int32, (TILE, LANES), 0)
    left = lax.broadcasted_iota(jnp.int32, (2 * TILE, LANES), 1) < LANES // 2

    def weights(block):
        placed = []
        for dim in range(3):
            shifted = cell - offsets_ref[block, pl.ds(dim, 1), :]
            value = jnp.zeros((TILE, LANES), F32)
            for tap in range(taps):
                value = jnp.where(shifted == tap, kernel_ref[block, dim, pl.ds(tap, 1), :], value)
            placed.append(value)
        plane = jnp.concatenate([placed[0][i : i + 1] * placed[1] for i in range(TILE)], axis=0)
        depth = jnp.concatenate([samples_ref[block, pl.ds(c, 1), :] * placed[2] for c in range(2)], axis=0)
        return depth, plane

    def pair_body(pair, carry):
        depth_a, plane_a = weights(2 * pair)
        depth_b, plane_b = weights(2 * pair + 1)
        depth_high, depth_low = split(jnp.concatenate((depth_a, depth_b), axis=0))
        plane_high, plane_low = split(jnp.concatenate((plane_a, plane_b), axis=0))
        piece = lax.dot_general(
            jnp.concatenate((depth_high, depth_low, depth_high), axis=1),
            jnp.concatenate((plane_high, plane_high, plane_low), axis=1),
            (((1,), (1,)), ((), ())),
            preferred_element_type=F32,
        )
        out_ref[pair] = jnp.where(left, piece[: 2 * TILE], piece[2 * TILE :])
        return carry

    lax.fori_loop(0, blocks // 2, pair_body, 0, unroll=2)
    out_ref[blocks // 2] = jnp.broadcast_to(codes_ref[...], (2 * TILE, LANES))


def tiles_kernel(codes_ref, tiles_ref, depth_ref, phases_ref, column_ref, out_ref, acc_ref, even_ref, odd_ref):
    half = NX // 2
    stride = NY
    sources = tiles_ref.shape[0]
    pairs = tiles_ref.shape[1] - 1
    batch = 8
    assert pairs % (2 * batch) == 0
    batches = pairs // batch
    rows = column_ref.shape[1] // 4
    width = out_ref.shape[0]

    def spectrum(source, number, to_ref):
        tiles = jnp.concatenate([tiles_ref[source, number * batch + index] for index in range(batch)], axis=1)
        high, low = split(tiles)
        to_ref[...] = lax.dot_general(
            jnp.concatenate((high, low, high), axis=0),
            depth_ref[...],
            (((0,), (0,)), ((), ())),
            preferred_element_type=F32,
        )

    def accumulate(source, number, from_ref):
        for tile in range(2 * batch):
            code = codes_ref[(source * batches + number) * 2 * batch + tile]
            base = lax.shift_right_logical(code, 7)
            phase = jnp.bitwise_and(code, PHASES - 1)
            cos = phases_ref[0, pl.ds(phase, 1), :]
            sin = phases_ref[1, pl.ds(phase, 1), :]
            for i in range(TILE):
                row = tile * TILE * TILE + i * TILE
                value = from_ref[row : row + TILE, :LANES] * cos + from_ref[row : row + TILE, LANES:] * sin
                at = pl.ds(pl.multiple_of(base * TILE + i * stride, TILE), TILE)
                acc_ref[at, :] = acc_ref[at, :] + value

    @pl.when(pl.program_id(0) == 0)
    def _():
        def clear(step, carry):
            acc_ref[pl.ds(pl.multiple_of(step * stride, stride), stride), :] = jnp.zeros((stride, LANES), F32)
            return carry

        lax.fori_loop(0, half, clear, 0)
        spectrum(0, 0, even_ref)

        def add_pair(step, carry):
            first = 2 * step
            source, number = first // batches, first % batches
            spectrum(source, number + 1, odd_ref)
            accumulate(source, number, even_ref)
            later = jnp.minimum(first + 2, sources * batches - 2)
            spectrum(later // batches, later % batches, even_ref)
            accumulate(source, number + 1, odd_ref)
            return carry

        lax.fori_loop(0, sources * batches // 2, add_pair, 0)

    turn = jnp.where(lax.broadcasted_iota(jnp.int32, (rows, LANES), 1) < LANES // 2, -1.0, 1.0)
    origin = pl.program_id(0) * width

    def columns(step, carry):
        folded = ([], [])
        for side in range(2):
            start = pl.multiple_of((origin + 2 * step + side) * stride, stride)
            lower = acc_ref[pl.ds(start, NY // 2), :]
            upper = acc_ref[pl.ds(start + NY // 2, NY // 2), :]
            folded[0].append(lower + upper)
            folded[1].append(lower - upper)
        for parity in range(2):
            high, low = split(jnp.concatenate(folded[parity], axis=1))
            both = jnp.dot(column_ref[parity], high, preferred_element_type=F32)
            rest = jnp.dot(column_ref[parity, : 2 * rows], low, preferred_element_type=F32)
            product = both[: 2 * rows] + both[2 * rows :] + rest
            for side in range(2):
                lanes = slice(side * LANES, (side + 1) * LANES)
                out_ref[2 * step + side, parity * rows : (parity + 1) * rows, :] = (
                    product[:rows, lanes] + pltpu.roll(product[rows:, lanes], LANES // 2, 1) * turn
                )
        return carry

    lax.fori_loop(0, width // 2, columns, 0, unroll=2)


def rows_kernel(planes_padded, place_ref, in_ref, row_ref, out_ref):
    half = NX // 2
    parity = pl.program_id(1)
    lane = lax.broadcasted_iota(jnp.int32, (PLANES, LANES), 1)
    flat = in_ref.reshape(half * TILE, LANES)
    turned = [flat[pl.ds(row, half, stride=TILE), :].T for row in range(TILE)]
    parts = []
    for odd in range(2):
        at = odd * PLANES
        stacked = [value[part * 64 + at : part * 64 + at + PLANES] for value in turned for part in range(2)]
        high, low = split(jnp.concatenate(stacked, axis=0))
        count = high.shape[0]
        both = jnp.dot(jnp.concatenate((high, low), axis=0), row_ref[odd, 0], preferred_element_type=F32)
        product = both[:count] + both[count:] + jnp.dot(high, row_ref[odd, 1], preferred_element_type=F32)
        sides = []
        for row in range(TILE):
            real = product[2 * row * PLANES : (2 * row + 1) * PLANES]
            imag = product[(2 * row + 1) * PLANES : (2 * row + 2) * PLANES]
            sides.append((real[:, :LANES] - imag[:, LANES:], real[:, LANES:] + imag[:, :LANES]))
        parts.append(sides)
    for slot in range(TILE // 2):
        for part in range(2):
            even = [parts[0][slot + side * TILE // 2][part] for side in range(2)]
            odd = [parts[1][slot + side * TILE // 2][part] for side in range(2)]
            values = [jnp.where(lane < NX // 4, even[side], odd[side]) for side in range(2)]
            values.append(jnp.where(lane < LANES // 2, odd[0], pltpu.roll(odd[1], LANES // 2, 1)))
            for number, value in enumerate(values):
                out_ref[2 * slot + parity, number, part * planes_padded : (part + 1) * planes_padded, :] = value[
                    :planes_padded
                ]


def finish_kernel(slots, parts, refs):
    part_refs = refs[:parts]
    order_ref, first_ref, second_ref, third_ref, out_ref = refs[parts:]
    first = first_ref[...]
    second = second_ref[...]
    flats = [ref.reshape(ref.shape[0] * 6 * TILE, LANES) for ref in part_refs]
    for part in range(2):
        mains, rests = [], []
        for plane in range(TILE):
            values = []
            for number in range(3):
                at = pl.ds((number * 2 + part) * TILE + plane, slots, stride=6 * TILE)
                total = flats[0][at, :]
                for flat in flats[1:]:
                    total = total + flat[at, :]
                values.append(total)
            mains += values[:2]
            rests += [values[2], pltpu.roll(values[2], LANES // 2, 1)]
        main = split(jnp.concatenate(mains, axis=0))
        rest = split(jnp.concatenate(rests, axis=0))
        ordered = jnp.dot(jnp.concatenate(main + rest, axis=1), order_ref[...], preferred_element_type=F32)
        for plane in range(TILE):
            third = third_ref[pl.program_id(0) * TILE + plane]
            out_ref[part, plane] = ordered[plane * 2 * slots : (plane + 1) * 2 * slots] * (second * third) * first


def on_device(samples, kernel, offsets, owners, tile_ids, deapod_first, deapod_second, deapod_third):
    grid_rows = lax.axis_size("gx")
    grid_cols = lax.axis_size("gy")
    blocks = samples.shape[0]
    block_width = samples.shape[2]
    assert block_width == LANES and blocks <= LANES
    tile_rows = NX // (TILE * grid_rows)
    tile_cols = NY // (TILE * grid_cols)
    tile_depth = NZ // TILE
    planes = deapod_third.shape[0]
    per_device = deapod_second.shape[0]
    rows = padded_rows(per_device)
    planes_padded = -(-planes // 8) * 8
    vmem = pl.BlockSpec(memory_space=pltpu.VMEM)
    params = pltpu.CompilerParams(vmem_limit_bytes=VMEM_LIMIT)

    owner = owners[:, 0]
    row = owner // grid_cols * tile_rows + tile_ids // (tile_cols * tile_depth)
    col = owner % grid_cols * tile_cols + tile_ids // tile_depth % tile_cols
    folds = NX // TILE // 2
    base = row % folds * NY + col
    phase = tile_ids % tile_depth + row // folds * tile_depth
    codes = (base * PHASES + phase).astype(F32)
    codes = jnp.pad(codes, (0, LANES - blocks))[None, :]

    tiles = pl.pallas_call(
        spread_kernel,
        out_shape=jax.ShapeDtypeStruct((blocks // 2 + 1, 2 * TILE, LANES), F32),
        in_specs=[vmem] * 4,
        out_specs=vmem,
        compiler_params=params,
        name="spread",
    )(samples, kernel, offsets, codes)

    gathered = lax.all_gather(tiles, "gy", axis=0, tiled=False)
    tile_codes = gathered[:, blocks // 2, 0, :blocks].astype(jnp.int32).reshape(-1)

    place = lax.axis_index("gx").astype(jnp.int32).reshape(1)
    gy = lax.axis_index("gy")
    matrices, phases = depth_tables(planes)
    matrix = lax.dynamic_index_in_dim(jnp.asarray(matrices), gy, 0, keepdims=False)
    phase_rows = lax.dynamic_index_in_dim(jnp.asarray(phases), gy, 0, keepdims=False)
    column = jnp.asarray(column_tables(grid_rows, per_device))

    def whole(shape):
        return pl.BlockSpec(shape, lambda step: (0,) * len(shape), pipeline_mode=pl.Buffered(1))

    half = NX // 2
    width = 16
    kept = 2 * grid_rows * rows
    spectra = pltpu.VMEM((16 * TILE * TILE, 2 * LANES), F32)
    columns = pl.pallas_call(
        tiles_kernel,
        grid=(half // width,),
        out_shape=jax.ShapeDtypeStruct((half, kept, LANES), F32),
        in_specs=[pl.BlockSpec(memory_space=pltpu.SMEM)]
        + [whole(array.shape) for array in (gathered, matrix, phase_rows, column)],
        out_specs=pl.BlockSpec((width, kept, LANES), lambda step: (step, 0, 0)),
        scratch_shapes=[pltpu.VMEM((half * NY, LANES), F32), spectra, spectra],
        compiler_params=params,
        name="tiles",
    )(tile_codes, gathered, matrix, phase_rows, column)

    row_table = jnp.asarray(row_tables())
    slots = rows
    part_shape = (slots, 3, 2 * planes_padded, LANES)

    def rows_for(relative):
        def block(step, parity, place_ref):
            device = jnp.bitwise_xor(place_ref[0], relative)
            return (0, (parity * grid_rows + device) * (rows // TILE) + step, 0)

        return pl.pallas_call(
            functools.partial(rows_kernel, planes_padded),
            grid_spec=pltpu.PrefetchScalarGridSpec(
                num_scalar_prefetch=1,
                grid=(rows // TILE, 2),
                in_specs=[
                    pl.BlockSpec((half, TILE, LANES), block),
                    pl.BlockSpec(row_table.shape, lambda step, parity, place_ref: (0, 0, 0, 0)),
                ],
                out_specs=pl.BlockSpec((TILE,) + part_shape[1:], lambda step, parity, place_ref: (step, 0, 0, 0)),
            ),
            out_shape=jax.ShapeDtypeStruct(part_shape, F32),
            compiler_params=params,
            cost_estimate=pl.CostEstimate(
                flops=2 * 3 * slots * 2 * LANES * half * 2 * LANES,
                bytes_accessed=4 * (half * 2 * slots * LANES + math.prod(part_shape)),
                transcendentals=0,
            ),
            name="rows",
        )(place, columns, row_table)

    def sums(relatives, bit):
        if bit == 0:
            return [rows_for(relatives)]
        swap = [(index, index ^ bit) for index in range(grid_rows)]
        sent = sum(sums(relatives | bit, bit // 2))
        arrived = lax.ppermute(sent, "gx", swap)
        return sums(relatives, bit // 2) + [arrived]

    finals = sums(0, grid_rows // 2)
    finals = [layer.reshape(slots, 3, 2, planes_padded, LANES) for layer in finals]

    def finish(*refs):
        finish_kernel(per_device // 2, len(finals), refs)

    def shared(shape):
        return pl.BlockSpec(shape, lambda step: (0,) * len(shape))

    return pl.pallas_call(
        finish,
        grid=(planes_padded // TILE,),
        out_shape=jax.ShapeDtypeStruct((2, planes, per_device, NX // 2), F32),
        in_specs=[pl.BlockSpec((slots, 3, 2, TILE, LANES), lambda step: (0, 0, 0, step, 0))] * len(finals)
        + [shared((4 * LANES, NX // 2)), shared((1, NX // 2)), shared((per_device, 1)), pl.BlockSpec(memory_space=pltpu.SMEM)],
        out_specs=pl.BlockSpec((2, TILE, per_device, NX // 2), lambda step: (0, step, 0, 0)),
        compiler_params=params,
        name="finish",
    )(
        *finals,
        jnp.asarray(order_tables()),
        deapod_first[None, :],
        deapod_second[:, None],
        jnp.pad(deapod_third, (0, planes_padded - planes)),
    )


def solution(mesh):
    in_specs = (
        P(("gx", "gy"), None, None),
        P(("gx", "gy"), None, None, None),
        P(("gx", "gy"), None, None),
        P(("gx", "gy"), None),
        P(("gx", "gy")),
        P(),
        P("gx"),
        P("gy"),
    )
    out_specs = P(None, "gy", "gx", None)
    return jax.shard_map(
        on_device, mesh=mesh, in_specs=in_specs, out_specs=out_specs, check_vma=False
    )
```

time: 326 us -> 230 us (0.71)
  Pallas kernels: 178 us -> 97.2 us
  waiting for transfers between devices: 115 us -> 102 us
  local copies, waits for them, and re-layouts: 10.2 us -> 6.55 us
    pallas_call x2 -> x6, Pallas kernels: 170 us -> 88.9 us  [the longest x1 50.5 us: on_device(): pl.pallas_call(tiles_kernel, grid=(half // width,), out_shape=jax.ShapeDt...]
    ppermute x3, waiting for transfers between devices: 43.2 us -> 30.5 us  [sums(): arrived = lax.ppermute(sent, 'gx', swap)]
    squeeze x1 -> x0, local copies, waits for them, and re-layouts: 3.59 us -> none  [on_device(): sent = [send[index] for index in range(group // 2)]]
  transfers between devices with their start and end apart: 4 -> 4, of which waited for: 3 -> 2; matrix products, arithmetic and copies ran while one was open for 2% -> 3% of each run, Pallas kernels for 0% -> 11%
where the time goes in v2:
time: 230 us; the launch traced here: 227 us
  waiting for transfers between devices  102 us (44%)
  Pallas kernels  97.2 us (42%)
  between operations  13.4 us (6%)
  local copies, waits for them, and re-layouts  6.55 us (3%)
  other arithmetic  5.51 us (2%)
    all_gather x1, waiting for transfers between devices, on_device(): gathered = lax.all_gather(tiles, 'gy', axis=0, tiled=False)  71.7 us
    pallas_call x1, Pallas kernels, on_device(): pl.pallas_call(tiles_kernel, grid=(half // width,), out_shape=jax.ShapeDt...  50.5 us
    pallas_call x4, Pallas kernels, rows_for(): pl.pallas_call(functools.partial(rows_kernel, planes_padded), grid_spec=p...  32.5 us
    ppermute x3, waiting for transfers between devices, sums(): arrived = lax.ppermute(sent, 'gx', swap)  30.5 us
    pallas_call x1, Pallas kernels, on_device(): pl.pallas_call(spread_kernel, out_shape=jax.ShapeDtypeStruct((blocks // 2...  8.27 us
    pallas_call x1, Pallas kernels, on_device(): pl.pallas_call(finish, grid=(planes_padded // TILE,), out_shape=jax.Shape...  5.98 us
  transfers between devices with their start and end apart: 4, of which 2 were waited for; matrix products, arithmetic and copies ran while one was open for 3% of the time, Pallas kernels for 11%

profile of v2, /device:TPU:16, one launch (start us, length us, event | category | flops | bytes accessed | tf_op | source)
XLA Modules:
  0.0 226.8 jit_solution(2253534537761934436)
XLA Ops:
  6.5 0.0 all-gather.3.cloned.1.call-start
  6.5 1.8 copy.16.offsets_ref
  8.3 1.2 convert_bitcast_fusion.codes_ref
  9.5 8.3 %spread.1 = f32[65,16,128]{2,1,0:T(8,128)} custom-call(f32[128,2,128]{2,1,0:T(2,128)} %samples_ref.1, f32[128,3,4,128]{3,2,1,0:T(4,128)} %kernel_ref.1, s32[128,3,128]{2,1,0:T(4,128)} %copy.16.offsets_ref, f32[1,128]{1,0:T(1,128)} %convert_bitcast_fusion.codes_ref), custom_call_target="tpu_custom_call" | custom-call | tf_op jit(solution)/shard_map/spread/pallas_call | solution.py:314
  17.8 0.0 all-gather.3.cloned.1.call-update
  17.8 1.3 dynamic-slice_bitcast_fusion.1.depth_ref
  19.2 1.5 dynamic-slice_bitcast_fusion.phases_ref
  20.7 71.7 %all-gather.3.cloned.1.call-done = f32[520,16,128]{2,1,0:T(8,128)} async-done(((f32[65,16,128]{2,1,0:T(8,128)}), f32[520,16,128]{2,1,0:T(8,128)}) %all-gather.3.cloned.1.call-update) | async-done | bytes 4259856 | tf_op jit(solution)/shard_map/all_gather | solution.py:323
  92.4 1.4 slice_convert_fusion
  93.8 50.5 %tiles.1.in_ref = f32[192,192,128]{2,1,0:T(8,128)} custom-call(s32[1024]{0:T(1024)} %bitcast.34, f32[8,65,16,128]{3,2,1,0:T(8,128)} %bitcast.31, bf16[48,256]{1,0:T(8,128)(2,1)} %dynamic-slice_bitcast_fusion.1.depth_ref, f32[2,96,128]{2,1,0:T(8,128)} %dynamic-slice_bitcast_fusion.phases_ref, bf16[2,384,192]{2,1,0:T(8,128)(2,1)} %constant.103.clone.column_ref), custom_call_target="tpu_custom_call" | custom-call | tf_op jit(solution)/shard_map/tiles/pallas_call | solution.py:340
  144.2 8.1 %rows.7 = f32[24,3,48,128]{3,2,1,0:T(8,128)} custom-call(s32[1]{0:T(128)} %bitcast.place_ref, f32[192,192,128]{2,1,0:T(8,128)} %tiles.1.in_ref, bf16[2,2,192,256]{3,2,1,0:T(8,128)(2,1)} %constant.104.clone.row_ref), custom_call_target="tpu_custom_call" | custom-call | flops 1811939328 | bytes 6488064 | tf_op jit(solution)/shard_map/rows/pallas_call | solution.py:361
  152.3 0.0 collective-permute-start.1
  152.3 8.1 %rows.5 = f32[24,3,48,128]{3,2,1,0:T(8,128)} custom-call(s32[1]{0:T(128)} %bitcast.place_ref, f32[192,192,128]{2,1,0:T(8,128)} %tiles.1.in_ref, bf16[2,2,192,256]{3,2,1,0:T(8,128)(2,1)} %constant.104.clone.row_ref), custom_call_target="tpu_custom_call" | custom-call | flops 1811939328 | bytes 6488064 | tf_op jit(solution)/shard_map/rows/pallas_call | solution.py:361
  160.4 0.5 collective-permute-start
  160.9 8.1 %rows.6 = f32[24,3,48,128]{3,2,1,0:T(8,128)} custom-call(s32[1]{0:T(128)} %bitcast.place_ref, f32[192,192,128]{2,1,0:T(8,128)} %tiles.1.in_ref, bf16[2,2,192,256]{3,2,1,0:T(8,128)(2,1)} %constant.104.clone.row_ref), custom_call_target="tpu_custom_call" | custom-call | flops 1811939328 | bytes 6488064 | tf_op jit(solution)/shard_map/rows/pallas_call | solution.py:361
  169.1 0.0 collective-permute-done.1
  169.1 2.9 %add.56 = f32[24,3,48,128]{3,2,1,0:T(8,128)} add(f32[24,3,48,128]{3,2,1,0:T(8,128)} %rows.6, f32[24,3,48,128]{3,2,1,0:T(8,128)S(1)} %collective-permute-done.1) | non-fusion elementwise | flops 442368 | bytes 5308416 | tf_op jit(solution)/shard_map/add | solution.py:386
  172.0 1.4 collective-permute-start.2
  173.4 0.7 copy.17.refs_5_
  174.1 8.1 %rows.4 = f32[24,3,48,128]{3,2,1,0:T(8,128)} custom-call(s32[1]{0:T(128)} %bitcast.place_ref, f32[192,192,128]{2,1,0:T(8,128)} %tiles.1.in_ref, bf16[2,2,192,256]{3,2,1,0:T(8,128)(2,1)} %constant.104.clone.row_ref), custom_call_target="tpu_custom_call" | custom-call | flops 1811939328 | bytes 6488064 | tf_op jit(solution)/shard_map/rows/pallas_call | solution.py:361
  182.2 0.0 collective-permute-done
  182.3 30.5 %collective-permute-done.2 = f32[24,3,48,128]{3,2,1,0:T(8,128)S(1)} collective-permute-done((f32[24,3,48,128]{3,2,1,0:T(8,128)}, f32[24,3,48,128]{3,2,1,0:T(8,128)S(1)}, u32[]{:S(2)}, u32[]{:S(2)}) %collective-permute-start.2) | collective-permute-done | bytes 1769504 | tf_op jit(solution)/shard_map/ppermute | solution.py:387
  212.7 1.2 copy-done.1
  213.9 6.0 %finish.1 = f32[2,24,48,192]{3,2,1,0:T(8,128)} custom-call(f32[24,3,2,24,128]{4,3,2,1,0:T(8,128)} %bitcast.29, f32[24,3,2,24,128]{4,3,2,1,0:T(8,128)} %bitcast.32, f32[24,3,2,24,128]{4,3,2,1,0:T(8,128)} %bitcast.33, bf16[512,192]{1,0:T(8,128)(2,1)} %constant.105.clone.refs_3_, f32[1,192]{1,0:T(1,128)} %bitcast.35, f32[48,1]{1,0:T(8,128)} %copy.17.refs_5_, ...), custom_call_target="tpu_custom_call" | custom-call | tf_op jit(solution)/shard_map/finish/pallas_call | solution.py:399
  (5 shorter events, 0.0 us)
Async XLA Ops:
  6.5 85.9 %all-gather.3.cloned.1.call-start = ((), (), s32[]{:S(2)}) async-start(), calls=%async_computation | async-start | bytes 4792320 | tf_op jit(solution)/shard_map/all_gather | solution.py:323
  152.3 16.7 %collective-permute-start.1 = (f32[24,3,48,128]{3,2,1,0:T(8,128)}, f32[24,3,48,128]{3,2,1,0:T(8,128)S(1)}, u32[]{:S(2)}, u32[]{:S(2)}) collective-permute-start(f32[24,3,48,128]{3,2,1,0:T(8,128)} %rows.7), channel_id=1, source_target_pairs={{0,8},{8,0},{16,24},{24,16},{1,9},{9,1},{17,25},{25,17},{2,10},{10... | collective-permute-start | bytes 5308424 | tf_op jit(solution)/shard_map/ppermute | solution.py:387
  160.4 21.8 %collective-permute-start = (f32[24,3,48,128]{3,2,1,0:T(8,128)}, f32[24,3,48,128]{3,2,1,0:T(8,128)S(1)}, u32[]{:S(2)}, u32[]{:S(2)}) collective-permute-start(f32[24,3,48,128]{3,2,1,0:T(8,128)} %rows.5), channel_id=1, source_target_pairs={{0,8},{8,0},{16,24},{24,16},{1,9},{9,1},{17,25},{25,17},{2,10},{10... | collective-permute-start | bytes 5308424 | tf_op jit(solution)/shard_map/ppermute | solution.py:387
  169.1 4.4 %copy-start.2 = (f32[48]{0:T(128)S(1)}, f32[48]{0:T(128)}, u32[]{:S(2)}) copy-start(f32[48]{0:T(128)} %param.19) | copy-start | bytes 580
  172.0 40.7 %collective-permute-start.2 = (f32[24,3,48,128]{3,2,1,0:T(8,128)}, f32[24,3,48,128]{3,2,1,0:T(8,128)S(1)}, u32[]{:S(2)}, u32[]{:S(2)}) collective-permute-start(f32[24,3,48,128]{3,2,1,0:T(8,128)} %add.56), channel_id=1, source_target_pairs={{0,16},{8,24},{16,0},{24,8},{1,17},{9,25},{17,1},{25,9},{2,18},{10... | collective-permute-start | bytes 5308424 | tf_op jit(solution)/shard_map/ppermute | solution.py:387
  182.2 30.5 %copy-start = (f32[24,3,48,128]{3,2,1,0:T(8,128)}, f32[24,3,48,128]{3,2,1,0:T(8,128)S(1)}, u32[]{:S(2)}) copy-start(f32[24,3,48,128]{3,2,1,0:T(8,128)S(1)} %collective-permute-done) | copy-start | bytes 5308420
  212.7 1.2 copy-start.1
Sparse Core Ops, SparseCore 0:
  17.9 74.4 all-gather.2

commit v3 on v2

--- a/solution.py
+++ b/solution.py
@@ -16,6 +16,7 @@
 TILE = 8
 LANES = 128
 PLANES = 32
+Z_CHIPS = 4
 PHASES = 128
 BF16 = jnp.bfloat16
 F32 = jnp.float32
@@ -111,7 +112,7 @@
     return np.concatenate((first, first, second, second)).astype(ml_dtypes.bfloat16)
 
 
-def spread_kernel(samples_ref, kernel_ref, offsets_ref, codes_ref, out_ref):
+def spread_kernel(samples_ref, kernel_ref, offsets_ref, out_ref):
     blocks = samples_ref.shape[0]
     taps = kernel_ref.shape[2]
     cell = lax.broadcasted_iota(jnp.int32, (TILE, LANES), 0)
@@ -120,7 +121,7 @@
     def weights(block):
         placed = []
         for dim in range(3):
-            shifted = cell - offsets_ref[block, pl.ds(dim, 1), :]
+            shifted = cell - offsets_ref[dim, pl.ds(block, 1), :]
             value = jnp.zeros((TILE, LANES), F32)
             for tap in range(taps):
                 value = jnp.where(shifted == tap, kernel_ref[block, dim, pl.ds(tap, 1), :], value)
@@ -143,15 +144,16 @@
         out_ref[pair] = jnp.where(left, piece[: 2 * TILE], piece[2 * TILE :])
         return carry
 
-    lax.fori_loop(0, blocks // 2, pair_body, 0, unroll=2)
-    out_ref[blocks // 2] = jnp.broadcast_to(codes_ref[...], (2 * TILE, LANES))
-
-
-def tiles_kernel(codes_ref, tiles_ref, depth_ref, phases_ref, column_ref, out_ref, acc_ref, even_ref, odd_ref):
+    lax.fori_loop(0, blocks // 2, pair_body, 0, unroll=4)
+
+
+def tiles_kernel(sources, *refs):
+    source_refs = refs[1 : 1 + sources]
+    codes_ref, depth_ref, phases_ref, column_ref, out_ref = refs[:1] + refs[1 + sources : 5 + sources]
+    tiles_ref, acc_ref, even_ref, odd_ref, arrived = refs[5 + sources :]
     half = NX // 2
     stride = NY
-    sources = tiles_ref.shape[0]
-    pairs = tiles_ref.shape[1] - 1
+    pairs = tiles_ref.shape[1]
     batch = 8
     assert pairs % (2 * batch) == 0
     batches = pairs // batch
@@ -183,11 +185,20 @@
 
     @pl.when(pl.program_id(0) == 0)
     def _():
+        copies = [
+            pltpu.make_async_copy(source_ref, tiles_ref.at[index], arrived.at[index])
+            for index, source_ref in enumerate(source_refs)
+        ]
+        for copy in copies:
+            copy.start()
+
         def clear(step, carry):
             acc_ref[pl.ds(pl.multiple_of(step * stride, stride), stride), :] = jnp.zeros((stride, LANES), F32)
             return carry
 
         lax.fori_loop(0, half, clear, 0)
+        for copy in copies:
+            copy.wait()
         spectrum(0, 0, even_ref)
 
         def add_pair(step, carry):
@@ -228,7 +239,8 @@
     lax.fori_loop(0, width // 2, columns, 0, unroll=2)
 
 
-def rows_kernel(planes_padded, place_ref, in_ref, row_ref, out_ref):
+def rows_kernel(planes_padded, addends, place_ref, in_ref, row_ref, *refs):
+    out_ref = refs[-1]
     half = NX // 2
     parity = pl.program_id(1)
     lane = lax.broadcasted_iota(jnp.int32, (PLANES, LANES), 1)
@@ -255,35 +267,43 @@
             values = [jnp.where(lane < NX // 4, even[side], odd[side]) for side in range(2)]
             values.append(jnp.where(lane < LANES // 2, odd[0], pltpu.roll(odd[1], LANES // 2, 1)))
             for number, value in enumerate(values):
-                out_ref[2 * slot + parity, number, part * planes_padded : (part + 1) * planes_padded, :] = value[
-                    :planes_padded
-                ]
-
-
-def finish_kernel(slots, parts, refs):
+                at = (2 * slot + parity, number, pl.ds(part * planes_padded, planes_padded))
+                total = value[:planes_padded]
+                for ref in refs[:addends]:
+                    total = total + ref[at]
+                out_ref[at] = total
+
+
+def finish_kernel(planes_padded, parts, refs):
     part_refs = refs[:parts]
-    order_ref, first_ref, second_ref, third_ref, out_ref = refs[parts:]
-    first = first_ref[...]
-    second = second_ref[...]
-    flats = [ref.reshape(ref.shape[0] * 6 * TILE, LANES) for ref in part_refs]
+    order_ref, first_ref, second_ref, third_ref = refs[parts : parts + 4]
+    out_ref = refs[-1]
+    planes = out_ref.shape[1]
+    stride = 6 * planes_padded
+    flats = [ref.reshape(TILE * stride, LANES) for ref in part_refs]
+    order = order_ref[...]
     for part in range(2):
-        mains, rests = [], []
-        for plane in range(TILE):
-            values = []
-            for number in range(3):
-                at = pl.ds((number * 2 + part) * TILE + plane, slots, stride=6 * TILE)
-                total = flats[0][at, :]
-                for flat in flats[1:]:
-                    total = total + flat[at, :]
-                values.append(total)
-            mains += values[:2]
-            rests += [values[2], pltpu.roll(values[2], LANES // 2, 1)]
-        main = split(jnp.concatenate(mains, axis=0))
-        rest = split(jnp.concatenate(rests, axis=0))
-        ordered = jnp.dot(jnp.concatenate(main + rest, axis=1), order_ref[...], preferred_element_type=F32)
-        for plane in range(TILE):
-            third = third_ref[pl.program_id(0) * TILE + plane]
-            out_ref[part, plane] = ordered[plane * 2 * slots : (plane + 1) * 2 * slots] * (second * third) * first
+        for group in range(0, planes, TILE):
+            members = range(group, min(group + TILE, planes))
+            mains, rests = [], []
+            for plane in members:
+                values = []
+                for number in range(3):
+                    at = pl.ds((number * 2 + part) * planes_padded + plane, TILE, stride=stride)
+                    total = flats[0][at, :]
+                    for flat in flats[1:]:
+                        total = total + flat[at, :]
+                    values.append(total)
+                mains += values[:2]
+                rests += [values[2], pltpu.roll(values[2], LANES // 2, 1)]
+            main = split(jnp.concatenate(mains, axis=0))
+            rest = split(jnp.concatenate(rests, axis=0))
+            ordered = jnp.dot(jnp.concatenate(main + rest, axis=1), order, preferred_element_type=F32)
+            for index, plane in enumerate(members):
+                for side in range(2):
+                    row = (2 * index + side) * TILE
+                    scale = second_ref[side] * third_ref[plane] * first_ref[...]
+                    out_ref[part, plane, side] = ordered[row : row + TILE] * scale
 
 
 def on_device(samples, kernel, offsets, owners, tile_ids, deapod_first, deapod_second, deapod_third):
@@ -308,20 +328,33 @@
     folds = NX // TILE // 2
     base = row % folds * NY + col
     phase = tile_ids % tile_depth + row // folds * tile_depth
-    codes = (base * PHASES + phase).astype(F32)
-    codes = jnp.pad(codes, (0, LANES - blocks))[None, :]
+    codes = base * PHASES + phase
 
     tiles = pl.pallas_call(
         spread_kernel,
-        out_shape=jax.ShapeDtypeStruct((blocks // 2 + 1, 2 * TILE, LANES), F32),
-        in_specs=[vmem] * 4,
+        out_shape=jax.ShapeDtypeStruct((blocks // 2, 2 * TILE, LANES), F32),
+        in_specs=[vmem] * 3,
         out_specs=vmem,
         compiler_params=params,
         name="spread",
-    )(samples, kernel, offsets, codes)
-
-    gathered = lax.all_gather(tiles, "gy", axis=0, tiled=False)
-    tile_codes = gathered[:, blocks // 2, 0, :blocks].astype(jnp.int32).reshape(-1)
+    )(samples, kernel, offsets.transpose(1, 0, 2))
+
+    along = grid_cols // Z_CHIPS
+
+    def shift(value, deep, wide):
+        moves = [
+            (z * along + y, (z + deep) % Z_CHIPS * along + (y + wide) % along)
+            for z in range(Z_CHIPS)
+            for y in range(along)
+        ]
+        return lax.ppermute(value, "gy", moves)
+
+    def collect(value):
+        stack = [value] + [shift(value, deep, 0) for deep in (1, 3, 2)]
+        return stack + [shift(held, 0, wide) for wide in range(1, along) for held in stack]
+
+    tile_codes = jnp.concatenate(collect(codes))
+    gathered = collect(tiles)
 
     place = lax.axis_index("gx").astype(jnp.int32).reshape(1)
     gy = lax.axis_index("gy")
@@ -338,80 +371,116 @@
     kept = 2 * grid_rows * rows
     spectra = pltpu.VMEM((16 * TILE * TILE, 2 * LANES), F32)
     columns = pl.pallas_call(
-        tiles_kernel,
+        functools.partial(tiles_kernel, len(gathered)),
         grid=(half // width,),
         out_shape=jax.ShapeDtypeStruct((half, kept, LANES), F32),
         in_specs=[pl.BlockSpec(memory_space=pltpu.SMEM)]
-        + [whole(array.shape) for array in (gathered, matrix, phase_rows, column)],
+        + [pl.BlockSpec(memory_space=pl.ANY)] * len(gathered)
+        + [whole(array.shape) for array in (matrix, phase_rows, column)],
         out_specs=pl.BlockSpec((width, kept, LANES), lambda step: (step, 0, 0)),
-        scratch_shapes=[pltpu.VMEM((half * NY, LANES), F32), spectra, spectra],
+        scratch_shapes=[
+            pltpu.VMEM((len(gathered),) + tiles.shape, F32),
+            pltpu.VMEM((half * NY, LANES), F32),
+            spectra,
+            spectra,
+            pltpu.SemaphoreType.DMA((len(gathered),)),
+        ],
         compiler_params=params,
         name="tiles",
-    )(tile_codes, gathered, matrix, phase_rows, column)
+    )(tile_codes, *gathered, matrix, phase_rows, column)
 
     row_table = jnp.asarray(row_tables())
-    slots = rows
-    part_shape = (slots, 3, 2 * planes_padded, LANES)
-
-    def rows_for(relative):
+    chunks = rows // TILE
+    part_shape = (3, 2 * planes_padded, LANES)
+
+    def rows_for(relative, first, count, addends, after):
         def block(step, parity, place_ref):
             device = jnp.bitwise_xor(place_ref[0], relative)
-            return (0, (parity * grid_rows + device) * (rows // TILE) + step, 0)
+            return (0, (parity * grid_rows + device) * chunks + first + step, 0)
+
+        part = pl.BlockSpec((TILE,) + part_shape, lambda step, parity, place_ref: (step, 0, 0, 0))
+        slots = count * TILE
+
+        def body(*refs):
+            rows_kernel(planes_padded, len(addends), *refs[: 3 + len(addends)], refs[-1])
 
         return pl.pallas_call(
-            functools.partial(rows_kernel, planes_padded),
+            body,
             grid_spec=pltpu.PrefetchScalarGridSpec(
                 num_scalar_prefetch=1,
-                grid=(rows // TILE, 2),
+                grid=(count, 2),
                 in_specs=[
                     pl.BlockSpec((half, TILE, LANES), block),
                     pl.BlockSpec(row_table.shape, lambda step, parity, place_ref: (0, 0, 0, 0)),
-                ],
-                out_specs=pl.BlockSpec((TILE,) + part_shape[1:], lambda step, parity, place_ref: (step, 0, 0, 0)),
+                ]
+                + [part] * len(addends)
+                + [pl.BlockSpec(memory_space=pl.ANY)] * len(after),
+                out_specs=part,
             ),
-            out_shape=jax.ShapeDtypeStruct(part_shape, F32),
+            out_shape=jax.ShapeDtypeStruct((slots,) + part_shape, F32),
             compiler_params=params,
             cost_estimate=pl.CostEstimate(
                 flops=2 * 3 * slots * 2 * LANES * half * 2 * LANES,
-                bytes_accessed=4 * (half * 2 * slots * LANES + math.prod(part_shape)),
+                bytes_accessed=4 * (half * 2 * slots * LANES + slots * math.prod(part_shape)),
                 transcendentals=0,
             ),
             name="rows",
-        )(place, columns, row_table)
-
-    def sums(relatives, bit):
-        if bit == 0:
-            return [rows_for(relatives)]
-        swap = [(index, index ^ bit) for index in range(grid_rows)]
-        sent = sum(sums(relatives | bit, bit // 2))
-        arrived = lax.ppermute(sent, "gx", swap)
-        return sums(relatives, bit // 2) + [arrived]
-
-    finals = sums(0, grid_rows // 2)
-    finals = [layer.reshape(slots, 3, 2, planes_padded, LANES) for layer in finals]
-
-    def finish(*refs):
-        finish_kernel(per_device // 2, len(finals), refs)
-
-    def shared(shape):
-        return pl.BlockSpec(shape, lambda step: (0,) * len(shape))
-
-    return pl.pallas_call(
-        finish,
-        grid=(planes_padded // TILE,),
-        out_shape=jax.ShapeDtypeStruct((2, planes, per_device, NX // 2), F32),
-        in_specs=[pl.BlockSpec((slots, 3, 2, TILE, LANES), lambda step: (0, 0, 0, step, 0))] * len(finals)
-        + [shared((4 * LANES, NX // 2)), shared((1, NX // 2)), shared((per_device, 1)), pl.BlockSpec(memory_space=pltpu.SMEM)],
-        out_specs=pl.BlockSpec((2, TILE, per_device, NX // 2), lambda step: (0, step, 0, 0)),
-        compiler_params=params,
-        name="finish",
-    )(
-        *finals,
-        jnp.asarray(order_tables()),
-        deapod_first[None, :],
-        deapod_second[:, None],
-        jnp.pad(deapod_third, (0, planes_padded - planes)),
-    )
+        )(place, columns, row_table, *addends, *after)
+
+    def swap(value, bit):
+        return lax.ppermute(value, "gx", [(index, index ^ bit) for index in range(grid_rows)])
+
+    def total(relative, top, first, count, after):
+        arrived = []
+        bit = 1
+        while bit <= top:
+            arrived.append(swap(total(relative | bit, bit // 2, first, count, after), bit))
+            bit *= 2
+        return rows_for(relative, first, count, arrived, after)
+
+    top = grid_rows // 2
+    crossing = [total(top, top // 2, chunk, 1, []) for chunk in range(chunks)]
+    kept_part = total(0, top // 2, 0, chunks, [crossing[-1]])
+    crossed = [swap(value, top) for value in crossing]
+
+    image = None
+    shape = (2, planes, 2, per_device // 2, NX // 2)
+    for chunk in range(chunks):
+
+        def at_chunk(_, chunk=chunk):
+            return (chunk, 0, 0, 0)
+
+        def finish(*refs):
+            finish_kernel(planes_padded, 2, refs)
+
+        earlier = [] if image is None else [image]
+        image = pl.pallas_call(
+            finish,
+            grid=(1,),
+            out_shape=jax.ShapeDtypeStruct(shape, F32),
+            in_specs=[
+                pl.BlockSpec((TILE,) + part_shape, at_chunk),
+                pl.BlockSpec((TILE,) + part_shape, lambda step: (0, 0, 0, 0)),
+                pl.BlockSpec((4 * LANES, NX // 2), lambda step: (0, 0)),
+                pl.BlockSpec((1, NX // 2), lambda step: (0, 0)),
+                pl.BlockSpec((2, TILE, 1), lambda step, chunk=chunk: (0, chunk, 0)),
+                pl.BlockSpec(memory_space=pltpu.SMEM),
+            ]
+            + [pl.BlockSpec(memory_space=pl.ANY)] * len(earlier),
+            out_specs=pl.BlockSpec((2, planes, 2, TILE, NX // 2), lambda step, chunk=chunk: (0, 0, 0, chunk, 0)),
+            input_output_aliases={6: 0} if earlier else {},
+            compiler_params=params,
+            name="finish",
+        )(
+            kept_part,
+            crossed[chunk],
+            jnp.asarray(order_tables()),
+            deapod_first[None, :],
+            deapod_second.reshape(2, per_device // 2, 1),
+            deapod_third,
+            *earlier,
+        )
+    return image.reshape(2, planes, per_device, NX // 2)
 
 
 def solution(mesh):

time: 230 us -> 241 us (1.048)
  starting transfers between devices: 1.94 us -> 20.5 us
  between operations: 13.4 us -> 0.15 us
  Pallas kernels: 97.2 us -> 103 us
  other arithmetic: 5.51 us -> 0.7 us
  local copies, waits for them, and re-layouts: 6.55 us -> 10.8 us
    ppermute x3 -> x21, waiting for transfers between devices: 30.5 us -> 103 us  [the longest x14 84.5 us: shift(): return lax.ppermute(value, 'gy', moves)]
    all_gather x1 -> x0, waiting for transfers between devices: 71.7 us -> none  [on_device(): gathered = lax.all_gather(tiles, 'gy', axis=0, tiled=False)]
    ppermute x3 -> x21, starting transfers between devices: 1.93 us -> 20.5 us  [the longest x14 16.3 us: shift(): return lax.ppermute(value, 'gy', moves)]
    pallas_call x6 -> x12, Pallas kernels: 88.9 us -> 96.9 us  [the longest x1 49.2 us: on_device(): pl.pallas_call(functools.partial(tiles_kernel, len(gathered)), grid=(half...]
    unnamed x7 -> x38, local copies, waits for them, and re-layouts: 2.96 us -> 7.24 us
    add x1 -> x0, other arithmetic: 2.93 us -> none  [sums(): sent = sum(sums(relatives | bit, bit // 2))]
  transfers between devices with their start and end apart: 4 -> 21, of which waited for: 2 -> 8; matrix products, arithmetic and copies ran while one was open for 3% -> 2% of each run, Pallas kernels for 11% -> 12%
where the time goes in v3:
time: 241 us; the launch traced here: 238 us
  Pallas kernels  103 us (43%)
  waiting for transfers between devices  103 us (43%)
  starting transfers between devices  20.5 us (9%)
  local copies, waits for them, and re-layouts  10.8 us (4%)
    ppermute x14, waiting for transfers between devices, shift(): return lax.ppermute(value, 'gy', moves)  84.5 us
    pallas_call x1, Pallas kernels, on_device(): pl.pallas_call(functools.partial(tiles_kernel, len(gathered)), grid=(half...  49.2 us
    pallas_call x8, Pallas kernels, rows_for(): pl.pallas_call(body, grid_spec=pltpu.PrefetchScalarGridSpec(num_scalar_pr...  39.3 us
    ppermute x7, waiting for transfers between devices, swap(): lax.ppermute(value, 'gx', [(index, index ^ bit) for index in range(grid_r...  18.3 us
    ppermute x14, starting transfers between devices, shift(): return lax.ppermute(value, 'gy', moves)  16.3 us
    pallas_call x3, Pallas kernels, on_device(): pl.pallas_call(finish, grid=(1,), out_shape=jax.ShapeDtypeStruct(shape, F...  8.39 us
    unnamed x38, local copies, waits for them, and re-layouts  7.24 us
    pallas_call x1, Pallas kernels, on_device(): pl.pallas_call(spread_kernel, out_shape=jax.ShapeDtypeStruct((blocks // 2...  6.21 us
  transfers between devices with their start and end apart: 21, of which 8 were waited for; matrix products, arithmetic and copies ran while one was open for 2% of the time, Pallas kernels for 12%

profile of v3, /device:TPU:16, one launch (start us, length us, event | category | flops | bytes accessed | tf_op | source)
XLA Modules:
  0.0 238.1 jit_solution(10583653689620269146)
XLA Ops:
  0.0 6.2 %spread.1.refs_1_ = f32[64,16,128]{2,1,0:T(8,128)} custom-call(f32[128,2,128]{2,1,0:T(2,128)} %samples_ref.1, f32[128,3,4,128]{3,2,1,0:T(4,128)} %kernel_ref.1, s32[3,128,128]{2,1,0:T(8,128)} %bitcast.22), custom_call_target="tpu_custom_call" | custom-call | tf_op jit(solution)/shard_map/spread/pallas_call | solution.py:333
  8.2 1.9 collective-permute-start.9
  10.9 2.0 collective-permute-start.1
  15.8 38.0 %collective-permute-done = s32[128]{0:T(128)S(1)} collective-permute-done((s32[128]{0:T(128)S(1)}, s32[128]{0:T(128)S(1)}, u32[]{:S(2)}, u32[]{:S(2)}) %collective-permute-start) | collective-permute-done | bytes 544 | tf_op jit(solution)/shard_map/ppermute | solution.py:350
  53.8 1.6 collective-permute-start.3
  55.4 2.8 %collective-permute-done.2 = s32[128]{0:T(128)S(1)} collective-permute-done((s32[128]{0:T(128)S(1)}, s32[128]{0:T(128)S(1)}, u32[]{:S(2)}, u32[]{:S(2)}) %collective-permute-start.2) | collective-permute-done | bytes 544 | tf_op jit(solution)/shard_map/ppermute | solution.py:350
  63.9 39.7 %collective-permute-done.4 = s32[128]{0:T(128)S(1)} collective-permute-done((s32[128]{0:T(128)S(1)}, s32[128]{0:T(128)S(1)}, u32[]{:S(2)}, u32[]{:S(2)}) %collective-permute-start.4) | collective-permute-done | bytes 544 | tf_op jit(solution)/shard_map/ppermute | solution.py:350
  105.1 2.0 collective-permute-done.5
  108.6 2.0 collective-permute-done.6
  112.6 49.2 %tiles.1.refs_1_ = f32[192,192,128]{2,1,0:T(8,128)} custom-call(s32[1024]{0:T(1024)} %copy-done.14, f32[64,16,128]{2,1,0:T(8,128)} %spread.1.refs_1_, f32[64,16,128]{2,1,0:T(8,128)} %copy-done.7, f32[64,16,128]{2,1,0:T(8,128)} %copy-done.8, f32[64,16,128]{2,1,0:T(8,128)} %copy-done.9, f32[64,16,128]{2,1,0:T(8,128)} %copy-done.10, f32[64,16,128]{2,1,0:T(8,128)} %copy-done.11, ...), custom_call_target="tpu_custom_call" | custom-call | tf_op jit(solution)/shard_map/tiles/pallas_call | solution.py:373
  161.9 3.7 %rows.8 = f32[8,3,48,128]{3,2,1,0:T(8,128)} custom-call(s32[1]{0:T(128)} %bitcast.refs_0_, f32[192,192,128]{2,1,0:T(8,128)} %tiles.1.refs_1_, bf16[2,2,192,256]{3,2,1,0:T(8,128)(2,1)} %constant.103.clone.refs_2_), custom_call_target="tpu_custom_call" | custom-call | flops 603979776 | bytes 2162688 | tf_op jit(solution)/shard_map/rows/pallas_call | solution.py:407
  165.6 2.2 collective-permute-done.14.refs_3_
  168.6 3.9 %rows.9.refs_3_.refs_4_ = f32[8,3,48,128]{3,2,1,0:T(8,128)} custom-call(s32[1]{0:T(128)} %bitcast.refs_0_, f32[192,192,128]{2,1,0:T(8,128)} %tiles.1.refs_1_, bf16[2,2,192,256]{3,2,1,0:T(8,128)(2,1)} %constant.103.clone.refs_2_, f32[8,3,48,128]{3,2,1,0:T(8,128)} %copy-done.6), custom_call_target="tpu_custom_call" | custom-call | flops 603979776 | bytes 2162688 | tf_op jit(solution)/shard_map/rows/pallas_call | solution.py:407
  172.5 8.1 %rows.10 = f32[24,3,48,128]{3,2,1,0:T(8,128)} custom-call(s32[1]{0:T(128)} %bitcast.refs_0_, f32[192,192,128]{2,1,0:T(8,128)} %tiles.1.refs_1_, bf16[2,2,192,256]{3,2,1,0:T(8,128)(2,1)} %constant.103.clone.refs_2_, f32[8,3,48,128]{3,2,1,0:T(8,128)} %rows.9.refs_3_.refs_4_), custom_call_target="tpu_custom_call" | custom-call | flops 1811939328 | bytes 6488064 | tf_op jit(solution)/shard_map/rows/pallas_call | solution.py:407
  180.7 3.7 %rows.14 = f32[8,3,48,128]{3,2,1,0:T(8,128)} custom-call(s32[1]{0:T(128)} %bitcast.refs_0_, f32[192,192,128]{2,1,0:T(8,128)} %tiles.1.refs_1_, bf16[2,2,192,256]{3,2,1,0:T(8,128)(2,1)} %constant.103.clone.refs_2_), custom_call_target="tpu_custom_call" | custom-call | flops 603979776 | bytes 2162688 | tf_op jit(solution)/shard_map/rows/pallas_call | solution.py:407
  184.8 3.7 %rows.12 = f32[8,3,48,128]{3,2,1,0:T(8,128)} custom-call(s32[1]{0:T(128)} %bitcast.refs_0_, f32[192,192,128]{2,1,0:T(8,128)} %tiles.1.refs_1_, bf16[2,2,192,256]{3,2,1,0:T(8,128)(2,1)} %constant.103.clone.refs_2_), custom_call_target="tpu_custom_call" | custom-call | flops 603979776 | bytes 2162688 | tf_op jit(solution)/shard_map/rows/pallas_call | solution.py:407
  189.5 3.9 %rows.15 = f32[8,3,48,128]{3,2,1,0:T(8,128)} custom-call(s32[1]{0:T(128)} %bitcast.refs_0_, f32[192,192,128]{2,1,0:T(8,128)} %tiles.1.refs_1_, bf16[2,2,192,256]{3,2,1,0:T(8,128)(2,1)} %constant.103.clone.refs_2_, f32[8,3,48,128]{3,2,1,0:T(8,128)} %copy-done.5), custom_call_target="tpu_custom_call" | custom-call | flops 603979776 | bytes 2162688 | tf_op jit(solution)/shard_map/rows/pallas_call | solution.py:407
  195.7 3.9 %rows.13 = f32[8,3,48,128]{3,2,1,0:T(8,128)} custom-call(s32[1]{0:T(128)} %bitcast.refs_0_, f32[192,192,128]{2,1,0:T(8,128)} %tiles.1.refs_1_, bf16[2,2,192,256]{3,2,1,0:T(8,128)(2,1)} %constant.103.clone.refs_2_, f32[8,3,48,128]{3,2,1,0:T(8,128)} %copy-done.4), custom_call_target="tpu_custom_call" | custom-call | flops 603979776 | bytes 2162688 | tf_op jit(solution)/shard_map/rows/pallas_call | solution.py:407
  203.6 8.4 %rows.11.refs_0_ = f32[24,3,48,128]{3,2,1,0:T(8,128)} custom-call(s32[1]{0:T(128)} %bitcast.refs_0_, f32[192,192,128]{2,1,0:T(8,128)} %tiles.1.refs_1_, bf16[2,2,192,256]{3,2,1,0:T(8,128)(2,1)} %constant.103.clone.refs_2_, f32[24,3,48,128]{3,2,1,0:T(8,128)} %copy-done.1, f32[8,3,48,128]{3,2,1,0:T(8,128)} %rows.9.refs_3_.refs_4_), custom_call_target="tpu_custom_call" | custom-call | flops 1811939328 | bytes 6488064 | tf_op jit(solution)/shard_map/rows/pallas_call | solution.py:407
  212.0 2.8 %finish.3.refs_6_ = f32[2,24,2,24,192]{4,3,2,1,0:T(8,128)} custom-call(f32[24,3,48,128]{3,2,1,0:T(8,128)} %rows.11.refs_0_, f32[8,3,48,128]{3,2,1,0:T(8,128)} %collective-permute-done.20.refs_1_, bf16[512,192]{1,0:T(8,128)(2,1)} %constant.104.clone.refs_2_, f32[1,192]{1,0:T(1,128)} %bitcast.23, f32[2,24,1]{2,1,0:T(8,128)} %reshape.14.refs_4_, f32[24]{0:T(128)} %refs_5_.5), custom_call_target="tpu_custom_call" | custom-call | tf_op jit(solution)/shard_map/finish/pallas_call | solution.py:457
  214.8 7.6 %collective-permute-done.18.refs_1_ = f32[8,3,48,128]{3,2,1,0:T(8,128)S(1)} collective-permute-done((f32[8,3,48,128]{3,2,1,0:T(8,128)}, f32[8,3,48,128]{3,2,1,0:T(8,128)S(1)}, u32[]{:S(2)}, u32[]{:S(2)}) %collective-permute-start.18) | collective-permute-done | bytes 589856 | tf_op jit(solution)/shard_map/ppermute | solution.py:431
  223.2 2.8 %finish.4.refs_6_ = f32[2,24,2,24,192]{4,3,2,1,0:T(8,128)} custom-call(f32[24,3,48,128]{3,2,1,0:T(8,128)} %rows.11.refs_0_, f32[8,3,48,128]{3,2,1,0:T(8,128)} %copy-done.3, bf16[512,192]{1,0:T(8,128)(2,1)} %constant.104.clone.refs_2_, f32[1,192]{1,0:T(1,128)} %bitcast.24, f32[2,24,1]{2,1,0:T(8,128)} %reshape.14.refs_4_, ...), custom_call_target="tpu_custom_call", output_to_operand_aliasing={{}: (6, {})} | custom-call | tf_op jit(solution)/shard_map/finish/pallas_call | solution.py:457
  226.0 8.5 %collective-permute-done.16.refs_1_ = f32[8,3,48,128]{3,2,1,0:T(8,128)S(1)} collective-permute-done((f32[8,3,48,128]{3,2,1,0:T(8,128)S(1)}, f32[8,3,48,128]{3,2,1,0:T(8,128)S(1)}, u32[]{:S(2)}, u32[]{:S(2)}) %collective-permute-start.16) | collective-permute-done | bytes 589856 | tf_op jit(solution)/shard_map/ppermute | solution.py:431
  235.3 2.8 %finish.5 = f32[2,24,2,24,192]{4,3,2,1,0:T(8,128)} custom-call(f32[24,3,48,128]{3,2,1,0:T(8,128)} %rows.11.refs_0_, f32[8,3,48,128]{3,2,1,0:T(8,128)} %copy-done.2, bf16[512,192]{1,0:T(8,128)(2,1)} %constant.104.clone.refs_2_, f32[1,192]{1,0:T(1,128)} %bitcast.25, f32[2,24,1]{2,1,0:T(8,128)} %reshape.14.refs_4_, ...), custom_call_target="tpu_custom_call", output_to_operand_aliasing={{}: (6, {})} | custom-call | tf_op jit(solution)/shard_map/finish/pallas_call | solution.py:457
  (75 shorter events, 26.6 us)
Async XLA Ops:
  6.2 53.5 %collective-permute-start.7 = (f32[64,16,128]{2,1,0:T(8,128)}, f32[64,16,128]{2,1,0:T(8,128)S(1)}, u32[]{:S(2)}, u32[]{:S(2)}) collective-permute-start(f32[64,16,128]{2,1,0:T(8,128)} %spread.1.refs_1_), channel_id=1, source_target_pairs={{0,2},{1,3},{2,4},{3,5},{4,6},{5,7},{6,0},{7,1},{8,10},{9,11},{10,... | collective-permute-start | bytes 1572872 | tf_op jit(solution)/shard_map/ppermute | solution.py:350
  7.8 52.5 %collective-permute-start.8 = (f32[64,16,128]{2,1,0:T(8,128)}, f32[64,16,128]{2,1,0:T(8,128)S(1)}, u32[]{:S(2)}, u32[]{:S(2)}) collective-permute-start(f32[64,16,128]{2,1,0:T(8,128)} %spread.1.refs_1_), channel_id=1, source_target_pairs={{0,6},{1,7},{2,0},{3,1},{4,2},{5,3},{6,4},{7,5},{8,14},{9,15},{10,... | collective-permute-start | bytes 1572872 | tf_op jit(solution)/shard_map/ppermute | solution.py:350
  8.2 53.6 %collective-permute-start.9 = (f32[64,16,128]{2,1,0:T(8,128)}, f32[64,16,128]{2,1,0:T(8,128)S(1)}, u32[]{:S(2)}, u32[]{:S(2)}) collective-permute-start(f32[64,16,128]{2,1,0:T(8,128)} %spread.1.refs_1_), channel_id=1, source_target_pairs={{0,4},{1,5},{2,6},{3,7},{4,0},{5,1},{6,2},{7,3},{8,12},{9,13},{10,... | collective-permute-start | bytes 1572872 | tf_op jit(solution)/shard_map/ppermute | solution.py:350
  10.9 42.9 %collective-permute-start = (s32[128]{0:T(128)S(1)}, s32[128]{0:T(128)S(1)}, u32[]{:S(2)}, u32[]{:S(2)}) collective-permute-start(s32[128]{0:T(128)S(1)} %get-tuple-element.6), channel_id=1, source_target_pairs={{0,2},{1,3},{2,4},{3,5},{4,6},{5,7},{6,0},{7,1},{8,10},{9,11},{10,... | collective-permute-start | bytes 1544 | tf_op jit(solution)/shard_map/ppermute | solution.py:350
  10.9 42.9 %collective-permute-start.1 = (s32[128]{0:T(128)S(1)}, s32[128]{0:T(128)S(1)}, u32[]{:S(2)}, u32[]{:S(2)}) collective-permute-start(s32[128]{0:T(128)S(1)} %get-tuple-element.6), channel_id=1, source_target_pairs={{0,6},{1,7},{2,0},{3,1},{4,2},{5,3},{6,4},{7,5},{8,14},{9,15},{10,... | collective-permute-start | bytes 1544 | tf_op jit(solution)/shard_map/ppermute | solution.py:350
  53.8 4.4 %collective-permute-start.2 = (s32[128]{0:T(128)S(1)}, s32[128]{0:T(128)S(1)}, u32[]{:S(2)}, u32[]{:S(2)}) collective-permute-start(s32[128]{0:T(128)S(1)} %get-tuple-element.6), channel_id=1, source_target_pairs={{0,4},{1,5},{2,6},{3,7},{4,0},{5,1},{6,2},{7,3},{8,12},{9,13},{10,... | collective-permute-start | bytes 1544 | tf_op jit(solution)/shard_map/ppermute | solution.py:350
  53.8 8.5 %collective-permute-start.3 = (s32[128]{0:T(128)S(1)}, s32[128]{0:T(128)S(1)}, u32[]{:S(2)}, u32[]{:S(2)}) collective-permute-start(s32[128]{0:T(128)S(1)} %get-tuple-element.6), channel_id=1, source_target_pairs={{0,1},{1,0},{2,3},{3,2},{4,5},{5,4},{6,7},{7,6},{8,9},{9,8},{10,11... | collective-permute-start | bytes 1544 | tf_op jit(solution)/shard_map/ppermute | solution.py:350
  58.2 52.4 %collective-permute-start.10 = (f32[64,16,128]{2,1,0:T(8,128)}, f32[64,16,128]{2,1,0:T(8,128)S(1)}, u32[]{:S(2)}, u32[]{:S(2)}) collective-permute-start(f32[64,16,128]{2,1,0:T(8,128)} %spread.1.refs_1_), channel_id=1, source_target_pairs={{0,1},{1,0},{2,3},{3,2},{4,5},{5,4},{6,7},{7,6},{8,9},{9,8},{10,11... | collective-permute-start | bytes 1572872 | tf_op jit(solution)/shard_map/ppermute | solution.py:350
  59.8 51.0 %copy-start.7 = (f32[64,16,128]{2,1,0:T(8,128)}, f32[64,16,128]{2,1,0:T(8,128)S(1)}, u32[]{:S(2)}) copy-start(f32[64,16,128]{2,1,0:T(8,128)S(1)} %collective-permute-done.7.refs_2_) | copy-start | bytes 1572868
  59.8 50.9 %collective-permute-start.11 = (f32[64,16,128]{2,1,0:T(8,128)S(1)}, f32[64,16,128]{2,1,0:T(8,128)S(1)}, u32[]{:S(2)}, u32[]{:S(2)}) collective-permute-start(f32[64,16,128]{2,1,0:T(8,128)S(1)} %collective-permute-done.7.refs_2_), channel_id=1, source_target_pairs={{0,1},{1,0},{2,3},{3,2},{4,5},{5,4},{6,7},{7,6},{8,9},{9,8},{10,11... | collective-permute-start | bytes 1572872 | tf_op jit(solution)/shard_map/ppermute | solution.py:350
  60.3 50.5 %copy-start.8 = (f32[64,16,128]{2,1,0:T(8,128)}, f32[64,16,128]{2,1,0:T(8,128)S(1)}, u32[]{:S(2)}) copy-start(f32[64,16,128]{2,1,0:T(8,128)S(1)} %collective-permute-done.8.refs_3_) | copy-start | bytes 1572868
  60.3 50.4 %collective-permute-start.12 = (f32[64,16,128]{2,1,0:T(8,128)S(1)}, f32[64,16,128]{2,1,0:T(8,128)S(1)}, u32[]{:S(2)}, u32[]{:S(2)}) collective-permute-start(f32[64,16,128]{2,1,0:T(8,128)S(1)} %collective-permute-done.8.refs_3_), channel_id=1, source_target_pairs={{0,1},{1,0},{2,3},{3,2},{4,5},{5,4},{6,7},{7,6},{8,9},{9,8},{10,11... | collective-permute-start | bytes 1572872 | tf_op jit(solution)/shard_map/ppermute | solution.py:350
  61.8 48.9 %copy-start.9 = (f32[64,16,128]{2,1,0:T(8,128)}, f32[64,16,128]{2,1,0:T(8,128)S(1)}, u32[]{:S(2)}) copy-start(f32[64,16,128]{2,1,0:T(8,128)S(1)} %collective-permute-done.9.refs_4_) | copy-start | bytes 1572868
  61.8 48.9 %collective-permute-start.13 = (f32[64,16,128]{2,1,0:T(8,128)S(1)}, f32[64,16,128]{2,1,0:T(8,128)S(1)}, u32[]{:S(2)}, u32[]{:S(2)}) collective-permute-start(f32[64,16,128]{2,1,0:T(8,128)S(1)} %collective-permute-done.9.refs_4_), channel_id=1, source_target_pairs={{0,1},{1,0},{2,3},{3,2},{4,5},{5,4},{6,7},{7,6},{8,9},{9,8},{10,11... | collective-permute-start | bytes 1572872 | tf_op jit(solution)/shard_map/ppermute | solution.py:350
  62.3 41.2 %collective-permute-start.4 = (s32[128]{0:T(128)S(1)}, s32[128]{0:T(128)S(1)}, u32[]{:S(2)}, u32[]{:S(2)}) collective-permute-start(s32[128]{0:T(128)S(1)} %collective-permute-done), channel_id=1, source_target_pairs={{0,1},{1,0},{2,3},{3,2},{4,5},{5,4},{6,7},{7,6},{8,9},{9,8},{10,11... | collective-permute-start | bytes 1544 | tf_op jit(solution)/shard_map/ppermute | solution.py:350
  103.6 3.5 %collective-permute-start.5 = (s32[128]{0:T(128)S(1)}, s32[128]{0:T(128)S(1)}, u32[]{:S(2)}, u32[]{:S(2)}) collective-permute-start(s32[128]{0:T(128)S(1)} %collective-permute-done.1), channel_id=1, source_target_pairs={{0,1},{1,0},{2,3},{3,2},{4,5},{5,4},{6,7},{7,6},{8,9},{9,8},{10,11... | collective-permute-start | bytes 1544 | tf_op jit(solution)/shard_map/ppermute | solution.py:350
  107.1 3.5 %collective-permute-start.6 = (s32[128]{0:T(128)S(1)}, s32[128]{0:T(128)S(1)}, u32[]{:S(2)}, u32[]{:S(2)}) collective-permute-start(s32[128]{0:T(128)S(1)} %collective-permute-done.2), channel_id=1, source_target_pairs={{0,1},{1,0},{2,3},{3,2},{4,5},{5,4},{6,7},{7,6},{8,9},{9,8},{10,11... | collective-permute-start | bytes 1544 | tf_op jit(solution)/shard_map/ppermute | solution.py:350
  165.6 2.2 collective-permute-start.14
  180.6 21.8 %collective-permute-start.15 = (f32[24,3,48,128]{3,2,1,0:T(8,128)}, f32[24,3,48,128]{3,2,1,0:T(8,128)S(1)}, u32[]{:S(2)}, u32[]{:S(2)}) collective-permute-start(f32[24,3,48,128]{3,2,1,0:T(8,128)} %rows.10), channel_id=1, source_target_pairs={{0,8},{8,0},{16,24},{24,16},{1,9},{9,1},{17,25},{25,17},{2,10},{10... | collective-permute-start | bytes 5308424 | tf_op jit(solution)/shard_map/ppermute | solution.py:431
  184.4 4.2 %collective-permute-start.19 = (f32[8,3,48,128]{3,2,1,0:T(8,128)}, f32[8,3,48,128]{3,2,1,0:T(8,128)S(1)}, u32[]{:S(2)}, u32[]{:S(2)}) collective-permute-start(f32[8,3,48,128]{3,2,1,0:T(8,128)} %rows.14), channel_id=1, source_target_pairs={{0,8},{8,0},{16,24},{24,16},{1,9},{9,1},{17,25},{25,17},{2,10},{10... | collective-permute-start | bytes 1769480 | tf_op jit(solution)/shard_map/ppermute | solution.py:431
  188.5 6.4 %collective-permute-start.17 = (f32[8,3,48,128]{3,2,1,0:T(8,128)}, f32[8,3,48,128]{3,2,1,0:T(8,128)S(1)}, u32[]{:S(2)}, u32[]{:S(2)}) collective-permute-start(f32[8,3,48,128]{3,2,1,0:T(8,128)} %rows.12), channel_id=1, source_target_pairs={{0,8},{8,0},{16,24},{24,16},{1,9},{9,1},{17,25},{25,17},{2,10},{10... | collective-permute-start | bytes 1769480 | tf_op jit(solution)/shard_map/ppermute | solution.py:431
  193.4 18.7 %collective-permute-start.20 = (f32[8,3,48,128]{3,2,1,0:T(8,128)}, f32[8,3,48,128]{3,2,1,0:T(8,128)}, u32[]{:S(2)}, u32[]{:S(2)}) collective-permute-start(f32[8,3,48,128]{3,2,1,0:T(8,128)} %rows.15), channel_id=1, source_target_pairs={{0,16},{8,24},{16,0},{24,8},{1,17},{9,25},{17,1},{25,9},{2,18},{10... | collective-permute-start | bytes 1769480 | tf_op jit(solution)/shard_map/ppermute | solution.py:431
  199.6 22.8 %collective-permute-start.18 = (f32[8,3,48,128]{3,2,1,0:T(8,128)}, f32[8,3,48,128]{3,2,1,0:T(8,128)S(1)}, u32[]{:S(2)}, u32[]{:S(2)}) collective-permute-start(f32[8,3,48,128]{3,2,1,0:T(8,128)} %rows.13), channel_id=1, source_target_pairs={{0,16},{8,24},{16,0},{24,8},{1,17},{9,25},{17,1},{25,9},{2,18},{10... | collective-permute-start | bytes 1769480 | tf_op jit(solution)/shard_map/ppermute | solution.py:431
  200.1 34.3 %collective-permute-start.16 = (f32[8,3,48,128]{3,2,1,0:T(8,128)S(1)}, f32[8,3,48,128]{3,2,1,0:T(8,128)S(1)}, u32[]{:S(2)}, u32[]{:S(2)}) collective-permute-start(f32[8,3,48,128]{3,2,1,0:T(8,128)S(1)} %copy-done), channel_id=1, source_target_pairs={{0,16},{8,24},{16,0},{24,8},{1,17},{9,25},{17,1},{25,9},{2,18},{10... | collective-permute-start | bytes 1769480 | tf_op jit(solution)/shard_map/ppermute | solution.py:431
  (13 other events, 24.6 us)

commit v4 on v3

--- a/solution.py
+++ b/solution.py
@@ -54,12 +54,11 @@
         imag = np.where(lane_part == 0, -sin, cos)
         plain = np.concatenate((real, imag))
         turned = np.concatenate((-np.where(lane_part == 0, sin, -cos), -np.where(lane_part == 0, cos, sin)))
-        high, low = halves(np.concatenate((plain, turned), axis=1))
-        matrices.append(np.concatenate((high, high, low), axis=0))
+        matrices.append(np.stack((plain, turned)))
         cos, sin = waves(np.arange(NZ // TILE), position, NZ // TILE)
         sign = np.where(lane_odd == 1, -1.0, 1.0)[None, :]
         phases.append(np.stack((np.concatenate((cos, cos * sign)), np.concatenate((sin, sin * sign)))))
-    return np.stack(matrices), np.stack(phases).astype(np.float32)
+    return np.stack(matrices).astype(np.float32), np.stack(phases).astype(np.float32)
 
 
 def padded_rows(per_device):
@@ -112,7 +111,30 @@
     return np.concatenate((first, first, second, second)).astype(ml_dtypes.bfloat16)
 
 
-def spread_kernel(samples_ref, kernel_ref, offsets_ref, out_ref):
+def divide(value, divisor, limit):
+    for shift in range(8, 24):
+        factor = (1 << shift) // divisor + 1
+        tried = np.arange(limit, dtype=np.int64)
+        if factor * limit < 1 << 31 and np.array_equal(tried * factor >> shift, tried // divisor):
+            return lax.shift_right_logical(value * factor, shift)
+    raise ValueError(divisor)
+
+
+def spread_kernel(tile_rows, tile_cols, grid_cols, devices, samples_ref, kernel_ref, offsets_ref, owners_ref, ids_ref, out_ref):
+    owner, tile_id = owners_ref[...], ids_ref[...]
+    tile_depth = NZ // TILE
+    tiles_device = tile_rows * tile_cols * tile_depth
+    owner_row = divide(owner, grid_cols, devices)
+    tile_row = divide(tile_id, tile_cols * tile_depth, tiles_device)
+    tile_col = divide(tile_id, tile_depth, tiles_device)
+    row = owner_row * tile_rows + tile_row
+    col = (owner - owner_row * grid_cols) * tile_cols + tile_col - tile_row * tile_cols
+    folds = NX // TILE // 2
+    upper = (row >= folds).astype(jnp.int32)
+    base = (row - upper * folds) * NY + col
+    phase = tile_id - tile_col * tile_depth + upper * tile_depth
+    codes = (base * PHASES + phase).astype(F32)
+
     blocks = samples_ref.shape[0]
     taps = kernel_ref.shape[2]
     cell = lax.broadcasted_iota(jnp.int32, (TILE, LANES), 0)
@@ -145,50 +167,36 @@
         return carry
 
     lax.fori_loop(0, blocks // 2, pair_body, 0, unroll=4)
+    out_ref[blocks // 2] = jnp.broadcast_to(codes, (2 * TILE, LANES))
+
+
+def weights_kernel(matrix_ref, phases_ref, out_ref):
+    plain, turned = matrix_ref[0], matrix_ref[1]
+
+    def body(row, carry):
+        high, low = split(plain * phases_ref[0, pl.ds(row, 1), :] + turned * phases_ref[1, pl.ds(row, 1), :])
+        out_ref[row] = jnp.concatenate((high, high, low), axis=0)
+        return carry
+
+    lax.fori_loop(0, out_ref.shape[0], body, 0, unroll=4)
 
 
 def tiles_kernel(sources, *refs):
-    source_refs = refs[1 : 1 + sources]
-    codes_ref, depth_ref, phases_ref, column_ref, out_ref = refs[:1] + refs[1 + sources : 5 + sources]
-    tiles_ref, acc_ref, even_ref, odd_ref, arrived = refs[5 + sources :]
+    source_refs = refs[:sources]
+    weights_ref, column_ref, out_ref, tiles_ref, codes_ref, acc_ref, arrived = refs[sources:]
     half = NX // 2
     stride = NY
     pairs = tiles_ref.shape[1]
     batch = 8
-    assert pairs % (2 * batch) == 0
-    batches = pairs // batch
     rows = column_ref.shape[1] // 4
     width = out_ref.shape[0]
 
-    def spectrum(source, number, to_ref):
-        tiles = jnp.concatenate([tiles_ref[source, number * batch + index] for index in range(batch)], axis=1)
-        high, low = split(tiles)
-        to_ref[...] = lax.dot_general(
-            jnp.concatenate((high, low, high), axis=0),
-            depth_ref[...],
-            (((0,), (0,)), ((), ())),
-            preferred_element_type=F32,
-        )
-
-    def accumulate(source, number, from_ref):
-        for tile in range(2 * batch):
-            code = codes_ref[(source * batches + number) * 2 * batch + tile]
-            base = lax.shift_right_logical(code, 7)
-            phase = jnp.bitwise_and(code, PHASES - 1)
-            cos = phases_ref[0, pl.ds(phase, 1), :]
-            sin = phases_ref[1, pl.ds(phase, 1), :]
-            for i in range(TILE):
-                row = tile * TILE * TILE + i * TILE
-                value = from_ref[row : row + TILE, :LANES] * cos + from_ref[row : row + TILE, LANES:] * sin
-                at = pl.ds(pl.multiple_of(base * TILE + i * stride, TILE), TILE)
-                acc_ref[at, :] = acc_ref[at, :] + value
-
     @pl.when(pl.program_id(0) == 0)
     def _():
-        copies = [
-            pltpu.make_async_copy(source_ref, tiles_ref.at[index], arrived.at[index])
-            for index, source_ref in enumerate(source_refs)
-        ]
+        copies = []
+        for index, ref in enumerate(source_refs):
+            copies.append(pltpu.make_async_copy(ref.at[pl.ds(0, pairs)], tiles_ref.at[index], arrived.at[0, index]))
+            copies.append(pltpu.make_async_copy(ref.at[pairs, pl.ds(0, TILE)], codes_ref.at[index], arrived.at[1, index]))
         for copy in copies:
             copy.start()
 
@@ -199,19 +207,28 @@
         lax.fori_loop(0, half, clear, 0)
         for copy in copies:
             copy.wait()
-        spectrum(0, 0, even_ref)
-
-        def add_pair(step, carry):
-            first = 2 * step
-            source, number = first // batches, first % batches
-            spectrum(source, number + 1, odd_ref)
-            accumulate(source, number, even_ref)
-            later = jnp.minimum(first + 2, sources * batches - 2)
-            spectrum(later // batches, later % batches, even_ref)
-            accumulate(source, number + 1, odd_ref)
+
+        def add_batch(step, carry):
+            source = step // (pairs // batch)
+            first = step % (pairs // batch) * batch
+            for index in range(batch):
+                high, low = split(tiles_ref[source, first + index])
+                stacked = jnp.concatenate((high, low, high), axis=0).T
+                for side in range(2):
+                    code = codes_ref[source, 0, 2 * (first + index) + side].astype(jnp.int32)
+                    base = lax.shift_right_logical(code, 7)
+                    phase = jnp.bitwise_and(code, PHASES - 1)
+                    value = jnp.dot(
+                        stacked[side * TILE * TILE : (side + 1) * TILE * TILE],
+                        weights_ref[phase],
+                        preferred_element_type=F32,
+                    )
+                    for i in range(TILE):
+                        at = pl.ds(pl.multiple_of(base * TILE + i * stride, TILE), TILE)
+                        acc_ref[at, :] = acc_ref[at, :] + value[i * TILE : (i + 1) * TILE]
             return carry
 
-        lax.fori_loop(0, sources * batches // 2, add_pair, 0)
+        lax.fori_loop(0, sources * pairs // batch, add_batch, 0)
 
     turn = jnp.where(lax.broadcasted_iota(jnp.int32, (rows, LANES), 1) < LANES // 2, -1.0, 1.0)
     origin = pl.program_id(0) * width
@@ -311,10 +328,9 @@
     grid_cols = lax.axis_size("gy")
     blocks = samples.shape[0]
     block_width = samples.shape[2]
-    assert block_width == LANES and blocks <= LANES
+    assert block_width == LANES and blocks == LANES
     tile_rows = NX // (TILE * grid_rows)
     tile_cols = NY // (TILE * grid_cols)
-    tile_depth = NZ // TILE
     planes = deapod_third.shape[0]
     per_device = deapod_second.shape[0]
     rows = padded_rows(per_device)
@@ -322,22 +338,14 @@
     vmem = pl.BlockSpec(memory_space=pltpu.VMEM)
     params = pltpu.CompilerParams(vmem_limit_bytes=VMEM_LIMIT)
 
-    owner = owners[:, 0]
-    row = owner // grid_cols * tile_rows + tile_ids // (tile_cols * tile_depth)
-    col = owner % grid_cols * tile_cols + tile_ids // tile_depth % tile_cols
-    folds = NX // TILE // 2
-    base = row % folds * NY + col
-    phase = tile_ids % tile_depth + row // folds * tile_depth
-    codes = base * PHASES + phase
-
     tiles = pl.pallas_call(
-        spread_kernel,
-        out_shape=jax.ShapeDtypeStruct((blocks // 2, 2 * TILE, LANES), F32),
-        in_specs=[vmem] * 3,
+        functools.partial(spread_kernel, tile_rows, tile_cols, grid_cols, grid_rows * grid_cols),
+        out_shape=jax.ShapeDtypeStruct((blocks // 2 + 1, 2 * TILE, LANES), F32),
+        in_specs=[vmem] * 5,
         out_specs=vmem,
         compiler_params=params,
         name="spread",
-    )(samples, kernel, offsets.transpose(1, 0, 2))
+    )(samples, kernel, offsets.transpose(1, 0, 2), owners.reshape(1, blocks), tile_ids.reshape(1, blocks))
 
     along = grid_cols // Z_CHIPS
 
@@ -349,12 +357,14 @@
         ]
         return lax.ppermute(value, "gy", moves)
 
-    def collect(value):
-        stack = [value] + [shift(value, deep, 0) for deep in (1, 3, 2)]
-        return stack + [shift(held, 0, wide) for wide in range(1, along) for held in stack]
-
-    tile_codes = jnp.concatenate(collect(codes))
-    gathered = collect(tiles)
+    gathered = [tiles] + [shift(tiles, deep, 0) for deep in (1, 3, 2)]
+    crossed_y = []
+    for held in list(gathered):
+        for wide in range(1, along):
+            if len(crossed_y) > 1:
+                held, _ = lax.optimization_barrier((held, crossed_y[-2]))
+            crossed_y.append(shift(held, 0, wide))
+    gathered += crossed_y
 
     place = lax.axis_index("gx").astype(jnp.int32).reshape(1)
     gy = lax.axis_index("gy")
@@ -362,6 +372,14 @@
     matrix = lax.dynamic_index_in_dim(jnp.asarray(matrices), gy, 0, keepdims=False)
     phase_rows = lax.dynamic_index_in_dim(jnp.asarray(phases), gy, 0, keepdims=False)
     column = jnp.asarray(column_tables(grid_rows, per_device))
+    weights = pl.pallas_call(
+        weights_kernel,
+        out_shape=jax.ShapeDtypeStruct((phases.shape[2], 6 * TILE, LANES), BF16),
+        in_specs=[vmem] * 2,
+        out_specs=vmem,
+        compiler_params=params,
+        name="weights",
+    )(matrix, phase_rows)
 
     def whole(shape):
         return pl.BlockSpec(shape, lambda step: (0,) * len(shape), pipeline_mode=pl.Buffered(1))
@@ -369,25 +387,22 @@
     half = NX // 2
     width = 16
     kept = 2 * grid_rows * rows
-    spectra = pltpu.VMEM((16 * TILE * TILE, 2 * LANES), F32)
     columns = pl.pallas_call(
         functools.partial(tiles_kernel, len(gathered)),
         grid=(half // width,),
         out_shape=jax.ShapeDtypeStruct((half, kept, LANES), F32),
-        in_specs=[pl.BlockSpec(memory_space=pltpu.SMEM)]
-        + [pl.BlockSpec(memory_space=pl.ANY)] * len(gathered)
-        + [whole(array.shape) for array in (matrix, phase_rows, column)],
+        in_specs=[pl.BlockSpec(memory_space=pl.ANY)] * len(gathered)
+        + [whole(array.shape) for array in (weights, column)],
         out_specs=pl.BlockSpec((width, kept, LANES), lambda step: (step, 0, 0)),
         scratch_shapes=[
-            pltpu.VMEM((len(gathered),) + tiles.shape, F32),
+            pltpu.VMEM((len(gathered), blocks // 2) + tiles.shape[1:], F32),
+            pltpu.SMEM((len(gathered), TILE, LANES), F32),
             pltpu.VMEM((half * NY, LANES), F32),
-            spectra,
-            spectra,
-            pltpu.SemaphoreType.DMA((len(gathered),)),
+            pltpu.SemaphoreType.DMA((2, len(gathered))),
         ],
         compiler_params=params,
         name="tiles",
-    )(tile_codes, *gathered, matrix, phase_rows, column)
+    )(*gathered, weights, column)
 
     row_table = jnp.asarray(row_tables())
     chunks = rows // TILE
@@ -419,11 +434,7 @@
             ),
             out_shape=jax.ShapeDtypeStruct((slots,) + part_shape, F32),
             compiler_params=params,
-            cost_estimate=pl.CostEstimate(
-                flops=2 * 3 * slots * 2 * LANES * half * 2 * LANES,
-                bytes_accessed=4 * (half * 2 * slots * LANES + slots * math.prod(part_shape)),
-                transcendentals=0,
-            ),
+            cost_estimate=pl.CostEstimate(flops=1, bytes_accessed=1, transcendentals=0),
             name="rows",
         )(place, columns, row_table, *addends, *after)
 
@@ -439,9 +450,21 @@
         return rows_for(relative, first, count, arrived, after)
 
     top = grid_rows // 2
-    crossing = [total(top, top // 2, chunk, 1, []) for chunk in range(chunks)]
-    kept_part = total(0, top // 2, 0, chunks, [crossing[-1]])
-    crossed = [swap(value, top) for value in crossing]
+    others, last = [], []
+    for chunk in range(chunks):
+        others.append(total(top | 1, 0, chunk, 1, last) if top == 2 else None)
+        last = others[-1:] if top == 2 else []
+    crossed, ready = [], []
+    for chunk in range(chunks):
+        after = others[chunk + 1 : chunk + 2] + ready[-1:]
+        if top == 2:
+            whole_part = rows_for(top, chunk, 1, [swap(others[chunk], 1)], after)
+        else:
+            whole_part = total(top, top // 2, chunk, 1, [])
+        ready.append(whole_part)
+        crossed.append(swap(whole_part, top))
+    near = [swap(total(bit, bit // 2, 0, chunks, ready[-1:]), bit) for bit in (1 << n for n in range(top.bit_length() - 1))]
+    kept_parts = [rows_for(0, 0, chunks, [], ready[-1:])] + near
 
     image = None
     shape = (2, planes, 2, per_device // 2, NX // 2)
@@ -451,15 +474,15 @@
             return (chunk, 0, 0, 0)
 
         def finish(*refs):
-            finish_kernel(planes_padded, 2, refs)
+            finish_kernel(planes_padded, len(kept_parts) + 1, refs)
 
         earlier = [] if image is None else [image]
         image = pl.pallas_call(
             finish,
             grid=(1,),
             out_shape=jax.ShapeDtypeStruct(shape, F32),
-            in_specs=[
-                pl.BlockSpec((TILE,) + part_shape, at_chunk),
+            in_specs=[pl.BlockSpec((TILE,) + part_shape, at_chunk)] * len(kept_parts)
+            + [
                 pl.BlockSpec((TILE,) + part_shape, lambda step: (0, 0, 0, 0)),
                 pl.BlockSpec((4 * LANES, NX // 2), lambda step: (0, 0)),
                 pl.BlockSpec((1, NX // 2), lambda step: (0, 0)),
@@ -468,11 +491,11 @@
             ]
             + [pl.BlockSpec(memory_space=pl.ANY)] * len(earlier),
             out_specs=pl.BlockSpec((2, planes, 2, TILE, NX // 2), lambda step, chunk=chunk: (0, 0, 0, chunk, 0)),
-            input_output_aliases={6: 0} if earlier else {},
+            input_output_aliases={len(kept_parts) + 5: 0} if earlier else {},
             compiler_params=params,
             name="finish",
         )(
-            kept_part,
+            *kept_parts,
             crossed[chunk],
             jnp.asarray(order_tables()),
             deapod_first[None, :],

time: 241 us -> 204 us (0.85)
  waiting for transfers between devices: 103 us -> 70.9 us
  Pallas kernels: 103 us -> 110 us
  starting transfers between devices: 20.5 us -> 13.8 us
  local copies, waits for them, and re-layouts: 10.8 us -> 7.3 us
    ppermute x14 -> x7, waiting for transfers between devices: 84.5 us -> 50.1 us  [shift(): return lax.ppermute(value, 'gy', moves)]
    ppermute x14 -> x7, starting transfers between devices: 16.3 us -> 9.29 us  [shift(): return lax.ppermute(value, 'gy', moves)]
    pallas_call x1, Pallas kernels: 49.2 us -> 53 us  [on_device(): pl.pallas_call(functools.partial(tiles_kernel, len(gathered)), grid=(half...]
    unnamed x38 -> x28, local copies, waits for them, and re-layouts: 7.24 us -> 3.73 us
    ppermute x7, waiting for transfers between devices: 18.3 us -> 20.8 us  [swap(): lax.ppermute(value, 'gx', [(index, index ^ bit) for index in range(grid_r...]
    pallas_call x1 -> x2, Pallas kernels: 6.21 us -> 8.44 us  [the longest x1 6.25 us: on_device(): pl.pallas_call(functools.partial(spread_kernel, tile_rows, tile_cols, gri...]
  transfers between devices with their start and end apart: 21 -> 14, of which waited for: 8 -> 8; matrix products, arithmetic and copies ran while one was open for 2% -> 2% of each run, Pallas kernels for 12% -> 16%
where the time goes in v4:
time: 204 us; the launch traced here: 202 us
  Pallas kernels  110 us (54%)
  waiting for transfers between devices  70.9 us (35%)
  starting transfers between devices  13.8 us (7%)
  local copies, waits for them, and re-layouts  7.3 us (4%)
    pallas_call x1, Pallas kernels, on_device(): pl.pallas_call(functools.partial(tiles_kernel, len(gathered)), grid=(half...  53 us
    ppermute x7, waiting for transfers between devices, shift(): return lax.ppermute(value, 'gy', moves)  50.1 us
    pallas_call x8, Pallas kernels, rows_for(): pl.pallas_call(body, grid_spec=pltpu.PrefetchScalarGridSpec(num_scalar_pr...  39 us
    ppermute x7, waiting for transfers between devices, swap(): lax.ppermute(value, 'gx', [(index, index ^ bit) for index in range(grid_r...  20.8 us
    pallas_call x3, Pallas kernels, on_device(): pl.pallas_call(finish, grid=(1,), out_shape=jax.ShapeDtypeStruct(shape, F...  9.51 us
    ppermute x7, starting transfers between devices, shift(): return lax.ppermute(value, 'gy', moves)  9.29 us
    pallas_call x1, Pallas kernels, on_device(): pl.pallas_call(functools.partial(spread_kernel, tile_rows, tile_cols, gri...  6.25 us
    ppermute x7, starting transfers between devices, swap(): lax.ppermute(value, 'gx', [(index, index ^ bit) for index in range(grid_r...  4.53 us
  transfers between devices with their start and end apart: 14, of which 8 were waited for; matrix products, arithmetic and copies ran while one was open for 2% of the time, Pallas kernels for 16%

profile of v4, /device:TPU:16, one launch (start us, length us, event | category | flops | bytes accessed | tf_op | source)
XLA Modules:
  0.0 202.2 jit_solution(11896585128900968800)
XLA Ops:
  0.0 6.2 %spread.1.refs_0_ = f32[65,16,128]{2,1,0:T(8,128)} custom-call(f32[128,2,128]{2,1,0:T(2,128)} %samples_ref.1, f32[128,3,4,128]{3,2,1,0:T(4,128)} %kernel_ref.1, s32[3,128,128]{2,1,0:T(8,128)} %bitcast.10, s32[1,128]{1,0:T(1,128)} %bitcast.14, s32[1,128]{1,0:T(1,128)} %bitcast.15), custom_call_target="tpu_custom_call" | custom-call | tf_op jit(solution)/shard_map/spread/pallas_call | solution.py:341
  6.2 1.6 collective-permute-start
  9.8 2.1 %collective-permute-start.2 = (f32[65,16,128]{2,1,0:T(8,128)}, f32[65,16,128]{2,1,0:T(8,128)S(1)}, u32[]{:S(2)}, u32[]{:S(2)}) collective-permute-start(f32[65,16,128]{2,1,0:T(8,128)} %spread.1.refs_0_), channel_id=1, source_target_pairs={{0,4},{1,5},{2,6},{3,7},{4,0},{5,1},{6,2},{7,3},{8,12},{9,13},{10,... | collective-permute-start | bytes 1597448 | tf_op jit(solution)/shard_map/ppermute | solution.py:358
  11.9 32.3 %collective-permute-done.refs_1_ = f32[65,16,128]{2,1,0:T(8,128)S(1)} collective-permute-done((f32[65,16,128]{2,1,0:T(8,128)}, f32[65,16,128]{2,1,0:T(8,128)S(1)}, u32[]{:S(2)}, u32[]{:S(2)}) %collective-permute-start) | collective-permute-done | bytes 532512 | tf_op jit(solution)/shard_map/ppermute | solution.py:358
  46.4 7.1 %collective-permute-done.2.refs_3_ = f32[65,16,128]{2,1,0:T(8,128)S(1)} collective-permute-done((f32[65,16,128]{2,1,0:T(8,128)}, f32[65,16,128]{2,1,0:T(8,128)S(1)}, u32[]{:S(2)}, u32[]{:S(2)}) %collective-permute-start.2) | collective-permute-done | bytes 532512 | tf_op jit(solution)/shard_map/ppermute | solution.py:358
  56.4 1.5 dynamic-slice_bitcast_fusion.phases_ref
  57.9 2.2 %weights.1.refs_8_ = bf16[96,48,128]{2,1,0:T(8,128)(2,1)} custom-call(f32[2,16,128]{2,1,0:T(8,128)} %dynamic-slice_bitcast_fusion.1.matrix_ref, f32[2,96,128]{2,1,0:T(8,128)} %dynamic-slice_bitcast_fusion.phases_ref), custom_call_target="tpu_custom_call" | custom-call | tf_op jit(solution)/shard_map/weights/pallas_call | solution.py:375
  60.1 2.2 %collective-permute-done.5.refs_6_ = f32[65,16,128]{2,1,0:T(8,128)S(1)} collective-permute-done((f32[65,16,128]{2,1,0:T(8,128)S(1)}, f32[65,16,128]{2,1,0:T(8,128)S(1)}, u32[]{:S(2)}, u32[]{:S(2)}) %collective-permute-start.5) | collective-permute-done | bytes 532512 | tf_op jit(solution)/shard_map/ppermute | solution.py:358
  62.4 8.4 %collective-permute-done.6.refs_7_ = f32[65,16,128]{2,1,0:T(8,128)} collective-permute-done((f32[65,16,128]{2,1,0:T(8,128)S(1)}, f32[65,16,128]{2,1,0:T(8,128)}, u32[]{:S(2)}, u32[]{:S(2)}) %collective-permute-start.6) | collective-permute-done | bytes 532512 | tf_op jit(solution)/shard_map/ppermute | solution.py:358
  70.8 53.0 %tiles.1.refs_1_ = f32[192,192,128]{2,1,0:T(8,128)} custom-call(f32[65,16,128]{2,1,0:T(8,128)} %spread.1.refs_0_, f32[65,16,128]{2,1,0:T(8,128)} %copy-done.7, f32[65,16,128]{2,1,0:T(8,128)} %copy-done.8, f32[65,16,128]{2,1,0:T(8,128)} %copy-done.10, f32[65,16,128]{2,1,0:T(8,128)} %copy-done.9, f32[65,16,128]{2,1,0:T(8,128)} %copy-done.11, ...), custom_call_target="tpu_custom_call" | custom-call | tf_op jit(solution)/shard_map/tiles/pallas_call | solution.py:390
  123.8 3.7 %rows.8.refs_3_ = f32[8,3,48,128]{3,2,1,0:T(8,128)} custom-call(s32[1]{0:T(128)} %bitcast.refs_0_, f32[192,192,128]{2,1,0:T(8,128)} %tiles.1.refs_1_, bf16[2,2,192,256]{3,2,1,0:T(8,128)(2,1)} %constant.31.clone.refs_2_), custom_call_target="tpu_custom_call" | custom-call | flops 1 | bytes 1 | tf_op jit(solution)/shard_map/rows/pallas_call | solution.py:422
  127.5 3.7 %rows.9.refs_3_.refs_4_ = f32[8,3,48,128]{3,2,1,0:T(8,128)} custom-call(s32[1]{0:T(128)} %bitcast.refs_0_, f32[192,192,128]{2,1,0:T(8,128)} %tiles.1.refs_1_, bf16[2,2,192,256]{3,2,1,0:T(8,128)(2,1)} %constant.31.clone.refs_2_, f32[8,3,48,128]{3,2,1,0:T(8,128)} %rows.8.refs_3_), custom_call_target="tpu_custom_call" | custom-call | flops 1 | bytes 1 | tf_op jit(solution)/shard_map/rows/pallas_call | solution.py:422
  131.7 3.7 %rows.10.refs_4_ = f32[8,3,48,128]{3,2,1,0:T(8,128)} custom-call(s32[1]{0:T(128)} %bitcast.refs_0_, f32[192,192,128]{2,1,0:T(8,128)} %tiles.1.refs_1_, bf16[2,2,192,256]{3,2,1,0:T(8,128)(2,1)} %constant.31.clone.refs_2_, f32[8,3,48,128]{3,2,1,0:T(8,128)} %rows.9.refs_3_.refs_4_), custom_call_target="tpu_custom_call" | custom-call | flops 1 | bytes 1 | tf_op jit(solution)/shard_map/rows/pallas_call | solution.py:422
  136.2 3.9 %rows.11.refs_5_ = f32[8,3,48,128]{3,2,1,0:T(8,128)} custom-call(s32[1]{0:T(128)} %bitcast.refs_0_, f32[192,192,128]{2,1,0:T(8,128)} %tiles.1.refs_1_, bf16[2,2,192,256]{3,2,1,0:T(8,128)(2,1)} %constant.31.clone.refs_2_, f32[8,3,48,128]{3,2,1,0:T(8,128)} %copy-done.6, f32[8,3,48,128]{3,2,1,0:T(8,128)} %rows.9.refs_3_.refs_4_), custom_call_target="tpu_custom_call" | custom-call | flops 1 | bytes 1 | tf_op jit(solution)/shard_map/rows/pallas_call | solution.py:422
  140.9 3.9 %rows.12.refs_4_ = f32[8,3,48,128]{3,2,1,0:T(8,128)} custom-call(s32[1]{0:T(128)} %bitcast.refs_0_, f32[192,192,128]{2,1,0:T(8,128)} %tiles.1.refs_1_, bf16[2,2,192,256]{3,2,1,0:T(8,128)(2,1)} %constant.31.clone.refs_2_, f32[8,3,48,128]{3,2,1,0:T(8,128)} %copy-done.5, f32[8,3,48,128]{3,2,1,0:T(8,128)} %rows.10.refs_4_, f32[8,3,48,128]{3,2,1,0:T(8,128)} %rows.11.refs_5_), custom_call_target="tpu_custom_call" | custom-call | flops 1 | bytes 1 | tf_op jit(solution)/shard_map/rows/pallas_call | solution.py:422
  145.6 3.9 %rows.13.refs_3_ = f32[8,3,48,128]{3,2,1,0:T(8,128)} custom-call(s32[1]{0:T(128)} %bitcast.refs_0_, f32[192,192,128]{2,1,0:T(8,128)} %tiles.1.refs_1_, bf16[2,2,192,256]{3,2,1,0:T(8,128)(2,1)} %constant.31.clone.refs_2_, f32[8,3,48,128]{3,2,1,0:T(8,128)} %copy-done.4, f32[8,3,48,128]{3,2,1,0:T(8,128)} %rows.12.refs_4_), custom_call_target="tpu_custom_call" | custom-call | flops 1 | bytes 1 | tf_op jit(solution)/shard_map/rows/pallas_call | solution.py:422
  149.5 8.3 %rows.15 = f32[24,3,48,128]{3,2,1,0:T(8,128)} custom-call(s32[1]{0:T(128)} %bitcast.refs_0_, f32[192,192,128]{2,1,0:T(8,128)} %tiles.1.refs_1_, bf16[2,2,192,256]{3,2,1,0:T(8,128)(2,1)} %constant.31.clone.refs_2_, f32[8,3,48,128]{3,2,1,0:T(8,128)} %rows.13.refs_3_), custom_call_target="tpu_custom_call" | custom-call | flops 1 | bytes 1 | tf_op jit(solution)/shard_map/rows/pallas_call | solution.py:422
  162.5 8.1 %rows.14.refs_0_ = f32[24,3,48,128]{3,2,1,0:T(8,128)} custom-call(s32[1]{0:T(128)} %bitcast.refs_0_, f32[192,192,128]{2,1,0:T(8,128)} %tiles.1.refs_1_, bf16[2,2,192,256]{3,2,1,0:T(8,128)(2,1)} %constant.31.clone.refs_2_, f32[8,3,48,128]{3,2,1,0:T(8,128)} %rows.13.refs_3_), custom_call_target="tpu_custom_call" | custom-call | flops 1 | bytes 1 | tf_op jit(solution)/shard_map/rows/pallas_call | solution.py:422
  170.6 4.0 %collective-permute-done.13.refs_2_ = f32[8,3,48,128]{3,2,1,0:T(8,128)} collective-permute-done((f32[8,3,48,128]{3,2,1,0:T(8,128)S(1)}, f32[8,3,48,128]{3,2,1,0:T(8,128)}, u32[]{:S(2)}, u32[]{:S(2)}) %collective-permute-start.13) | collective-permute-done | bytes 589856 | tf_op jit(solution)/shard_map/ppermute | solution.py:442
  175.8 3.2 %finish.3.refs_7_ = f32[2,24,2,24,192]{4,3,2,1,0:T(8,128)} custom-call(f32[24,3,48,128]{3,2,1,0:T(8,128)} %rows.14.refs_0_, f32[24,3,48,128]{3,2,1,0:T(8,128)} %copy-done, f32[8,3,48,128]{3,2,1,0:T(8,128)} %collective-permute-done.13.refs_2_, bf16[512,192]{1,0:T(8,128)(2,1)} %constant.32.clone.refs_3_, f32[1,192]{1,0:T(1,128)} %bitcast.11, ...), custom_call_target="tpu_custom_call" | custom-call | tf_op jit(solution)/shard_map/finish/pallas_call | solution.py:480
  179.0 8.2 %collective-permute-done.12.refs_2_ = f32[8,3,48,128]{3,2,1,0:T(8,128)} collective-permute-done((f32[8,3,48,128]{3,2,1,0:T(8,128)S(1)}, f32[8,3,48,128]{3,2,1,0:T(8,128)}, u32[]{:S(2)}, u32[]{:S(2)}) %collective-permute-start.12) | collective-permute-done | bytes 589856 | tf_op jit(solution)/shard_map/ppermute | solution.py:442
  187.2 3.2 %finish.4.refs_7_ = f32[2,24,2,24,192]{4,3,2,1,0:T(8,128)} custom-call(f32[24,3,48,128]{3,2,1,0:T(8,128)} %rows.14.refs_0_, f32[24,3,48,128]{3,2,1,0:T(8,128)} %copy-done, f32[8,3,48,128]{3,2,1,0:T(8,128)} %collective-permute-done.12.refs_2_, bf16[512,192]{1,0:T(8,128)(2,1)} %constant.32.clone.refs_3_, ...), custom_call_target="tpu_custom_call", output_to_operand_aliasing={{}: (7, {})} | custom-call | tf_op jit(solution)/shard_map/finish/pallas_call | solution.py:480
  190.4 8.6 %collective-permute-done.11.refs_2_ = f32[8,3,48,128]{3,2,1,0:T(8,128)} collective-permute-done((f32[8,3,48,128]{3,2,1,0:T(8,128)S(1)}, f32[8,3,48,128]{3,2,1,0:T(8,128)}, u32[]{:S(2)}, u32[]{:S(2)}) %collective-permute-start.11) | collective-permute-done | bytes 589856 | tf_op jit(solution)/shard_map/ppermute | solution.py:442
  199.0 3.2 %finish.5 = f32[2,24,2,24,192]{4,3,2,1,0:T(8,128)} custom-call(f32[24,3,48,128]{3,2,1,0:T(8,128)} %rows.14.refs_0_, f32[24,3,48,128]{3,2,1,0:T(8,128)} %copy-done, f32[8,3,48,128]{3,2,1,0:T(8,128)} %collective-permute-done.11.refs_2_, bf16[512,192]{1,0:T(8,128)(2,1)} %constant.32.clone.refs_3_, f32[1,192]{1,0:T(1,128)} %bitcast.13, ...), custom_call_target="tpu_custom_call", output_to_operand_aliasing={{}: (7, {})} | custom-call | tf_op jit(solution)/shard_map/finish/pallas_call | solution.py:480
  (49 shorter events, 16.0 us)
Async XLA Ops:
  6.2 38.0 %collective-permute-start = (f32[65,16,128]{2,1,0:T(8,128)}, f32[65,16,128]{2,1,0:T(8,128)S(1)}, u32[]{:S(2)}, u32[]{:S(2)}) collective-permute-start(f32[65,16,128]{2,1,0:T(8,128)} %spread.1.refs_0_), channel_id=1, source_target_pairs={{0,2},{1,3},{2,4},{3,5},{4,6},{5,7},{6,0},{7,1},{8,10},{9,11},{10,... | collective-permute-start | bytes 1597448 | tf_op jit(solution)/shard_map/ppermute | solution.py:358
  7.8 38.0 %collective-permute-start.1 = (f32[65,16,128]{2,1,0:T(8,128)}, f32[65,16,128]{2,1,0:T(8,128)S(1)}, u32[]{:S(2)}, u32[]{:S(2)}) collective-permute-start(f32[65,16,128]{2,1,0:T(8,128)} %spread.1.refs_0_), channel_id=1, source_target_pairs={{0,6},{1,7},{2,0},{3,1},{4,2},{5,3},{6,4},{7,5},{8,14},{9,15},{10,... | collective-permute-start | bytes 1597448 | tf_op jit(solution)/shard_map/ppermute | solution.py:358
  8.3 37.5 %collective-permute-start.3 = (f32[65,16,128]{2,1,0:T(8,128)}, f32[65,16,128]{2,1,0:T(8,128)S(1)}, u32[]{:S(2)}, u32[]{:S(2)}) collective-permute-start(f32[65,16,128]{2,1,0:T(8,128)} %spread.1.refs_0_), channel_id=1, source_target_pairs={{0,1},{1,0},{2,3},{3,2},{4,5},{5,4},{6,7},{7,6},{8,9},{9,8},{10,11... | collective-permute-start | bytes 1597448 | tf_op jit(solution)/shard_map/ppermute | solution.py:358
  9.8 43.7 %collective-permute-start.2 = (f32[65,16,128]{2,1,0:T(8,128)}, f32[65,16,128]{2,1,0:T(8,128)S(1)}, u32[]{:S(2)}, u32[]{:S(2)}) collective-permute-start(f32[65,16,128]{2,1,0:T(8,128)} %spread.1.refs_0_), channel_id=1, source_target_pairs={{0,4},{1,5},{2,6},{3,7},{4,0},{5,1},{6,2},{7,3},{8,12},{9,13},{10,... | collective-permute-start | bytes 1597448 | tf_op jit(solution)/shard_map/ppermute | solution.py:358
  44.3 26.5 %copy-start.7 = (f32[65,16,128]{2,1,0:T(8,128)}, f32[65,16,128]{2,1,0:T(8,128)S(1)}, u32[]{:S(2)}) copy-start(f32[65,16,128]{2,1,0:T(8,128)S(1)} %collective-permute-done.refs_1_) | copy-start | bytes 1597444
  44.3 9.3 %collective-permute-start.4 = (f32[65,16,128]{2,1,0:T(8,128)S(1)}, f32[65,16,128]{2,1,0:T(8,128)S(1)}, u32[]{:S(2)}, u32[]{:S(2)}) collective-permute-start(f32[65,16,128]{2,1,0:T(8,128)S(1)} %collective-permute-done.refs_1_), channel_id=1, source_target_pairs={{0,1},{1,0},{2,3},{3,2},{4,5},{5,4},{6,7},{7,6},{8,9},{9,8},{10,11... | collective-permute-start | bytes 1597448 | tf_op jit(solution)/shard_map/ppermute | solution.py:358
  45.8 25.0 %copy-start.8 = (f32[65,16,128]{2,1,0:T(8,128)}, f32[65,16,128]{2,1,0:T(8,128)S(1)}, u32[]{:S(2)}) copy-start(f32[65,16,128]{2,1,0:T(8,128)S(1)} %collective-permute-done.1.refs_2_) | copy-start | bytes 1597444
  45.8 25.0 %copy-start.9 = (f32[65,16,128]{2,1,0:T(8,128)}, f32[65,16,128]{2,1,0:T(8,128)S(1)}, u32[]{:S(2)}) copy-start(f32[65,16,128]{2,1,0:T(8,128)S(1)} %collective-permute-done.3.refs_4_) | copy-start | bytes 1597444
  45.8 16.5 %collective-permute-start.5 = (f32[65,16,128]{2,1,0:T(8,128)S(1)}, f32[65,16,128]{2,1,0:T(8,128)S(1)}, u32[]{:S(2)}, u32[]{:S(2)}) collective-permute-start(f32[65,16,128]{2,1,0:T(8,128)S(1)} %collective-permute-done.1.refs_2_), channel_id=1, source_target_pairs={{0,1},{1,0},{2,3},{3,2},{4,5},{5,4},{6,7},{7,6},{8,9},{9,8},{10,11... | collective-permute-start | bytes 1597448 | tf_op jit(solution)/shard_map/ppermute | solution.py:358
  53.5 17.3 %copy-start.10 = (f32[65,16,128]{2,1,0:T(8,128)}, f32[65,16,128]{2,1,0:T(8,128)S(1)}, u32[]{:S(2)}) copy-start(f32[65,16,128]{2,1,0:T(8,128)S(1)} %collective-permute-done.2.refs_3_) | copy-start | bytes 1597444
  53.5 17.2 %copy-start.11 = (f32[65,16,128]{2,1,0:T(8,128)}, f32[65,16,128]{2,1,0:T(8,128)S(1)}, u32[]{:S(2)}) copy-start(f32[65,16,128]{2,1,0:T(8,128)S(1)} %collective-permute-done.4.refs_5_) | copy-start | bytes 1597444
  53.5 17.2 %collective-permute-start.6 = (f32[65,16,128]{2,1,0:T(8,128)S(1)}, f32[65,16,128]{2,1,0:T(8,128)}, u32[]{:S(2)}, u32[]{:S(2)}) collective-permute-start(f32[65,16,128]{2,1,0:T(8,128)S(1)} %collective-permute-done.2.refs_3_), channel_id=1, source_target_pairs={{0,1},{1,0},{2,3},{3,2},{4,5},{5,4},{6,7},{7,6},{8,9},{9,8},{10,11... | collective-permute-start | bytes 1597448 | tf_op jit(solution)/shard_map/ppermute | solution.py:358
  62.4 8.4 %copy-start.12 = (f32[65,16,128]{2,1,0:T(8,128)}, f32[65,16,128]{2,1,0:T(8,128)S(1)}, u32[]{:S(2)}) copy-start(f32[65,16,128]{2,1,0:T(8,128)S(1)} %collective-permute-done.5.refs_6_) | copy-start | bytes 1597444
  127.5 7.9 %collective-permute-start.9 = (f32[8,3,48,128]{3,2,1,0:T(8,128)}, f32[8,3,48,128]{3,2,1,0:T(8,128)S(1)}, u32[]{:S(2)}, u32[]{:S(2)}) collective-permute-start(f32[8,3,48,128]{3,2,1,0:T(8,128)} %rows.8.refs_3_), channel_id=1, source_target_pairs={{0,8},{8,0},{16,24},{24,16},{1,9},{9,1},{17,25},{25,17},{2,10},{10... | collective-permute-start | bytes 1769480 | tf_op jit(solution)/shard_map/ppermute | solution.py:442
  131.2 8.9 %collective-permute-start.8 = (f32[8,3,48,128]{3,2,1,0:T(8,128)}, f32[8,3,48,128]{3,2,1,0:T(8,128)S(1)}, u32[]{:S(2)}, u32[]{:S(2)}) collective-permute-start(f32[8,3,48,128]{3,2,1,0:T(8,128)} %rows.9.refs_3_.refs_4_), channel_id=1, source_target_pairs={{0,8},{8,0},{16,24},{24,16},{1,9},{9,1},{17,25},{25,17},{2,10},{10... | collective-permute-start | bytes 1769480 | tf_op jit(solution)/shard_map/ppermute | solution.py:442
  135.4 9.4 %collective-permute-start.7 = (f32[8,3,48,128]{3,2,1,0:T(8,128)}, f32[8,3,48,128]{3,2,1,0:T(8,128)S(1)}, u32[]{:S(2)}, u32[]{:S(2)}) collective-permute-start(f32[8,3,48,128]{3,2,1,0:T(8,128)} %rows.10.refs_4_), channel_id=1, source_target_pairs={{0,8},{8,0},{16,24},{24,16},{1,9},{9,1},{17,25},{25,17},{2,10},{10... | collective-permute-start | bytes 1769480 | tf_op jit(solution)/shard_map/ppermute | solution.py:442
  149.5 8.8 %copy-start.3 = (f32[8,3,48,128]{3,2,1,0:T(8,128)S(1)}, f32[8,3,48,128]{3,2,1,0:T(8,128)}, u32[]{:S(2)}) copy-start(f32[8,3,48,128]{3,2,1,0:T(8,128)} %rows.11.refs_5_) | copy-start | bytes 1769476
  149.5 10.3 %copy-start.2 = (f32[8,3,48,128]{3,2,1,0:T(8,128)S(1)}, f32[8,3,48,128]{3,2,1,0:T(8,128)}, u32[]{:S(2)}) copy-start(f32[8,3,48,128]{3,2,1,0:T(8,128)} %rows.12.refs_4_) | copy-start | bytes 1769476
  149.5 10.8 %copy-start.1 = (f32[8,3,48,128]{3,2,1,0:T(8,128)S(1)}, f32[8,3,48,128]{3,2,1,0:T(8,128)}, u32[]{:S(2)}) copy-start(f32[8,3,48,128]{3,2,1,0:T(8,128)} %rows.13.refs_3_) | copy-start | bytes 1769476
  149.5 12.3 %copy-start.13 = (f32[48]{0:T(128)S(1)}, f32[48]{0:T(128)}, u32[]{:S(2)}) copy-start(f32[48]{0:T(128)} %param.21) | copy-start | bytes 580
  157.8 16.8 %collective-permute-start.10 = (f32[24,3,48,128]{3,2,1,0:T(8,128)}, f32[24,3,48,128]{3,2,1,0:T(8,128)S(1)}, u32[]{:S(2)}, u32[]{:S(2)}) collective-permute-start(f32[24,3,48,128]{3,2,1,0:T(8,128)} %rows.15), channel_id=1, source_target_pairs={{0,8},{8,0},{16,24},{24,16},{1,9},{9,1},{17,25},{25,17},{2,10},{10... | collective-permute-start | bytes 5308424 | tf_op jit(solution)/shard_map/ppermute | solution.py:442
  158.3 16.3 %collective-permute-start.13 = (f32[8,3,48,128]{3,2,1,0:T(8,128)S(1)}, f32[8,3,48,128]{3,2,1,0:T(8,128)}, u32[]{:S(2)}, u32[]{:S(2)}) collective-permute-start(f32[8,3,48,128]{3,2,1,0:T(8,128)S(1)} %copy-done.3), channel_id=1, source_target_pairs={{0,16},{8,24},{16,0},{24,8},{1,17},{9,25},{17,1},{25,9},{2,18},{10... | collective-permute-start | bytes 1769480 | tf_op jit(solution)/shard_map/ppermute | solution.py:442
  159.8 27.5 %collective-permute-start.12 = (f32[8,3,48,128]{3,2,1,0:T(8,128)S(1)}, f32[8,3,48,128]{3,2,1,0:T(8,128)}, u32[]{:S(2)}, u32[]{:S(2)}) collective-permute-start(f32[8,3,48,128]{3,2,1,0:T(8,128)S(1)} %copy-done.2), channel_id=1, source_target_pairs={{0,16},{8,24},{16,0},{24,8},{1,17},{9,25},{17,1},{25,9},{2,18},{10... | collective-permute-start | bytes 1769480 | tf_op jit(solution)/shard_map/ppermute | solution.py:442
  160.3 38.6 %collective-permute-start.11 = (f32[8,3,48,128]{3,2,1,0:T(8,128)S(1)}, f32[8,3,48,128]{3,2,1,0:T(8,128)}, u32[]{:S(2)}, u32[]{:S(2)}) collective-permute-start(f32[8,3,48,128]{3,2,1,0:T(8,128)S(1)} %copy-done.1), channel_id=1, source_target_pairs={{0,16},{8,24},{16,0},{24,8},{1,17},{9,25},{17,1},{25,9},{2,18},{10... | collective-permute-start | bytes 1769480 | tf_op jit(solution)/shard_map/ppermute | solution.py:442
  (4 other events, 3.7 us)

commit v5 on v4

--- a/solution.py
+++ b/solution.py
@@ -52,13 +52,13 @@
         cos, sin = cos * used / math.sqrt(NZ), sin * used / math.sqrt(NZ)
         real = np.where(lane_part == 0, cos, sin)
         imag = np.where(lane_part == 0, -sin, cos)
-        plain = np.concatenate((real, imag))
-        turned = np.concatenate((-np.where(lane_part == 0, sin, -cos), -np.where(lane_part == 0, cos, sin)))
-        matrices.append(np.stack((plain, turned)))
+        high, low = halves(np.concatenate((real, imag)))
+        matrices.append(np.concatenate((high, high, low)))
         cos, sin = waves(np.arange(NZ // TILE), position, NZ // TILE)
         sign = np.where(lane_odd == 1, -1.0, 1.0)[None, :]
+        sin = sin * np.where(lane_part == 0, -1.0, 1.0)[None, :]
         phases.append(np.stack((np.concatenate((cos, cos * sign)), np.concatenate((sin, sin * sign)))))
-    return np.stack(matrices).astype(np.float32), np.stack(phases).astype(np.float32)
+    return np.stack(matrices), np.stack(phases).astype(np.float32)
 
 
 def padded_rows(per_device):
@@ -170,20 +170,11 @@
     out_ref[blocks // 2] = jnp.broadcast_to(codes, (2 * TILE, LANES))
 
 
-def weights_kernel(matrix_ref, phases_ref, out_ref):
-    plain, turned = matrix_ref[0], matrix_ref[1]
-
-    def body(row, carry):
-        high, low = split(plain * phases_ref[0, pl.ds(row, 1), :] + turned * phases_ref[1, pl.ds(row, 1), :])
-        out_ref[row] = jnp.concatenate((high, high, low), axis=0)
-        return carry
-
-    lax.fori_loop(0, out_ref.shape[0], body, 0, unroll=4)
-
-
-def tiles_kernel(sources, *refs):
-    source_refs = refs[:sources]
-    weights_ref, column_ref, out_ref, tiles_ref, codes_ref, acc_ref, arrived = refs[sources:]
+def tiles_kernel(arrays, *refs):
+    deep_ref = refs[0]
+    source_refs = refs[1 : 1 + arrays]
+    depth_ref, phases_ref, column_ref, out_ref, tiles_ref, codes_ref, acc_ref, even_ref, odd_ref, arrived = refs[1 + arrays :]
+    sources = tiles_ref.shape[0]
     half = NX // 2
     stride = NY
     pairs = tiles_ref.shape[1]
@@ -193,42 +184,77 @@
 
     @pl.when(pl.program_id(0) == 0)
     def _():
-        copies = []
-        for index, ref in enumerate(source_refs):
-            copies.append(pltpu.make_async_copy(ref.at[pl.ds(0, pairs)], tiles_ref.at[index], arrived.at[0, index]))
-            copies.append(pltpu.make_async_copy(ref.at[pairs, pl.ds(0, TILE)], codes_ref.at[index], arrived.at[1, index]))
-        for copy in copies:
-            copy.start()
+        def copies(array, slot):
+            ref = source_refs[array]
+            return (
+                pltpu.make_async_copy(ref.at[pl.ds(0, pairs)], tiles_ref.at[slot], arrived.at[0, slot]),
+                pltpu.make_async_copy(ref.at[pairs, pl.ds(0, TILE)], codes_ref.at[slot], arrived.at[1, slot]),
+            )
+
+        def start(array, slot):
+            for copy in copies(array, slot):
+                copy.start()
+
+        chips = Z_CHIPS
+        for slot in range(sources):
+            array = slot // chips * (2 * chips - 1) + max(2 * (slot % chips) - 1, 0)
+            if slot % chips == 0:
+                start(array, slot)
+            else:
+                upper = deep_ref[0] >= slot % chips
+                pl.when(upper)(functools.partial(start, array, slot))
+                pl.when(jnp.logical_not(upper))(functools.partial(start, array + 1, slot))
 
         def clear(step, carry):
             acc_ref[pl.ds(pl.multiple_of(step * stride, stride), stride), :] = jnp.zeros((stride, LANES), F32)
             return carry
 
         lax.fori_loop(0, half, clear, 0)
-        for copy in copies:
-            copy.wait()
-
-        def add_batch(step, carry):
-            source = step // (pairs // batch)
-            first = step % (pairs // batch) * batch
-            for index in range(batch):
-                high, low = split(tiles_ref[source, first + index])
-                stacked = jnp.concatenate((high, low, high), axis=0).T
-                for side in range(2):
-                    code = codes_ref[source, 0, 2 * (first + index) + side].astype(jnp.int32)
-                    base = lax.shift_right_logical(code, 7)
-                    phase = jnp.bitwise_and(code, PHASES - 1)
-                    value = jnp.dot(
-                        stacked[side * TILE * TILE : (side + 1) * TILE * TILE],
-                        weights_ref[phase],
-                        preferred_element_type=F32,
-                    )
-                    for i in range(TILE):
-                        at = pl.ds(pl.multiple_of(base * TILE + i * stride, TILE), TILE)
-                        acc_ref[at, :] = acc_ref[at, :] + value[i * TILE : (i + 1) * TILE]
+        for slot in range(sources):
+            for copy in copies(0, slot):
+                copy.wait()
+
+        batches = pairs // batch
+        assert batches % 2 == 0
+
+        def spectrum(source, number, to_ref):
+            first = number * batch
+            tiles = jnp.concatenate([tiles_ref[source, first + index] for index in range(batch)], axis=1)
+            high, low = split(tiles)
+            to_ref[...] = lax.dot_general(
+                jnp.concatenate((high, low, high), axis=0),
+                depth_ref[...],
+                (((0,), (0,)), ((), ())),
+                preferred_element_type=F32,
+            )
+
+        def accumulate(source, number, from_ref):
+            for tile in range(2 * batch):
+                code = codes_ref[source, 0, number * 2 * batch + tile].astype(jnp.int32)
+                base = lax.shift_right_logical(code, 7)
+                phase = jnp.bitwise_and(code, PHASES - 1)
+                cos = phases_ref[0, pl.ds(phase, 1), :]
+                sin = phases_ref[1, pl.ds(phase, 1), :]
+                for i in range(TILE):
+                    row = tile * TILE * TILE + i * TILE
+                    value = from_ref[row : row + TILE, :]
+                    value = value * cos + pltpu.roll(value, LANES // 2, 1) * sin
+                    at = pl.ds(pl.multiple_of(base * TILE + i * stride, TILE), TILE)
+                    acc_ref[at, :] = acc_ref[at, :] + value
+
+        spectrum(0, 0, even_ref)
+
+        def add_pair(step, carry):
+            source = step // (batches // 2)
+            number = step % (batches // 2) * 2
+            spectrum(source, number + 1, odd_ref)
+            accumulate(source, number, even_ref)
+            later = jnp.minimum(step + 1, sources * batches // 2 - 1)
+            spectrum(later // (batches // 2), later % (batches // 2) * 2, even_ref)
+            accumulate(source, number + 1, odd_ref)
             return carry
 
-        lax.fori_loop(0, sources * pairs // batch, add_batch, 0)
+        lax.fori_loop(0, sources * batches // 2, add_pair, 0)
 
     turn = jnp.where(lax.broadcasted_iota(jnp.int32, (rows, LANES), 1) < LANES // 2, -1.0, 1.0)
     origin = pl.program_id(0) * width
@@ -348,61 +374,73 @@
     )(samples, kernel, offsets.transpose(1, 0, 2), owners.reshape(1, blocks), tile_ids.reshape(1, blocks))
 
     along = grid_cols // Z_CHIPS
-
-    def shift(value, deep, wide):
+    deep_at = lax.div(lax.axis_index("gy").astype(jnp.int32), jnp.int32(along))
+
+    def shift(value, senders, deep, wide):
         moves = [
-            (z * along + y, (z + deep) % Z_CHIPS * along + (y + wide) % along)
-            for z in range(Z_CHIPS)
-            for y in range(along)
+            (z * along + y, (z + deep) * along + (y + wide) % along) for z in senders for y in range(along)
         ]
         return lax.ppermute(value, "gy", moves)
 
-    gathered = [tiles] + [shift(tiles, deep, 0) for deep in (1, 3, 2)]
-    crossed_y = []
-    for held in list(gathered):
+    held = {0: tiles}
+    for steps in range(1, Z_CHIPS):
+        held[steps] = shift(held[steps - 1], range(steps - 1, Z_CHIPS - 1), 1, 0)
+        held[-steps] = shift(held[1 - steps], range(1, Z_CHIPS + 1 - steps), -1, 0)
+    holders = {0: range(Z_CHIPS)}
+    for steps in range(1, Z_CHIPS):
+        holders[steps] = range(steps, Z_CHIPS)
+        holders[-steps] = range(Z_CHIPS - steps)
+    crossed_y = {}
+    chain = []
+    for steps in sorted(held, key=abs):
         for wide in range(1, along):
-            if len(crossed_y) > 1:
-                held, _ = lax.optimization_barrier((held, crossed_y[-2]))
-            crossed_y.append(shift(held, 0, wide))
-    gathered += crossed_y
-
+            value = held[steps]
+            if len(chain) > 1:
+                value, _ = lax.optimization_barrier((value, chain[-2]))
+            crossed_y[steps, wide] = shift(value, holders[steps], 0, wide)
+            chain.append(crossed_y[steps, wide])
+    gathered = [tiles]
+    for wide in range(along):
+        def pick(steps):
+            return crossed_y[steps, wide] if wide else held[steps]
+
+        if wide:
+            gathered.append(pick(0))
+        for steps in range(1, Z_CHIPS):
+            gathered += [pick(steps), pick(steps - Z_CHIPS)]
     place = lax.axis_index("gx").astype(jnp.int32).reshape(1)
+    deep_place = deep_at.reshape(1)
     gy = lax.axis_index("gy")
     matrices, phases = depth_tables(planes)
     matrix = lax.dynamic_index_in_dim(jnp.asarray(matrices), gy, 0, keepdims=False)
     phase_rows = lax.dynamic_index_in_dim(jnp.asarray(phases), gy, 0, keepdims=False)
     column = jnp.asarray(column_tables(grid_rows, per_device))
-    weights = pl.pallas_call(
-        weights_kernel,
-        out_shape=jax.ShapeDtypeStruct((phases.shape[2], 6 * TILE, LANES), BF16),
-        in_specs=[vmem] * 2,
-        out_specs=vmem,
-        compiler_params=params,
-        name="weights",
-    )(matrix, phase_rows)
-
     def whole(shape):
         return pl.BlockSpec(shape, lambda step: (0,) * len(shape), pipeline_mode=pl.Buffered(1))
 
     half = NX // 2
     width = 16
     kept = 2 * grid_rows * rows
+    spectra = pltpu.VMEM((16 * TILE * TILE, LANES), F32)
     columns = pl.pallas_call(
         functools.partial(tiles_kernel, len(gathered)),
         grid=(half // width,),
         out_shape=jax.ShapeDtypeStruct((half, kept, LANES), F32),
-        in_specs=[pl.BlockSpec(memory_space=pl.ANY)] * len(gathered)
-        + [whole(array.shape) for array in (weights, column)],
+        in_specs=[pl.BlockSpec(memory_space=pltpu.SMEM)]
+        + [pl.BlockSpec(memory_space=pl.ANY)] * len(gathered)
+        + [whole(array.shape) for array in (matrix, phase_rows, column)],
         out_specs=pl.BlockSpec((width, kept, LANES), lambda step: (step, 0, 0)),
         scratch_shapes=[
-            pltpu.VMEM((len(gathered), blocks // 2) + tiles.shape[1:], F32),
-            pltpu.SMEM((len(gathered), TILE, LANES), F32),
+            pltpu.VMEM((grid_cols, blocks // 2) + tiles.shape[1:], F32),
+            pltpu.SMEM((grid_cols, TILE, LANES), F32),
             pltpu.VMEM((half * NY, LANES), F32),
-            pltpu.SemaphoreType.DMA((2, len(gathered))),
+            spectra,
+            spectra,
+            pltpu.SemaphoreType.DMA((2, grid_cols)),
         ],
         compiler_params=params,
         name="tiles",
-    )(*gathered, weights, column)
+    )(deep_place, *gathered, matrix, phase_rows, column)
 
     row_table = jnp.asarray(row_tables())
     chunks = rows // TILE
@@ -414,6 +452,7 @@
             return (0, (parity * grid_rows + device) * chunks + first + step, 0)
 
         part = pl.BlockSpec((TILE,) + part_shape, lambda step, parity, place_ref: (step, 0, 0, 0))
+        addend = pl.BlockSpec((TILE,) + part_shape, lambda step, parity, place_ref: (first + step, 0, 0, 0))
         slots = count * TILE
 
         def body(*refs):
@@ -428,7 +467,7 @@
                     pl.BlockSpec((half, TILE, LANES), block),
                     pl.BlockSpec(row_table.shape, lambda step, parity, place_ref: (0, 0, 0, 0)),
                 ]
-                + [part] * len(addends)
+                + [addend] * len(addends)
                 + [pl.BlockSpec(memory_space=pl.ANY)] * len(after),
                 out_specs=part,
             ),
@@ -441,30 +480,27 @@
     def swap(value, bit):
         return lax.ppermute(value, "gx", [(index, index ^ bit) for index in range(grid_rows)])
 
-    def total(relative, top, first, count, after):
+    last = []
+
+    def arrivals(relative, top):
         arrived = []
         bit = 1
         while bit <= top:
-            arrived.append(swap(total(relative | bit, bit // 2, first, count, after), bit))
+            part = rows_for(relative | bit, 0, chunks, arrivals(relative | bit, bit // 2), last)
+            last[:] = [part]
+            arrived.append(swap(part, bit))
             bit *= 2
-        return rows_for(relative, first, count, arrived, after)
+        return arrived
 
     top = grid_rows // 2
-    others, last = [], []
+    far = arrivals(top, top // 2)
+    near = arrivals(0, top // 2)
+    crossed = []
     for chunk in range(chunks):
-        others.append(total(top | 1, 0, chunk, 1, last) if top == 2 else None)
-        last = others[-1:] if top == 2 else []
-    crossed, ready = [], []
-    for chunk in range(chunks):
-        after = others[chunk + 1 : chunk + 2] + ready[-1:]
-        if top == 2:
-            whole_part = rows_for(top, chunk, 1, [swap(others[chunk], 1)], after)
-        else:
-            whole_part = total(top, top // 2, chunk, 1, [])
-        ready.append(whole_part)
-        crossed.append(swap(whole_part, top))
-    near = [swap(total(bit, bit // 2, 0, chunks, ready[-1:]), bit) for bit in (1 << n for n in range(top.bit_length() - 1))]
-    kept_parts = [rows_for(0, 0, chunks, [], ready[-1:])] + near
+        part = rows_for(top, chunk, 1, far, last)
+        last[:] = [part]
+        crossed.append(swap(part, top))
+    kept_parts = [rows_for(0, 0, chunks, [], last)] + near
 
     image = None
     shape = (2, planes, 2, per_device // 2, NX // 2)

time: 204 us -> 195 us (0.956)
  the two profiles are of different devices: /device:TPU:16 before, /device:TPU:26 now
where the time goes in v5:
time: 195 us; the launch traced here: 194 us
  Pallas kernels  102 us (52%)
  waiting for transfers between devices  60.2 us (31%)
  starting transfers between devices  23.1 us (12%)
  local copies, waits for them, and re-layouts  7.95 us (4%)
    pallas_call x1, Pallas kernels, on_device(): pl.pallas_call(functools.partial(tiles_kernel, len(gathered)), grid=(half...  50.5 us
    ppermute x13, waiting for transfers between devices, shift(): return lax.ppermute(value, 'gy', moves)  47.3 us
    pallas_call x6, Pallas kernels, rows_for(): pl.pallas_call(body, grid_spec=pltpu.PrefetchScalarGridSpec(num_scalar_pr...  36 us
    ppermute x13, starting transfers between devices, shift(): return lax.ppermute(value, 'gy', moves)  20 us
    ppermute x5, waiting for transfers between devices, swap(): lax.ppermute(value, 'gx', [(index, index ^ bit) for index in range(grid_r...  12.9 us
    pallas_call x3, Pallas kernels, on_device(): pl.pallas_call(finish, grid=(1,), out_shape=jax.ShapeDtypeStruct(shape, F...  9.51 us
    pallas_call x1, Pallas kernels, on_device(): pl.pallas_call(functools.partial(spread_kernel, tile_rows, tile_cols, gri...  6.24 us
    unnamed x30, local copies, waits for them, and re-layouts  4.38 us
  transfers between devices with their start and end apart: 18, of which 10 were waited for; matrix products, arithmetic and copies ran while one was open for 2% of the time, Pallas kernels for 18%

profile of v5, /device:TPU:26, one launch (start us, length us, event | category | flops | bytes accessed | tf_op | source)
XLA Modules:
  0.0 193.8 jit_solution(14058863320792042175)
XLA Ops:
  0.0 6.2 %spread.1.refs_1_ = f32[65,16,128]{2,1,0:T(8,128)} custom-call(f32[128,2,128]{2,1,0:T(2,128)} %samples_ref.1, f32[128,3,4,128]{3,2,1,0:T(4,128)} %kernel_ref.1, s32[3,128,128]{2,1,0:T(8,128)} %bitcast.11, s32[1,128]{1,0:T(1,128)} %bitcast.15, s32[1,128]{1,0:T(1,128)} %bitcast.16), custom_call_target="tpu_custom_call" | custom-call | tf_op jit(solution)/shard_map/spread/pallas_call | solution.py:367
  6.2 2.4 %collective-permute-start.1 = (f32[65,16,128]{2,1,0:T(8,128)}, f32[65,16,128]{2,1,0:T(8,128)S(1)}, u32[]{:S(2)}, u32[]{:S(2)}) collective-permute-start(f32[65,16,128]{2,1,0:T(8,128)} %spread.1.refs_1_), channel_id=1, source_target_pairs={{2,0},{3,1},{4,2},{5,3},{6,4},{7,5},{10,8},{11,9},{12,10},{13,11},... | collective-permute-start | bytes 1597448 | tf_op jit(solution)/shard_map/ppermute | solution.py:383
  11.5 8.7 %collective-permute-done.1.refs_7_ = f32[65,16,128]{2,1,0:T(8,128)S(1)} collective-permute-done((f32[65,16,128]{2,1,0:T(8,128)}, f32[65,16,128]{2,1,0:T(8,128)S(1)}, u32[]{:S(2)}, u32[]{:S(2)}) %collective-permute-start.1) | collective-permute-done | bytes 532512 | tf_op jit(solution)/shard_map/ppermute | solution.py:383
  20.2 2.2 %collective-permute-done.6.refs_8_ = f32[65,16,128]{2,1,0:T(8,128)S(1)} collective-permute-done((f32[65,16,128]{2,1,0:T(8,128)}, f32[65,16,128]{2,1,0:T(8,128)S(1)}, u32[]{:S(2)}, u32[]{:S(2)}) %collective-permute-start.6) | collective-permute-done | bytes 532512 | tf_op jit(solution)/shard_map/ppermute | solution.py:383
  23.9 1.7 collective-permute-done.refs_2_
  26.9 2.4 %collective-permute-start.7 = (f32[65,16,128]{2,1,0:T(8,128)S(1)}, f32[65,16,128]{2,1,0:T(8,128)S(1)}, u32[]{:S(2)}, u32[]{:S(2)}) collective-permute-start(f32[65,16,128]{2,1,0:T(8,128)S(1)} %collective-permute-done.refs_2_), channel_id=1, source_target_pairs={{2,3},{3,2},{4,5},{5,4},{6,7},{7,6},{10,11},{11,10},{12,13},{13,12... | collective-permute-start | bytes 1597448 | tf_op jit(solution)/shard_map/ppermute | solution.py:383
  31.5 9.6 %collective-permute-done.4.refs_4_ = f32[65,16,128]{2,1,0:T(8,128)S(1)} collective-permute-done((f32[65,16,128]{2,1,0:T(8,128)S(1)}, f32[65,16,128]{2,1,0:T(8,128)S(1)}, u32[]{:S(2)}, u32[]{:S(2)}) %collective-permute-start.4) | collective-permute-done | bytes 532512 | tf_op jit(solution)/shard_map/ppermute | solution.py:383
  41.1 2.4 %collective-permute-start.11 = (f32[65,16,128]{2,1,0:T(8,128)S(1)}, f32[65,16,128]{2,1,0:T(8,128)S(1)}, u32[]{:S(2)}, u32[]{:S(2)}) collective-permute-start(f32[65,16,128]{2,1,0:T(8,128)S(1)} %collective-permute-done.4.refs_4_), channel_id=1, source_target_pairs={{4,5},{5,4},{6,7},{7,6},{12,13},{13,12},{14,15},{15,14},{20,21},{2... | collective-permute-start | bytes 1597448 | tf_op jit(solution)/shard_map/ppermute | solution.py:383
  46.3 8.1 %collective-permute-done.11.refs_11_ = f32[65,16,128]{2,1,0:T(8,128)S(1)} collective-permute-done((f32[65,16,128]{2,1,0:T(8,128)S(1)}, f32[65,16,128]{2,1,0:T(8,128)S(1)}, u32[]{:S(2)}, u32[]{:S(2)}) %collective-permute-start.11) | collective-permute-done | bytes 532512 | tf_op jit(solution)/shard_map/ppermute | solution.py:383
  54.5 9.0 %collective-permute-done.5.refs_6_ = f32[65,16,128]{2,1,0:T(8,128)} collective-permute-done((f32[65,16,128]{2,1,0:T(8,128)S(1)}, f32[65,16,128]{2,1,0:T(8,128)}, u32[]{:S(2)}, u32[]{:S(2)}) %collective-permute-start.5) | collective-permute-done | bytes 532512 | tf_op jit(solution)/shard_map/ppermute | solution.py:383
  63.5 2.4 %collective-permute-start.12 = (f32[65,16,128]{2,1,0:T(8,128)}, f32[65,16,128]{2,1,0:T(8,128)}, u32[]{:S(2)}, u32[]{:S(2)}) collective-permute-start(f32[65,16,128]{2,1,0:T(8,128)} %collective-permute-done.5.refs_6_), channel_id=1, source_target_pairs={{6,7},{7,6},{14,15},{15,14},{22,23},{23,22},{30,31},{31,30}} | collective-permute-start | bytes 1597448 | tf_op jit(solution)/shard_map/ppermute | solution.py:383
  68.8 7.8 %collective-permute-done.12.refs_13_ = f32[65,16,128]{2,1,0:T(8,128)} collective-permute-done((f32[65,16,128]{2,1,0:T(8,128)}, f32[65,16,128]{2,1,0:T(8,128)}, u32[]{:S(2)}, u32[]{:S(2)}) %collective-permute-start.12) | collective-permute-done | bytes 532512 | tf_op jit(solution)/shard_map/ppermute | solution.py:383
  76.6 50.5 %tiles.1.refs_1_ = f32[192,192,128]{2,1,0:T(8,128)} custom-call(s32[1]{0:T(128)} %bitcast.1.refs_0_, f32[65,16,128]{2,1,0:T(8,128)} %spread.1.refs_1_, f32[65,16,128]{2,1,0:T(8,128)} %copy-done.7, f32[65,16,128]{2,1,0:T(8,128)} %collective-permute-done.3.refs_3_, f32[65,16,128]{2,1,0:T(8,128)} %copy-done.10, f32[65,16,128]{2,1,0:T(8,128)} %copy-done.9, ...), custom_call_target="tpu_custom_call" | custom-call | tf_op jit(solution)/shard_map/tiles/pallas_call | solution.py:425
  127.1 8.1 %rows.6.refs_3_ = f32[24,3,48,128]{3,2,1,0:T(8,128)} custom-call(s32[1]{0:T(128)} %bitcast.refs_0_, f32[192,192,128]{2,1,0:T(8,128)} %tiles.1.refs_1_, bf16[2,2,192,256]{3,2,1,0:T(8,128)(2,1)} %constant.35.clone.refs_2_), custom_call_target="tpu_custom_call" | custom-call | flops 1 | bytes 1 | tf_op jit(solution)/shard_map/rows/pallas_call | solution.py:461
  135.3 8.1 %rows.7.refs_4_ = f32[24,3,48,128]{3,2,1,0:T(8,128)} custom-call(s32[1]{0:T(128)} %bitcast.refs_0_, f32[192,192,128]{2,1,0:T(8,128)} %tiles.1.refs_1_, bf16[2,2,192,256]{3,2,1,0:T(8,128)(2,1)} %constant.35.clone.refs_2_, f32[24,3,48,128]{3,2,1,0:T(8,128)} %rows.6.refs_3_), custom_call_target="tpu_custom_call" | custom-call | flops 1 | bytes 1 | tf_op jit(solution)/shard_map/rows/pallas_call | solution.py:461
  145.1 3.9 %rows.8.refs_4_ = f32[8,3,48,128]{3,2,1,0:T(8,128)} custom-call(s32[1]{0:T(128)} %bitcast.refs_0_, f32[192,192,128]{2,1,0:T(8,128)} %tiles.1.refs_1_, bf16[2,2,192,256]{3,2,1,0:T(8,128)(2,1)} %constant.35.clone.refs_2_, f32[24,3,48,128]{3,2,1,0:T(8,128)} %copy-done, f32[24,3,48,128]{3,2,1,0:T(8,128)} %rows.7.refs_4_), custom_call_target="tpu_custom_call" | custom-call | flops 1 | bytes 1 | tf_op jit(solution)/shard_map/rows/pallas_call | solution.py:461
  149.5 3.9 %rows.9.refs_4_ = f32[8,3,48,128]{3,2,1,0:T(8,128)} custom-call(s32[1]{0:T(128)} %bitcast.refs_0_, f32[192,192,128]{2,1,0:T(8,128)} %tiles.1.refs_1_, bf16[2,2,192,256]{3,2,1,0:T(8,128)(2,1)} %constant.35.clone.refs_2_, f32[24,3,48,128]{3,2,1,0:T(8,128)} %copy-done, f32[8,3,48,128]{3,2,1,0:T(8,128)} %rows.8.refs_4_), custom_call_target="tpu_custom_call" | custom-call | flops 1 | bytes 1 | tf_op jit(solution)/shard_map/rows/pallas_call | solution.py:461
  154.9 3.9 %rows.10.refs_3_ = f32[8,3,48,128]{3,2,1,0:T(8,128)} custom-call(s32[1]{0:T(128)} %bitcast.refs_0_, f32[192,192,128]{2,1,0:T(8,128)} %tiles.1.refs_1_, bf16[2,2,192,256]{3,2,1,0:T(8,128)(2,1)} %constant.35.clone.refs_2_, f32[24,3,48,128]{3,2,1,0:T(8,128)} %copy-done, f32[8,3,48,128]{3,2,1,0:T(8,128)} %rows.9.refs_4_), custom_call_target="tpu_custom_call" | custom-call | flops 1 | bytes 1 | tf_op jit(solution)/shard_map/rows/pallas_call | solution.py:461
  160.1 8.1 %rows.11.refs_0_ = f32[24,3,48,128]{3,2,1,0:T(8,128)} custom-call(s32[1]{0:T(128)} %bitcast.refs_0_, f32[192,192,128]{2,1,0:T(8,128)} %tiles.1.refs_1_, bf16[2,2,192,256]{3,2,1,0:T(8,128)(2,1)} %constant.35.clone.refs_2_, f32[8,3,48,128]{3,2,1,0:T(8,128)} %rows.10.refs_3_), custom_call_target="tpu_custom_call" | custom-call | flops 1 | bytes 1 | tf_op jit(solution)/shard_map/rows/pallas_call | solution.py:461
  169.6 3.2 %finish.3.refs_7_ = f32[2,24,2,24,192]{4,3,2,1,0:T(8,128)} custom-call(f32[24,3,48,128]{3,2,1,0:T(8,128)} %rows.11.refs_0_, f32[24,3,48,128]{3,2,1,0:T(8,128)} %copy-done.1, f32[8,3,48,128]{3,2,1,0:T(8,128)} %copy-done.4, bf16[512,192]{1,0:T(8,128)(2,1)} %constant.36.clone.refs_3_, f32[1,192]{1,0:T(1,128)} %bitcast.12, f32[2,24,1]{2,1,0:T(8,128)} %reshape.26.refs_5_, ...), custom_call_target="tpu_custom_call" | custom-call | tf_op jit(solution)/shard_map/finish/pallas_call | solution.py:516
  172.8 5.2 %collective-permute-done.16.refs_2_ = f32[8,3,48,128]{3,2,1,0:T(8,128)S(1)} collective-permute-done((f32[8,3,48,128]{3,2,1,0:T(8,128)}, f32[8,3,48,128]{3,2,1,0:T(8,128)S(1)}, u32[]{:S(2)}, u32[]{:S(2)}) %collective-permute-start.16) | collective-permute-done | bytes 589856 | tf_op jit(solution)/shard_map/ppermute | solution.py:481
  178.9 3.2 %finish.4.refs_7_ = f32[2,24,2,24,192]{4,3,2,1,0:T(8,128)} custom-call(f32[24,3,48,128]{3,2,1,0:T(8,128)} %rows.11.refs_0_, f32[24,3,48,128]{3,2,1,0:T(8,128)} %copy-done.1, f32[8,3,48,128]{3,2,1,0:T(8,128)} %copy-done.3, bf16[512,192]{1,0:T(8,128)(2,1)} %constant.36.clone.refs_3_, f32[1,192]{1,0:T(1,128)} %bitcast.13, ...), custom_call_target="tpu_custom_call", output_to_operand_aliasing={{}: (7, {})} | custom-call | tf_op jit(solution)/shard_map/finish/pallas_call | solution.py:516
  182.0 7.7 %collective-permute-done.15.refs_2_ = f32[8,3,48,128]{3,2,1,0:T(8,128)S(1)} collective-permute-done((f32[8,3,48,128]{3,2,1,0:T(8,128)}, f32[8,3,48,128]{3,2,1,0:T(8,128)S(1)}, u32[]{:S(2)}, u32[]{:S(2)}) %collective-permute-start.15) | collective-permute-done | bytes 589856 | tf_op jit(solution)/shard_map/ppermute | solution.py:481
  190.6 3.2 %finish.5 = f32[2,24,2,24,192]{4,3,2,1,0:T(8,128)} custom-call(f32[24,3,48,128]{3,2,1,0:T(8,128)} %rows.11.refs_0_, f32[24,3,48,128]{3,2,1,0:T(8,128)} %copy-done.1, f32[8,3,48,128]{3,2,1,0:T(8,128)} %copy-done.2, bf16[512,192]{1,0:T(8,128)(2,1)} %constant.36.clone.refs_3_, f32[1,192]{1,0:T(1,128)} %bitcast.14, ...), custom_call_target="tpu_custom_call", output_to_operand_aliasing={{}: (7, {})} | custom-call | tf_op jit(solution)/shard_map/finish/pallas_call | solution.py:516
  (56 shorter events, 21.5 us)
Async XLA Ops:
  6.2 14.0 %collective-permute-start.1 = (f32[65,16,128]{2,1,0:T(8,128)}, f32[65,16,128]{2,1,0:T(8,128)S(1)}, u32[]{:S(2)}, u32[]{:S(2)}) collective-permute-start(f32[65,16,128]{2,1,0:T(8,128)} %spread.1.refs_1_), channel_id=1, source_target_pairs={{2,0},{3,1},{4,2},{5,3},{6,4},{7,5},{10,8},{11,9},{12,10},{13,11},... | collective-permute-start | bytes 1597448 | tf_op jit(solution)/shard_map/ppermute | solution.py:383
  8.6 13.8 %collective-permute-start.6 = (f32[65,16,128]{2,1,0:T(8,128)}, f32[65,16,128]{2,1,0:T(8,128)S(1)}, u32[]{:S(2)}, u32[]{:S(2)}) collective-permute-start(f32[65,16,128]{2,1,0:T(8,128)} %spread.1.refs_1_), channel_id=1, source_target_pairs={{0,1},{1,0},{2,3},{3,2},{4,5},{5,4},{6,7},{7,6},{8,9},{9,8},{10,11... | collective-permute-start | bytes 1597448 | tf_op jit(solution)/shard_map/ppermute | solution.py:383
  10.2 15.4 %collective-permute-start = (f32[65,16,128]{2,1,0:T(8,128)}, f32[65,16,128]{2,1,0:T(8,128)S(1)}, u32[]{:S(2)}, u32[]{:S(2)}) collective-permute-start(f32[65,16,128]{2,1,0:T(8,128)} %spread.1.refs_1_), channel_id=1, source_target_pairs={{0,2},{1,3},{2,4},{3,5},{4,6},{5,7},{8,10},{9,11},{10,12},{11,13},... | collective-permute-start | bytes 1597448 | tf_op jit(solution)/shard_map/ppermute | solution.py:383
  20.2 56.3 %copy-start.5 = (f32[65,16,128]{2,1,0:T(8,128)}, f32[65,16,128]{2,1,0:T(8,128)S(1)}, u32[]{:S(2)}) copy-start(f32[65,16,128]{2,1,0:T(8,128)S(1)} %collective-permute-done.1.refs_7_) | copy-start | bytes 1597444
  22.5 54.1 %copy-start.6 = (f32[65,16,128]{2,1,0:T(8,128)}, f32[65,16,128]{2,1,0:T(8,128)S(1)}, u32[]{:S(2)}) copy-start(f32[65,16,128]{2,1,0:T(8,128)S(1)} %collective-permute-done.6.refs_8_) | copy-start | bytes 1597444
  22.5 6.8 %collective-permute-start.8 = (f32[65,16,128]{2,1,0:T(8,128)S(1)}, f32[65,16,128]{2,1,0:T(8,128)S(1)}, u32[]{:S(2)}, u32[]{:S(2)}) collective-permute-start(f32[65,16,128]{2,1,0:T(8,128)S(1)} %collective-permute-done.1.refs_7_), channel_id=1, source_target_pairs={{0,1},{1,0},{2,3},{3,2},{4,5},{5,4},{8,9},{9,8},{10,11},{11,10},{1... | collective-permute-start | bytes 1597448 | tf_op jit(solution)/shard_map/ppermute | solution.py:383
  23.2 6.2 %collective-permute-start.2 = (f32[65,16,128]{2,1,0:T(8,128)S(1)}, f32[65,16,128]{2,1,0:T(8,128)S(1)}, u32[]{:S(2)}, u32[]{:S(2)}) collective-permute-start(f32[65,16,128]{2,1,0:T(8,128)S(1)} %collective-permute-done.1.refs_7_), channel_id=1, source_target_pairs={{2,0},{3,1},{4,2},{5,3},{10,8},{11,9},{12,10},{13,11},{18,16},{19,... | collective-permute-start | bytes 1597448 | tf_op jit(solution)/shard_map/ppermute | solution.py:383
  25.6 51.0 %copy-start.7 = (f32[65,16,128]{2,1,0:T(8,128)}, f32[65,16,128]{2,1,0:T(8,128)S(1)}, u32[]{:S(2)}) copy-start(f32[65,16,128]{2,1,0:T(8,128)S(1)} %collective-permute-done.refs_2_) | copy-start | bytes 1597444
  25.6 15.5 %collective-permute-start.4 = (f32[65,16,128]{2,1,0:T(8,128)S(1)}, f32[65,16,128]{2,1,0:T(8,128)S(1)}, u32[]{:S(2)}, u32[]{:S(2)}) collective-permute-start(f32[65,16,128]{2,1,0:T(8,128)S(1)} %collective-permute-done.refs_2_), channel_id=1, source_target_pairs={{2,4},{3,5},{4,6},{5,7},{10,12},{11,13},{12,14},{13,15},{18,20},{1... | collective-permute-start | bytes 1597448 | tf_op jit(solution)/shard_map/ppermute | solution.py:383
  26.9 14.2 %collective-permute-start.7 = (f32[65,16,128]{2,1,0:T(8,128)S(1)}, f32[65,16,128]{2,1,0:T(8,128)S(1)}, u32[]{:S(2)}, u32[]{:S(2)}) collective-permute-start(f32[65,16,128]{2,1,0:T(8,128)S(1)} %collective-permute-done.refs_2_), channel_id=1, source_target_pairs={{2,3},{3,2},{4,5},{5,4},{6,7},{7,6},{10,11},{11,10},{12,13},{13,12... | collective-permute-start | bytes 1597448 | tf_op jit(solution)/shard_map/ppermute | solution.py:383
  29.3 47.3 %copy-start.8 = (f32[65,16,128]{2,1,0:T(8,128)}, f32[65,16,128]{2,1,0:T(8,128)S(1)}, u32[]{:S(2)}) copy-start(f32[65,16,128]{2,1,0:T(8,128)S(1)} %collective-permute-done.8.refs_14_) | copy-start | bytes 1597444
  29.3 47.3 %copy-start.9 = (f32[65,16,128]{2,1,0:T(8,128)}, f32[65,16,128]{2,1,0:T(8,128)S(1)}, u32[]{:S(2)}) copy-start(f32[65,16,128]{2,1,0:T(8,128)S(1)} %collective-permute-done.2.refs_5_) | copy-start | bytes 1597444
  29.3 15.5 %collective-permute-start.9 = (f32[65,16,128]{2,1,0:T(8,128)S(1)}, f32[65,16,128]{2,1,0:T(8,128)S(1)}, u32[]{:S(2)}, u32[]{:S(2)}) collective-permute-start(f32[65,16,128]{2,1,0:T(8,128)S(1)} %collective-permute-done.2.refs_5_), channel_id=1, source_target_pairs={{0,1},{1,0},{2,3},{3,2},{8,9},{9,8},{10,11},{11,10},{16,17},{17,16... | collective-permute-start | bytes 1597448 | tf_op jit(solution)/shard_map/ppermute | solution.py:383
  30.0 14.8 %collective-permute-start.3 = (f32[65,16,128]{2,1,0:T(8,128)S(1)}, f32[65,16,128]{2,1,0:T(8,128)}, u32[]{:S(2)}, u32[]{:S(2)}) collective-permute-start(f32[65,16,128]{2,1,0:T(8,128)S(1)} %collective-permute-done.2.refs_5_), channel_id=1, source_target_pairs={{2,0},{3,1},{10,8},{11,9},{18,16},{19,17},{26,24},{27,25}} | collective-permute-start | bytes 1597448 | tf_op jit(solution)/shard_map/ppermute | solution.py:383
  41.0 35.6 %copy-start.10 = (f32[65,16,128]{2,1,0:T(8,128)}, f32[65,16,128]{2,1,0:T(8,128)S(1)}, u32[]{:S(2)}) copy-start(f32[65,16,128]{2,1,0:T(8,128)S(1)} %collective-permute-done.4.refs_4_) | copy-start | bytes 1597444
  41.1 13.3 %collective-permute-start.11 = (f32[65,16,128]{2,1,0:T(8,128)S(1)}, f32[65,16,128]{2,1,0:T(8,128)S(1)}, u32[]{:S(2)}, u32[]{:S(2)}) collective-permute-start(f32[65,16,128]{2,1,0:T(8,128)S(1)} %collective-permute-done.4.refs_4_), channel_id=1, source_target_pairs={{4,5},{5,4},{6,7},{7,6},{12,13},{13,12},{14,15},{15,14},{20,21},{2... | collective-permute-start | bytes 1597448 | tf_op jit(solution)/shard_map/ppermute | solution.py:383
  43.5 20.0 %collective-permute-start.5 = (f32[65,16,128]{2,1,0:T(8,128)S(1)}, f32[65,16,128]{2,1,0:T(8,128)}, u32[]{:S(2)}, u32[]{:S(2)}) collective-permute-start(f32[65,16,128]{2,1,0:T(8,128)S(1)} %collective-permute-done.4.refs_4_), channel_id=1, source_target_pairs={{4,6},{5,7},{12,14},{13,15},{20,22},{21,23},{28,30},{29,31}} | collective-permute-start | bytes 1597448 | tf_op jit(solution)/shard_map/ppermute | solution.py:383
  44.9 23.9 %collective-permute-start.10 = (f32[65,16,128]{2,1,0:T(8,128)}, f32[65,16,128]{2,1,0:T(8,128)}, u32[]{:S(2)}, u32[]{:S(2)}) collective-permute-start(f32[65,16,128]{2,1,0:T(8,128)} %collective-permute-done.3.refs_3_), channel_id=1, source_target_pairs={{0,1},{1,0},{8,9},{9,8},{16,17},{17,16},{24,25},{25,24}} | collective-permute-start | bytes 1597448 | tf_op jit(solution)/shard_map/ppermute | solution.py:383
  63.5 13.1 %collective-permute-start.12 = (f32[65,16,128]{2,1,0:T(8,128)}, f32[65,16,128]{2,1,0:T(8,128)}, u32[]{:S(2)}, u32[]{:S(2)}) collective-permute-start(f32[65,16,128]{2,1,0:T(8,128)} %collective-permute-done.5.refs_6_), channel_id=1, source_target_pairs={{6,7},{7,6},{14,15},{15,14},{22,23},{23,22},{30,31},{31,30}} | collective-permute-start | bytes 1597448 | tf_op jit(solution)/shard_map/ppermute | solution.py:383
  135.3 8.6 %collective-permute-start.13 = (f32[24,3,48,128]{3,2,1,0:T(8,128)}, f32[24,3,48,128]{3,2,1,0:T(8,128)S(1)}, u32[]{:S(2)}, u32[]{:S(2)}) collective-permute-start(f32[24,3,48,128]{3,2,1,0:T(8,128)} %rows.6.refs_3_), channel_id=1, source_target_pairs={{0,8},{8,0},{16,24},{24,16},{1,9},{9,1},{17,25},{25,17},{2,10},{10... | collective-permute-start | bytes 5308424 | tf_op jit(solution)/shard_map/ppermute | solution.py:481
  143.4 24.7 %collective-permute-start.14 = (f32[24,3,48,128]{3,2,1,0:T(8,128)}, f32[24,3,48,128]{3,2,1,0:T(8,128)S(1)}, u32[]{:S(2)}, u32[]{:S(2)}) collective-permute-start(f32[24,3,48,128]{3,2,1,0:T(8,128)} %rows.7.refs_4_), channel_id=1, source_target_pairs={{0,8},{8,0},{16,24},{24,16},{1,9},{9,1},{17,25},{25,17},{2,10},{10... | collective-permute-start | bytes 5308424 | tf_op jit(solution)/shard_map/ppermute | solution.py:481
  149.0 19.2 %collective-permute-start.17 = (f32[8,3,48,128]{3,2,1,0:T(8,128)}, f32[8,3,48,128]{3,2,1,0:T(8,128)S(1)}, u32[]{:S(2)}, u32[]{:S(2)}) collective-permute-start(f32[8,3,48,128]{3,2,1,0:T(8,128)} %rows.8.refs_4_), channel_id=1, source_target_pairs={{0,16},{8,24},{16,0},{24,8},{1,17},{9,25},{17,1},{25,9},{2,18},{10... | collective-permute-start | bytes 1769480 | tf_op jit(solution)/shard_map/ppermute | solution.py:481
  153.4 24.6 %collective-permute-start.16 = (f32[8,3,48,128]{3,2,1,0:T(8,128)}, f32[8,3,48,128]{3,2,1,0:T(8,128)S(1)}, u32[]{:S(2)}, u32[]{:S(2)}) collective-permute-start(f32[8,3,48,128]{3,2,1,0:T(8,128)} %rows.9.refs_4_), channel_id=1, source_target_pairs={{0,16},{8,24},{16,0},{24,8},{1,17},{9,25},{17,1},{25,9},{2,18},{10... | collective-permute-start | bytes 1769480 | tf_op jit(solution)/shard_map/ppermute | solution.py:481
  158.8 30.9 %collective-permute-start.15 = (f32[8,3,48,128]{3,2,1,0:T(8,128)}, f32[8,3,48,128]{3,2,1,0:T(8,128)S(1)}, u32[]{:S(2)}, u32[]{:S(2)}) collective-permute-start(f32[8,3,48,128]{3,2,1,0:T(8,128)} %rows.10.refs_3_), channel_id=1, source_target_pairs={{0,16},{8,24},{16,0},{24,8},{1,17},{9,25},{17,1},{25,9},{2,18},{10... | collective-permute-start | bytes 1769480 | tf_op jit(solution)/shard_map/ppermute | solution.py:481
  (9 other events, 66.4 us)

commit v6 on v5

--- a/solution.py
+++ b/solution.py
@@ -16,6 +16,7 @@
 TILE = 8
 LANES = 128
 PLANES = 32
+CHUNK = 24
 Z_CHIPS = 4
 PHASES = 128
 BF16 = jnp.bfloat16
@@ -61,25 +62,13 @@
     return np.stack(matrices), np.stack(phases).astype(np.float32)
 
 
-def padded_rows(per_device):
-    return -(-(per_device // 2) // TILE) * TILE
-
-
-def column_tables(devices, per_device):
-    half = NY // 2
-    rows = padded_rows(per_device)
-    place = np.arange(rows)
-    slot = place // 8 * 4 + place % 4
-    local = 2 * slot + place % 8 // 4 * (per_device // 2)
-    used = (slot < per_device // 4).astype(np.float64)[:, None]
+def column_tables():
+    third = NY // 3
     out = []
-    for parity in range(2):
-        cos_parts, sin_parts = [], []
-        for device in range(devices):
-            cos, sin = waves(device * per_device + local + parity - NY // 4, np.arange(half) - half, NY)
-            cos_parts.append(cos * used)
-            sin_parts.append(sin * used)
-        out.append(np.concatenate(halves(np.concatenate(cos_parts + sin_parts) / math.sqrt(NY))))
+    for residue in range(3):
+        cos, sin = waves(3 * np.arange(NY // 6) + residue - NY // 4, np.arange(third) - NY // 2, NY)
+        high, low = halves(np.concatenate((cos, sin)) / math.sqrt(NY))
+        out.append(np.block([[high, high], [low, np.zeros_like(low)]]))
     return np.stack(out)
 
 
@@ -256,25 +245,28 @@
 
         lax.fori_loop(0, sources * batches // 2, add_pair, 0)
 
-    turn = jnp.where(lax.broadcasted_iota(jnp.int32, (rows, LANES), 1) < LANES // 2, -1.0, 1.0)
+    turn = jnp.where(lax.broadcasted_iota(jnp.int32, (1, LANES), 1) < LANES // 2, -1.0, 1.0)
     origin = pl.program_id(0) * width
+    third = NY // 3
 
     def columns(step, carry):
-        folded = ([], [])
+        folded = ([], [], [])
         for side in range(2):
             start = pl.multiple_of((origin + 2 * step + side) * stride, stride)
-            lower = acc_ref[pl.ds(start, NY // 2), :]
-            upper = acc_ref[pl.ds(start + NY // 2, NY // 2), :]
-            folded[0].append(lower + upper)
-            folded[1].append(lower - upper)
-        for parity in range(2):
-            high, low = split(jnp.concatenate(folded[parity], axis=1))
-            both = jnp.dot(column_ref[parity], high, preferred_element_type=F32)
-            rest = jnp.dot(column_ref[parity, : 2 * rows], low, preferred_element_type=F32)
-            product = both[: 2 * rows] + both[2 * rows :] + rest
+            first, second, last = (acc_ref[pl.ds(start + third * part, third), :] for part in range(3))
+            both = second + last
+            across = pltpu.roll(second - last, LANES // 2, 1) * (turn * math.sqrt(0.75))
+            middle = first - 0.5 * both
+            folded[0].append(first + both)
+            folded[1].append(middle + across)
+            folded[2].append(middle - across)
+        for residue in range(3):
+            high_low = split(jnp.concatenate(folded[residue], axis=1))
+            product = jnp.dot(column_ref[residue], jnp.concatenate(high_low, axis=0), preferred_element_type=F32)
+            product = product[: 2 * rows] + product[2 * rows :]
             for side in range(2):
                 lanes = slice(side * LANES, (side + 1) * LANES)
-                out_ref[2 * step + side, parity * rows : (parity + 1) * rows, :] = (
+                out_ref[2 * step + side, residue * rows : (residue + 1) * rows, :] = (
                     product[:rows, lanes] + pltpu.roll(product[rows:, lanes], LANES // 2, 1) * turn
                 )
         return carry
@@ -285,7 +277,7 @@
 def rows_kernel(planes_padded, addends, place_ref, in_ref, row_ref, *refs):
     out_ref = refs[-1]
     half = NX // 2
-    parity = pl.program_id(1)
+    residue = pl.program_id(1)
     lane = lax.broadcasted_iota(jnp.int32, (PLANES, LANES), 1)
     flat = in_ref.reshape(half * TILE, LANES)
     turned = [flat[pl.ds(row, half, stride=TILE), :].T for row in range(TILE)]
@@ -310,7 +302,7 @@
             values = [jnp.where(lane < NX // 4, even[side], odd[side]) for side in range(2)]
             values.append(jnp.where(lane < LANES // 2, odd[0], pltpu.roll(odd[1], LANES // 2, 1)))
             for number, value in enumerate(values):
-                at = (2 * slot + parity, number, pl.ds(part * planes_padded, planes_padded))
+                at = (3 * slot + residue, number, pl.ds(part * planes_padded, planes_padded))
                 total = value[:planes_padded]
                 for ref in refs[:addends]:
                     total = total + ref[at]
@@ -322,9 +314,11 @@
     order_ref, first_ref, second_ref, third_ref = refs[parts : parts + 4]
     out_ref = refs[-1]
     planes = out_ref.shape[1]
+    slots = part_refs[0].shape[0]
     stride = 6 * planes_padded
-    flats = [ref.reshape(TILE * stride, LANES) for ref in part_refs]
+    flats = [ref.reshape(slots * stride, LANES) for ref in part_refs]
     order = order_ref[...]
+    scale = second_ref[...] * first_ref[...]
     for part in range(2):
         for group in range(0, planes, TILE):
             members = range(group, min(group + TILE, planes))
@@ -332,21 +326,18 @@
             for plane in members:
                 values = []
                 for number in range(3):
-                    at = pl.ds((number * 2 + part) * planes_padded + plane, TILE, stride=stride)
+                    at = pl.ds((number * 2 + part) * planes_padded + plane, slots, stride=stride)
                     total = flats[0][at, :]
                     for flat in flats[1:]:
                         total = total + flat[at, :]
                     values.append(total)
-                mains += values[:2]
-                rests += [values[2], pltpu.roll(values[2], LANES // 2, 1)]
+                mains.append(jnp.concatenate(values[:2], axis=0))
+                rests.append(jnp.concatenate((values[2], pltpu.roll(values[2], LANES // 2, 1)), axis=0))
             main = split(jnp.concatenate(mains, axis=0))
             rest = split(jnp.concatenate(rests, axis=0))
             ordered = jnp.dot(jnp.concatenate(main + rest, axis=1), order, preferred_element_type=F32)
             for index, plane in enumerate(members):
-                for side in range(2):
-                    row = (2 * index + side) * TILE
-                    scale = second_ref[side] * third_ref[plane] * first_ref[...]
-                    out_ref[part, plane, side] = ordered[row : row + TILE] * scale
+                out_ref[part, plane] = ordered[index * 2 * slots : (index + 1) * 2 * slots] * (scale * third_ref[plane])
 
 
 def on_device(samples, kernel, offsets, owners, tile_ids, deapod_first, deapod_second, deapod_third):
@@ -359,7 +350,9 @@
     tile_cols = NY // (TILE * grid_cols)
     planes = deapod_third.shape[0]
     per_device = deapod_second.shape[0]
-    rows = padded_rows(per_device)
+    assert per_device % CHUNK == 0
+    chunks = per_device // CHUNK
+    slots = CHUNK // 2
     planes_padded = -(-planes // 8) * 8
     vmem = pl.BlockSpec(memory_space=pltpu.VMEM)
     params = pltpu.CompilerParams(vmem_limit_bytes=VMEM_LIMIT)
@@ -414,13 +407,13 @@
     matrices, phases = depth_tables(planes)
     matrix = lax.dynamic_index_in_dim(jnp.asarray(matrices), gy, 0, keepdims=False)
     phase_rows = lax.dynamic_index_in_dim(jnp.asarray(phases), gy, 0, keepdims=False)
-    column = jnp.asarray(column_tables(grid_rows, per_device))
+    column = jnp.asarray(column_tables())
     def whole(shape):
         return pl.BlockSpec(shape, lambda step: (0,) * len(shape), pipeline_mode=pl.Buffered(1))
 
     half = NX // 2
     width = 16
-    kept = 2 * grid_rows * rows
+    kept = NY // 2
     spectra = pltpu.VMEM((16 * TILE * TILE, LANES), F32)
     columns = pl.pallas_call(
         functools.partial(tiles_kernel, len(gathered)),
@@ -443,17 +436,15 @@
     )(deep_place, *gathered, matrix, phase_rows, column)
 
     row_table = jnp.asarray(row_tables())
-    chunks = rows // TILE
     part_shape = (3, 2 * planes_padded, LANES)
 
     def rows_for(relative, first, count, addends, after):
-        def block(step, parity, place_ref):
+        def block(step, residue, place_ref):
             device = jnp.bitwise_xor(place_ref[0], relative)
-            return (0, (parity * grid_rows + device) * chunks + first + step, 0)
-
-        part = pl.BlockSpec((TILE,) + part_shape, lambda step, parity, place_ref: (step, 0, 0, 0))
-        addend = pl.BlockSpec((TILE,) + part_shape, lambda step, parity, place_ref: (first + step, 0, 0, 0))
-        slots = count * TILE
+            return (0, (residue * grid_rows + device) * chunks + first + step, 0)
+
+        part = pl.BlockSpec((slots,) + part_shape, lambda step, residue, place_ref: (step, 0, 0, 0))
+        addend = pl.BlockSpec((slots,) + part_shape, lambda step, residue, place_ref: (first + step, 0, 0, 0))
 
         def body(*refs):
             rows_kernel(planes_padded, len(addends), *refs[: 3 + len(addends)], refs[-1])
@@ -462,16 +453,16 @@
             body,
             grid_spec=pltpu.PrefetchScalarGridSpec(
                 num_scalar_prefetch=1,
-                grid=(count, 2),
+                grid=(count, 3),
                 in_specs=[
                     pl.BlockSpec((half, TILE, LANES), block),
-                    pl.BlockSpec(row_table.shape, lambda step, parity, place_ref: (0, 0, 0, 0)),
+                    pl.BlockSpec(row_table.shape, lambda step, residue, place_ref: (0, 0, 0, 0)),
                 ]
                 + [addend] * len(addends)
                 + [pl.BlockSpec(memory_space=pl.ANY)] * len(after),
                 out_specs=part,
             ),
-            out_shape=jax.ShapeDtypeStruct((slots,) + part_shape, F32),
+            out_shape=jax.ShapeDtypeStruct((count * slots,) + part_shape, F32),
             compiler_params=params,
             cost_estimate=pl.CostEstimate(flops=1, bytes_accessed=1, transcendentals=0),
             name="rows",
@@ -482,32 +473,27 @@
 
     last = []
 
+    def rows_next(relative, first, count, addends):
+        part = rows_for(relative, first, count, addends, last)
+        last[:] = [part]
+        return part
+
     def arrivals(relative, top):
         arrived = []
         bit = 1
         while bit <= top:
-            part = rows_for(relative | bit, 0, chunks, arrivals(relative | bit, bit // 2), last)
-            last[:] = [part]
-            arrived.append(swap(part, bit))
+            arrived.append(swap(rows_next(relative | bit, 0, chunks, arrivals(relative | bit, bit // 2)), bit))
             bit *= 2
         return arrived
 
     top = grid_rows // 2
     far = arrivals(top, top // 2)
     near = arrivals(0, top // 2)
-    crossed = []
+    crossed = [swap(rows_next(top, chunk, 1, far), top) for chunk in range(chunks)]
+    kept_parts = [rows_next(0, 0, chunks, [])] + near
+
+    image = None
     for chunk in range(chunks):
-        part = rows_for(top, chunk, 1, far, last)
-        last[:] = [part]
-        crossed.append(swap(part, top))
-    kept_parts = [rows_for(0, 0, chunks, [], last)] + near
-
-    image = None
-    shape = (2, planes, 2, per_device // 2, NX // 2)
-    for chunk in range(chunks):
-
-        def at_chunk(_, chunk=chunk):
-            return (chunk, 0, 0, 0)
 
         def finish(*refs):
             finish_kernel(planes_padded, len(kept_parts) + 1, refs)
@@ -516,17 +502,17 @@
         image = pl.pallas_call(
             finish,
             grid=(1,),
-            out_shape=jax.ShapeDtypeStruct(shape, F32),
-            in_specs=[pl.BlockSpec((TILE,) + part_shape, at_chunk)] * len(kept_parts)
+            out_shape=jax.ShapeDtypeStruct((2, planes, per_device, NX // 2), F32),
+            in_specs=[pl.BlockSpec((slots,) + part_shape, lambda step, chunk=chunk: (chunk, 0, 0, 0))] * len(kept_parts)
             + [
-                pl.BlockSpec((TILE,) + part_shape, lambda step: (0, 0, 0, 0)),
+                pl.BlockSpec((slots,) + part_shape, lambda step: (0, 0, 0, 0)),
                 pl.BlockSpec((4 * LANES, NX // 2), lambda step: (0, 0)),
                 pl.BlockSpec((1, NX // 2), lambda step: (0, 0)),
-                pl.BlockSpec((2, TILE, 1), lambda step, chunk=chunk: (0, chunk, 0)),
+                pl.BlockSpec((CHUNK, 1), lambda step, chunk=chunk: (chunk, 0)),
                 pl.BlockSpec(memory_space=pltpu.SMEM),
             ]
             + [pl.BlockSpec(memory_space=pl.ANY)] * len(earlier),
-            out_specs=pl.BlockSpec((2, planes, 2, TILE, NX // 2), lambda step, chunk=chunk: (0, 0, 0, chunk, 0)),
+            out_specs=pl.BlockSpec((2, planes, CHUNK, NX // 2), lambda step, chunk=chunk: (0, 0, chunk, 0)),
             input_output_aliases={len(kept_parts) + 5: 0} if earlier else {},
             compiler_params=params,
             name="finish",
@@ -535,11 +521,11 @@
             crossed[chunk],
             jnp.asarray(order_tables()),
             deapod_first[None, :],
-            deapod_second.reshape(2, per_device // 2, 1),
+            deapod_second[:, None],
             deapod_third,
             *earlier,
         )
-    return image.reshape(2, planes, per_device, NX // 2)
+    return image
 
 
 def solution(mesh):

time: 195 us -> 196 us (level)
  waiting for transfers between devices: 60.2 us -> 67.2 us
  Pallas kernels: 102 us -> 98.3 us
    ppermute x5 -> x4, waiting for transfers between devices: 12.9 us -> 19.9 us  [swap(): lax.ppermute(value, 'gx', [(index, index ^ bit) for index in range(grid_r...]
    pallas_call x3 -> x2, Pallas kernels: 9.51 us -> 7.83 us  [on_device(): pl.pallas_call(finish, grid=(1,), out_shape=jax.ShapeDtypeStruct((2, plan...]
    pallas_call x6 -> x5, Pallas kernels: 36 us -> 34.6 us  [rows_for(): pl.pallas_call(body, grid_spec=pltpu.PrefetchScalarGridSpec(num_scalar_pr...]
    unnamed x30 -> x28, local copies, waits for them, and re-layouts: 4.38 us -> 3.1 us
  transfers between devices with their start and end apart: 18 -> 17, of which waited for: 10 -> 10; matrix products, arithmetic and copies ran while one was open for 2% -> 2% of each run, Pallas kernels for 18% -> 16%
where the time goes in v6:
time: 196 us; the launch traced here: 195 us
  Pallas kernels  98.3 us (50%)
  waiting for transfers between devices  67.2 us (34%)
  starting transfers between devices  22.6 us (12%)
  local copies, waits for them, and re-layouts  6.66 us (3%)
    pallas_call x1, Pallas kernels, on_device(): pl.pallas_call(functools.partial(tiles_kernel, len(gathered)), grid=(half...  49.7 us
    ppermute x13, waiting for transfers between devices, shift(): return lax.ppermute(value, 'gy', moves)  47.2 us
    pallas_call x5, Pallas kernels, rows_for(): pl.pallas_call(body, grid_spec=pltpu.PrefetchScalarGridSpec(num_scalar_pr...  34.6 us
    ppermute x13, starting transfers between devices, shift(): return lax.ppermute(value, 'gy', moves)  20 us
    ppermute x4, waiting for transfers between devices, swap(): lax.ppermute(value, 'gx', [(index, index ^ bit) for index in range(grid_r...  19.9 us
    pallas_call x2, Pallas kernels, on_device(): pl.pallas_call(finish, grid=(1,), out_shape=jax.ShapeDtypeStruct((2, plan...  7.83 us
    pallas_call x1, Pallas kernels, on_device(): pl.pallas_call(functools.partial(spread_kernel, tile_rows, tile_cols, gri...  6.24 us
  transfers between devices with their start and end apart: 17, of which 10 were waited for; matrix products, arithmetic and copies ran while one was open for 2% of the time, Pallas kernels for 16%

profile of v6, /device:TPU:26, one launch (start us, length us, event | category | flops | bytes accessed | tf_op | source)
XLA Modules:
  0.0 194.9 jit_solution(8116873858138959190)
XLA Ops:
  0.0 6.2 %spread.1.refs_1_ = f32[65,16,128]{2,1,0:T(8,128)} custom-call(f32[128,2,128]{2,1,0:T(2,128)} %samples_ref.1, f32[128,3,4,128]{3,2,1,0:T(4,128)} %kernel_ref.1, s32[3,128,128]{2,1,0:T(8,128)} %bitcast.11, s32[1,128]{1,0:T(1,128)} %bitcast.14, s32[1,128]{1,0:T(1,128)} %bitcast.15), custom_call_target="tpu_custom_call" | custom-call | tf_op jit(solution)/shard_map/spread/pallas_call | solution.py:360
  6.2 2.4 %collective-permute-start.1 = (f32[65,16,128]{2,1,0:T(8,128)}, f32[65,16,128]{2,1,0:T(8,128)S(1)}, u32[]{:S(2)}, u32[]{:S(2)}) collective-permute-start(f32[65,16,128]{2,1,0:T(8,128)} %spread.1.refs_1_), channel_id=1, source_target_pairs={{2,0},{3,1},{4,2},{5,3},{6,4},{7,5},{10,8},{11,9},{12,10},{13,11},... | collective-permute-start | bytes 1597448 | tf_op jit(solution)/shard_map/ppermute | solution.py:376
  8.6 1.6 collective-permute-start.6
  11.5 8.7 %collective-permute-done.1.refs_7_ = f32[65,16,128]{2,1,0:T(8,128)S(1)} collective-permute-done((f32[65,16,128]{2,1,0:T(8,128)}, f32[65,16,128]{2,1,0:T(8,128)S(1)}, u32[]{:S(2)}, u32[]{:S(2)}) %collective-permute-start.1) | collective-permute-done | bytes 532512 | tf_op jit(solution)/shard_map/ppermute | solution.py:376
  20.2 2.2 %collective-permute-done.6.refs_8_ = f32[65,16,128]{2,1,0:T(8,128)S(1)} collective-permute-done((f32[65,16,128]{2,1,0:T(8,128)}, f32[65,16,128]{2,1,0:T(8,128)S(1)}, u32[]{:S(2)}, u32[]{:S(2)}) %collective-permute-start.6) | collective-permute-done | bytes 532512 | tf_op jit(solution)/shard_map/ppermute | solution.py:376
  23.9 1.7 collective-permute-done.refs_2_
  26.9 2.4 %collective-permute-start.7 = (f32[65,16,128]{2,1,0:T(8,128)S(1)}, f32[65,16,128]{2,1,0:T(8,128)S(1)}, u32[]{:S(2)}, u32[]{:S(2)}) collective-permute-start(f32[65,16,128]{2,1,0:T(8,128)S(1)} %collective-permute-done.refs_2_), channel_id=1, source_target_pairs={{2,3},{3,2},{4,5},{5,4},{6,7},{7,6},{10,11},{11,10},{12,13},{13,12... | collective-permute-start | bytes 1597448 | tf_op jit(solution)/shard_map/ppermute | solution.py:376
  31.5 9.5 %collective-permute-done.4.refs_4_ = f32[65,16,128]{2,1,0:T(8,128)S(1)} collective-permute-done((f32[65,16,128]{2,1,0:T(8,128)S(1)}, f32[65,16,128]{2,1,0:T(8,128)S(1)}, u32[]{:S(2)}, u32[]{:S(2)}) %collective-permute-start.4) | collective-permute-done | bytes 532512 | tf_op jit(solution)/shard_map/ppermute | solution.py:376
  41.1 2.4 %collective-permute-start.11 = (f32[65,16,128]{2,1,0:T(8,128)S(1)}, f32[65,16,128]{2,1,0:T(8,128)S(1)}, u32[]{:S(2)}, u32[]{:S(2)}) collective-permute-start(f32[65,16,128]{2,1,0:T(8,128)S(1)} %collective-permute-done.4.refs_4_), channel_id=1, source_target_pairs={{4,5},{5,4},{6,7},{7,6},{12,13},{13,12},{14,15},{15,14},{20,21},{2... | collective-permute-start | bytes 1597448 | tf_op jit(solution)/shard_map/ppermute | solution.py:376
  46.3 8.1 %collective-permute-done.11.refs_11_ = f32[65,16,128]{2,1,0:T(8,128)S(1)} collective-permute-done((f32[65,16,128]{2,1,0:T(8,128)S(1)}, f32[65,16,128]{2,1,0:T(8,128)S(1)}, u32[]{:S(2)}, u32[]{:S(2)}) %collective-permute-start.11) | collective-permute-done | bytes 532512 | tf_op jit(solution)/shard_map/ppermute | solution.py:376
  54.5 9.0 %collective-permute-done.5.refs_6_ = f32[65,16,128]{2,1,0:T(8,128)} collective-permute-done((f32[65,16,128]{2,1,0:T(8,128)S(1)}, f32[65,16,128]{2,1,0:T(8,128)}, u32[]{:S(2)}, u32[]{:S(2)}) %collective-permute-start.5) | collective-permute-done | bytes 532512 | tf_op jit(solution)/shard_map/ppermute | solution.py:376
  63.5 2.4 %collective-permute-start.12 = (f32[65,16,128]{2,1,0:T(8,128)}, f32[65,16,128]{2,1,0:T(8,128)}, u32[]{:S(2)}, u32[]{:S(2)}) collective-permute-start(f32[65,16,128]{2,1,0:T(8,128)} %collective-permute-done.5.refs_6_), channel_id=1, source_target_pairs={{6,7},{7,6},{14,15},{15,14},{22,23},{23,22},{30,31},{31,30}} | collective-permute-start | bytes 1597448 | tf_op jit(solution)/shard_map/ppermute | solution.py:376
  67.3 1.5 dynamic-slice_bitcast_fusion.refs_16_
  68.8 7.8 %collective-permute-done.12.refs_13_ = f32[65,16,128]{2,1,0:T(8,128)} collective-permute-done((f32[65,16,128]{2,1,0:T(8,128)}, f32[65,16,128]{2,1,0:T(8,128)}, u32[]{:S(2)}, u32[]{:S(2)}) %collective-permute-start.12) | collective-permute-done | bytes 532512 | tf_op jit(solution)/shard_map/ppermute | solution.py:376
  76.6 49.7 %tiles.1.refs_1_ = f32[192,192,128]{2,1,0:T(8,128)} custom-call(s32[1]{0:T(128)} %bitcast.1.refs_0_, f32[65,16,128]{2,1,0:T(8,128)} %spread.1.refs_1_, f32[65,16,128]{2,1,0:T(8,128)} %copy-done.6, f32[65,16,128]{2,1,0:T(8,128)} %collective-permute-done.3.refs_3_, f32[65,16,128]{2,1,0:T(8,128)} %copy-done.9, f32[65,16,128]{2,1,0:T(8,128)} %copy-done.8, ...), custom_call_target="tpu_custom_call" | custom-call | tf_op jit(solution)/shard_map/tiles/pallas_call | solution.py:418
  126.3 8.1 %rows.5.refs_3_ = f32[24,3,48,128]{3,2,1,0:T(8,128)} custom-call(s32[1]{0:T(128)} %bitcast.refs_0_, f32[192,192,128]{2,1,0:T(8,128)} %tiles.1.refs_1_, bf16[2,2,192,256]{3,2,1,0:T(8,128)(2,1)} %constant.35.clone.refs_2_), custom_call_target="tpu_custom_call" | custom-call | flops 1 | bytes 1 | tf_op jit(solution)/shard_map/rows/pallas_call | solution.py:452
  134.4 8.1 %rows.6.refs_4_ = f32[24,3,48,128]{3,2,1,0:T(8,128)} custom-call(s32[1]{0:T(128)} %bitcast.refs_0_, f32[192,192,128]{2,1,0:T(8,128)} %tiles.1.refs_1_, bf16[2,2,192,256]{3,2,1,0:T(8,128)(2,1)} %constant.35.clone.refs_2_, f32[24,3,48,128]{3,2,1,0:T(8,128)} %rows.5.refs_3_), custom_call_target="tpu_custom_call" | custom-call | flops 1 | bytes 1 | tf_op jit(solution)/shard_map/rows/pallas_call | solution.py:452
  144.1 5.2 %rows.7.refs_4_ = f32[12,3,48,128]{3,2,1,0:T(8,128)} custom-call(s32[1]{0:T(128)} %bitcast.refs_0_, f32[192,192,128]{2,1,0:T(8,128)} %tiles.1.refs_1_, bf16[2,2,192,256]{3,2,1,0:T(8,128)(2,1)} %constant.35.clone.refs_2_, f32[24,3,48,128]{3,2,1,0:T(8,128)} %copy-done, f32[24,3,48,128]{3,2,1,0:T(8,128)} %rows.6.refs_4_), custom_call_target="tpu_custom_call" | custom-call | flops 1 | bytes 1 | tf_op jit(solution)/shard_map/rows/pallas_call | solution.py:452
  149.8 5.2 %rows.8.refs_3_ = f32[12,3,48,128]{3,2,1,0:T(8,128)} custom-call(s32[1]{0:T(128)} %bitcast.refs_0_, f32[192,192,128]{2,1,0:T(8,128)} %tiles.1.refs_1_, bf16[2,2,192,256]{3,2,1,0:T(8,128)(2,1)} %constant.35.clone.refs_2_, f32[24,3,48,128]{3,2,1,0:T(8,128)} %copy-done, f32[12,3,48,128]{3,2,1,0:T(8,128)} %rows.7.refs_4_), custom_call_target="tpu_custom_call" | custom-call | flops 1 | bytes 1 | tf_op jit(solution)/shard_map/rows/pallas_call | solution.py:452
  157.3 8.1 %rows.9.refs_0_ = f32[24,3,48,128]{3,2,1,0:T(8,128)} custom-call(s32[1]{0:T(128)} %bitcast.refs_0_, f32[192,192,128]{2,1,0:T(8,128)} %tiles.1.refs_1_, bf16[2,2,192,256]{3,2,1,0:T(8,128)(2,1)} %constant.35.clone.refs_2_, f32[12,3,48,128]{3,2,1,0:T(8,128)} %rows.8.refs_3_), custom_call_target="tpu_custom_call" | custom-call | flops 1 | bytes 1 | tf_op jit(solution)/shard_map/rows/pallas_call | solution.py:452
  165.3 6.7 %collective-permute-done.16.refs_2_ = f32[12,3,48,128]{3,2,1,0:T(8,128)S(1)} collective-permute-done((f32[12,3,48,128]{3,2,1,0:T(8,128)}, f32[12,3,48,128]{3,2,1,0:T(8,128)S(1)}, u32[]{:S(2)}, u32[]{:S(2)}) %collective-permute-start.16) | collective-permute-done | bytes 884768 | tf_op jit(solution)/shard_map/ppermute | solution.py:472
  173.0 3.9 %finish.2.refs_7_ = f32[2,24,48,192]{3,2,1,0:T(8,128)} custom-call(f32[24,3,48,128]{3,2,1,0:T(8,128)} %rows.9.refs_0_, f32[24,3,48,128]{3,2,1,0:T(8,128)} %copy-done.1, f32[12,3,48,128]{3,2,1,0:T(8,128)} %copy-done.3, bf16[512,192]{1,0:T(8,128)(2,1)} %constant.36.clone.refs_3_, f32[1,192]{1,0:T(1,128)} %bitcast.12, f32[48,1]{1,0:T(8,128)} %copy.17.refs_5_, ...), custom_call_target="tpu_custom_call" | custom-call | tf_op jit(solution)/shard_map/finish/pallas_call | solution.py:502
  176.9 13.2 %collective-permute-done.15.refs_2_ = f32[12,3,48,128]{3,2,1,0:T(8,128)S(1)} collective-permute-done((f32[12,3,48,128]{3,2,1,0:T(8,128)}, f32[12,3,48,128]{3,2,1,0:T(8,128)S(1)}, u32[]{:S(2)}, u32[]{:S(2)}) %collective-permute-start.15) | collective-permute-done | bytes 884768 | tf_op jit(solution)/shard_map/ppermute | solution.py:472
  191.0 3.9 %finish.3 = f32[2,24,48,192]{3,2,1,0:T(8,128)} custom-call(f32[24,3,48,128]{3,2,1,0:T(8,128)} %rows.9.refs_0_, f32[24,3,48,128]{3,2,1,0:T(8,128)} %copy-done.1, f32[12,3,48,128]{3,2,1,0:T(8,128)} %copy-done.2, bf16[512,192]{1,0:T(8,128)(2,1)} %constant.36.clone.refs_3_, f32[1,192]{1,0:T(1,128)} %bitcast.13, ...), custom_call_target="tpu_custom_call", output_to_operand_aliasing={{}: (7, {})} | custom-call | tf_op jit(solution)/shard_map/finish/pallas_call | solution.py:502
  (50 shorter events, 16.6 us)
Async XLA Ops:
  6.2 14.0 %collective-permute-start.1 = (f32[65,16,128]{2,1,0:T(8,128)}, f32[65,16,128]{2,1,0:T(8,128)S(1)}, u32[]{:S(2)}, u32[]{:S(2)}) collective-permute-start(f32[65,16,128]{2,1,0:T(8,128)} %spread.1.refs_1_), channel_id=1, source_target_pairs={{2,0},{3,1},{4,2},{5,3},{6,4},{7,5},{10,8},{11,9},{12,10},{13,11},... | collective-permute-start | bytes 1597448 | tf_op jit(solution)/shard_map/ppermute | solution.py:376
  8.6 13.8 %collective-permute-start.6 = (f32[65,16,128]{2,1,0:T(8,128)}, f32[65,16,128]{2,1,0:T(8,128)S(1)}, u32[]{:S(2)}, u32[]{:S(2)}) collective-permute-start(f32[65,16,128]{2,1,0:T(8,128)} %spread.1.refs_1_), channel_id=1, source_target_pairs={{0,1},{1,0},{2,3},{3,2},{4,5},{5,4},{6,7},{7,6},{8,9},{9,8},{10,11... | collective-permute-start | bytes 1597448 | tf_op jit(solution)/shard_map/ppermute | solution.py:376
  10.2 15.4 %collective-permute-start = (f32[65,16,128]{2,1,0:T(8,128)}, f32[65,16,128]{2,1,0:T(8,128)S(1)}, u32[]{:S(2)}, u32[]{:S(2)}) collective-permute-start(f32[65,16,128]{2,1,0:T(8,128)} %spread.1.refs_1_), channel_id=1, source_target_pairs={{0,2},{1,3},{2,4},{3,5},{4,6},{5,7},{8,10},{9,11},{10,12},{11,13},... | collective-permute-start | bytes 1597448 | tf_op jit(solution)/shard_map/ppermute | solution.py:376
  20.2 56.3 %copy-start.4 = (f32[65,16,128]{2,1,0:T(8,128)}, f32[65,16,128]{2,1,0:T(8,128)S(1)}, u32[]{:S(2)}) copy-start(f32[65,16,128]{2,1,0:T(8,128)S(1)} %collective-permute-done.1.refs_7_) | copy-start | bytes 1597444
  22.5 54.1 %copy-start.5 = (f32[65,16,128]{2,1,0:T(8,128)}, f32[65,16,128]{2,1,0:T(8,128)S(1)}, u32[]{:S(2)}) copy-start(f32[65,16,128]{2,1,0:T(8,128)S(1)} %collective-permute-done.6.refs_8_) | copy-start | bytes 1597444
  22.5 6.8 %collective-permute-start.8 = (f32[65,16,128]{2,1,0:T(8,128)S(1)}, f32[65,16,128]{2,1,0:T(8,128)S(1)}, u32[]{:S(2)}, u32[]{:S(2)}) collective-permute-start(f32[65,16,128]{2,1,0:T(8,128)S(1)} %collective-permute-done.1.refs_7_), channel_id=1, source_target_pairs={{0,1},{1,0},{2,3},{3,2},{4,5},{5,4},{8,9},{9,8},{10,11},{11,10},{1... | collective-permute-start | bytes 1597448 | tf_op jit(solution)/shard_map/ppermute | solution.py:376
  23.2 6.2 %collective-permute-start.2 = (f32[65,16,128]{2,1,0:T(8,128)S(1)}, f32[65,16,128]{2,1,0:T(8,128)S(1)}, u32[]{:S(2)}, u32[]{:S(2)}) collective-permute-start(f32[65,16,128]{2,1,0:T(8,128)S(1)} %collective-permute-done.1.refs_7_), channel_id=1, source_target_pairs={{2,0},{3,1},{4,2},{5,3},{10,8},{11,9},{12,10},{13,11},{18,16},{19,... | collective-permute-start | bytes 1597448 | tf_op jit(solution)/shard_map/ppermute | solution.py:376
  25.6 51.0 %copy-start.6 = (f32[65,16,128]{2,1,0:T(8,128)}, f32[65,16,128]{2,1,0:T(8,128)S(1)}, u32[]{:S(2)}) copy-start(f32[65,16,128]{2,1,0:T(8,128)S(1)} %collective-permute-done.refs_2_) | copy-start | bytes 1597444
  25.6 15.5 %collective-permute-start.4 = (f32[65,16,128]{2,1,0:T(8,128)S(1)}, f32[65,16,128]{2,1,0:T(8,128)S(1)}, u32[]{:S(2)}, u32[]{:S(2)}) collective-permute-start(f32[65,16,128]{2,1,0:T(8,128)S(1)} %collective-permute-done.refs_2_), channel_id=1, source_target_pairs={{2,4},{3,5},{4,6},{5,7},{10,12},{11,13},{12,14},{13,15},{18,20},{1... | collective-permute-start | bytes 1597448 | tf_op jit(solution)/shard_map/ppermute | solution.py:376
  26.9 14.2 %collective-permute-start.7 = (f32[65,16,128]{2,1,0:T(8,128)S(1)}, f32[65,16,128]{2,1,0:T(8,128)S(1)}, u32[]{:S(2)}, u32[]{:S(2)}) collective-permute-start(f32[65,16,128]{2,1,0:T(8,128)S(1)} %collective-permute-done.refs_2_), channel_id=1, source_target_pairs={{2,3},{3,2},{4,5},{5,4},{6,7},{7,6},{10,11},{11,10},{12,13},{13,12... | collective-permute-start | bytes 1597448 | tf_op jit(solution)/shard_map/ppermute | solution.py:376
  29.3 47.3 %copy-start.7 = (f32[65,16,128]{2,1,0:T(8,128)}, f32[65,16,128]{2,1,0:T(8,128)S(1)}, u32[]{:S(2)}) copy-start(f32[65,16,128]{2,1,0:T(8,128)S(1)} %collective-permute-done.8.refs_14_) | copy-start | bytes 1597444
  29.3 47.3 %copy-start.8 = (f32[65,16,128]{2,1,0:T(8,128)}, f32[65,16,128]{2,1,0:T(8,128)S(1)}, u32[]{:S(2)}) copy-start(f32[65,16,128]{2,1,0:T(8,128)S(1)} %collective-permute-done.2.refs_5_) | copy-start | bytes 1597444
  29.3 15.5 %collective-permute-start.9 = (f32[65,16,128]{2,1,0:T(8,128)S(1)}, f32[65,16,128]{2,1,0:T(8,128)S(1)}, u32[]{:S(2)}, u32[]{:S(2)}) collective-permute-start(f32[65,16,128]{2,1,0:T(8,128)S(1)} %collective-permute-done.2.refs_5_), channel_id=1, source_target_pairs={{0,1},{1,0},{2,3},{3,2},{8,9},{9,8},{10,11},{11,10},{16,17},{17,16... | collective-permute-start | bytes 1597448 | tf_op jit(solution)/shard_map/ppermute | solution.py:376
  30.0 14.8 %collective-permute-start.3 = (f32[65,16,128]{2,1,0:T(8,128)S(1)}, f32[65,16,128]{2,1,0:T(8,128)}, u32[]{:S(2)}, u32[]{:S(2)}) collective-permute-start(f32[65,16,128]{2,1,0:T(8,128)S(1)} %collective-permute-done.2.refs_5_), channel_id=1, source_target_pairs={{2,0},{3,1},{10,8},{11,9},{18,16},{19,17},{26,24},{27,25}} | collective-permute-start | bytes 1597448 | tf_op jit(solution)/shard_map/ppermute | solution.py:376
  41.0 35.6 %copy-start.9 = (f32[65,16,128]{2,1,0:T(8,128)}, f32[65,16,128]{2,1,0:T(8,128)S(1)}, u32[]{:S(2)}) copy-start(f32[65,16,128]{2,1,0:T(8,128)S(1)} %collective-permute-done.4.refs_4_) | copy-start | bytes 1597444
  41.1 22.4 %copy-start.10 = (f32[65,16,128]{2,1,0:T(8,128)}, f32[65,16,128]{2,1,0:T(8,128)S(1)}, u32[]{:S(2)}) copy-start(f32[65,16,128]{2,1,0:T(8,128)S(1)} %collective-permute-done.7.refs_9_) | copy-start | bytes 1597444
  41.1 13.3 %collective-permute-start.11 = (f32[65,16,128]{2,1,0:T(8,128)S(1)}, f32[65,16,128]{2,1,0:T(8,128)S(1)}, u32[]{:S(2)}, u32[]{:S(2)}) collective-permute-start(f32[65,16,128]{2,1,0:T(8,128)S(1)} %collective-permute-done.4.refs_4_), channel_id=1, source_target_pairs={{4,5},{5,4},{6,7},{7,6},{12,13},{13,12},{14,15},{15,14},{20,21},{2... | collective-permute-start | bytes 1597448 | tf_op jit(solution)/shard_map/ppermute | solution.py:376
  43.5 20.0 %collective-permute-start.5 = (f32[65,16,128]{2,1,0:T(8,128)S(1)}, f32[65,16,128]{2,1,0:T(8,128)}, u32[]{:S(2)}, u32[]{:S(2)}) collective-permute-start(f32[65,16,128]{2,1,0:T(8,128)S(1)} %collective-permute-done.4.refs_4_), channel_id=1, source_target_pairs={{4,6},{5,7},{12,14},{13,15},{20,22},{21,23},{28,30},{29,31}} | collective-permute-start | bytes 1597448 | tf_op jit(solution)/shard_map/ppermute | solution.py:376
  44.9 23.9 %collective-permute-start.10 = (f32[65,16,128]{2,1,0:T(8,128)}, f32[65,16,128]{2,1,0:T(8,128)}, u32[]{:S(2)}, u32[]{:S(2)}) collective-permute-start(f32[65,16,128]{2,1,0:T(8,128)} %collective-permute-done.3.refs_3_), channel_id=1, source_target_pairs={{0,1},{1,0},{8,9},{9,8},{16,17},{17,16},{24,25},{25,24}} | collective-permute-start | bytes 1597448 | tf_op jit(solution)/shard_map/ppermute | solution.py:376
  63.5 13.1 %collective-permute-start.12 = (f32[65,16,128]{2,1,0:T(8,128)}, f32[65,16,128]{2,1,0:T(8,128)}, u32[]{:S(2)}, u32[]{:S(2)}) collective-permute-start(f32[65,16,128]{2,1,0:T(8,128)} %collective-permute-done.5.refs_6_), channel_id=1, source_target_pairs={{6,7},{7,6},{14,15},{15,14},{22,23},{23,22},{30,31},{31,30}} | collective-permute-start | bytes 1597448 | tf_op jit(solution)/shard_map/ppermute | solution.py:376
  134.4 8.6 %collective-permute-start.13 = (f32[24,3,48,128]{3,2,1,0:T(8,128)}, f32[24,3,48,128]{3,2,1,0:T(8,128)S(1)}, u32[]{:S(2)}, u32[]{:S(2)}) collective-permute-start(f32[24,3,48,128]{3,2,1,0:T(8,128)} %rows.5.refs_3_), channel_id=1, source_target_pairs={{0,8},{8,0},{16,24},{24,16},{1,9},{9,1},{17,25},{25,17},{2,10},{10... | collective-permute-start | bytes 5308424 | tf_op jit(solution)/shard_map/ppermute | solution.py:472
  142.4 22.9 %collective-permute-start.14 = (f32[24,3,48,128]{3,2,1,0:T(8,128)}, f32[24,3,48,128]{3,2,1,0:T(8,128)S(1)}, u32[]{:S(2)}, u32[]{:S(2)}) collective-permute-start(f32[24,3,48,128]{3,2,1,0:T(8,128)} %rows.6.refs_4_), channel_id=1, source_target_pairs={{0,8},{8,0},{16,24},{24,16},{1,9},{9,1},{17,25},{25,17},{2,10},{10... | collective-permute-start | bytes 5308424 | tf_op jit(solution)/shard_map/ppermute | solution.py:472
  149.3 22.7 %collective-permute-start.16 = (f32[12,3,48,128]{3,2,1,0:T(8,128)}, f32[12,3,48,128]{3,2,1,0:T(8,128)S(1)}, u32[]{:S(2)}, u32[]{:S(2)}) collective-permute-start(f32[12,3,48,128]{3,2,1,0:T(8,128)} %rows.7.refs_4_), channel_id=1, source_target_pairs={{0,16},{8,24},{16,0},{24,8},{1,17},{9,25},{17,1},{25,9},{2,18},{10... | collective-permute-start | bytes 2654216 | tf_op jit(solution)/shard_map/ppermute | solution.py:472
  155.0 35.0 %collective-permute-start.15 = (f32[12,3,48,128]{3,2,1,0:T(8,128)}, f32[12,3,48,128]{3,2,1,0:T(8,128)S(1)}, u32[]{:S(2)}, u32[]{:S(2)}) collective-permute-start(f32[12,3,48,128]{3,2,1,0:T(8,128)} %rows.8.refs_3_), channel_id=1, source_target_pairs={{0,16},{8,24},{16,0},{24,8},{1,17},{9,25},{17,1},{25,9},{2,18},{10... | collective-permute-start | bytes 2654216 | tf_op jit(solution)/shard_map/ppermute | solution.py:472
  (7 other events, 49.5 us)

commit v7 on v6

--- a/solution.py
+++ b/solution.py
@@ -21,7 +21,7 @@
 PHASES = 128
 BF16 = jnp.bfloat16
 F32 = jnp.float32
-VMEM_LIMIT = 60 * 1024 * 1024
+VMEM_LIMIT = 8 * 1024 * 1024
 
 
 def halves(array):
@@ -74,11 +74,12 @@
 
 def row_tables():
     half = NX // 2
+    freq = np.arange(half).reshape(-1, 2, TILE // 2).transpose(1, 0, 2).reshape(-1) - half
     quarter = NX // 4
     out = []
     for parity in range(2):
         position = 2 * np.arange(quarter) + parity - NX // 4
-        cos, sin = waves(np.arange(half) - half, position, NX)
+        cos, sin = waves(freq, position, NX)
         table = np.zeros((half, 2 * LANES))
         lanes = (np.arange(quarter) + parity * quarter) % LANES
         table[:, lanes] = cos / math.sqrt(NX)
@@ -120,7 +121,7 @@
     col = (owner - owner_row * grid_cols) * tile_cols + tile_col - tile_row * tile_cols
     folds = NX // TILE // 2
     upper = (row >= folds).astype(jnp.int32)
-    base = (row - upper * folds) * NY + col
+    base = (row - upper * folds) * (NY // 2) + col
     phase = tile_id - tile_col * tile_depth + upper * tile_depth
     codes = (base * PHASES + phase).astype(F32)
 
@@ -159,56 +160,45 @@
     out_ref[blocks // 2] = jnp.broadcast_to(codes, (2 * TILE, LANES))
 
 
-def tiles_kernel(arrays, *refs):
+def tiles_kernel(conditions, first, *refs):
+    arrays = len(conditions)
     deep_ref = refs[0]
     source_refs = refs[1 : 1 + arrays]
-    depth_ref, phases_ref, column_ref, out_ref, tiles_ref, codes_ref, acc_ref, even_ref, odd_ref, arrived = refs[1 + arrays :]
-    sources = tiles_ref.shape[0]
-    half = NX // 2
+    depth_ref, phases_ref = refs[1 + arrays : 3 + arrays]
+    low_ref, high_ref, token_ref, codes_ref, even_ref, odd_ref, arrived = refs[-7:]
+    token_ref[...] = jnp.zeros_like(token_ref)
     stride = NY
-    pairs = tiles_ref.shape[1]
+    pairs = source_refs[0].shape[0] - 1
     batch = 8
-    rows = column_ref.shape[1] // 4
-    width = out_ref.shape[0]
-
-    @pl.when(pl.program_id(0) == 0)
-    def _():
-        def copies(array, slot):
-            ref = source_refs[array]
-            return (
-                pltpu.make_async_copy(ref.at[pl.ds(0, pairs)], tiles_ref.at[slot], arrived.at[0, slot]),
-                pltpu.make_async_copy(ref.at[pairs, pl.ds(0, TILE)], codes_ref.at[slot], arrived.at[1, slot]),
-            )
-
-        def start(array, slot):
-            for copy in copies(array, slot):
-                copy.start()
-
-        chips = Z_CHIPS
-        for slot in range(sources):
-            array = slot // chips * (2 * chips - 1) + max(2 * (slot % chips) - 1, 0)
-            if slot % chips == 0:
-                start(array, slot)
-            else:
-                upper = deep_ref[0] >= slot % chips
-                pl.when(upper)(functools.partial(start, array, slot))
-                pl.when(jnp.logical_not(upper))(functools.partial(start, array + 1, slot))
+    batches = pairs // batch
+    assert batches % 2 == 0
+
+    def copies(index):
+        return pltpu.make_async_copy(
+            source_refs[index].at[pairs, pl.ds(0, TILE)], codes_ref.at[index], arrived.at[index]
+        )
+
+    for index in range(arrays):
+        copies(index).start()
+
+    if first:
 
         def clear(step, carry):
-            acc_ref[pl.ds(pl.multiple_of(step * stride, stride), stride), :] = jnp.zeros((stride, LANES), F32)
+            at = pl.ds(pl.multiple_of(step * stride, stride), stride)
+            low_ref[at, :] = jnp.zeros((stride, LANES), F32)
+            high_ref[at, :] = jnp.zeros((stride, LANES), F32)
             return carry
 
-        lax.fori_loop(0, half, clear, 0)
-        for slot in range(sources):
-            for copy in copies(0, slot):
-                copy.wait()
-
-        batches = pairs // batch
-        assert batches % 2 == 0
-
-        def spectrum(source, number, to_ref):
-            first = number * batch
-            tiles = jnp.concatenate([tiles_ref[source, first + index] for index in range(batch)], axis=1)
+        lax.fori_loop(0, NX // 4, clear, 0)
+
+    for index in range(arrays):
+        copies(index).wait()
+
+    def add_source(index):
+        tiles_ref = source_refs[index]
+
+        def spectrum(number, to_ref):
+            tiles = jnp.concatenate([tiles_ref[number * batch + place] for place in range(batch)], axis=1)
             high, low = split(tiles)
             to_ref[...] = lax.dot_general(
                 jnp.concatenate((high, low, high), axis=0),
@@ -217,9 +207,9 @@
                 preferred_element_type=F32,
             )
 
-        def accumulate(source, number, from_ref):
+        def accumulate(number, from_ref):
             for tile in range(2 * batch):
-                code = codes_ref[source, 0, number * 2 * batch + tile].astype(jnp.int32)
+                code = codes_ref[index, 0, number * 2 * batch + tile].astype(jnp.int32)
                 base = lax.shift_right_logical(code, 7)
                 phase = jnp.bitwise_and(code, PHASES - 1)
                 cos = phases_ref[0, pl.ds(phase, 1), :]
@@ -228,32 +218,43 @@
                     row = tile * TILE * TILE + i * TILE
                     value = from_ref[row : row + TILE, :]
                     value = value * cos + pltpu.roll(value, LANES // 2, 1) * sin
-                    at = pl.ds(pl.multiple_of(base * TILE + i * stride, TILE), TILE)
+                    acc_ref = high_ref if i >= TILE // 2 else low_ref
+                    at = pl.ds(pl.multiple_of(base * TILE + i % (TILE // 2) * stride, TILE), TILE)
                     acc_ref[at, :] = acc_ref[at, :] + value
 
-        spectrum(0, 0, even_ref)
+        spectrum(0, even_ref)
 
         def add_pair(step, carry):
-            source = step // (batches // 2)
-            number = step % (batches // 2) * 2
-            spectrum(source, number + 1, odd_ref)
-            accumulate(source, number, even_ref)
-            later = jnp.minimum(step + 1, sources * batches // 2 - 1)
-            spectrum(later // (batches // 2), later % (batches // 2) * 2, even_ref)
-            accumulate(source, number + 1, odd_ref)
+            number = 2 * step
+            spectrum(number + 1, odd_ref)
+            accumulate(number, even_ref)
+            spectrum(jnp.minimum(number + 2, batches - 2), even_ref)
+            accumulate(number + 1, odd_ref)
             return carry
 
-        lax.fori_loop(0, sources * batches // 2, add_pair, 0)
-
+        lax.fori_loop(0, batches // 2, add_pair, 0)
+
+    for index, condition in enumerate(conditions):
+        if condition is None:
+            add_source(index)
+        else:
+            side, depth = condition
+            holds = deep_ref[0] >= depth if side == "from" else deep_ref[0] < depth
+            pl.when(holds)(functools.partial(add_source, index))
+
+
+def columns_kernel(low_in, high_in, column_ref, low_ref, high_ref):
+    del low_in, high_in
+    stride = NY
+    third = NY // 3
+    rows = column_ref.shape[1] // 4
     turn = jnp.where(lax.broadcasted_iota(jnp.int32, (1, LANES), 1) < LANES // 2, -1.0, 1.0)
-    origin = pl.program_id(0) * width
-    third = NY // 3
 
     def columns(step, carry):
+        start = pl.multiple_of(step * stride, stride)
         folded = ([], [], [])
-        for side in range(2):
-            start = pl.multiple_of((origin + 2 * step + side) * stride, stride)
-            first, second, last = (acc_ref[pl.ds(start + third * part, third), :] for part in range(3))
+        for ref in (low_ref, high_ref):
+            first, second, last = (ref[pl.ds(start + third * part, third), :] for part in range(3))
             both = second + last
             across = pltpu.roll(second - last, LANES // 2, 1) * (turn * math.sqrt(0.75))
             middle = first - 0.5 * both
@@ -264,49 +265,59 @@
             high_low = split(jnp.concatenate(folded[residue], axis=1))
             product = jnp.dot(column_ref[residue], jnp.concatenate(high_low, axis=0), preferred_element_type=F32)
             product = product[: 2 * rows] + product[2 * rows :]
-            for side in range(2):
+            for side, ref in enumerate((low_ref, high_ref)):
                 lanes = slice(side * LANES, (side + 1) * LANES)
-                out_ref[2 * step + side, residue * rows : (residue + 1) * rows, :] = (
+                ref[pl.ds(start + residue * rows, rows), :] = (
                     product[:rows, lanes] + pltpu.roll(product[rows:, lanes], LANES // 2, 1) * turn
                 )
         return carry
 
-    lax.fori_loop(0, width // 2, columns, 0, unroll=2)
-
-
-def rows_kernel(planes_padded, addends, place_ref, in_ref, row_ref, *refs):
+    lax.fori_loop(0, NX // 4, columns, 0, unroll=2)
+
+
+def rows_kernel(relative, first, count, chunks, grid_rows, addends, planes_padded, place_ref, low_ref, high_ref, row_ref, *refs):
     out_ref = refs[-1]
-    half = NX // 2
-    residue = pl.program_id(1)
+    rows = grid_rows * chunks * TILE
+    device = jnp.bitwise_xor(place_ref[0], relative)
     lane = lax.broadcasted_iota(jnp.int32, (PLANES, LANES), 1)
-    flat = in_ref.reshape(half * TILE, LANES)
-    turned = [flat[pl.ds(row, half, stride=TILE), :].T for row in range(TILE)]
-    parts = []
-    for odd in range(2):
-        at = odd * PLANES
-        stacked = [value[part * 64 + at : part * 64 + at + PLANES] for value in turned for part in range(2)]
-        high, low = split(jnp.concatenate(stacked, axis=0))
-        count = high.shape[0]
-        both = jnp.dot(jnp.concatenate((high, low), axis=0), row_ref[odd, 0], preferred_element_type=F32)
-        product = both[:count] + both[count:] + jnp.dot(high, row_ref[odd, 1], preferred_element_type=F32)
-        sides = []
+
+    def block(step, carry):
+        chunk, residue = step // 3, step % 3
+        start = residue * rows + (device * chunks + first + chunk) * TILE
+        turned = []
         for row in range(TILE):
-            real = product[2 * row * PLANES : (2 * row + 1) * PLANES]
-            imag = product[(2 * row + 1) * PLANES : (2 * row + 2) * PLANES]
-            sides.append((real[:, :LANES] - imag[:, LANES:], real[:, LANES:] + imag[:, :LANES]))
-        parts.append(sides)
-    for slot in range(TILE // 2):
-        for part in range(2):
-            even = [parts[0][slot + side * TILE // 2][part] for side in range(2)]
-            odd = [parts[1][slot + side * TILE // 2][part] for side in range(2)]
-            values = [jnp.where(lane < NX // 4, even[side], odd[side]) for side in range(2)]
-            values.append(jnp.where(lane < LANES // 2, odd[0], pltpu.roll(odd[1], LANES // 2, 1)))
-            for number, value in enumerate(values):
-                at = (3 * slot + residue, number, pl.ds(part * planes_padded, planes_padded))
-                total = value[:planes_padded]
-                for ref in refs[:addends]:
-                    total = total + ref[at]
-                out_ref[at] = total
+            at = pl.ds(start + row, NX // 4, stride=NY)
+            turned.append(jnp.concatenate((low_ref[at, :], high_ref[at, :]), axis=0).T)
+        parts = []
+        for odd in range(2):
+            at = odd * PLANES
+            stacked = [value[part * 64 + at : part * 64 + at + PLANES] for value in turned for part in range(2)]
+            high, low = split(jnp.concatenate(stacked, axis=0))
+            size = high.shape[0]
+            both = jnp.dot(jnp.concatenate((high, low), axis=0), row_ref[odd, 0], preferred_element_type=F32)
+            product = both[:size] + both[size:] + jnp.dot(high, row_ref[odd, 1], preferred_element_type=F32)
+            sides = []
+            for row in range(TILE):
+                real = product[2 * row * PLANES : (2 * row + 1) * PLANES]
+                imag = product[(2 * row + 1) * PLANES : (2 * row + 2) * PLANES]
+                sides.append((real[:, :LANES] - imag[:, LANES:], real[:, LANES:] + imag[:, :LANES]))
+            parts.append(sides)
+        for slot in range(TILE // 2):
+            place = chunk * (CHUNK // 2) + 3 * slot + residue
+            for part in range(2):
+                even = [parts[0][slot + side * TILE // 2][part] for side in range(2)]
+                odd = [parts[1][slot + side * TILE // 2][part] for side in range(2)]
+                values = [jnp.where(lane < NX // 4, even[side], odd[side]) for side in range(2)]
+                values.append(jnp.where(lane < LANES // 2, odd[0], pltpu.roll(odd[1], LANES // 2, 1)))
+                for number, value in enumerate(values):
+                    planes = pl.ds(part * planes_padded, planes_padded)
+                    total = value[:planes_padded]
+                    for ref in refs[:addends]:
+                        total = total + ref[first * (CHUNK // 2) + place, number, planes]
+                    out_ref[place, number, planes] = total
+        return carry
+
+    lax.fori_loop(0, 3 * count, block, 0)
 
 
 def finish_kernel(planes_padded, parts, refs):
@@ -359,7 +370,7 @@
 
     tiles = pl.pallas_call(
         functools.partial(spread_kernel, tile_rows, tile_cols, grid_cols, grid_rows * grid_cols),
-        out_shape=jax.ShapeDtypeStruct((blocks // 2 + 1, 2 * TILE, LANES), F32),
+        out_shape=pltpu.HBM((blocks // 2 + 1, 2 * TILE, LANES), F32),
         in_specs=[vmem] * 5,
         out_specs=vmem,
         compiler_params=params,
@@ -375,32 +386,6 @@
         ]
         return lax.ppermute(value, "gy", moves)
 
-    held = {0: tiles}
-    for steps in range(1, Z_CHIPS):
-        held[steps] = shift(held[steps - 1], range(steps - 1, Z_CHIPS - 1), 1, 0)
-        held[-steps] = shift(held[1 - steps], range(1, Z_CHIPS + 1 - steps), -1, 0)
-    holders = {0: range(Z_CHIPS)}
-    for steps in range(1, Z_CHIPS):
-        holders[steps] = range(steps, Z_CHIPS)
-        holders[-steps] = range(Z_CHIPS - steps)
-    crossed_y = {}
-    chain = []
-    for steps in sorted(held, key=abs):
-        for wide in range(1, along):
-            value = held[steps]
-            if len(chain) > 1:
-                value, _ = lax.optimization_barrier((value, chain[-2]))
-            crossed_y[steps, wide] = shift(value, holders[steps], 0, wide)
-            chain.append(crossed_y[steps, wide])
-    gathered = [tiles]
-    for wide in range(along):
-        def pick(steps):
-            return crossed_y[steps, wide] if wide else held[steps]
-
-        if wide:
-            gathered.append(pick(0))
-        for steps in range(1, Z_CHIPS):
-            gathered += [pick(steps), pick(steps - Z_CHIPS)]
     place = lax.axis_index("gx").astype(jnp.int32).reshape(1)
     deep_place = deep_at.reshape(1)
     gy = lax.axis_index("gy")
@@ -408,65 +393,99 @@
     matrix = lax.dynamic_index_in_dim(jnp.asarray(matrices), gy, 0, keepdims=False)
     phase_rows = lax.dynamic_index_in_dim(jnp.asarray(phases), gy, 0, keepdims=False)
     column = jnp.asarray(column_tables())
-    def whole(shape):
-        return pl.BlockSpec(shape, lambda step: (0,) * len(shape), pipeline_mode=pl.Buffered(1))
-
     half = NX // 2
-    width = 16
-    kept = NY // 2
-    spectra = pltpu.VMEM((16 * TILE * TILE, LANES), F32)
-    columns = pl.pallas_call(
-        functools.partial(tiles_kernel, len(gathered)),
-        grid=(half // width,),
-        out_shape=jax.ShapeDtypeStruct((half, kept, LANES), F32),
-        in_specs=[pl.BlockSpec(memory_space=pltpu.SMEM)]
-        + [pl.BlockSpec(memory_space=pl.ANY)] * len(gathered)
-        + [whole(array.shape) for array in (matrix, phase_rows, column)],
-        out_specs=pl.BlockSpec((width, kept, LANES), lambda step: (step, 0, 0)),
-        scratch_shapes=[
-            pltpu.VMEM((grid_cols, blocks // 2) + tiles.shape[1:], F32),
-            pltpu.SMEM((grid_cols, TILE, LANES), F32),
-            pltpu.VMEM((half * NY, LANES), F32),
-            spectra,
-            spectra,
-            pltpu.SemaphoreType.DMA((2, grid_cols)),
-        ],
+    smem = pl.BlockSpec(memory_space=pltpu.SMEM)
+    acc_shape = (half // 2 * NY, LANES)
+
+    def in_vmem(arrays):
+        return [pltpu.with_memory_space_constraint(array, pltpu.VMEM) for array in arrays]
+
+    def in_hbm(arrays):
+        return [pltpu.with_memory_space_constraint(array, pltpu.HBM) for array in arrays]
+
+    def condition(steps):
+        if steps == 0:
+            return None
+        return ("from", steps) if steps > 0 else ("below", Z_CHIPS + steps)
+
+    def add_tiles(sources, acc):
+        conditions = [condition(steps) for steps, _ in sources]
+        spectra = pltpu.VMEM((16 * TILE * TILE, LANES), F32)
+        kept = [jax.ShapeDtypeStruct(acc_shape, F32)] * 2 if acc else [pltpu.VMEM(acc_shape, F32)] * 2
+        inputs = len(sources) + 3
+        *acc, token = pl.pallas_call(
+            functools.partial(tiles_kernel, conditions, not acc),
+            out_shape=kept + [jax.ShapeDtypeStruct((TILE, LANES), F32)],
+            in_specs=[smem] + [vmem] * (inputs - 1 + len(acc)),
+            out_specs=[vmem] * 3,
+            input_output_aliases={inputs: 0, inputs + 1: 1} if acc else {},
+            scratch_shapes=[
+                pltpu.SMEM((len(sources), TILE, LANES), F32),
+                spectra,
+                spectra,
+                pltpu.SemaphoreType.DMA((len(sources),)),
+            ],
+            compiler_params=params,
+            cost_estimate=pl.CostEstimate(flops=0, bytes_accessed=len(sources) << 23, transcendentals=0),
+            name="tiles",
+        )(deep_place, *in_hbm([array for _, array in sources] + [matrix, phase_rows]), *in_vmem(acc))
+        return acc, token
+
+    def after(value, token):
+        return lax.optimization_barrier((value, token))[0]
+
+    held, crossed_y = {0: tiles}, {}
+    acc, waiting = [], [(0, tiles)]
+    token = None
+    for steps in range(1, Z_CHIPS + 1):
+        if steps < Z_CHIPS:
+            for signed in (steps, -steps):
+                value = held[signed - signed // steps]
+                value = value if token is None else after(value, token)
+                senders = range(steps - 1, Z_CHIPS - 1) if signed > 0 else range(1, Z_CHIPS + 1 - steps)
+                held[signed] = shift(value, senders, signed // steps, 0)
+        behind = []
+        for signed in sorted({steps - 1, 1 - steps}):
+            holders = range(signed, Z_CHIPS) if signed >= 0 else range(Z_CHIPS + signed)
+            for wide in range(1, along):
+                value = held[signed] if token is None else after(held[signed], token)
+                crossed_y[signed, wide] = shift(value, holders, 0, wide)
+                behind.append((signed, crossed_y[signed, wide]))
+        acc, token = add_tiles(waiting, acc)
+        waiting = behind
+        if steps < Z_CHIPS:
+            waiting = [(steps, held[steps]), (-steps, held[-steps])] + behind
+    acc, _ = add_tiles(waiting, acc)
+
+    acc = pl.pallas_call(
+        columns_kernel,
+        out_shape=[jax.ShapeDtypeStruct(acc_shape, F32)] * 2,
+        in_specs=[vmem] * 3,
+        out_specs=[vmem] * 2,
+        input_output_aliases={0: 0, 1: 1},
         compiler_params=params,
-        name="tiles",
-    )(deep_place, *gathered, matrix, phase_rows, column)
+        name="columns",
+    )(*in_vmem(acc), *in_hbm([column]))
 
     row_table = jnp.asarray(row_tables())
     part_shape = (3, 2 * planes_padded, LANES)
 
     def rows_for(relative, first, count, addends, after):
-        def block(step, residue, place_ref):
-            device = jnp.bitwise_xor(place_ref[0], relative)
-            return (0, (residue * grid_rows + device) * chunks + first + step, 0)
-
-        part = pl.BlockSpec((slots,) + part_shape, lambda step, residue, place_ref: (step, 0, 0, 0))
-        addend = pl.BlockSpec((slots,) + part_shape, lambda step, residue, place_ref: (first + step, 0, 0, 0))
-
         def body(*refs):
-            rows_kernel(planes_padded, len(addends), *refs[: 3 + len(addends)], refs[-1])
+            operands = 4 + len(addends)
+            rows_kernel(
+                relative, first, count, chunks, grid_rows, len(addends), planes_padded, *refs[:operands], refs[-1]
+            )
 
         return pl.pallas_call(
             body,
-            grid_spec=pltpu.PrefetchScalarGridSpec(
-                num_scalar_prefetch=1,
-                grid=(count, 3),
-                in_specs=[
-                    pl.BlockSpec((half, TILE, LANES), block),
-                    pl.BlockSpec(row_table.shape, lambda step, residue, place_ref: (0, 0, 0, 0)),
-                ]
-                + [addend] * len(addends)
-                + [pl.BlockSpec(memory_space=pl.ANY)] * len(after),
-                out_specs=part,
-            ),
-            out_shape=jax.ShapeDtypeStruct((count * slots,) + part_shape, F32),
+            in_specs=[smem] + [vmem] * (3 + len(addends)) + [pl.BlockSpec(memory_space=pl.ANY)] * len(after),
+            out_specs=vmem,
+            out_shape=pltpu.HBM((count * slots,) + part_shape, F32),
             compiler_params=params,
             cost_estimate=pl.CostEstimate(flops=1, bytes_accessed=1, transcendentals=0),
             name="rows",
-        )(place, columns, row_table, *addends, *after)
+        )(place, *in_vmem(acc), *in_hbm([row_table] + addends + after))
 
     def swap(value, bit):
         return lax.ppermute(value, "gx", [(index, index ^ bit) for index in range(grid_rows)])
@@ -517,8 +536,7 @@
             compiler_params=params,
             name="finish",
         )(
-            *kept_parts,
-            crossed[chunk],
+            *in_hbm(kept_parts + [crossed[chunk]]),
             jnp.asarray(order_tables()),
             deapod_first[None, :],
             deapod_second[:, None],

time: 196 us -> 244 us (1.24)
  the two profiles are of different devices: /device:TPU:26 before, /device:TPU:16 now
where the time goes in v7:
time: 244 us; the launch traced here: 242 us
  Pallas kernels  118 us (48%)
  local copies, waits for them, and re-layouts  84 us (34%)
  starting transfers between devices  29.6 us (12%)
  waiting for transfers between devices  9.82 us (4%)
    unnamed x66, local copies, waits for them, and re-layouts  81.1 us
    pallas_call x5, Pallas kernels, rows_for(): pl.pallas_call(body, in_specs=[smem] + [vmem] * (3 + len(addends)) + [pl....  43.5 us
    pallas_call x5, Pallas kernels, add_tiles(): pl.pallas_call(functools.partial(tiles_kernel, conditions, not acc), out_...  34.4 us
    pallas_call x1, Pallas kernels, on_device(): pl.pallas_call(columns_kernel, out_shape=[jax.ShapeDtypeStruct(acc_shape,...  27.7 us
    ppermute x13, starting transfers between devices, shift(): return lax.ppermute(value, 'gy', moves)  27.1 us
    pallas_call x2, Pallas kernels, on_device(): pl.pallas_call(finish, grid=(1,), out_shape=jax.ShapeDtypeStruct((2, plan...  7.68 us
    ppermute x13, waiting for transfers between devices, shift(): return lax.ppermute(value, 'gy', moves)  5.71 us
    pallas_call x1, Pallas kernels, on_device(): pl.pallas_call(functools.partial(spread_kernel, tile_rows, tile_cols, gri...  5.02 us
  transfers between devices with their start and end apart: 17, of which 2 were waited for; matrix products, arithmetic and copies ran while one was open for 1% of the time, Pallas kernels for 28%

profile of v7, /device:TPU:16, one launch (start us, length us, event | category | flops | bytes accessed | tf_op | source)
XLA Modules:
  0.0 242.0 jit_solution(5230044889632779748)
XLA Ops:
  4.3 5.0 %spread.1.refs_1_ = f32[65,16,128]{2,1,0:T(8,128)} custom-call(f32[128,2,128]{2,1,0:T(2,128)S(1)} %copy-done.14, f32[128,3,4,128]{3,2,1,0:T(4,128)S(1)} %copy-done.12, s32[3,128,128]{2,1,0:T(8,128)S(1)} %bitcast.11, s32[1,128]{1,0:T(1,128)S(1)} %bitcast.14, s32[1,128]{1,0:T(1,128)S(1)} %bitcast.15), custom_call_target="tpu_custom_call" | custom-call | tf_op jit(solution)/shard_map/spread/pallas_call | solution.py:371
  19.6 6.6 %tiles.5 = (f32[36864,128]{1,0:T(8,128)S(1)}, f32[36864,128]{1,0:T(8,128)S(1)}, f32[8,128]{1,0:T(8,128)}) custom-call(s32[1]{0:T(128)} %bitcast.1.refs_0_, f32[65,16,128]{2,1,0:T(8,128)} %spread.1.refs_1_, bf16[48,128]{1,0:T(8,128)(2,1)} %dynamic-slice_bitcast_fusion.1.refs_2_.refs_4_.refs_5_.refs_3_, ...), custom_call_target="tpu_custom_call" | custom-call | bytes 8388608 | tf_op jit(solution)/shard_map/tiles/pallas_call | solution.py:416
  37.6 9.7 %tiles.6 = (f32[36864,128]{1,0:T(8,128)S(1)}, f32[36864,128]{1,0:T(8,128)S(1)}, f32[8,128]{1,0:T(8,128)}) custom-call(s32[1]{0:T(128)} %bitcast.1.refs_0_, f32[65,16,128]{2,1,0:T(8,128)} %collective-permute-done.2.refs_1_, f32[65,16,128]{2,1,0:T(8,128)} %copy-done.30, f32[65,16,128]{2,1,0:T(8,128)} %copy-done.31, ...), custom_call_target="tpu_custom_call", output_to_operand_aliasing={{0}: (6, {}), {1}: (7, {})} | custom-call | bytes 25165824 | tf_op jit(solution)/shard_map/tiles/pallas_call | solution.py:416
  53.6 5.7 %collective-permute-done.7.refs_4_ = f32[65,16,128]{2,1,0:T(8,128)S(1)} collective-permute-done((f32[65,16,128]{2,1,0:T(8,128)}, f32[65,16,128]{2,1,0:T(8,128)S(1)}, u32[]{:S(2)}, u32[]{:S(2)}) %collective-permute-start.7) | collective-permute-done | bytes 532512 | tf_op jit(solution)/shard_map/ppermute | solution.py:387
  60.1 10.0 %tiles.7 = (f32[36864,128]{1,0:T(8,128)S(1)}, f32[36864,128]{1,0:T(8,128)S(1)}, f32[8,128]{1,0:T(8,128)}) custom-call(s32[1]{0:T(128)} %bitcast.1.refs_0_, f32[65,16,128]{2,1,0:T(8,128)} %copy-done.23, f32[65,16,128]{2,1,0:T(8,128)} %copy-done.22, f32[65,16,128]{2,1,0:T(8,128)} %copy-done.27, ...), custom_call_target="tpu_custom_call", output_to_operand_aliasing={{0}: (7, {}), {1}: (8, {})} | custom-call | bytes 33554432 | tf_op jit(solution)/shard_map/tiles/pallas_call | solution.py:416
  70.1 6.5 %copy-done = f32[36864,128]{1,0:T(8,128)} copy-done((f32[36864,128]{1,0:T(8,128)}, f32[36864,128]{1,0:T(8,128)S(1)}, u32[]{:S(2)}) %copy-start) | copy-done | bytes 18874392
  76.6 6.5 %copy-done.6 = f32[36864,128]{1,0:T(8,128)} copy-done((f32[36864,128]{1,0:T(8,128)}, f32[36864,128]{1,0:T(8,128)S(1)}, u32[]{:S(2)}) %copy-start.6) | copy-done | bytes 18874392
  87.0 6.4 %copy-done.1 = f32[36864,128]{1,0:T(8,128)S(1)} copy-done((f32[36864,128]{1,0:T(8,128)S(1)}, f32[36864,128]{1,0:T(8,128)}, u32[]{:S(2)}) %copy-start.1) | copy-done | bytes 18874392
  93.4 6.4 %copy-done.7 = f32[36864,128]{1,0:T(8,128)S(1)} copy-done((f32[36864,128]{1,0:T(8,128)S(1)}, f32[36864,128]{1,0:T(8,128)}, u32[]{:S(2)}) %copy-start.7) | copy-done | bytes 18874392
  99.8 5.3 %tiles.8 = (f32[36864,128]{1,0:T(8,128)S(1)}, f32[36864,128]{1,0:T(8,128)S(1)}, f32[8,128]{1,0:T(8,128)}) custom-call(s32[1]{0:T(128)} %bitcast.1.refs_0_, f32[65,16,128]{2,1,0:T(8,128)} %copy-done.25, f32[65,16,128]{2,1,0:T(8,128)} %copy-done.24, f32[65,16,128]{2,1,0:T(8,128)} %copy-done.26, ...), custom_call_target="tpu_custom_call", output_to_operand_aliasing={{0}: (7, {}), {1}: (8, {})} | custom-call | bytes 33554432 | tf_op jit(solution)/shard_map/tiles/pallas_call | solution.py:416
  107.9 6.5 %copy-done.2 = f32[36864,128]{1,0:T(8,128)} copy-done((f32[36864,128]{1,0:T(8,128)}, f32[36864,128]{1,0:T(8,128)S(1)}, u32[]{:S(2)}) %copy-start.2) | copy-done | bytes 18874392
  114.3 6.4 %copy-done.3 = f32[36864,128]{1,0:T(8,128)S(1)} copy-done((f32[36864,128]{1,0:T(8,128)S(1)}, f32[36864,128]{1,0:T(8,128)}, u32[]{:S(2)}) %copy-start.3) | copy-done | bytes 18874392
  120.7 27.7 %columns.1 = (f32[36864,128]{1,0:T(8,128)S(1)}, f32[36864,128]{1,0:T(8,128)S(1)}) custom-call(f32[36864,128]{1,0:T(8,128)S(1)} %copy-done.3, f32[36864,128]{1,0:T(8,128)S(1)} %get-tuple-element.44.high_in, bf16[3,256,256]{2,1,0:T(8,128)(2,1)} %constant.34.clone.column_ref), custom_call_target="tpu_custom_call", output_to_operand_aliasing={{0}: (0, {}), {1}: (1, {})} | custom-call | tf_op jit(solution)/shard_map/columns/pallas_call | solution.py:460
  148.4 6.5 %copy-done.8 = f32[36864,128]{1,0:T(8,128)} copy-done((f32[36864,128]{1,0:T(8,128)}, f32[36864,128]{1,0:T(8,128)S(1)}, u32[]{:S(2)}) %copy-start.8) | copy-done | bytes 18874392
  154.9 13.2 %copy-done.9 = f32[36864,128]{1,0:T(8,128)S(1)} copy-done((f32[36864,128]{1,0:T(8,128)S(1)}, f32[36864,128]{1,0:T(8,128)}, u32[]{:S(2)}) %copy-start.9) | copy-done | bytes 18874392
  168.0 10.1 %rows.5.refs_4_ = f32[24,3,48,128]{3,2,1,0:T(8,128)} custom-call(s32[1]{0:T(128)} %bitcast.refs_0_, f32[36864,128]{1,0:T(8,128)S(1)} %get-tuple-element.45.refs_1_, f32[36864,128]{1,0:T(8,128)S(1)} %copy-done.9, bf16[2,2,192,256]{3,2,1,0:T(8,128)(2,1)} %constant.35.clone.refs_3_), custom_call_target="tpu_custom_call" | custom-call | flops 1 | bytes 1 | tf_op jit(solution)/shard_map/rows/pallas_call | solution.py:480
  178.2 10.1 %rows.6.refs_5_ = f32[24,3,48,128]{3,2,1,0:T(8,128)} custom-call(s32[1]{0:T(128)} %bitcast.refs_0_, f32[36864,128]{1,0:T(8,128)S(1)} %get-tuple-element.45.refs_1_, f32[36864,128]{1,0:T(8,128)S(1)} %copy-done.9, bf16[2,2,192,256]{3,2,1,0:T(8,128)(2,1)} %constant.35.clone.refs_3_, f32[24,3,48,128]{3,2,1,0:T(8,128)} %rows.5.refs_4_), custom_call_target="tpu_custom_call" | custom-call | flops 1 | bytes 1 | tf_op jit(solution)/shard_map/rows/pallas_call | solution.py:480
  190.0 6.5 %rows.7.refs_5_ = f32[12,3,48,128]{3,2,1,0:T(8,128)} custom-call(s32[1]{0:T(128)} %bitcast.refs_0_, f32[36864,128]{1,0:T(8,128)S(1)} %get-tuple-element.45.refs_1_, f32[36864,128]{1,0:T(8,128)S(1)} %copy-done.9, bf16[2,2,192,256]{3,2,1,0:T(8,128)(2,1)} %constant.35.clone.refs_3_, f32[24,3,48,128]{3,2,1,0:T(8,128)} %copy-done.20, f32[24,3,48,128]{3,2,1,0:T(8,128)} %rows.6.refs_5_), custom_call_target="tpu_custom_call" | custom-call | flops 1 | bytes 1 | tf_op jit(solution)/shard_map/rows/pallas_call | solution.py:480
  197.9 6.5 %rows.8.refs_4_ = f32[12,3,48,128]{3,2,1,0:T(8,128)} custom-call(s32[1]{0:T(128)} %bitcast.refs_0_, f32[36864,128]{1,0:T(8,128)S(1)} %get-tuple-element.45.refs_1_, f32[36864,128]{1,0:T(8,128)S(1)} %copy-done.9, bf16[2,2,192,256]{3,2,1,0:T(8,128)(2,1)} %constant.35.clone.refs_3_, f32[24,3,48,128]{3,2,1,0:T(8,128)} %copy-done.20, f32[12,3,48,128]{3,2,1,0:T(8,128)} %rows.7.refs_5_), custom_call_target="tpu_custom_call" | custom-call | flops 1 | bytes 1 | tf_op jit(solution)/shard_map/rows/pallas_call | solution.py:480
  205.1 6.4 %copy-done.5 = f32[36864,128]{1,0:T(8,128)S(1)} copy-done((f32[36864,128]{1,0:T(8,128)S(1)}, f32[36864,128]{1,0:T(8,128)}, u32[]{:S(2)}) %copy-start.5) | copy-done | bytes 18874392
  211.5 6.4 %copy-done.10 = f32[36864,128]{1,0:T(8,128)S(1)} copy-done((f32[36864,128]{1,0:T(8,128)S(1)}, f32[36864,128]{1,0:T(8,128)}, u32[]{:S(2)}) %copy-start.10) | copy-done | bytes 18874392
  217.8 10.2 %rows.9.refs_0_ = f32[24,3,48,128]{3,2,1,0:T(8,128)} custom-call(s32[1]{0:T(128)} %bitcast.refs_0_, f32[36864,128]{1,0:T(8,128)S(1)} %copy-done.5, f32[36864,128]{1,0:T(8,128)S(1)} %copy-done.10, bf16[2,2,192,256]{3,2,1,0:T(8,128)(2,1)} %constant.35.clone.refs_3_, f32[12,3,48,128]{3,2,1,0:T(8,128)} %rows.8.refs_4_), custom_call_target="tpu_custom_call" | custom-call | flops 1 | bytes 1 | tf_op jit(solution)/shard_map/rows/pallas_call | solution.py:480
  229.3 3.8 %finish.2.refs_7_ = f32[2,24,48,192]{3,2,1,0:T(8,128)} custom-call(f32[24,3,48,128]{3,2,1,0:T(8,128)} %rows.9.refs_0_, f32[24,3,48,128]{3,2,1,0:T(8,128)} %copy-done.19, f32[12,3,48,128]{3,2,1,0:T(8,128)} %collective-permute-done.16.refs_2_, bf16[512,192]{1,0:T(8,128)(2,1)S(1)} %copy-done.11, f32[1,192]{1,0:T(1,128)S(1)} %bitcast.12, ...), custom_call_target="tpu_custom_call" | custom-call | tf_op jit(solution)/shard_map/finish/pallas_call | solution.py:521
  233.1 4.1 %collective-permute-done.15.refs_2_ = f32[12,3,48,128]{3,2,1,0:T(8,128)S(1)} collective-permute-done((f32[12,3,48,128]{3,2,1,0:T(8,128)}, f32[12,3,48,128]{3,2,1,0:T(8,128)S(1)}, u32[]{:S(2)}, u32[]{:S(2)}) %collective-permute-start.15) | collective-permute-done | bytes 884768 | tf_op jit(solution)/shard_map/ppermute | solution.py:491
  (93 shorter events, 49.3 us)
Async XLA Ops:
  9.3 16.9 %collective-permute-start = (f32[65,16,128]{2,1,0:T(8,128)}, f32[65,16,128]{2,1,0:T(8,128)S(1)}, u32[]{:S(2)}, u32[]{:S(2)}) collective-permute-start(f32[65,16,128]{2,1,0:T(8,128)} %spread.1.refs_1_), channel_id=1, source_target_pairs={{2,0},{3,1},{4,2},{5,3},{6,4},{7,5},{10,8},{11,9},{12,10},{13,11},... | collective-permute-start | bytes 1597448 | tf_op jit(solution)/shard_map/ppermute | solution.py:387
  11.7 16.9 %collective-permute-start.2 = (f32[65,16,128]{2,1,0:T(8,128)}, f32[65,16,128]{2,1,0:T(8,128)}, u32[]{:S(2)}, u32[]{:S(2)}) collective-permute-start(f32[65,16,128]{2,1,0:T(8,128)} %spread.1.refs_1_), channel_id=1, source_target_pairs={{0,2},{1,3},{2,4},{3,5},{4,6},{5,7},{8,10},{9,11},{10,12},{11,13},... | collective-permute-start | bytes 1597448 | tf_op jit(solution)/shard_map/ppermute | solution.py:387
  15.2 21.6 %collective-permute-start.3 = (f32[65,16,128]{2,1,0:T(8,128)}, f32[65,16,128]{2,1,0:T(8,128)S(1)}, u32[]{:S(2)}, u32[]{:S(2)}) collective-permute-start(f32[65,16,128]{2,1,0:T(8,128)} %spread.1.refs_1_), channel_id=1, source_target_pairs={{0,1},{1,0},{2,3},{3,2},{4,5},{5,4},{6,7},{7,6},{8,9},{9,8},{10,11... | collective-permute-start | bytes 1597448 | tf_op jit(solution)/shard_map/ppermute | solution.py:387
  26.2 21.2 %collective-permute-start.1 = (f32[65,16,128]{2,1,0:T(8,128)S(1)}, f32[65,16,128]{2,1,0:T(8,128)S(1)}, u32[]{:S(2)}, u32[]{:S(2)}) collective-permute-start(f32[65,16,128]{2,1,0:T(8,128)S(1)} %collective-permute-done.refs_2_), channel_id=1, source_target_pairs={{2,0},{3,1},{4,2},{5,3},{10,8},{11,9},{12,10},{13,11},{18,16},{19,... | collective-permute-start | bytes 1597448 | tf_op jit(solution)/shard_map/ppermute | solution.py:387
  28.6 19.5 %collective-permute-start.5 = (f32[65,16,128]{2,1,0:T(8,128)}, f32[65,16,128]{2,1,0:T(8,128)S(1)}, u32[]{:S(2)}, u32[]{:S(2)}) collective-permute-start(f32[65,16,128]{2,1,0:T(8,128)} %collective-permute-done.2.refs_1_), channel_id=1, source_target_pairs={{2,4},{3,5},{4,6},{5,7},{10,12},{11,13},{12,14},{13,15},{18,20},{1... | collective-permute-start | bytes 1597448 | tf_op jit(solution)/shard_map/ppermute | solution.py:387
  30.9 19.2 %collective-permute-start.6 = (f32[65,16,128]{2,1,0:T(8,128)S(1)}, f32[65,16,128]{2,1,0:T(8,128)S(1)}, u32[]{:S(2)}, u32[]{:S(2)}) collective-permute-start(f32[65,16,128]{2,1,0:T(8,128)S(1)} %collective-permute-done.refs_2_), channel_id=1, source_target_pairs={{0,1},{1,0},{2,3},{3,2},{4,5},{5,4},{8,9},{9,8},{10,11},{11,10},{1... | collective-permute-start | bytes 1597448 | tf_op jit(solution)/shard_map/ppermute | solution.py:387
  34.4 24.9 %collective-permute-start.7 = (f32[65,16,128]{2,1,0:T(8,128)}, f32[65,16,128]{2,1,0:T(8,128)S(1)}, u32[]{:S(2)}, u32[]{:S(2)}) collective-permute-start(f32[65,16,128]{2,1,0:T(8,128)} %collective-permute-done.2.refs_1_), channel_id=1, source_target_pairs={{2,3},{3,2},{4,5},{5,4},{6,7},{7,6},{10,11},{11,10},{12,13},{13,12... | collective-permute-start | bytes 1597448 | tf_op jit(solution)/shard_map/ppermute | solution.py:387
  47.4 11.9 %copy-start.22 = (f32[65,16,128]{2,1,0:T(8,128)}, f32[65,16,128]{2,1,0:T(8,128)S(1)}, u32[]{:S(2)}) copy-start(f32[65,16,128]{2,1,0:T(8,128)S(1)} %collective-permute-done.1.refs_2_) | copy-start | bytes 1597444
  47.4 35.7 %collective-permute-start.4 = (f32[65,16,128]{2,1,0:T(8,128)S(1)}, f32[65,16,128]{2,1,0:T(8,128)S(1)}, u32[]{:S(2)}, u32[]{:S(2)}) collective-permute-start(f32[65,16,128]{2,1,0:T(8,128)S(1)} %collective-permute-done.1.refs_2_), channel_id=1, source_target_pairs={{2,0},{3,1},{10,8},{11,9},{18,16},{19,17},{26,24},{27,25}} | collective-permute-start | bytes 1597448 | tf_op jit(solution)/shard_map/ppermute | solution.py:387
  48.1 11.2 %copy-start.23 = (f32[65,16,128]{2,1,0:T(8,128)}, f32[65,16,128]{2,1,0:T(8,128)S(1)}, u32[]{:S(2)}) copy-start(f32[65,16,128]{2,1,0:T(8,128)S(1)} %collective-permute-done.5.refs_1_) | copy-start | bytes 1597444
  48.1 36.5 %collective-permute-start.9 = (f32[65,16,128]{2,1,0:T(8,128)S(1)}, f32[65,16,128]{2,1,0:T(8,128)S(1)}, u32[]{:S(2)}, u32[]{:S(2)}) collective-permute-start(f32[65,16,128]{2,1,0:T(8,128)S(1)} %collective-permute-done.5.refs_1_), channel_id=1, source_target_pairs={{4,6},{5,7},{12,14},{13,15},{20,22},{21,23},{28,30},{29,31}} | collective-permute-start | bytes 1597448 | tf_op jit(solution)/shard_map/ppermute | solution.py:387
  49.4 36.6 %collective-permute-start.11 = (f32[65,16,128]{2,1,0:T(8,128)S(1)}, f32[65,16,128]{2,1,0:T(8,128)S(1)}, u32[]{:S(2)}, u32[]{:S(2)}) collective-permute-start(f32[65,16,128]{2,1,0:T(8,128)S(1)} %collective-permute-done.1.refs_2_), channel_id=1, source_target_pairs={{0,1},{1,0},{2,3},{3,2},{8,9},{9,8},{10,11},{11,10},{16,17},{17,16... | collective-permute-start | bytes 1597448 | tf_op jit(solution)/shard_map/ppermute | solution.py:387
  50.2 35.9 %collective-permute-start.12 = (f32[65,16,128]{2,1,0:T(8,128)S(1)}, f32[65,16,128]{2,1,0:T(8,128)S(1)}, u32[]{:S(2)}, u32[]{:S(2)}) collective-permute-start(f32[65,16,128]{2,1,0:T(8,128)S(1)} %collective-permute-done.5.refs_1_), channel_id=1, source_target_pairs={{4,5},{5,4},{6,7},{7,6},{12,13},{13,12},{14,15},{15,14},{20,21},{2... | collective-permute-start | bytes 1597448 | tf_op jit(solution)/shard_map/ppermute | solution.py:387
  83.1 22.0 %collective-permute-start.8 = (f32[65,16,128]{2,1,0:T(8,128)S(1)}, f32[65,16,128]{2,1,0:T(8,128)}, u32[]{:S(2)}, u32[]{:S(2)}) collective-permute-start(f32[65,16,128]{2,1,0:T(8,128)S(1)} %collective-permute-done.4.refs_2_), channel_id=1, source_target_pairs={{0,1},{1,0},{8,9},{9,8},{16,17},{17,16},{24,25},{25,24}} | collective-permute-start | bytes 1597448 | tf_op jit(solution)/shard_map/ppermute | solution.py:387
  84.6 20.5 %collective-permute-start.10 = (f32[65,16,128]{2,1,0:T(8,128)S(1)}, f32[65,16,128]{2,1,0:T(8,128)}, u32[]{:S(2)}, u32[]{:S(2)}) collective-permute-start(f32[65,16,128]{2,1,0:T(8,128)S(1)} %collective-permute-done.9.refs_1_), channel_id=1, source_target_pairs={{6,7},{7,6},{14,15},{15,14},{22,23},{23,22},{30,31},{31,30}} | collective-permute-start | bytes 1597448 | tf_op jit(solution)/shard_map/ppermute | solution.py:387
  154.8 43.1 %copy-start.4 = (f32[36864,128]{1,0:T(8,128)}, f32[36864,128]{1,0:T(8,128)S(1)}, u32[]{:S(2)}) copy-start(f32[36864,128]{1,0:T(8,128)S(1)} %get-tuple-element.45.refs_1_) | copy-start | bytes 56623108
  154.8 13.2 %copy-start.9 = (f32[36864,128]{1,0:T(8,128)S(1)}, f32[36864,128]{1,0:T(8,128)}, u32[]{:S(2)}) copy-start(f32[36864,128]{1,0:T(8,128)} %copy-done.8) | copy-start | bytes 56623108
  178.2 10.6 %collective-permute-start.13 = (f32[24,3,48,128]{3,2,1,0:T(8,128)}, f32[24,3,48,128]{3,2,1,0:T(8,128)S(1)}, u32[]{:S(2)}, u32[]{:S(2)}) collective-permute-start(f32[24,3,48,128]{3,2,1,0:T(8,128)} %rows.5.refs_4_), channel_id=1, source_target_pairs={{0,8},{8,0},{16,24},{24,16},{1,9},{9,1},{17,25},{25,17},{2,10},{10... | collective-permute-start | bytes 5308424 | tf_op jit(solution)/shard_map/ppermute | solution.py:491
  188.3 39.8 %collective-permute-start.14 = (f32[24,3,48,128]{3,2,1,0:T(8,128)}, f32[24,3,48,128]{3,2,1,0:T(8,128)S(1)}, u32[]{:S(2)}, u32[]{:S(2)}) collective-permute-start(f32[24,3,48,128]{3,2,1,0:T(8,128)} %rows.6.refs_5_), channel_id=1, source_target_pairs={{0,8},{8,0},{16,24},{24,16},{1,9},{9,1},{17,25},{25,17},{2,10},{10... | collective-permute-start | bytes 5308424 | tf_op jit(solution)/shard_map/ppermute | solution.py:491
  196.4 31.6 %collective-permute-start.16 = (f32[12,3,48,128]{3,2,1,0:T(8,128)}, f32[12,3,48,128]{3,2,1,0:T(8,128)}, u32[]{:S(2)}, u32[]{:S(2)}) collective-permute-start(f32[12,3,48,128]{3,2,1,0:T(8,128)} %rows.7.refs_5_), channel_id=1, source_target_pairs={{0,16},{8,24},{16,0},{24,8},{1,17},{9,25},{17,1},{25,9},{2,18},{10... | collective-permute-start | bytes 2654216 | tf_op jit(solution)/shard_map/ppermute | solution.py:491
  204.5 32.7 %collective-permute-start.15 = (f32[12,3,48,128]{3,2,1,0:T(8,128)}, f32[12,3,48,128]{3,2,1,0:T(8,128)S(1)}, u32[]{:S(2)}, u32[]{:S(2)}) collective-permute-start(f32[12,3,48,128]{3,2,1,0:T(8,128)} %rows.8.refs_4_), channel_id=1, source_target_pairs={{0,16},{8,24},{16,0},{24,8},{1,17},{9,25},{17,1},{25,9},{2,18},{10... | collective-permute-start | bytes 2654216 | tf_op jit(solution)/shard_map/ppermute | solution.py:491
  217.8 11.4 %copy-start.11 = (bf16[512,192]{1,0:T(8,128)(2,1)S(1)}, bf16[512,192]{1,0:T(8,128)(2,1)}, u32[]{:S(2)}) copy-start(bf16[512,192]{1,0:T(8,128)(2,1)} %constant.36.clone.refs_3_) | copy-start | bytes 589828
  217.8 11.4 %copy-start.15 = (f32[192]{0:T(256)S(1)}, f32[192]{0:T(256)}, u32[]{:S(2)}) copy-start(f32[192]{0:T(256)} %param.19) | copy-start | bytes 2308
  217.8 11.4 %copy-start.16 = (f32[24]{0:T(128)S(1)}, f32[24]{0:T(128)}, u32[]{:S(2)}) copy-start(f32[24]{0:T(128)} %refs_6_.3) | copy-start | bytes 292
  (26 other events, 101.6 us)

commit v8 on v7

--- a/solution.py
+++ b/solution.py
@@ -18,6 +18,9 @@
 PLANES = 32
 CHUNK = 24
 Z_CHIPS = 4
+PARTS = 4
+CELLS = TILE // PARTS
+STRIDE = NY + TILE
 PHASES = 128
 BF16 = jnp.bfloat16
 F32 = jnp.float32
@@ -68,13 +71,13 @@
     for residue in range(3):
         cos, sin = waves(3 * np.arange(NY // 6) + residue - NY // 4, np.arange(third) - NY // 2, NY)
         high, low = halves(np.concatenate((cos, sin)) / math.sqrt(NY))
-        out.append(np.block([[high, high], [low, np.zeros_like(low)]]))
+        out.append(np.concatenate((high, high, low), axis=1))
     return np.stack(out)
 
 
 def row_tables():
     half = NX // 2
-    freq = np.arange(half).reshape(-1, 2, TILE // 2).transpose(1, 0, 2).reshape(-1) - half
+    freq = np.arange(half).reshape(-1, PARTS, CELLS).transpose(1, 0, 2).reshape(-1) - half
     quarter = NX // 4
     out = []
     for parity in range(2):
@@ -121,7 +124,7 @@
     col = (owner - owner_row * grid_cols) * tile_cols + tile_col - tile_row * tile_cols
     folds = NX // TILE // 2
     upper = (row >= folds).astype(jnp.int32)
-    base = (row - upper * folds) * (NY // 2) + col
+    base = (row - upper * folds) * (CELLS * STRIDE // TILE) + col
     phase = tile_id - tile_col * tile_depth + upper * tile_depth
     codes = (base * PHASES + phase).astype(F32)
 
@@ -165,9 +168,10 @@
     deep_ref = refs[0]
     source_refs = refs[1 : 1 + arrays]
     depth_ref, phases_ref = refs[1 + arrays : 3 + arrays]
-    low_ref, high_ref, token_ref, codes_ref, even_ref, odd_ref, arrived = refs[-7:]
+    acc_refs = refs[-5 - PARTS : -5]
+    token_ref, codes_ref, even_ref, odd_ref, arrived = refs[-5:]
     token_ref[...] = jnp.zeros_like(token_ref)
-    stride = NY
+    stride = STRIDE
     pairs = source_refs[0].shape[0] - 1
     batch = 8
     batches = pairs // batch
@@ -185,11 +189,11 @@
 
         def clear(step, carry):
             at = pl.ds(pl.multiple_of(step * stride, stride), stride)
-            low_ref[at, :] = jnp.zeros((stride, LANES), F32)
-            high_ref[at, :] = jnp.zeros((stride, LANES), F32)
+            for ref in acc_refs:
+                ref[at, :] = jnp.zeros((stride, LANES), F32)
             return carry
 
-        lax.fori_loop(0, NX // 4, clear, 0)
+        lax.fori_loop(0, NX // 2 // PARTS, clear, 0)
 
     for index in range(arrays):
         copies(index).wait()
@@ -218,8 +222,8 @@
                     row = tile * TILE * TILE + i * TILE
                     value = from_ref[row : row + TILE, :]
                     value = value * cos + pltpu.roll(value, LANES // 2, 1) * sin
-                    acc_ref = high_ref if i >= TILE // 2 else low_ref
-                    at = pl.ds(pl.multiple_of(base * TILE + i % (TILE // 2) * stride, TILE), TILE)
+                    acc_ref = acc_refs[i // CELLS]
+                    at = pl.ds(pl.multiple_of(base * TILE + i % CELLS * stride, TILE), TILE)
                     acc_ref[at, :] = acc_ref[at, :] + value
 
         spectrum(0, even_ref)
@@ -243,40 +247,43 @@
             pl.when(holds)(functools.partial(add_source, index))
 
 
-def columns_kernel(low_in, high_in, column_ref, low_ref, high_ref):
-    del low_in, high_in
-    stride = NY
+def columns_kernel(*refs):
+    column_ref = refs[PARTS]
+    acc_refs = refs[PARTS + 1 :]
     third = NY // 3
-    rows = column_ref.shape[1] // 4
+    rows = column_ref.shape[1] // 2
     turn = jnp.where(lax.broadcasted_iota(jnp.int32, (1, LANES), 1) < LANES // 2, -1.0, 1.0)
 
     def columns(step, carry):
-        start = pl.multiple_of(step * stride, stride)
-        folded = ([], [], [])
-        for ref in (low_ref, high_ref):
-            first, second, last = (ref[pl.ds(start + third * part, third), :] for part in range(3))
-            both = second + last
-            across = pltpu.roll(second - last, LANES // 2, 1) * (turn * math.sqrt(0.75))
-            middle = first - 0.5 * both
-            folded[0].append(first + both)
-            folded[1].append(middle + across)
-            folded[2].append(middle - across)
-        for residue in range(3):
-            high_low = split(jnp.concatenate(folded[residue], axis=1))
-            product = jnp.dot(column_ref[residue], jnp.concatenate(high_low, axis=0), preferred_element_type=F32)
-            product = product[: 2 * rows] + product[2 * rows :]
-            for side, ref in enumerate((low_ref, high_ref)):
-                lanes = slice(side * LANES, (side + 1) * LANES)
-                ref[pl.ds(start + residue * rows, rows), :] = (
-                    product[:rows, lanes] + pltpu.roll(product[rows:, lanes], LANES // 2, 1) * turn
+        start = pl.multiple_of(step * STRIDE, TILE)
+        for pair in range(0, PARTS, 2):
+            folded = ([], [], [])
+            for ref in acc_refs[pair : pair + 2]:
+                first, second, last = (ref[pl.ds(start + third * part, third), :] for part in range(3))
+                both = second + last
+                across = pltpu.roll(second - last, LANES // 2, 1) * (turn * math.sqrt(0.75))
+                middle = first - 0.5 * both
+                folded[0].append(first + both)
+                folded[1].append(middle + across)
+                folded[2].append(middle - across)
+            for residue in range(3):
+                high, low = split(jnp.concatenate(folded[residue], axis=1))
+                product = jnp.dot(
+                    column_ref[residue], jnp.concatenate((high, low, high), axis=0), preferred_element_type=F32
                 )
+                for side, ref in enumerate(acc_refs[pair : pair + 2]):
+                    lanes = slice(side * LANES, (side + 1) * LANES)
+                    ref[pl.ds(start + residue * rows, rows), :] = (
+                        product[:rows, lanes] + pltpu.roll(product[rows:, lanes], LANES // 2, 1) * turn
+                    )
         return carry
 
-    lax.fori_loop(0, NX // 4, columns, 0, unroll=2)
-
-
-def rows_kernel(relative, first, count, chunks, grid_rows, addends, planes_padded, place_ref, low_ref, high_ref, row_ref, *refs):
-    out_ref = refs[-1]
+    lax.fori_loop(0, NX // 2 // PARTS, columns, 0)
+
+
+def rows_kernel(relative, first, count, chunks, grid_rows, addends, planes_padded, place_ref, *refs):
+    acc_refs, row_ref, addend_refs, out_ref = refs[:PARTS], refs[PARTS], refs[PARTS + 1 : -1], refs[-1]
+    assert len(addend_refs) == addends
     rows = grid_rows * chunks * TILE
     device = jnp.bitwise_xor(place_ref[0], relative)
     lane = lax.broadcasted_iota(jnp.int32, (PLANES, LANES), 1)
@@ -286,8 +293,8 @@
         start = residue * rows + (device * chunks + first + chunk) * TILE
         turned = []
         for row in range(TILE):
-            at = pl.ds(start + row, NX // 4, stride=NY)
-            turned.append(jnp.concatenate((low_ref[at, :], high_ref[at, :]), axis=0).T)
+            at = pl.ds(start + row, NX // 2 // PARTS, stride=STRIDE)
+            turned.append(jnp.concatenate([ref[at, :] for ref in acc_refs], axis=0).T)
         parts = []
         for odd in range(2):
             at = odd * PLANES
@@ -312,7 +319,7 @@
                 for number, value in enumerate(values):
                     planes = pl.ds(part * planes_padded, planes_padded)
                     total = value[:planes_padded]
-                    for ref in refs[:addends]:
+                    for ref in addend_refs:
                         total = total + ref[first * (CHUNK // 2) + place, number, planes]
                     out_ref[place, number, planes] = total
         return carry
@@ -320,7 +327,7 @@
     lax.fori_loop(0, 3 * count, block, 0)
 
 
-def finish_kernel(planes_padded, parts, refs):
+def finish_kernel(chunk, planes_padded, parts, refs):
     part_refs = refs[:parts]
     order_ref, first_ref, second_ref, third_ref = refs[parts : parts + 4]
     out_ref = refs[-1]
@@ -329,7 +336,10 @@
     stride = 6 * planes_padded
     flats = [ref.reshape(slots * stride, LANES) for ref in part_refs]
     order = order_ref[...]
-    scale = second_ref[...] * first_ref[...]
+    shape = (CHUNK, second_ref.shape[1])
+    here = lax.broadcasted_iota(jnp.int32, shape, 1) == lax.broadcasted_iota(jnp.int32, shape, 0) + chunk * CHUNK
+    second = jnp.sum(jnp.where(here, second_ref[...], 0.0), axis=1, keepdims=True)
+    scale = second * first_ref[...]
     for part in range(2):
         for group in range(0, planes, TILE):
             members = range(group, min(group + TILE, planes))
@@ -368,6 +378,9 @@
     vmem = pl.BlockSpec(memory_space=pltpu.VMEM)
     params = pltpu.CompilerParams(vmem_limit_bytes=VMEM_LIMIT)
 
+    def in_hbm(arrays):
+        return [pltpu.with_memory_space_constraint(array, pltpu.HBM) for array in arrays]
+
     tiles = pl.pallas_call(
         functools.partial(spread_kernel, tile_rows, tile_cols, grid_cols, grid_rows * grid_cols),
         out_shape=pltpu.HBM((blocks // 2 + 1, 2 * TILE, LANES), F32),
@@ -375,7 +388,7 @@
         out_specs=vmem,
         compiler_params=params,
         name="spread",
-    )(samples, kernel, offsets.transpose(1, 0, 2), owners.reshape(1, blocks), tile_ids.reshape(1, blocks))
+    )(*in_hbm([samples, kernel, offsets.transpose(1, 0, 2), owners.reshape(1, blocks), tile_ids.reshape(1, blocks)]))
 
     along = grid_cols // Z_CHIPS
     deep_at = lax.div(lax.axis_index("gy").astype(jnp.int32), jnp.int32(along))
@@ -395,13 +408,10 @@
     column = jnp.asarray(column_tables())
     half = NX // 2
     smem = pl.BlockSpec(memory_space=pltpu.SMEM)
-    acc_shape = (half // 2 * NY, LANES)
+    acc_shape = (half // PARTS * STRIDE, LANES)
 
     def in_vmem(arrays):
         return [pltpu.with_memory_space_constraint(array, pltpu.VMEM) for array in arrays]
-
-    def in_hbm(arrays):
-        return [pltpu.with_memory_space_constraint(array, pltpu.HBM) for array in arrays]
 
     def condition(steps):
         if steps == 0:
@@ -411,14 +421,14 @@
     def add_tiles(sources, acc):
         conditions = [condition(steps) for steps, _ in sources]
         spectra = pltpu.VMEM((16 * TILE * TILE, LANES), F32)
-        kept = [jax.ShapeDtypeStruct(acc_shape, F32)] * 2 if acc else [pltpu.VMEM(acc_shape, F32)] * 2
+        kept = [jax.ShapeDtypeStruct(acc_shape, F32) if acc else pltpu.VMEM(acc_shape, F32)] * PARTS
         inputs = len(sources) + 3
         *acc, token = pl.pallas_call(
             functools.partial(tiles_kernel, conditions, not acc),
             out_shape=kept + [jax.ShapeDtypeStruct((TILE, LANES), F32)],
             in_specs=[smem] + [vmem] * (inputs - 1 + len(acc)),
-            out_specs=[vmem] * 3,
-            input_output_aliases={inputs: 0, inputs + 1: 1} if acc else {},
+            out_specs=[vmem] * (PARTS + 1),
+            input_output_aliases={inputs + part: part for part in range(PARTS)} if acc else {},
             scratch_shapes=[
                 pltpu.SMEM((len(sources), TILE, LANES), F32),
                 spectra,
@@ -459,10 +469,10 @@
 
     acc = pl.pallas_call(
         columns_kernel,
-        out_shape=[jax.ShapeDtypeStruct(acc_shape, F32)] * 2,
-        in_specs=[vmem] * 3,
-        out_specs=[vmem] * 2,
-        input_output_aliases={0: 0, 1: 1},
+        out_shape=[jax.ShapeDtypeStruct(acc_shape, F32)] * PARTS,
+        in_specs=[vmem] * (PARTS + 1),
+        out_specs=[vmem] * PARTS,
+        input_output_aliases={part: part for part in range(PARTS)},
         compiler_params=params,
         name="columns",
     )(*in_vmem(acc), *in_hbm([column]))
@@ -472,14 +482,14 @@
 
     def rows_for(relative, first, count, addends, after):
         def body(*refs):
-            operands = 4 + len(addends)
+            operands = 2 + PARTS + len(addends)
             rows_kernel(
                 relative, first, count, chunks, grid_rows, len(addends), planes_padded, *refs[:operands], refs[-1]
             )
 
         return pl.pallas_call(
             body,
-            in_specs=[smem] + [vmem] * (3 + len(addends)) + [pl.BlockSpec(memory_space=pl.ANY)] * len(after),
+            in_specs=[smem] + [vmem] * (1 + PARTS + len(addends)) + [pl.BlockSpec(memory_space=pl.ANY)] * len(after),
             out_specs=vmem,
             out_shape=pltpu.HBM((count * slots,) + part_shape, F32),
             compiler_params=params,
@@ -514,8 +524,8 @@
     image = None
     for chunk in range(chunks):
 
-        def finish(*refs):
-            finish_kernel(planes_padded, len(kept_parts) + 1, refs)
+        def finish(*refs, chunk=chunk):
+            finish_kernel(chunk, planes_padded, len(kept_parts) + 1, refs)
 
         earlier = [] if image is None else [image]
         image = pl.pallas_call(
@@ -527,7 +537,7 @@
                 pl.BlockSpec((slots,) + part_shape, lambda step: (0, 0, 0, 0)),
                 pl.BlockSpec((4 * LANES, NX // 2), lambda step: (0, 0)),
                 pl.BlockSpec((1, NX // 2), lambda step: (0, 0)),
-                pl.BlockSpec((CHUNK, 1), lambda step, chunk=chunk: (chunk, 0)),
+                pl.BlockSpec((1, per_device), lambda step: (0, 0)),
                 pl.BlockSpec(memory_space=pltpu.SMEM),
             ]
             + [pl.BlockSpec(memory_space=pl.ANY)] * len(earlier),
@@ -539,7 +549,7 @@
             *in_hbm(kept_parts + [crossed[chunk]]),
             jnp.asarray(order_tables()),
             deapod_first[None, :],
-            deapod_second[:, None],
+            deapod_second[None, :],
             deapod_third,
             *earlier,
         )

time: 244 us -> 236 us (0.967)
  waiting for transfers between devices: 9.82 us -> 27.5 us
  local copies, waits for them, and re-layouts: 84 us -> 67.8 us
  Pallas kernels: 118 us -> 109 us
    ppermute x4, waiting for transfers between devices: 4.12 us -> 21.7 us  [swap(): lax.ppermute(value, 'gx', [(index, index ^ bit) for index in range(grid_r...]
    unnamed x66 -> x68, local copies, waits for them, and re-layouts: 81.1 us -> 64.9 us
    pallas_call x5, Pallas kernels: 43.5 us -> 31.4 us  [rows_for(): pl.pallas_call(body, in_specs=[smem] + [vmem] * (1 + PARTS + len(addends)...]
  transfers between devices with their start and end apart: 17 -> 17, of which waited for: 2 -> 3; matrix products, arithmetic and copies ran while one was open for 1% -> 1% of each run, Pallas kernels for 28% -> 25%
where the time goes in v8:
time: 236 us; the launch traced here: 234 us
  Pallas kernels  109 us (46%)
  local copies, waits for them, and re-layouts  67.8 us (29%)
  starting transfers between devices  29.7 us (13%)
  waiting for transfers between devices  27.5 us (12%)
    unnamed x68, local copies, waits for them, and re-layouts  64.9 us
    pallas_call x5, Pallas kernels, add_tiles(): pl.pallas_call(functools.partial(tiles_kernel, conditions, not acc), out_...  34.1 us
    pallas_call x5, Pallas kernels, rows_for(): pl.pallas_call(body, in_specs=[smem] + [vmem] * (1 + PARTS + len(addends)...  31.4 us
    pallas_call x1, Pallas kernels, on_device(): pl.pallas_call(columns_kernel, out_shape=[jax.ShapeDtypeStruct(acc_shape,...  29.2 us
    ppermute x13, starting transfers between devices, shift(): return lax.ppermute(value, 'gy', moves)  27.1 us
    ppermute x4, waiting for transfers between devices, swap(): lax.ppermute(value, 'gx', [(index, index ^ bit) for index in range(grid_r...  21.7 us
    pallas_call x2, Pallas kernels, on_device(): pl.pallas_call(finish, grid=(1,), out_shape=jax.ShapeDtypeStruct((2, plan...  7.68 us
    pallas_call x1, Pallas kernels, on_device(): pl.pallas_call(functools.partial(spread_kernel, tile_rows, tile_cols, gri...  6.24 us
  transfers between devices with their start and end apart: 17, of which 3 were waited for; matrix products, arithmetic and copies ran while one was open for 1% of the time, Pallas kernels for 25%

profile of v8, /device:TPU:16, one launch (start us, length us, event | category | flops | bytes accessed | tf_op | source)
XLA Modules:
  0.0 233.9 jit_solution(15974871677312576792)
XLA Ops:
  0.0 6.2 %spread.1.refs_1_ = f32[65,16,128]{2,1,0:T(8,128)} custom-call(f32[128,2,128]{2,1,0:T(2,128)} %samples_ref.1, f32[128,3,4,128]{3,2,1,0:T(4,128)} %kernel_ref.1, s32[3,128,128]{2,1,0:T(8,128)} %bitcast.15, s32[1,128]{1,0:T(1,128)} %bitcast.16, s32[1,128]{1,0:T(1,128)} %bitcast.17), custom_call_target="tpu_custom_call" | custom-call | tf_op jit(solution)/shard_map/spread/pallas_call | solution.py:384
  16.5 6.5 %tiles.5 = (f32[18816,128]{1,0:T(8,128)S(1)}, f32[18816,128]{1,0:T(8,128)S(1)}, f32[18816,128]{1,0:T(8,128)S(1)}, f32[18816,128]{1,0:T(8,128)S(1)}, f32[8,128]{1,0:T(8,128)}) custom-call(s32[1]{0:T(128)} %bitcast.1.refs_0_, f32[65,16,128]{2,1,0:T(8,128)} %spread.1.refs_1_, bf16[48,128]{1,0:T(8,128)(2,1)} %dynamic-slice_bitcast_fusion.1.refs_2_.refs_4_.refs_5_.refs_3_, ...), custom_call_target="tpu_custom_call" | custom-call | bytes 8388608 | tf_op jit(solution)/shard_map/tiles/pallas_call | solution.py:426
  34.5 9.6 %tiles.6 = (f32[18816,128]{1,0:T(8,128)S(1)}, f32[18816,128]{1,0:T(8,128)S(1)}, f32[18816,128]{1,0:T(8,128)S(1)}, f32[18816,128]{1,0:T(8,128)S(1)}, f32[8,128]{1,0:T(8,128)}) custom-call(s32[1]{0:T(128)} %bitcast.1.refs_0_, f32[65,16,128]{2,1,0:T(8,128)} %collective-permute-done.2.refs_1_, ...), custom_call_target="tpu_custom_call", output_to_operand_aliasing={{0}: (6, {}), {1}: (7, {}), {2}: (8, {}), {3}: (9, {})} | custom-call | bytes 25165824 | tf_op jit(solution)/shard_map/tiles/pallas_call | solution.py:426
  50.4 5.8 %collective-permute-done.7.refs_4_ = f32[65,16,128]{2,1,0:T(8,128)S(1)} collective-permute-done((f32[65,16,128]{2,1,0:T(8,128)}, f32[65,16,128]{2,1,0:T(8,128)S(1)}, u32[]{:S(2)}, u32[]{:S(2)}) %collective-permute-start.7) | collective-permute-done | bytes 532512 | tf_op jit(solution)/shard_map/ppermute | solution.py:400
  57.0 9.9 %tiles.7 = (f32[18816,128]{1,0:T(8,128)S(1)}, f32[18816,128]{1,0:T(8,128)S(1)}, f32[18816,128]{1,0:T(8,128)S(1)}, f32[18816,128]{1,0:T(8,128)S(1)}, f32[8,128]{1,0:T(8,128)}) custom-call(s32[1]{0:T(128)} %bitcast.1.refs_0_, f32[65,16,128]{2,1,0:T(8,128)} %copy-done.25, ...), custom_call_target="tpu_custom_call", output_to_operand_aliasing={{0}: (7, {}), {1}: (8, {}), {2}: (9, {}), {3}: (10, {})} | custom-call | bytes 33554432 | tf_op jit(solution)/shard_map/tiles/pallas_call | solution.py:426
  85.5 3.7 %copy-done.1 = f32[18816,128]{1,0:T(8,128)S(1)} copy-done((f32[18816,128]{1,0:T(8,128)S(1)}, f32[18816,128]{1,0:T(8,128)}, u32[]{:S(2)}) %copy-start.1) | copy-done | bytes 9633816
  89.3 3.7 %copy-done.5 = f32[18816,128]{1,0:T(8,128)S(1)} copy-done((f32[18816,128]{1,0:T(8,128)S(1)}, f32[18816,128]{1,0:T(8,128)}, u32[]{:S(2)}) %copy-start.5) | copy-done | bytes 9633816
  93.0 3.7 %copy-done.9 = f32[18816,128]{1,0:T(8,128)S(1)} copy-done((f32[18816,128]{1,0:T(8,128)S(1)}, f32[18816,128]{1,0:T(8,128)}, u32[]{:S(2)}) %copy-start.9) | copy-done | bytes 9633816
  96.8 3.7 %copy-done.13 = f32[18816,128]{1,0:T(8,128)S(1)} copy-done((f32[18816,128]{1,0:T(8,128)S(1)}, f32[18816,128]{1,0:T(8,128)}, u32[]{:S(2)}) %copy-start.13) | copy-done | bytes 9633816
  100.5 5.3 %tiles.8 = (f32[18816,128]{1,0:T(8,128)S(1)}, f32[18816,128]{1,0:T(8,128)S(1)}, f32[18816,128]{1,0:T(8,128)S(1)}, f32[18816,128]{1,0:T(8,128)S(1)}, f32[8,128]{1,0:T(8,128)}) custom-call(s32[1]{0:T(128)} %bitcast.1.refs_0_, f32[65,16,128]{2,1,0:T(8,128)} %copy-done.27, ...), custom_call_target="tpu_custom_call", output_to_operand_aliasing={{0}: (7, {}), {1}: (8, {}), {2}: (9, {}), {3}: (10, {})} | custom-call | bytes 33554432 | tf_op jit(solution)/shard_map/tiles/pallas_call | solution.py:426
  119.5 3.7 %copy-done.3 = f32[18816,128]{1,0:T(8,128)S(1)} copy-done((f32[18816,128]{1,0:T(8,128)S(1)}, f32[18816,128]{1,0:T(8,128)}, u32[]{:S(2)}) %copy-start.3) | copy-done | bytes 9633816
  123.3 3.7 %copy-done.7 = f32[18816,128]{1,0:T(8,128)S(1)} copy-done((f32[18816,128]{1,0:T(8,128)S(1)}, f32[18816,128]{1,0:T(8,128)}, u32[]{:S(2)}) %copy-start.7) | copy-done | bytes 9633816
  127.0 3.7 %copy-done.11 = f32[18816,128]{1,0:T(8,128)S(1)} copy-done((f32[18816,128]{1,0:T(8,128)S(1)}, f32[18816,128]{1,0:T(8,128)}, u32[]{:S(2)}) %copy-start.11) | copy-done | bytes 9633816
  130.7 29.2 %columns.1 = (f32[18816,128]{1,0:T(8,128)S(1)}, f32[18816,128]{1,0:T(8,128)S(1)}, f32[18816,128]{1,0:T(8,128)S(1)}, f32[18816,128]{1,0:T(8,128)S(1)}) custom-call(f32[18816,128]{1,0:T(8,128)S(1)} %copy-done.3, f32[18816,128]{1,0:T(8,128)S(1)} %copy-done.7, ...), custom_call_target="tpu_custom_call", output_to_operand_aliasing={{0}: (0, {}), {1}: (1, {}), {2}: (2, {}), {3}: (3, {})} | custom-call | tf_op jit(solution)/shard_map/columns/pallas_call | solution.py:470
  163.7 3.7 %copy-done.15 = f32[18816,128]{1,0:T(8,128)S(1)} copy-done((f32[18816,128]{1,0:T(8,128)S(1)}, f32[18816,128]{1,0:T(8,128)}, u32[]{:S(2)}) %copy-start.15) | copy-done | bytes 9633816
  167.4 7.1 %rows.5.refs_6_ = f32[24,3,48,128]{3,2,1,0:T(8,128)} custom-call(s32[1]{0:T(128)} %bitcast.refs_0_, f32[18816,128]{1,0:T(8,128)S(1)} %get-tuple-element.67.refs_1_, f32[18816,128]{1,0:T(8,128)S(1)} %get-tuple-element.68.refs_2_, f32[18816,128]{1,0:T(8,128)S(1)} %get-tuple-element.69.refs_3_, f32[18816,128]{1,0:T(8,128)S(1)} %copy-done.15, ...), custom_call_target="tpu_custom_call" | custom-call | flops 1 | bytes 1 | tf_op jit(solution)/shard_map/rows/pallas_call | solution.py:490
  174.5 7.1 %rows.6.refs_7_ = f32[24,3,48,128]{3,2,1,0:T(8,128)} custom-call(s32[1]{0:T(128)} %bitcast.refs_0_, f32[18816,128]{1,0:T(8,128)S(1)} %get-tuple-element.67.refs_1_, f32[18816,128]{1,0:T(8,128)S(1)} %get-tuple-element.68.refs_2_, f32[18816,128]{1,0:T(8,128)S(1)} %get-tuple-element.69.refs_3_, f32[18816,128]{1,0:T(8,128)S(1)} %copy-done.15, ...), custom_call_target="tpu_custom_call" | custom-call | flops 1 | bytes 1 | tf_op jit(solution)/shard_map/rows/pallas_call | solution.py:490
  183.4 5.0 %rows.7.refs_7_ = f32[12,3,48,128]{3,2,1,0:T(8,128)} custom-call(s32[1]{0:T(128)} %bitcast.refs_0_, f32[18816,128]{1,0:T(8,128)S(1)} %get-tuple-element.67.refs_1_, f32[18816,128]{1,0:T(8,128)S(1)} %get-tuple-element.68.refs_2_, f32[18816,128]{1,0:T(8,128)S(1)} %get-tuple-element.69.refs_3_, f32[18816,128]{1,0:T(8,128)S(1)} %copy-done.15, ...), custom_call_target="tpu_custom_call" | custom-call | flops 1 | bytes 1 | tf_op jit(solution)/shard_map/rows/pallas_call | solution.py:490
  189.9 5.0 %rows.8.refs_6_ = f32[12,3,48,128]{3,2,1,0:T(8,128)} custom-call(s32[1]{0:T(128)} %bitcast.refs_0_, f32[18816,128]{1,0:T(8,128)S(1)} %get-tuple-element.67.refs_1_, f32[18816,128]{1,0:T(8,128)S(1)} %get-tuple-element.68.refs_2_, f32[18816,128]{1,0:T(8,128)S(1)} %get-tuple-element.69.refs_3_, f32[18816,128]{1,0:T(8,128)S(1)} %copy-done.15, ...), custom_call_target="tpu_custom_call" | custom-call | flops 1 | bytes 1 | tf_op jit(solution)/shard_map/rows/pallas_call | solution.py:490
  195.5 7.2 %rows.9.refs_0_ = f32[24,3,48,128]{3,2,1,0:T(8,128)} custom-call(s32[1]{0:T(128)} %bitcast.refs_0_, f32[18816,128]{1,0:T(8,128)S(1)} %get-tuple-element.67.refs_1_, f32[18816,128]{1,0:T(8,128)S(1)} %get-tuple-element.68.refs_2_, f32[18816,128]{1,0:T(8,128)S(1)} %get-tuple-element.69.refs_3_, f32[18816,128]{1,0:T(8,128)S(1)} %copy-done.15, ...), custom_call_target="tpu_custom_call" | custom-call | flops 1 | bytes 1 | tf_op jit(solution)/shard_map/rows/pallas_call | solution.py:490
  202.7 8.5 %collective-permute-done.16.refs_2_ = f32[12,3,48,128]{3,2,1,0:T(8,128)S(1)} collective-permute-done((f32[12,3,48,128]{3,2,1,0:T(8,128)}, f32[12,3,48,128]{3,2,1,0:T(8,128)S(1)}, u32[]{:S(2)}, u32[]{:S(2)}) %collective-permute-start.16) | collective-permute-done | bytes 884768 | tf_op jit(solution)/shard_map/ppermute | solution.py:501
  212.1 3.8 %finish.2.refs_7_ = f32[2,24,48,192]{3,2,1,0:T(8,128)} custom-call(f32[24,3,48,128]{3,2,1,0:T(8,128)} %rows.9.refs_0_, f32[24,3,48,128]{3,2,1,0:T(8,128)} %copy-done.20, f32[12,3,48,128]{3,2,1,0:T(8,128)} %copy-done.23, bf16[512,192]{1,0:T(8,128)(2,1)S(1)} %copy-done.16, f32[1,192]{1,0:T(1,128)S(1)} %bitcast.11, f32[1,48]{1,0:T(1,128)S(1)} %bitcast.13, ...), custom_call_target="tpu_custom_call" | custom-call | tf_op jit(solution)/shard_map/finish/pallas_call | solution.py:531
  216.0 13.2 %collective-permute-done.15.refs_2_ = f32[12,3,48,128]{3,2,1,0:T(8,128)S(1)} collective-permute-done((f32[12,3,48,128]{3,2,1,0:T(8,128)}, f32[12,3,48,128]{3,2,1,0:T(8,128)S(1)}, u32[]{:S(2)}, u32[]{:S(2)}) %collective-permute-start.15) | collective-permute-done | bytes 884768 | tf_op jit(solution)/shard_map/ppermute | solution.py:501
  230.1 3.8 %finish.3 = f32[2,24,48,192]{3,2,1,0:T(8,128)} custom-call(f32[24,3,48,128]{3,2,1,0:T(8,128)} %rows.9.refs_0_, f32[24,3,48,128]{3,2,1,0:T(8,128)} %copy-done.20, f32[12,3,48,128]{3,2,1,0:T(8,128)} %copy-done.22, bf16[512,192]{1,0:T(8,128)(2,1)S(1)} %copy-done.16, f32[1,192]{1,0:T(1,128)S(1)} %bitcast.12, ...), custom_call_target="tpu_custom_call", output_to_operand_aliasing={{}: (7, {})} | custom-call | tf_op jit(solution)/shard_map/finish/pallas_call | solution.py:531
  (94 shorter events, 70.3 us)
Async XLA Ops:
  6.2 16.8 %collective-permute-start = (f32[65,16,128]{2,1,0:T(8,128)}, f32[65,16,128]{2,1,0:T(8,128)S(1)}, u32[]{:S(2)}, u32[]{:S(2)}) collective-permute-start(f32[65,16,128]{2,1,0:T(8,128)} %spread.1.refs_1_), channel_id=1, source_target_pairs={{2,0},{3,1},{4,2},{5,3},{6,4},{7,5},{10,8},{11,9},{12,10},{13,11},... | collective-permute-start | bytes 1597448 | tf_op jit(solution)/shard_map/ppermute | solution.py:400
  8.6 16.9 %collective-permute-start.2 = (f32[65,16,128]{2,1,0:T(8,128)}, f32[65,16,128]{2,1,0:T(8,128)}, u32[]{:S(2)}, u32[]{:S(2)}) collective-permute-start(f32[65,16,128]{2,1,0:T(8,128)} %spread.1.refs_1_), channel_id=1, source_target_pairs={{0,2},{1,3},{2,4},{3,5},{4,6},{5,7},{8,10},{9,11},{10,12},{11,13},... | collective-permute-start | bytes 1597448 | tf_op jit(solution)/shard_map/ppermute | solution.py:400
  12.1 21.6 %collective-permute-start.3 = (f32[65,16,128]{2,1,0:T(8,128)}, f32[65,16,128]{2,1,0:T(8,128)S(1)}, u32[]{:S(2)}, u32[]{:S(2)}) collective-permute-start(f32[65,16,128]{2,1,0:T(8,128)} %spread.1.refs_1_), channel_id=1, source_target_pairs={{0,1},{1,0},{2,3},{3,2},{4,5},{5,4},{6,7},{7,6},{8,9},{9,8},{10,11... | collective-permute-start | bytes 1597448 | tf_op jit(solution)/shard_map/ppermute | solution.py:400
  23.1 10.7 %copy-start.32 = (f32[65,16,128]{2,1,0:T(8,128)}, f32[65,16,128]{2,1,0:T(8,128)S(1)}, u32[]{:S(2)}) copy-start(f32[65,16,128]{2,1,0:T(8,128)S(1)} %collective-permute-done.refs_2_) | copy-start | bytes 1597444
  23.1 21.1 %collective-permute-start.1 = (f32[65,16,128]{2,1,0:T(8,128)S(1)}, f32[65,16,128]{2,1,0:T(8,128)S(1)}, u32[]{:S(2)}, u32[]{:S(2)}) collective-permute-start(f32[65,16,128]{2,1,0:T(8,128)S(1)} %collective-permute-done.refs_2_), channel_id=1, source_target_pairs={{2,0},{3,1},{4,2},{5,3},{10,8},{11,9},{12,10},{13,11},{18,16},{19,... | collective-permute-start | bytes 1597448 | tf_op jit(solution)/shard_map/ppermute | solution.py:400
  25.5 19.4 %collective-permute-start.5 = (f32[65,16,128]{2,1,0:T(8,128)}, f32[65,16,128]{2,1,0:T(8,128)S(1)}, u32[]{:S(2)}, u32[]{:S(2)}) collective-permute-start(f32[65,16,128]{2,1,0:T(8,128)} %collective-permute-done.2.refs_1_), channel_id=1, source_target_pairs={{2,4},{3,5},{4,6},{5,7},{10,12},{11,13},{12,14},{13,15},{18,20},{1... | collective-permute-start | bytes 1597448 | tf_op jit(solution)/shard_map/ppermute | solution.py:400
  27.9 19.1 %collective-permute-start.6 = (f32[65,16,128]{2,1,0:T(8,128)S(1)}, f32[65,16,128]{2,1,0:T(8,128)S(1)}, u32[]{:S(2)}, u32[]{:S(2)}) collective-permute-start(f32[65,16,128]{2,1,0:T(8,128)S(1)} %collective-permute-done.refs_2_), channel_id=1, source_target_pairs={{0,1},{1,0},{2,3},{3,2},{4,5},{5,4},{8,9},{9,8},{10,11},{11,10},{1... | collective-permute-start | bytes 1597448 | tf_op jit(solution)/shard_map/ppermute | solution.py:400
  31.3 24.9 %collective-permute-start.7 = (f32[65,16,128]{2,1,0:T(8,128)}, f32[65,16,128]{2,1,0:T(8,128)S(1)}, u32[]{:S(2)}, u32[]{:S(2)}) collective-permute-start(f32[65,16,128]{2,1,0:T(8,128)} %collective-permute-done.2.refs_1_), channel_id=1, source_target_pairs={{2,3},{3,2},{4,5},{5,4},{6,7},{7,6},{10,11},{11,10},{12,13},{13,12... | collective-permute-start | bytes 1597448 | tf_op jit(solution)/shard_map/ppermute | solution.py:400
  44.2 12.0 %copy-start.24 = (f32[65,16,128]{2,1,0:T(8,128)}, f32[65,16,128]{2,1,0:T(8,128)S(1)}, u32[]{:S(2)}) copy-start(f32[65,16,128]{2,1,0:T(8,128)S(1)} %collective-permute-done.1.refs_2_) | copy-start | bytes 1597444
  44.2 37.4 %collective-permute-start.4 = (f32[65,16,128]{2,1,0:T(8,128)S(1)}, f32[65,16,128]{2,1,0:T(8,128)S(1)}, u32[]{:S(2)}, u32[]{:S(2)}) collective-permute-start(f32[65,16,128]{2,1,0:T(8,128)S(1)} %collective-permute-done.1.refs_2_), channel_id=1, source_target_pairs={{2,0},{3,1},{10,8},{11,9},{18,16},{19,17},{26,24},{27,25}} | collective-permute-start | bytes 1597448 | tf_op jit(solution)/shard_map/ppermute | solution.py:400
  44.9 11.3 %copy-start.25 = (f32[65,16,128]{2,1,0:T(8,128)}, f32[65,16,128]{2,1,0:T(8,128)S(1)}, u32[]{:S(2)}) copy-start(f32[65,16,128]{2,1,0:T(8,128)S(1)} %collective-permute-done.5.refs_1_) | copy-start | bytes 1597444
  44.9 38.1 %collective-permute-start.9 = (f32[65,16,128]{2,1,0:T(8,128)S(1)}, f32[65,16,128]{2,1,0:T(8,128)S(1)}, u32[]{:S(2)}, u32[]{:S(2)}) collective-permute-start(f32[65,16,128]{2,1,0:T(8,128)S(1)} %collective-permute-done.5.refs_1_), channel_id=1, source_target_pairs={{4,6},{5,7},{12,14},{13,15},{20,22},{21,23},{28,30},{29,31}} | collective-permute-start | bytes 1597448 | tf_op jit(solution)/shard_map/ppermute | solution.py:400
  46.3 38.3 %collective-permute-start.11 = (f32[65,16,128]{2,1,0:T(8,128)S(1)}, f32[65,16,128]{2,1,0:T(8,128)S(1)}, u32[]{:S(2)}, u32[]{:S(2)}) collective-permute-start(f32[65,16,128]{2,1,0:T(8,128)S(1)} %collective-permute-done.1.refs_2_), channel_id=1, source_target_pairs={{0,1},{1,0},{2,3},{3,2},{8,9},{9,8},{10,11},{11,10},{16,17},{17,16... | collective-permute-start | bytes 1597448 | tf_op jit(solution)/shard_map/ppermute | solution.py:400
  47.0 37.6 %collective-permute-start.12 = (f32[65,16,128]{2,1,0:T(8,128)S(1)}, f32[65,16,128]{2,1,0:T(8,128)S(1)}, u32[]{:S(2)}, u32[]{:S(2)}) collective-permute-start(f32[65,16,128]{2,1,0:T(8,128)S(1)} %collective-permute-done.5.refs_1_), channel_id=1, source_target_pairs={{4,5},{5,4},{6,7},{7,6},{12,13},{13,12},{14,15},{15,14},{20,21},{2... | collective-permute-start | bytes 1597448 | tf_op jit(solution)/shard_map/ppermute | solution.py:400
  81.6 24.2 %collective-permute-start.8 = (f32[65,16,128]{2,1,0:T(8,128)S(1)}, f32[65,16,128]{2,1,0:T(8,128)}, u32[]{:S(2)}, u32[]{:S(2)}) collective-permute-start(f32[65,16,128]{2,1,0:T(8,128)S(1)} %collective-permute-done.4.refs_2_), channel_id=1, source_target_pairs={{0,1},{1,0},{8,9},{9,8},{16,17},{17,16},{24,25},{25,24}} | collective-permute-start | bytes 1597448 | tf_op jit(solution)/shard_map/ppermute | solution.py:400
  83.0 22.8 %collective-permute-start.10 = (f32[65,16,128]{2,1,0:T(8,128)S(1)}, f32[65,16,128]{2,1,0:T(8,128)}, u32[]{:S(2)}, u32[]{:S(2)}) collective-permute-start(f32[65,16,128]{2,1,0:T(8,128)S(1)} %collective-permute-done.9.refs_1_), channel_id=1, source_target_pairs={{6,7},{7,6},{14,15},{15,14},{22,23},{23,22},{30,31},{31,30}} | collective-permute-start | bytes 1597448 | tf_op jit(solution)/shard_map/ppermute | solution.py:400
  174.5 7.7 %collective-permute-start.13 = (f32[24,3,48,128]{3,2,1,0:T(8,128)}, f32[24,3,48,128]{3,2,1,0:T(8,128)S(1)}, u32[]{:S(2)}, u32[]{:S(2)}) collective-permute-start(f32[24,3,48,128]{3,2,1,0:T(8,128)} %rows.5.refs_6_), channel_id=1, source_target_pairs={{0,8},{8,0},{16,24},{24,16},{1,9},{9,1},{17,25},{25,17},{2,10},{10... | collective-permute-start | bytes 5308424 | tf_op jit(solution)/shard_map/ppermute | solution.py:501
  181.7 21.0 %collective-permute-start.14 = (f32[24,3,48,128]{3,2,1,0:T(8,128)}, f32[24,3,48,128]{3,2,1,0:T(8,128)S(1)}, u32[]{:S(2)}, u32[]{:S(2)}) collective-permute-start(f32[24,3,48,128]{3,2,1,0:T(8,128)} %rows.6.refs_7_), channel_id=1, source_target_pairs={{0,8},{8,0},{16,24},{24,16},{1,9},{9,1},{17,25},{25,17},{2,10},{10... | collective-permute-start | bytes 5308424 | tf_op jit(solution)/shard_map/ppermute | solution.py:501
  188.4 22.7 %collective-permute-start.16 = (f32[12,3,48,128]{3,2,1,0:T(8,128)}, f32[12,3,48,128]{3,2,1,0:T(8,128)S(1)}, u32[]{:S(2)}, u32[]{:S(2)}) collective-permute-start(f32[12,3,48,128]{3,2,1,0:T(8,128)} %rows.7.refs_7_), channel_id=1, source_target_pairs={{0,16},{8,24},{16,0},{24,8},{1,17},{9,25},{17,1},{25,9},{2,18},{10... | collective-permute-start | bytes 2654216 | tf_op jit(solution)/shard_map/ppermute | solution.py:501
  194.9 17.2 %copy-start.16 = (bf16[512,192]{1,0:T(8,128)(2,1)S(1)}, bf16[512,192]{1,0:T(8,128)(2,1)}, u32[]{:S(2)}) copy-start(bf16[512,192]{1,0:T(8,128)(2,1)} %constant.36.clone.refs_3_) | copy-start | bytes 589828
  194.9 17.2 %copy-start.17 = (f32[192]{0:T(256)S(1)}, f32[192]{0:T(256)}, u32[]{:S(2)}) copy-start(f32[192]{0:T(256)} %param.19) | copy-start | bytes 2308
  194.9 17.2 %copy-start.18 = (f32[48]{0:T(128)S(1)}, f32[48]{0:T(128)}, u32[]{:S(2)}) copy-start(f32[48]{0:T(128)} %param.20) | copy-start | bytes 580
  194.9 17.2 %copy-start.19 = (f32[24]{0:T(128)S(1)}, f32[24]{0:T(128)}, u32[]{:S(2)}) copy-start(f32[24]{0:T(128)} %refs_6_.3) | copy-start | bytes 292
  194.9 34.2 %collective-permute-start.15 = (f32[12,3,48,128]{3,2,1,0:T(8,128)}, f32[12,3,48,128]{3,2,1,0:T(8,128)S(1)}, u32[]{:S(2)}, u32[]{:S(2)}) collective-permute-start(f32[12,3,48,128]{3,2,1,0:T(8,128)} %rows.8.refs_6_), channel_id=1, source_target_pairs={{0,16},{8,24},{16,0},{24,8},{1,17},{9,25},{17,1},{25,9},{2,18},{10... | collective-permute-start | bytes 2654216 | tf_op jit(solution)/shard_map/ppermute | solution.py:501
  (27 other events, 88.0 us)

commit v9 on v8

--- a/solution.py
+++ b/solution.py
@@ -165,7 +165,7 @@
 
 def tiles_kernel(conditions, first, *refs):
     arrays = len(conditions)
-    deep_ref = refs[0]
+    places_ref = refs[0]
     source_refs = refs[1 : 1 + arrays]
     depth_ref, phases_ref = refs[1 + arrays : 3 + arrays]
     acc_refs = refs[-5 - PARTS : -5]
@@ -243,7 +243,7 @@
             add_source(index)
         else:
             side, depth = condition
-            holds = deep_ref[0] >= depth if side == "from" else deep_ref[0] < depth
+            holds = places_ref[0] >= depth if side == "from" else places_ref[0] < depth
             pl.when(holds)(functools.partial(add_source, index))
 
 
@@ -281,11 +281,11 @@
     lax.fori_loop(0, NX // 2 // PARTS, columns, 0)
 
 
-def rows_kernel(relative, first, count, chunks, grid_rows, addends, planes_padded, place_ref, *refs):
+def rows_kernel(relative, first, count, chunks, grid_rows, addends, planes_padded, places_ref, *refs):
     acc_refs, row_ref, addend_refs, out_ref = refs[:PARTS], refs[PARTS], refs[PARTS + 1 : -1], refs[-1]
     assert len(addend_refs) == addends
     rows = grid_rows * chunks * TILE
-    device = jnp.bitwise_xor(place_ref[0], relative)
+    device = jnp.bitwise_xor(places_ref[1], relative)
     lane = lax.broadcasted_iota(jnp.int32, (PLANES, LANES), 1)
 
     def block(step, carry):
@@ -399,8 +399,7 @@
         ]
         return lax.ppermute(value, "gy", moves)
 
-    place = lax.axis_index("gx").astype(jnp.int32).reshape(1)
-    deep_place = deep_at.reshape(1)
+    places = jnp.stack((deep_at, lax.axis_index("gx").astype(jnp.int32)))
     gy = lax.axis_index("gy")
     matrices, phases = depth_tables(planes)
     matrix = lax.dynamic_index_in_dim(jnp.asarray(matrices), gy, 0, keepdims=False)
@@ -438,7 +437,7 @@
             compiler_params=params,
             cost_estimate=pl.CostEstimate(flops=0, bytes_accessed=len(sources) << 23, transcendentals=0),
             name="tiles",
-        )(deep_place, *in_hbm([array for _, array in sources] + [matrix, phase_rows]), *in_vmem(acc))
+        )(places, *in_hbm([array for _, array in sources] + [matrix, phase_rows]), *in_vmem(acc))
         return acc, token
 
     def after(value, token):
@@ -495,7 +494,7 @@
             compiler_params=params,
             cost_estimate=pl.CostEstimate(flops=1, bytes_accessed=1, transcendentals=0),
             name="rows",
-        )(place, *in_vmem(acc), *in_hbm([row_table] + addends + after))
+        )(places, *in_vmem(acc), *in_hbm([row_table] + addends + after))
 
     def swap(value, bit):
         return lax.ppermute(value, "gx", [(index, index ^ bit) for index in range(grid_rows)])

time: 236 us -> 176 us (0.75)
  local copies, waits for them, and re-layouts: 67.8 us -> 8.61 us
    unnamed x68 -> x38, local copies, waits for them, and re-layouts: 64.9 us -> 5.77 us
  transfers between devices with their start and end apart: 17 -> 17, of which waited for: 3 -> 3; matrix products, arithmetic and copies ran while one was open for 1% -> 2% of each run, Pallas kernels for 25% -> 34%
where the time goes in v9:
time: 176 us; the launch traced here: 175 us
  Pallas kernels  109 us (62%)
  starting transfers between devices  28.7 us (16%)
  waiting for transfers between devices  28.5 us (16%)
  local copies, waits for them, and re-layouts  8.61 us (5%)
    pallas_call x5, Pallas kernels, add_tiles(): pl.pallas_call(functools.partial(tiles_kernel, conditions, not acc), out_...  34.1 us
    pallas_call x5, Pallas kernels, rows_for(): pl.pallas_call(body, in_specs=[smem] + [vmem] * (1 + PARTS + len(addends)...  31.4 us
    pallas_call x1, Pallas kernels, on_device(): pl.pallas_call(columns_kernel, out_shape=[jax.ShapeDtypeStruct(acc_shape,...  29.4 us
    ppermute x13, starting transfers between devices, shift(): return lax.ppermute(value, 'gy', moves)  26.1 us
    ppermute x4, waiting for transfers between devices, swap(): lax.ppermute(value, 'gx', [(index, index ^ bit) for index in range(grid_r...  21.7 us
    pallas_call x2, Pallas kernels, on_device(): pl.pallas_call(finish, grid=(1,), out_shape=jax.ShapeDtypeStruct((2, plan...  7.69 us
    ppermute x13, waiting for transfers between devices, shift(): return lax.ppermute(value, 'gy', moves)  6.79 us
    pallas_call x1, Pallas kernels, on_device(): pl.pallas_call(functools.partial(spread_kernel, tile_rows, tile_cols, gri...  6.24 us
  transfers between devices with their start and end apart: 17, of which 3 were waited for; matrix products, arithmetic and copies ran while one was open for 2% of the time, Pallas kernels for 34%

profile of v9, /device:TPU:16, one launch (start us, length us, event | category | flops | bytes accessed | tf_op | source)
XLA Modules:
  0.0 175.0 jit_solution(14990415767879658698)
XLA Ops:
  0.0 6.2 %spread.1.refs_1_ = f32[65,16,128]{2,1,0:T(8,128)} custom-call(f32[128,2,128]{2,1,0:T(2,128)} %samples_ref.1, f32[128,3,4,128]{3,2,1,0:T(4,128)} %kernel_ref.1, s32[3,128,128]{2,1,0:T(8,128)} %bitcast.15, s32[1,128]{1,0:T(1,128)} %bitcast.16, s32[1,128]{1,0:T(1,128)} %bitcast.17), custom_call_target="tpu_custom_call" | custom-call | tf_op jit(solution)/shard_map/spread/pallas_call | solution.py:384
  6.2 2.3 %collective-permute-start = (f32[65,16,128]{2,1,0:T(8,128)}, f32[65,16,128]{2,1,0:T(8,128)}, u32[]{:S(2)}, u32[]{:S(2)}) collective-permute-start(f32[65,16,128]{2,1,0:T(8,128)} %spread.1.refs_1_), channel_id=1, source_target_pairs={{2,0},{3,1},{4,2},{5,3},{6,4},{7,5},{10,8},{11,9},{12,10},{13,11},... | collective-permute-start | bytes 1597448 | tf_op jit(solution)/shard_map/ppermute | solution.py:400
  8.6 4.3 %collective-permute-start.2 = (f32[65,16,128]{2,1,0:T(8,128)}, f32[65,16,128]{2,1,0:T(8,128)S(1)}, u32[]{:S(2)}, u32[]{:S(2)}) collective-permute-start(f32[65,16,128]{2,1,0:T(8,128)} %spread.1.refs_1_), channel_id=1, source_target_pairs={{0,2},{1,3},{2,4},{3,5},{4,6},{5,7},{8,10},{9,11},{10,12},{11,13},... | collective-permute-start | bytes 1597448 | tf_op jit(solution)/shard_map/ppermute | solution.py:400
  17.4 6.5 %tiles.5 = (f32[18816,128]{1,0:T(8,128)S(1)}, f32[18816,128]{1,0:T(8,128)S(1)}, f32[18816,128]{1,0:T(8,128)S(1)}, f32[18816,128]{1,0:T(8,128)S(1)}, f32[8,128]{1,0:T(8,128)}) custom-call(s32[2]{0:T(128)S(1)} %pad_add_fusion.refs_0_, f32[65,16,128]{2,1,0:T(8,128)} %spread.1.refs_1_, ...), custom_call_target="tpu_custom_call" | custom-call | bytes 8388608 | tf_op jit(solution)/shard_map/tiles/pallas_call | solution.py:425
  23.9 1.6 collective-permute-start.1
  25.6 2.9 %collective-permute-start.5 = (f32[65,16,128]{2,1,0:T(8,128)S(1)}, f32[65,16,128]{2,1,0:T(8,128)S(1)}, u32[]{:S(2)}, u32[]{:S(2)}) collective-permute-start(f32[65,16,128]{2,1,0:T(8,128)S(1)} %collective-permute-done.2.refs_1_), channel_id=1, source_target_pairs={{2,4},{3,5},{4,6},{5,7},{10,12},{11,13},{12,14},{13,15},{18,20},{1... | collective-permute-start | bytes 1597448 | tf_op jit(solution)/shard_map/ppermute | solution.py:400
  28.5 3.4 %collective-permute-start.6 = (f32[65,16,128]{2,1,0:T(8,128)}, f32[65,16,128]{2,1,0:T(8,128)S(1)}, u32[]{:S(2)}, u32[]{:S(2)}) collective-permute-start(f32[65,16,128]{2,1,0:T(8,128)} %collective-permute-done.refs_2_), channel_id=1, source_target_pairs={{0,1},{1,0},{2,3},{3,2},{4,5},{5,4},{8,9},{9,8},{10,11},{11,10},{1... | collective-permute-start | bytes 1597448 | tf_op jit(solution)/shard_map/ppermute | solution.py:400
  31.9 2.4 %collective-permute-start.7 = (f32[65,16,128]{2,1,0:T(8,128)S(1)}, f32[65,16,128]{2,1,0:T(8,128)S(1)}, u32[]{:S(2)}, u32[]{:S(2)}) collective-permute-start(f32[65,16,128]{2,1,0:T(8,128)S(1)} %collective-permute-done.2.refs_1_), channel_id=1, source_target_pairs={{2,3},{3,2},{4,5},{5,4},{6,7},{7,6},{10,11},{11,10},{12,13},{13,12... | collective-permute-start | bytes 1597448 | tf_op jit(solution)/shard_map/ppermute | solution.py:400
  34.4 9.7 %tiles.6 = (f32[18816,128]{1,0:T(8,128)S(1)}, f32[18816,128]{1,0:T(8,128)S(1)}, f32[18816,128]{1,0:T(8,128)S(1)}, f32[18816,128]{1,0:T(8,128)S(1)}, f32[8,128]{1,0:T(8,128)}) custom-call(s32[2]{0:T(128)S(1)} %pad_add_fusion.refs_0_, f32[65,16,128]{2,1,0:T(8,128)} %copy-done.18, ...), custom_call_target="tpu_custom_call", output_to_operand_aliasing={{0}: (6, {}), {1}: (7, {}), {2}: (8, {}), {3}: (9, {})} | custom-call | bytes 25165824 | tf_op jit(solution)/shard_map/tiles/pallas_call | solution.py:425
  46.9 3.4 %collective-permute-start.12 = (f32[65,16,128]{2,1,0:T(8,128)S(1)}, f32[65,16,128]{2,1,0:T(8,128)S(1)}, u32[]{:S(2)}, u32[]{:S(2)}) collective-permute-start(f32[65,16,128]{2,1,0:T(8,128)S(1)} %collective-permute-done.5.refs_1_), channel_id=1, source_target_pairs={{4,5},{5,4},{6,7},{7,6},{12,13},{13,12},{14,15},{15,14},{20,21},{2... | collective-permute-start | bytes 1597448 | tf_op jit(solution)/shard_map/ppermute | solution.py:400
  50.3 6.8 %collective-permute-done.7.refs_4_ = f32[65,16,128]{2,1,0:T(8,128)S(1)} collective-permute-done((f32[65,16,128]{2,1,0:T(8,128)S(1)}, f32[65,16,128]{2,1,0:T(8,128)S(1)}, u32[]{:S(2)}, u32[]{:S(2)}) %collective-permute-start.7) | collective-permute-done | bytes 532512 | tf_op jit(solution)/shard_map/ppermute | solution.py:400
  57.9 9.9 %tiles.7 = (f32[18816,128]{1,0:T(8,128)S(1)}, f32[18816,128]{1,0:T(8,128)S(1)}, f32[18816,128]{1,0:T(8,128)S(1)}, f32[18816,128]{1,0:T(8,128)S(1)}, f32[8,128]{1,0:T(8,128)}) custom-call(s32[2]{0:T(128)S(1)} %pad_add_fusion.refs_0_, f32[65,16,128]{2,1,0:T(8,128)} %copy-done.9, ...), custom_call_target="tpu_custom_call", output_to_operand_aliasing={{0}: (7, {}), {1}: (8, {}), {2}: (9, {}), {3}: (10, {})} | custom-call | bytes 33554432 | tf_op jit(solution)/shard_map/tiles/pallas_call | solution.py:425
  70.2 5.3 %tiles.8 = (f32[18816,128]{1,0:T(8,128)S(1)}, f32[18816,128]{1,0:T(8,128)S(1)}, f32[18816,128]{1,0:T(8,128)S(1)}, f32[18816,128]{1,0:T(8,128)S(1)}, f32[8,128]{1,0:T(8,128)}) custom-call(s32[2]{0:T(128)S(1)} %pad_add_fusion.refs_0_, f32[65,16,128]{2,1,0:T(8,128)} %copy-done.11, ...), custom_call_target="tpu_custom_call", output_to_operand_aliasing={{0}: (7, {}), {1}: (8, {}), {2}: (9, {}), {3}: (10, {})} | custom-call | bytes 33554432 | tf_op jit(solution)/shard_map/tiles/pallas_call | solution.py:425
  76.5 2.7 %tiles.9 = (f32[18816,128]{1,0:T(8,128)S(1)}, f32[18816,128]{1,0:T(8,128)S(1)}, f32[18816,128]{1,0:T(8,128)S(1)}, f32[18816,128]{1,0:T(8,128)S(1)}, f32[8,128]{1,0:T(8,128)}) custom-call(s32[2]{0:T(128)S(1)} %pad_add_fusion.refs_0_, f32[65,16,128]{2,1,0:T(8,128)} %copy-done.16, ...), custom_call_target="tpu_custom_call", output_to_operand_aliasing={{0}: (5, {}), {1}: (6, {}), {2}: (7, {}), {3}: (8, {})} | custom-call | bytes 16777216 | tf_op jit(solution)/shard_map/tiles/pallas_call | solution.py:425
  79.2 29.4 %columns.1 = (f32[18816,128]{1,0:T(8,128)S(1)}, f32[18816,128]{1,0:T(8,128)S(1)}, f32[18816,128]{1,0:T(8,128)S(1)}, f32[18816,128]{1,0:T(8,128)S(1)}) custom-call(f32[18816,128]{1,0:T(8,128)S(1)} %get-tuple-element.63.refs_0_, f32[18816,128]{1,0:T(8,128)S(1)} %get-tuple-element.64.refs_1_, ...), custom_call_target="tpu_custom_call", output_to_operand_aliasing={{0}: (0, {}), {1}: (1, {}), {2}: (2, {}), {3}: (3, {})} | custom-call | tf_op jit(solution)/shard_map/columns/pallas_call | solution.py:469
  108.6 7.1 %rows.5.refs_6_ = f32[24,3,48,128]{3,2,1,0:T(8,128)} custom-call(s32[2]{0:T(128)S(1)} %pad_add_fusion.refs_0_, f32[18816,128]{1,0:T(8,128)S(1)} %get-tuple-element.67.refs_1_, f32[18816,128]{1,0:T(8,128)S(1)} %get-tuple-element.68.refs_2_, f32[18816,128]{1,0:T(8,128)S(1)} %get-tuple-element.69.refs_3_, f32[18816,128]{1,0:T(8,128)S(1)} %get-tuple-element.70.refs_4_, ...), custom_call_target="tpu_custom_call" | custom-call | flops 1 | bytes 1 | tf_op jit(solution)/shard_map/rows/pallas_call | solution.py:489
  115.7 7.1 %rows.6.refs_7_ = f32[24,3,48,128]{3,2,1,0:T(8,128)} custom-call(s32[2]{0:T(128)S(1)} %pad_add_fusion.refs_0_, f32[18816,128]{1,0:T(8,128)S(1)} %get-tuple-element.67.refs_1_, f32[18816,128]{1,0:T(8,128)S(1)} %get-tuple-element.68.refs_2_, f32[18816,128]{1,0:T(8,128)S(1)} %get-tuple-element.69.refs_3_, f32[18816,128]{1,0:T(8,128)S(1)} %get-tuple-element.70.refs_4_, ...), custom_call_target="tpu_custom_call" | custom-call | flops 1 | bytes 1 | tf_op jit(solution)/shard_map/rows/pallas_call | solution.py:489
  124.5 5.0 %rows.7.refs_7_ = f32[12,3,48,128]{3,2,1,0:T(8,128)} custom-call(s32[2]{0:T(128)S(1)} %pad_add_fusion.refs_0_, f32[18816,128]{1,0:T(8,128)S(1)} %get-tuple-element.67.refs_1_, f32[18816,128]{1,0:T(8,128)S(1)} %get-tuple-element.68.refs_2_, f32[18816,128]{1,0:T(8,128)S(1)} %get-tuple-element.69.refs_3_, f32[18816,128]{1,0:T(8,128)S(1)} %get-tuple-element.70.refs_4_, ...), custom_call_target="tpu_custom_call" | custom-call | flops 1 | bytes 1 | tf_op jit(solution)/shard_map/rows/pallas_call | solution.py:489
  131.1 5.0 %rows.8.refs_6_ = f32[12,3,48,128]{3,2,1,0:T(8,128)} custom-call(s32[2]{0:T(128)S(1)} %pad_add_fusion.refs_0_, f32[18816,128]{1,0:T(8,128)S(1)} %get-tuple-element.67.refs_1_, f32[18816,128]{1,0:T(8,128)S(1)} %get-tuple-element.68.refs_2_, f32[18816,128]{1,0:T(8,128)S(1)} %get-tuple-element.69.refs_3_, f32[18816,128]{1,0:T(8,128)S(1)} %get-tuple-element.70.refs_4_, ...), custom_call_target="tpu_custom_call" | custom-call | flops 1 | bytes 1 | tf_op jit(solution)/shard_map/rows/pallas_call | solution.py:489
  136.7 7.1 %rows.9.refs_0_ = f32[24,3,48,128]{3,2,1,0:T(8,128)} custom-call(s32[2]{0:T(128)S(1)} %pad_add_fusion.refs_0_, f32[18816,128]{1,0:T(8,128)S(1)} %get-tuple-element.67.refs_1_, f32[18816,128]{1,0:T(8,128)S(1)} %get-tuple-element.68.refs_2_, f32[18816,128]{1,0:T(8,128)S(1)} %get-tuple-element.69.refs_3_, f32[18816,128]{1,0:T(8,128)S(1)} %get-tuple-element.70.refs_4_, ...), custom_call_target="tpu_custom_call" | custom-call | flops 1 | bytes 1 | tf_op jit(solution)/shard_map/rows/pallas_call | solution.py:489
  143.8 8.5 %collective-permute-done.16.refs_2_ = f32[12,3,48,128]{3,2,1,0:T(8,128)S(1)} collective-permute-done((f32[12,3,48,128]{3,2,1,0:T(8,128)}, f32[12,3,48,128]{3,2,1,0:T(8,128)S(1)}, u32[]{:S(2)}, u32[]{:S(2)}) %collective-permute-start.16) | collective-permute-done | bytes 884768 | tf_op jit(solution)/shard_map/ppermute | solution.py:500
  153.2 3.8 %finish.2.refs_7_ = f32[2,24,48,192]{3,2,1,0:T(8,128)} custom-call(f32[24,3,48,128]{3,2,1,0:T(8,128)} %rows.9.refs_0_, f32[24,3,48,128]{3,2,1,0:T(8,128)} %copy-done.4, f32[12,3,48,128]{3,2,1,0:T(8,128)} %copy-done.7, bf16[512,192]{1,0:T(8,128)(2,1)S(1)} %copy-done, f32[1,192]{1,0:T(1,128)S(1)} %bitcast.11, f32[1,48]{1,0:T(1,128)S(1)} %bitcast.13, ...), custom_call_target="tpu_custom_call" | custom-call | tf_op jit(solution)/shard_map/finish/pallas_call | solution.py:530
  157.1 13.2 %collective-permute-done.15.refs_2_ = f32[12,3,48,128]{3,2,1,0:T(8,128)S(1)} collective-permute-done((f32[12,3,48,128]{3,2,1,0:T(8,128)}, f32[12,3,48,128]{3,2,1,0:T(8,128)S(1)}, u32[]{:S(2)}, u32[]{:S(2)}) %collective-permute-start.15) | collective-permute-done | bytes 884768 | tf_op jit(solution)/shard_map/ppermute | solution.py:500
  171.2 3.8 %finish.3 = f32[2,24,48,192]{3,2,1,0:T(8,128)} custom-call(f32[24,3,48,128]{3,2,1,0:T(8,128)} %rows.9.refs_0_, f32[24,3,48,128]{3,2,1,0:T(8,128)} %copy-done.4, f32[12,3,48,128]{3,2,1,0:T(8,128)} %copy-done.6, bf16[512,192]{1,0:T(8,128)(2,1)S(1)} %copy-done, f32[1,192]{1,0:T(1,128)S(1)} %bitcast.12, ...), custom_call_target="tpu_custom_call", output_to_operand_aliasing={{}: (7, {})} | custom-call | tf_op jit(solution)/shard_map/finish/pallas_call | solution.py:530
  (65 shorter events, 17.0 us)
Async XLA Ops:
  6.2 17.7 %collective-permute-start = (f32[65,16,128]{2,1,0:T(8,128)}, f32[65,16,128]{2,1,0:T(8,128)}, u32[]{:S(2)}, u32[]{:S(2)}) collective-permute-start(f32[65,16,128]{2,1,0:T(8,128)} %spread.1.refs_1_), channel_id=1, source_target_pairs={{2,0},{3,1},{4,2},{5,3},{6,4},{7,5},{10,8},{11,9},{12,10},{13,11},... | collective-permute-start | bytes 1597448 | tf_op jit(solution)/shard_map/ppermute | solution.py:400
  8.6 17.0 %collective-permute-start.2 = (f32[65,16,128]{2,1,0:T(8,128)}, f32[65,16,128]{2,1,0:T(8,128)S(1)}, u32[]{:S(2)}, u32[]{:S(2)}) collective-permute-start(f32[65,16,128]{2,1,0:T(8,128)} %spread.1.refs_1_), channel_id=1, source_target_pairs={{0,2},{1,3},{2,4},{3,5},{4,6},{5,7},{8,10},{9,11},{10,12},{11,13},... | collective-permute-start | bytes 1597448 | tf_op jit(solution)/shard_map/ppermute | solution.py:400
  12.9 21.5 %collective-permute-start.3 = (f32[65,16,128]{2,1,0:T(8,128)}, f32[65,16,128]{2,1,0:T(8,128)}, u32[]{:S(2)}, u32[]{:S(2)}) collective-permute-start(f32[65,16,128]{2,1,0:T(8,128)} %spread.1.refs_1_), channel_id=1, source_target_pairs={{0,1},{1,0},{2,3},{3,2},{4,5},{5,4},{6,7},{7,6},{8,9},{9,8},{10,11... | collective-permute-start | bytes 1597448 | tf_op jit(solution)/shard_map/ppermute | solution.py:400
  23.9 20.1 %collective-permute-start.1 = (f32[65,16,128]{2,1,0:T(8,128)}, f32[65,16,128]{2,1,0:T(8,128)S(1)}, u32[]{:S(2)}, u32[]{:S(2)}) collective-permute-start(f32[65,16,128]{2,1,0:T(8,128)} %collective-permute-done.refs_2_), channel_id=1, source_target_pairs={{2,0},{3,1},{4,2},{5,3},{10,8},{11,9},{12,10},{13,11},{18,16},{19,... | collective-permute-start | bytes 1597448 | tf_op jit(solution)/shard_map/ppermute | solution.py:400
  25.6 19.2 %collective-permute-start.5 = (f32[65,16,128]{2,1,0:T(8,128)S(1)}, f32[65,16,128]{2,1,0:T(8,128)S(1)}, u32[]{:S(2)}, u32[]{:S(2)}) collective-permute-start(f32[65,16,128]{2,1,0:T(8,128)S(1)} %collective-permute-done.2.refs_1_), channel_id=1, source_target_pairs={{2,4},{3,5},{4,6},{5,7},{10,12},{11,13},{12,14},{13,15},{18,20},{1... | collective-permute-start | bytes 1597448 | tf_op jit(solution)/shard_map/ppermute | solution.py:400
  28.5 18.3 %collective-permute-start.6 = (f32[65,16,128]{2,1,0:T(8,128)}, f32[65,16,128]{2,1,0:T(8,128)S(1)}, u32[]{:S(2)}, u32[]{:S(2)}) collective-permute-start(f32[65,16,128]{2,1,0:T(8,128)} %collective-permute-done.refs_2_), channel_id=1, source_target_pairs={{0,1},{1,0},{2,3},{3,2},{4,5},{5,4},{8,9},{9,8},{10,11},{11,10},{1... | collective-permute-start | bytes 1597448 | tf_op jit(solution)/shard_map/ppermute | solution.py:400
  31.9 25.1 %collective-permute-start.7 = (f32[65,16,128]{2,1,0:T(8,128)S(1)}, f32[65,16,128]{2,1,0:T(8,128)S(1)}, u32[]{:S(2)}, u32[]{:S(2)}) collective-permute-start(f32[65,16,128]{2,1,0:T(8,128)S(1)} %collective-permute-done.2.refs_1_), channel_id=1, source_target_pairs={{2,3},{3,2},{4,5},{5,4},{6,7},{7,6},{10,11},{11,10},{12,13},{13,12... | collective-permute-start | bytes 1597448 | tf_op jit(solution)/shard_map/ppermute | solution.py:400
  44.1 13.0 %copy-start.8 = (f32[65,16,128]{2,1,0:T(8,128)}, f32[65,16,128]{2,1,0:T(8,128)S(1)}, u32[]{:S(2)}) copy-start(f32[65,16,128]{2,1,0:T(8,128)S(1)} %collective-permute-done.1.refs_2_) | copy-start | bytes 1597444
  44.1 23.7 %collective-permute-start.4 = (f32[65,16,128]{2,1,0:T(8,128)S(1)}, f32[65,16,128]{2,1,0:T(8,128)S(1)}, u32[]{:S(2)}, u32[]{:S(2)}) collective-permute-start(f32[65,16,128]{2,1,0:T(8,128)S(1)} %collective-permute-done.1.refs_2_), channel_id=1, source_target_pairs={{2,0},{3,1},{10,8},{11,9},{18,16},{19,17},{26,24},{27,25}} | collective-permute-start | bytes 1597448 | tf_op jit(solution)/shard_map/ppermute | solution.py:400
  44.8 12.3 %copy-start.9 = (f32[65,16,128]{2,1,0:T(8,128)}, f32[65,16,128]{2,1,0:T(8,128)S(1)}, u32[]{:S(2)}) copy-start(f32[65,16,128]{2,1,0:T(8,128)S(1)} %collective-permute-done.5.refs_1_) | copy-start | bytes 1597444
  44.8 23.7 %collective-permute-start.9 = (f32[65,16,128]{2,1,0:T(8,128)S(1)}, f32[65,16,128]{2,1,0:T(8,128)S(1)}, u32[]{:S(2)}, u32[]{:S(2)}) collective-permute-start(f32[65,16,128]{2,1,0:T(8,128)S(1)} %collective-permute-done.5.refs_1_), channel_id=1, source_target_pairs={{4,6},{5,7},{12,14},{13,15},{20,22},{21,23},{28,30},{29,31}} | collective-permute-start | bytes 1597448 | tf_op jit(solution)/shard_map/ppermute | solution.py:400
  46.1 23.1 %collective-permute-start.11 = (f32[65,16,128]{2,1,0:T(8,128)S(1)}, f32[65,16,128]{2,1,0:T(8,128)S(1)}, u32[]{:S(2)}, u32[]{:S(2)}) collective-permute-start(f32[65,16,128]{2,1,0:T(8,128)S(1)} %collective-permute-done.1.refs_2_), channel_id=1, source_target_pairs={{0,1},{1,0},{2,3},{3,2},{8,9},{9,8},{10,11},{11,10},{16,17},{17,16... | collective-permute-start | bytes 1597448 | tf_op jit(solution)/shard_map/ppermute | solution.py:400
  46.8 10.2 %copy-start.12 = (f32[65,16,128]{2,1,0:T(8,128)}, f32[65,16,128]{2,1,0:T(8,128)S(1)}, u32[]{:S(2)}) copy-start(f32[65,16,128]{2,1,0:T(8,128)S(1)} %collective-permute-done.6.refs_3_) | copy-start | bytes 1597444
  46.9 22.4 %collective-permute-start.12 = (f32[65,16,128]{2,1,0:T(8,128)S(1)}, f32[65,16,128]{2,1,0:T(8,128)S(1)}, u32[]{:S(2)}, u32[]{:S(2)}) collective-permute-start(f32[65,16,128]{2,1,0:T(8,128)S(1)} %collective-permute-done.5.refs_1_), channel_id=1, source_target_pairs={{4,5},{5,4},{6,7},{7,6},{12,13},{13,12},{14,15},{15,14},{20,21},{2... | collective-permute-start | bytes 1597448 | tf_op jit(solution)/shard_map/ppermute | solution.py:400
  67.8 7.7 %collective-permute-start.8 = (f32[65,16,128]{2,1,0:T(8,128)S(1)}, f32[65,16,128]{2,1,0:T(8,128)S(1)}, u32[]{:S(2)}, u32[]{:S(2)}) collective-permute-start(f32[65,16,128]{2,1,0:T(8,128)S(1)} %collective-permute-done.4.refs_2_), channel_id=1, source_target_pairs={{0,1},{1,0},{8,9},{9,8},{16,17},{17,16},{24,25},{25,24}} | collective-permute-start | bytes 1597448 | tf_op jit(solution)/shard_map/ppermute | solution.py:400
  68.5 7.0 %collective-permute-start.10 = (f32[65,16,128]{2,1,0:T(8,128)S(1)}, f32[65,16,128]{2,1,0:T(8,128)S(1)}, u32[]{:S(2)}, u32[]{:S(2)}) collective-permute-start(f32[65,16,128]{2,1,0:T(8,128)S(1)} %collective-permute-done.9.refs_1_), channel_id=1, source_target_pairs={{6,7},{7,6},{14,15},{15,14},{22,23},{23,22},{30,31},{31,30}} | collective-permute-start | bytes 1597448 | tf_op jit(solution)/shard_map/ppermute | solution.py:400
  115.7 7.6 %collective-permute-start.13 = (f32[24,3,48,128]{3,2,1,0:T(8,128)}, f32[24,3,48,128]{3,2,1,0:T(8,128)S(1)}, u32[]{:S(2)}, u32[]{:S(2)}) collective-permute-start(f32[24,3,48,128]{3,2,1,0:T(8,128)} %rows.5.refs_6_), channel_id=1, source_target_pairs={{0,8},{8,0},{16,24},{24,16},{1,9},{9,1},{17,25},{25,17},{2,10},{10... | collective-permute-start | bytes 5308424 | tf_op jit(solution)/shard_map/ppermute | solution.py:500
  122.8 21.0 %collective-permute-start.14 = (f32[24,3,48,128]{3,2,1,0:T(8,128)}, f32[24,3,48,128]{3,2,1,0:T(8,128)S(1)}, u32[]{:S(2)}, u32[]{:S(2)}) collective-permute-start(f32[24,3,48,128]{3,2,1,0:T(8,128)} %rows.6.refs_7_), channel_id=1, source_target_pairs={{0,8},{8,0},{16,24},{24,16},{1,9},{9,1},{17,25},{25,17},{2,10},{10... | collective-permute-start | bytes 5308424 | tf_op jit(solution)/shard_map/ppermute | solution.py:500
  129.6 22.7 %collective-permute-start.16 = (f32[12,3,48,128]{3,2,1,0:T(8,128)}, f32[12,3,48,128]{3,2,1,0:T(8,128)S(1)}, u32[]{:S(2)}, u32[]{:S(2)}) collective-permute-start(f32[12,3,48,128]{3,2,1,0:T(8,128)} %rows.7.refs_7_), channel_id=1, source_target_pairs={{0,16},{8,24},{16,0},{24,8},{1,17},{9,25},{17,1},{25,9},{2,18},{10... | collective-permute-start | bytes 2654216 | tf_op jit(solution)/shard_map/ppermute | solution.py:500
  136.1 17.2 %copy-start = (bf16[512,192]{1,0:T(8,128)(2,1)S(1)}, bf16[512,192]{1,0:T(8,128)(2,1)}, u32[]{:S(2)}) copy-start(bf16[512,192]{1,0:T(8,128)(2,1)} %constant.36.clone.refs_3_) | copy-start | bytes 589828
  136.1 17.2 %copy-start.1 = (f32[192]{0:T(256)S(1)}, f32[192]{0:T(256)}, u32[]{:S(2)}) copy-start(f32[192]{0:T(256)} %param.19) | copy-start | bytes 2308
  136.1 17.2 %copy-start.2 = (f32[48]{0:T(128)S(1)}, f32[48]{0:T(128)}, u32[]{:S(2)}) copy-start(f32[48]{0:T(128)} %param.20) | copy-start | bytes 580
  136.1 17.2 %copy-start.3 = (f32[24]{0:T(128)S(1)}, f32[24]{0:T(128)}, u32[]{:S(2)}) copy-start(f32[24]{0:T(128)} %refs_6_.3) | copy-start | bytes 292
  136.1 34.2 %collective-permute-start.15 = (f32[12,3,48,128]{3,2,1,0:T(8,128)}, f32[12,3,48,128]{3,2,1,0:T(8,128)S(1)}, u32[]{:S(2)}, u32[]{:S(2)}) collective-permute-start(f32[12,3,48,128]{3,2,1,0:T(8,128)} %rows.8.refs_6_), channel_id=1, source_target_pairs={{0,16},{8,24},{16,0},{24,8},{1,17},{9,25},{17,1},{25,9},{2,18},{10... | collective-permute-start | bytes 2654216 | tf_op jit(solution)/shard_map/ppermute | solution.py:500
  (12 other events, 27.0 us)

commit v10 on v9

--- a/solution.py
+++ b/solution.py
@@ -278,7 +278,7 @@
                     )
         return carry
 
-    lax.fori_loop(0, NX // 2 // PARTS, columns, 0)
+    lax.fori_loop(0, NX // 2 // PARTS, columns, 0, unroll=4)
 
 
 def rows_kernel(relative, first, count, chunks, grid_rows, addends, planes_padded, places_ref, *refs):
@@ -324,7 +324,7 @@
                     out_ref[place, number, planes] = total
         return carry
 
-    lax.fori_loop(0, 3 * count, block, 0)
+    lax.fori_loop(0, 3 * count, block, 0, unroll=3)
 
 
 def finish_kernel(chunk, planes_padded, parts, refs):
@@ -437,7 +437,7 @@
             compiler_params=params,
             cost_estimate=pl.CostEstimate(flops=0, bytes_accessed=len(sources) << 23, transcendentals=0),
             name="tiles",
-        )(places, *in_hbm([array for _, array in sources] + [matrix, phase_rows]), *in_vmem(acc))
+        )(places, *[array for _, array in sources], *in_hbm([matrix, phase_rows]), *in_vmem(acc))
         return acc, token
 
     def after(value, token):
@@ -516,24 +516,33 @@
 
     top = grid_rows // 2
     far = arrivals(top, top // 2)
-    near = arrivals(0, top // 2)
-    crossed = [swap(rows_next(top, chunk, 1, far), top) for chunk in range(chunks)]
-    kept_parts = [rows_next(0, 0, chunks, [])] + near
+    parts = []
+    for chunk in range(chunks):
+        if top == 2:
+            near = [(swap(rows_next(1, chunk, 1, []), 1), 0)]
+        elif chunk == 0:
+            near = [(array, None) for array in arrivals(0, top // 2)]
+        parts.append([(array, chunk if place is None else place) for array, place in near])
+        parts[-1].append((swap(rows_next(top, chunk, 1, far), top), 0))
+    kept = rows_next(0, 0, chunks, [])
+    parts = [[(kept, chunk)] + arrays for chunk, arrays in enumerate(parts)]
 
     image = None
     for chunk in range(chunks):
 
         def finish(*refs, chunk=chunk):
-            finish_kernel(chunk, planes_padded, len(kept_parts) + 1, refs)
+            finish_kernel(chunk, planes_padded, len(parts[chunk]), refs)
 
         earlier = [] if image is None else [image]
         image = pl.pallas_call(
             finish,
             grid=(1,),
             out_shape=jax.ShapeDtypeStruct((2, planes, per_device, NX // 2), F32),
-            in_specs=[pl.BlockSpec((slots,) + part_shape, lambda step, chunk=chunk: (chunk, 0, 0, 0))] * len(kept_parts)
+            in_specs=[
+                pl.BlockSpec((slots,) + part_shape, lambda step, place=place: (place, 0, 0, 0))
+                for _, place in parts[chunk]
+            ]
             + [
-                pl.BlockSpec((slots,) + part_shape, lambda step: (0, 0, 0, 0)),
                 pl.BlockSpec((4 * LANES, NX // 2), lambda step: (0, 0)),
                 pl.BlockSpec((1, NX // 2), lambda step: (0, 0)),
                 pl.BlockSpec((1, per_device), lambda step: (0, 0)),
@@ -541,11 +550,11 @@
             ]
             + [pl.BlockSpec(memory_space=pl.ANY)] * len(earlier),
             out_specs=pl.BlockSpec((2, planes, CHUNK, NX // 2), lambda step, chunk=chunk: (0, 0, chunk, 0)),
-            input_output_aliases={len(kept_parts) + 5: 0} if earlier else {},
+            input_output_aliases={len(parts[chunk]) + 4: 0} if earlier else {},
             compiler_params=params,
             name="finish",
         )(
-            *in_hbm(kept_parts + [crossed[chunk]]),
+            *in_hbm([array for array, _ in parts[chunk]]),
             jnp.asarray(order_tables()),
             deapod_first[None, :],
             deapod_second[None, :],

time: 176 us -> 159 us (0.903)
  the two profiles are of different devices: /device:TPU:16 before, /device:TPU:0 now
where the time goes in v10:
time: 159 us; the launch traced here: 158 us
  Pallas kernels  92.7 us (58%)
  waiting for transfers between devices  33.8 us (21%)
  starting transfers between devices  24.2 us (15%)
  local copies, waits for them, and re-layouts  6.95 us (4%)
    pallas_call x5, Pallas kernels, add_tiles(): pl.pallas_call(functools.partial(tiles_kernel, conditions, not acc), out_...  32 us
    pallas_call x6, Pallas kernels, rows_for(): pl.pallas_call(body, in_specs=[smem] + [vmem] * (1 + PARTS + len(addends)...  26.7 us
    ppermute x13, starting transfers between devices, shift(): return lax.ppermute(value, 'gy', moves)  21.6 us
    ppermute x5, waiting for transfers between devices, swap(): lax.ppermute(value, 'gx', [(index, index ^ bit) for index in range(grid_r...  20.5 us
    pallas_call x1, Pallas kernels, on_device(): pl.pallas_call(columns_kernel, out_shape=[jax.ShapeDtypeStruct(acc_shape,...  20.1 us
    ppermute x13, waiting for transfers between devices, shift(): return lax.ppermute(value, 'gy', moves)  13.3 us
    pallas_call x2, Pallas kernels, on_device(): pl.pallas_call(finish, grid=(1,), out_shape=jax.ShapeDtypeStruct((2, plan...  7.69 us
    pallas_call x1, Pallas kernels, on_device(): pl.pallas_call(functools.partial(spread_kernel, tile_rows, tile_cols, gri...  6.24 us
  transfers between devices with their start and end apart: 18, of which 5 were waited for; matrix products, arithmetic and copies ran while one was open for 2% of the time, Pallas kernels for 33%

profile of v10, /device:TPU:0, one launch (start us, length us, event | category | flops | bytes accessed | tf_op | source)
XLA Modules:
  0.0 158.0 jit_solution(16297217571088345698)
XLA Ops:
  0.0 6.2 %spread.1.refs_1_ = f32[65,16,128]{2,1,0:T(8,128)} custom-call(f32[128,2,128]{2,1,0:T(2,128)} %samples_ref.1, f32[128,3,4,128]{3,2,1,0:T(4,128)} %kernel_ref.1, s32[3,128,128]{2,1,0:T(8,128)} %bitcast.15, s32[1,128]{1,0:T(1,128)} %bitcast.16, s32[1,128]{1,0:T(1,128)} %bitcast.17), custom_call_target="tpu_custom_call" | custom-call | tf_op jit(solution)/shard_map/spread/pallas_call | solution.py:384
  7.5 5.6 %collective-permute-start.2 = (f32[65,16,128]{2,1,0:T(8,128)}, f32[65,16,128]{2,1,0:T(8,128)S(1)}, u32[]{:S(2)}, u32[]{:S(2)}) collective-permute-start(f32[65,16,128]{2,1,0:T(8,128)} %spread.1.refs_1_), channel_id=1, source_target_pairs={{0,2},{1,3},{2,4},{3,5},{4,6},{5,7},{8,10},{9,11},{10,12},{11,13},... | collective-permute-start | bytes 1597448 | tf_op jit(solution)/shard_map/ppermute | solution.py:400
  13.1 2.0 %collective-permute-start.3 = (f32[65,16,128]{2,1,0:T(8,128)}, f32[65,16,128]{2,1,0:T(8,128)S(1)}, u32[]{:S(2)}, u32[]{:S(2)}) collective-permute-start(f32[65,16,128]{2,1,0:T(8,128)} %spread.1.refs_1_), channel_id=1, source_target_pairs={{0,1},{1,0},{2,3},{3,2},{4,5},{5,4},{6,7},{7,6},{8,9},{9,8},{10,11... | collective-permute-start | bytes 1597448 | tf_op jit(solution)/shard_map/ppermute | solution.py:400
  19.1 6.4 %tiles.5 = (f32[18816,128]{1,0:T(8,128)S(1)}, f32[18816,128]{1,0:T(8,128)S(1)}, f32[18816,128]{1,0:T(8,128)S(1)}, f32[18816,128]{1,0:T(8,128)S(1)}, f32[8,128]{1,0:T(8,128)}) custom-call(s32[2]{0:T(128)S(1)} %pad_add_fusion.refs_0_, f32[65,16,128]{2,1,0:T(8,128)S(1)} %copy-done, bf16[48,128]{1,0:T(8,128)(2,1)} %dynamic-slice_bitcast_fusion.1.refs_2_.refs_4_.refs_5_.refs_3_, ...), custom_call_target="tpu_custom_call" | custom-call | bytes 8388608 | tf_op jit(solution)/shard_map/tiles/pallas_call | solution.py:425
  30.2 6.9 %tiles.6 = (f32[18816,128]{1,0:T(8,128)S(1)}, f32[18816,128]{1,0:T(8,128)S(1)}, f32[18816,128]{1,0:T(8,128)S(1)}, f32[18816,128]{1,0:T(8,128)S(1)}, f32[8,128]{1,0:T(8,128)}) custom-call(s32[2]{0:T(128)S(1)} %pad_add_fusion.refs_0_, ...), custom_call_target="tpu_custom_call", output_to_operand_aliasing={{0}: (6, {}), {1}: (7, {}), {2}: (8, {}), {3}: (9, {})} | custom-call | bytes 25165824 | tf_op jit(solution)/shard_map/tiles/pallas_call | solution.py:425
  37.2 3.3 %collective-permute-done.1.refs_2_ = f32[65,16,128]{2,1,0:T(8,128)S(1)} collective-permute-done((f32[65,16,128]{2,1,0:T(8,128)S(1)}, f32[65,16,128]{2,1,0:T(8,128)S(1)}, u32[]{:S(2)}, u32[]{:S(2)}) %collective-permute-start.1) | collective-permute-done | bytes 532512 | tf_op jit(solution)/shard_map/ppermute | solution.py:400
  42.4 2.3 %collective-permute-start.11 = (f32[65,16,128]{2,1,0:T(8,128)S(1)}, f32[65,16,128]{2,1,0:T(8,128)S(1)}, u32[]{:S(2)}, u32[]{:S(2)}) collective-permute-start(f32[65,16,128]{2,1,0:T(8,128)S(1)} %collective-permute-done.1.refs_2_), channel_id=1, source_target_pairs={{0,1},{1,0},{2,3},{3,2},{8,9},{9,8},{10,11},{11,10},{16,17},{17,16... | collective-permute-start | bytes 1597448 | tf_op jit(solution)/shard_map/ppermute | solution.py:400
  45.4 7.0 %tiles.7 = (f32[18816,128]{1,0:T(8,128)S(1)}, f32[18816,128]{1,0:T(8,128)S(1)}, f32[18816,128]{1,0:T(8,128)S(1)}, f32[18816,128]{1,0:T(8,128)S(1)}, f32[8,128]{1,0:T(8,128)}) custom-call(s32[2]{0:T(128)S(1)} %pad_add_fusion.refs_0_, ...), custom_call_target="tpu_custom_call", output_to_operand_aliasing={{0}: (7, {}), {1}: (8, {}), {2}: (9, {}), {3}: (10, {})} | custom-call | bytes 33554432 | tf_op jit(solution)/shard_map/tiles/pallas_call | solution.py:425
  52.5 7.1 %collective-permute-done.4.refs_2_ = f32[65,16,128]{2,1,0:T(8,128)S(1)} collective-permute-done((f32[65,16,128]{2,1,0:T(8,128)S(1)}, f32[65,16,128]{2,1,0:T(8,128)S(1)}, u32[]{:S(2)}, u32[]{:S(2)}) %collective-permute-start.4) | collective-permute-done | bytes 532512 | tf_op jit(solution)/shard_map/ppermute | solution.py:400
  59.5 2.4 %collective-permute-start.8 = (f32[65,16,128]{2,1,0:T(8,128)S(1)}, f32[65,16,128]{2,1,0:T(8,128)S(1)}, u32[]{:S(2)}, u32[]{:S(2)}) collective-permute-start(f32[65,16,128]{2,1,0:T(8,128)S(1)} %collective-permute-done.4.refs_2_), channel_id=1, source_target_pairs={{0,1},{1,0},{8,9},{9,8},{16,17},{17,16},{24,25},{25,24}} | collective-permute-start | bytes 1597448 | tf_op jit(solution)/shard_map/ppermute | solution.py:400
  62.7 7.0 %tiles.8 = (f32[18816,128]{1,0:T(8,128)S(1)}, f32[18816,128]{1,0:T(8,128)S(1)}, f32[18816,128]{1,0:T(8,128)S(1)}, f32[18816,128]{1,0:T(8,128)S(1)}, f32[8,128]{1,0:T(8,128)}) custom-call(s32[2]{0:T(128)S(1)} %pad_add_fusion.refs_0_, ...), custom_call_target="tpu_custom_call", output_to_operand_aliasing={{0}: (7, {}), {1}: (8, {}), {2}: (9, {}), {3}: (10, {})} | custom-call | bytes 33554432 | tf_op jit(solution)/shard_map/tiles/pallas_call | solution.py:425
  69.7 3.0 %collective-permute-done.8.refs_1_ = f32[65,16,128]{2,1,0:T(8,128)S(1)} collective-permute-done((f32[65,16,128]{2,1,0:T(8,128)S(1)}, f32[65,16,128]{2,1,0:T(8,128)S(1)}, u32[]{:S(2)}, u32[]{:S(2)}) %collective-permute-start.8) | collective-permute-done | bytes 532512 | tf_op jit(solution)/shard_map/ppermute | solution.py:400
  72.7 4.7 %tiles.9 = (f32[18816,128]{1,0:T(8,128)S(1)}, f32[18816,128]{1,0:T(8,128)S(1)}, f32[18816,128]{1,0:T(8,128)S(1)}, f32[18816,128]{1,0:T(8,128)S(1)}, f32[8,128]{1,0:T(8,128)}) custom-call(s32[2]{0:T(128)S(1)} %pad_add_fusion.refs_0_, ...), custom_call_target="tpu_custom_call", output_to_operand_aliasing={{0}: (5, {}), {1}: (6, {}), {2}: (7, {}), {3}: (8, {})} | custom-call | bytes 16777216 | tf_op jit(solution)/shard_map/tiles/pallas_call | solution.py:425
  77.4 20.1 %columns.1 = (f32[18816,128]{1,0:T(8,128)S(1)}, f32[18816,128]{1,0:T(8,128)S(1)}, f32[18816,128]{1,0:T(8,128)S(1)}, f32[18816,128]{1,0:T(8,128)S(1)}) custom-call(f32[18816,128]{1,0:T(8,128)S(1)} %get-tuple-element.63.refs_0_, f32[18816,128]{1,0:T(8,128)S(1)} %get-tuple-element.64.refs_1_, ...), custom_call_target="tpu_custom_call", output_to_operand_aliasing={{0}: (0, {}), {1}: (1, {}), {2}: (2, {}), {3}: (3, {})} | custom-call | tf_op jit(solution)/shard_map/columns/pallas_call | solution.py:469
  97.4 5.5 %rows.6.refs_6_ = f32[24,3,48,128]{3,2,1,0:T(8,128)} custom-call(s32[2]{0:T(128)S(1)} %pad_add_fusion.refs_0_, f32[18816,128]{1,0:T(8,128)S(1)} %get-tuple-element.67.refs_1_, f32[18816,128]{1,0:T(8,128)S(1)} %get-tuple-element.68.refs_2_, f32[18816,128]{1,0:T(8,128)S(1)} %get-tuple-element.69.refs_3_, f32[18816,128]{1,0:T(8,128)S(1)} %get-tuple-element.70.refs_4_, ...), custom_call_target="tpu_custom_call" | custom-call | flops 1 | bytes 1 | tf_op jit(solution)/shard_map/rows/pallas_call | solution.py:489
  103.0 3.6 %rows.7.refs_7_ = f32[12,3,48,128]{3,2,1,0:T(8,128)} custom-call(s32[2]{0:T(128)S(1)} %pad_add_fusion.refs_0_, f32[18816,128]{1,0:T(8,128)S(1)} %get-tuple-element.67.refs_1_, f32[18816,128]{1,0:T(8,128)S(1)} %get-tuple-element.68.refs_2_, f32[18816,128]{1,0:T(8,128)S(1)} %get-tuple-element.69.refs_3_, f32[18816,128]{1,0:T(8,128)S(1)} %get-tuple-element.70.refs_4_, ...), custom_call_target="tpu_custom_call" | custom-call | flops 1 | bytes 1 | tf_op jit(solution)/shard_map/rows/pallas_call | solution.py:489
  108.3 4.2 %rows.8.refs_6_ = f32[12,3,48,128]{3,2,1,0:T(8,128)} custom-call(s32[2]{0:T(128)S(1)} %pad_add_fusion.refs_0_, f32[18816,128]{1,0:T(8,128)S(1)} %get-tuple-element.67.refs_1_, f32[18816,128]{1,0:T(8,128)S(1)} %get-tuple-element.68.refs_2_, f32[18816,128]{1,0:T(8,128)S(1)} %get-tuple-element.69.refs_3_, f32[18816,128]{1,0:T(8,128)S(1)} %get-tuple-element.70.refs_4_, ...), custom_call_target="tpu_custom_call" | custom-call | flops 1 | bytes 1 | tf_op jit(solution)/shard_map/rows/pallas_call | solution.py:489
  114.0 3.6 %rows.9.refs_7_ = f32[12,3,48,128]{3,2,1,0:T(8,128)} custom-call(s32[2]{0:T(128)S(1)} %pad_add_fusion.refs_0_, f32[18816,128]{1,0:T(8,128)S(1)} %get-tuple-element.67.refs_1_, f32[18816,128]{1,0:T(8,128)S(1)} %get-tuple-element.68.refs_2_, f32[18816,128]{1,0:T(8,128)S(1)} %get-tuple-element.69.refs_3_, f32[18816,128]{1,0:T(8,128)S(1)} %get-tuple-element.70.refs_4_, ...), custom_call_target="tpu_custom_call" | custom-call | flops 1 | bytes 1 | tf_op jit(solution)/shard_map/rows/pallas_call | solution.py:489
  117.5 4.2 %rows.10.refs_6_ = f32[12,3,48,128]{3,2,1,0:T(8,128)} custom-call(s32[2]{0:T(128)S(1)} %pad_add_fusion.refs_0_, f32[18816,128]{1,0:T(8,128)S(1)} %get-tuple-element.67.refs_1_, f32[18816,128]{1,0:T(8,128)S(1)} %get-tuple-element.68.refs_2_, f32[18816,128]{1,0:T(8,128)S(1)} %get-tuple-element.69.refs_3_, f32[18816,128]{1,0:T(8,128)S(1)} %get-tuple-element.70.refs_4_, ...), custom_call_target="tpu_custom_call" | custom-call | flops 1 | bytes 1 | tf_op jit(solution)/shard_map/rows/pallas_call | solution.py:489
  122.4 5.6 %rows.11.refs_0_ = f32[24,3,48,128]{3,2,1,0:T(8,128)} custom-call(s32[2]{0:T(128)S(1)} %pad_add_fusion.refs_0_, f32[18816,128]{1,0:T(8,128)S(1)} %get-tuple-element.67.refs_1_, f32[18816,128]{1,0:T(8,128)S(1)} %get-tuple-element.68.refs_2_, f32[18816,128]{1,0:T(8,128)S(1)} %get-tuple-element.69.refs_3_, f32[18816,128]{1,0:T(8,128)S(1)} %get-tuple-element.70.refs_4_, ...), custom_call_target="tpu_custom_call" | custom-call | flops 1 | bytes 1 | tf_op jit(solution)/shard_map/rows/pallas_call | solution.py:489
  127.9 7.3 %collective-permute-done.17.refs_2_ = f32[12,3,48,128]{3,2,1,0:T(8,128)S(1)} collective-permute-done((f32[12,3,48,128]{3,2,1,0:T(8,128)}, f32[12,3,48,128]{3,2,1,0:T(8,128)S(1)}, u32[]{:S(2)}, u32[]{:S(2)}) %collective-permute-start.17) | collective-permute-done | bytes 884768 | tf_op jit(solution)/shard_map/ppermute | solution.py:500
  136.1 3.8 %finish.2.refs_7_ = f32[2,24,48,192]{3,2,1,0:T(8,128)} custom-call(f32[24,3,48,128]{3,2,1,0:T(8,128)} %rows.11.refs_0_, f32[12,3,48,128]{3,2,1,0:T(8,128)} %copy-done.8, f32[12,3,48,128]{3,2,1,0:T(8,128)} %copy-done.9, bf16[512,192]{1,0:T(8,128)(2,1)S(1)} %copy-done.1, f32[1,192]{1,0:T(1,128)S(1)} %bitcast.11, f32[1,48]{1,0:T(1,128)S(1)} %bitcast.13, ...), custom_call_target="tpu_custom_call" | custom-call | tf_op jit(solution)/shard_map/finish/pallas_call | solution.py:537
  140.0 13.2 %collective-permute-done.15.refs_2_ = f32[12,3,48,128]{3,2,1,0:T(8,128)S(1)} collective-permute-done((f32[12,3,48,128]{3,2,1,0:T(8,128)}, f32[12,3,48,128]{3,2,1,0:T(8,128)S(1)}, u32[]{:S(2)}, u32[]{:S(2)}) %collective-permute-start.15) | collective-permute-done | bytes 884768 | tf_op jit(solution)/shard_map/ppermute | solution.py:500
  154.1 3.8 %finish.3 = f32[2,24,48,192]{3,2,1,0:T(8,128)} custom-call(f32[24,3,48,128]{3,2,1,0:T(8,128)} %rows.11.refs_0_, f32[12,3,48,128]{3,2,1,0:T(8,128)} %copy-done.6, f32[12,3,48,128]{3,2,1,0:T(8,128)} %copy-done.7, bf16[512,192]{1,0:T(8,128)(2,1)S(1)} %copy-done.1, f32[1,192]{1,0:T(1,128)S(1)} %bitcast.12, ...), custom_call_target="tpu_custom_call", output_to_operand_aliasing={{}: (7, {})} | custom-call | tf_op jit(solution)/shard_map/finish/pallas_call | solution.py:537
  (50 shorter events, 19.0 us)
Async XLA Ops:
  6.2 19.3 %collective-permute-start = (f32[65,16,128]{2,1,0:T(8,128)}, f32[65,16,128]{2,1,0:T(8,128)S(1)}, u32[]{:S(2)}, u32[]{:S(2)}) collective-permute-start(f32[65,16,128]{2,1,0:T(8,128)} %spread.1.refs_1_), channel_id=1, source_target_pairs={{2,0},{3,1},{4,2},{5,3},{6,4},{7,5},{10,8},{11,9},{12,10},{13,11},... | collective-permute-start | bytes 1597448 | tf_op jit(solution)/shard_map/ppermute | solution.py:400
  7.5 19.3 %collective-permute-start.2 = (f32[65,16,128]{2,1,0:T(8,128)}, f32[65,16,128]{2,1,0:T(8,128)S(1)}, u32[]{:S(2)}, u32[]{:S(2)}) collective-permute-start(f32[65,16,128]{2,1,0:T(8,128)} %spread.1.refs_1_), channel_id=1, source_target_pairs={{0,2},{1,3},{2,4},{3,5},{4,6},{5,7},{8,10},{9,11},{10,12},{11,13},... | collective-permute-start | bytes 1597448 | tf_op jit(solution)/shard_map/ppermute | solution.py:400
  13.1 17.1 %collective-permute-start.3 = (f32[65,16,128]{2,1,0:T(8,128)}, f32[65,16,128]{2,1,0:T(8,128)S(1)}, u32[]{:S(2)}, u32[]{:S(2)}) collective-permute-start(f32[65,16,128]{2,1,0:T(8,128)} %spread.1.refs_1_), channel_id=1, source_target_pairs={{0,1},{1,0},{2,3},{3,2},{4,5},{5,4},{6,7},{7,6},{8,9},{9,8},{10,11... | collective-permute-start | bytes 1597448 | tf_op jit(solution)/shard_map/ppermute | solution.py:400
  25.5 14.9 %collective-permute-start.1 = (f32[65,16,128]{2,1,0:T(8,128)S(1)}, f32[65,16,128]{2,1,0:T(8,128)S(1)}, u32[]{:S(2)}, u32[]{:S(2)}) collective-permute-start(f32[65,16,128]{2,1,0:T(8,128)S(1)} %collective-permute-done.refs_2_), channel_id=1, source_target_pairs={{2,0},{3,1},{4,2},{5,3},{10,8},{11,9},{12,10},{13,11},{18,16},{19,... | collective-permute-start | bytes 1597448 | tf_op jit(solution)/shard_map/ppermute | solution.py:400
  26.8 14.9 %collective-permute-start.5 = (f32[65,16,128]{2,1,0:T(8,128)S(1)}, f32[65,16,128]{2,1,0:T(8,128)S(1)}, u32[]{:S(2)}, u32[]{:S(2)}) collective-permute-start(f32[65,16,128]{2,1,0:T(8,128)S(1)} %collective-permute-done.2.refs_1_), channel_id=1, source_target_pairs={{2,4},{3,5},{4,6},{5,7},{10,12},{11,13},{12,14},{13,15},{18,20},{1... | collective-permute-start | bytes 1597448 | tf_op jit(solution)/shard_map/ppermute | solution.py:400
  27.5 17.2 %collective-permute-start.6 = (f32[65,16,128]{2,1,0:T(8,128)S(1)}, f32[65,16,128]{2,1,0:T(8,128)S(1)}, u32[]{:S(2)}, u32[]{:S(2)}) collective-permute-start(f32[65,16,128]{2,1,0:T(8,128)S(1)} %collective-permute-done.refs_2_), channel_id=1, source_target_pairs={{0,1},{1,0},{2,3},{3,2},{4,5},{5,4},{8,9},{9,8},{10,11},{11,10},{1... | collective-permute-start | bytes 1597448 | tf_op jit(solution)/shard_map/ppermute | solution.py:400
  29.5 15.9 %collective-permute-start.7 = (f32[65,16,128]{2,1,0:T(8,128)S(1)}, f32[65,16,128]{2,1,0:T(8,128)S(1)}, u32[]{:S(2)}, u32[]{:S(2)}) collective-permute-start(f32[65,16,128]{2,1,0:T(8,128)S(1)} %collective-permute-done.2.refs_1_), channel_id=1, source_target_pairs={{2,3},{3,2},{4,5},{5,4},{6,7},{7,6},{10,11},{11,10},{12,13},{13,12... | collective-permute-start | bytes 1597448 | tf_op jit(solution)/shard_map/ppermute | solution.py:400
  40.4 19.1 %collective-permute-start.4 = (f32[65,16,128]{2,1,0:T(8,128)S(1)}, f32[65,16,128]{2,1,0:T(8,128)S(1)}, u32[]{:S(2)}, u32[]{:S(2)}) collective-permute-start(f32[65,16,128]{2,1,0:T(8,128)S(1)} %collective-permute-done.1.refs_2_), channel_id=1, source_target_pairs={{2,0},{3,1},{10,8},{11,9},{18,16},{19,17},{26,24},{27,25}} | collective-permute-start | bytes 1597448 | tf_op jit(solution)/shard_map/ppermute | solution.py:400
  41.7 20.2 %collective-permute-start.9 = (f32[65,16,128]{2,1,0:T(8,128)S(1)}, f32[65,16,128]{2,1,0:T(8,128)S(1)}, u32[]{:S(2)}, u32[]{:S(2)}) collective-permute-start(f32[65,16,128]{2,1,0:T(8,128)S(1)} %collective-permute-done.5.refs_1_), channel_id=1, source_target_pairs={{4,6},{5,7},{12,14},{13,15},{20,22},{21,23},{28,30},{29,31}} | collective-permute-start | bytes 1597448 | tf_op jit(solution)/shard_map/ppermute | solution.py:400
  42.4 20.2 %collective-permute-start.11 = (f32[65,16,128]{2,1,0:T(8,128)S(1)}, f32[65,16,128]{2,1,0:T(8,128)S(1)}, u32[]{:S(2)}, u32[]{:S(2)}) collective-permute-start(f32[65,16,128]{2,1,0:T(8,128)S(1)} %collective-permute-done.1.refs_2_), channel_id=1, source_target_pairs={{0,1},{1,0},{2,3},{3,2},{8,9},{9,8},{10,11},{11,10},{16,17},{17,16... | collective-permute-start | bytes 1597448 | tf_op jit(solution)/shard_map/ppermute | solution.py:400
  44.7 18.0 %collective-permute-start.12 = (f32[65,16,128]{2,1,0:T(8,128)S(1)}, f32[65,16,128]{2,1,0:T(8,128)S(1)}, u32[]{:S(2)}, u32[]{:S(2)}) collective-permute-start(f32[65,16,128]{2,1,0:T(8,128)S(1)} %collective-permute-done.5.refs_1_), channel_id=1, source_target_pairs={{4,5},{5,4},{6,7},{7,6},{12,13},{13,12},{14,15},{15,14},{20,21},{2... | collective-permute-start | bytes 1597448 | tf_op jit(solution)/shard_map/ppermute | solution.py:400
  59.5 13.1 %collective-permute-start.8 = (f32[65,16,128]{2,1,0:T(8,128)S(1)}, f32[65,16,128]{2,1,0:T(8,128)S(1)}, u32[]{:S(2)}, u32[]{:S(2)}) collective-permute-start(f32[65,16,128]{2,1,0:T(8,128)S(1)} %collective-permute-done.4.refs_2_), channel_id=1, source_target_pairs={{0,1},{1,0},{8,9},{9,8},{16,17},{17,16},{24,25},{25,24}} | collective-permute-start | bytes 1597448 | tf_op jit(solution)/shard_map/ppermute | solution.py:400
  61.9 10.7 %collective-permute-start.10 = (f32[65,16,128]{2,1,0:T(8,128)S(1)}, f32[65,16,128]{2,1,0:T(8,128)S(1)}, u32[]{:S(2)}, u32[]{:S(2)}) collective-permute-start(f32[65,16,128]{2,1,0:T(8,128)S(1)} %collective-permute-done.9.refs_1_), channel_id=1, source_target_pairs={{6,7},{7,6},{14,15},{15,14},{22,23},{23,22},{30,31},{31,30}} | collective-permute-start | bytes 1597448 | tf_op jit(solution)/shard_map/ppermute | solution.py:400
  103.0 4.1 %collective-permute-start.13 = (f32[24,3,48,128]{3,2,1,0:T(8,128)}, f32[24,3,48,128]{3,2,1,0:T(8,128)S(1)}, u32[]{:S(2)}, u32[]{:S(2)}) collective-permute-start(f32[24,3,48,128]{3,2,1,0:T(8,128)} %rows.6.refs_6_), channel_id=1, source_target_pairs={{0,8},{8,0},{16,24},{24,16},{1,9},{9,1},{17,25},{25,17},{2,10},{10... | collective-permute-start | bytes 5308424 | tf_op jit(solution)/shard_map/ppermute | solution.py:500
  106.6 21.3 %collective-permute-start.16 = (f32[12,3,48,128]{3,2,1,0:T(8,128)}, f32[12,3,48,128]{3,2,1,0:T(8,128)S(1)}, u32[]{:S(2)}, u32[]{:S(2)}) collective-permute-start(f32[12,3,48,128]{3,2,1,0:T(8,128)} %rows.7.refs_7_), channel_id=1, source_target_pairs={{0,8},{8,0},{16,24},{24,16},{1,9},{9,1},{17,25},{25,17},{2,10},{10... | collective-permute-start | bytes 2654216 | tf_op jit(solution)/shard_map/ppermute | solution.py:500
  112.5 22.7 %collective-permute-start.17 = (f32[12,3,48,128]{3,2,1,0:T(8,128)}, f32[12,3,48,128]{3,2,1,0:T(8,128)S(1)}, u32[]{:S(2)}, u32[]{:S(2)}) collective-permute-start(f32[12,3,48,128]{3,2,1,0:T(8,128)} %rows.8.refs_6_), channel_id=1, source_target_pairs={{0,16},{8,24},{16,0},{24,8},{1,17},{9,25},{17,1},{25,9},{2,18},{10... | collective-permute-start | bytes 2654216 | tf_op jit(solution)/shard_map/ppermute | solution.py:500
  117.5 22.5 %collective-permute-start.14 = (f32[12,3,48,128]{3,2,1,0:T(8,128)}, f32[12,3,48,128]{3,2,1,0:T(8,128)S(1)}, u32[]{:S(2)}, u32[]{:S(2)}) collective-permute-start(f32[12,3,48,128]{3,2,1,0:T(8,128)} %rows.9.refs_7_), channel_id=1, source_target_pairs={{0,8},{8,0},{16,24},{24,16},{1,9},{9,1},{17,25},{25,17},{2,10},{10... | collective-permute-start | bytes 2654216 | tf_op jit(solution)/shard_map/ppermute | solution.py:500
  121.7 14.4 %copy-start.1 = (bf16[512,192]{1,0:T(8,128)(2,1)S(1)}, bf16[512,192]{1,0:T(8,128)(2,1)}, u32[]{:S(2)}) copy-start(bf16[512,192]{1,0:T(8,128)(2,1)} %constant.36.clone.refs_3_) | copy-start | bytes 589828
  121.7 14.4 %copy-start.2 = (f32[192]{0:T(256)S(1)}, f32[192]{0:T(256)}, u32[]{:S(2)}) copy-start(f32[192]{0:T(256)} %param.19) | copy-start | bytes 2308
  121.7 14.4 %copy-start.3 = (f32[48]{0:T(128)S(1)}, f32[48]{0:T(128)}, u32[]{:S(2)}) copy-start(f32[48]{0:T(128)} %param.20) | copy-start | bytes 580
  121.7 14.4 %copy-start.4 = (f32[24]{0:T(128)S(1)}, f32[24]{0:T(128)}, u32[]{:S(2)}) copy-start(f32[24]{0:T(128)} %refs_6_.3) | copy-start | bytes 292
  121.7 31.5 %collective-permute-start.15 = (f32[12,3,48,128]{3,2,1,0:T(8,128)}, f32[12,3,48,128]{3,2,1,0:T(8,128)S(1)}, u32[]{:S(2)}, u32[]{:S(2)}) collective-permute-start(f32[12,3,48,128]{3,2,1,0:T(8,128)} %rows.10.refs_6_), channel_id=1, source_target_pairs={{0,16},{8,24},{16,0},{24,8},{1,17},{9,25},{17,1},{25,9},{2,18},{10... | collective-permute-start | bytes 2654216 | tf_op jit(solution)/shard_map/ppermute | solution.py:500
  127.9 7.3 %copy-start.8 = (f32[12,3,48,128]{3,2,1,0:T(8,128)}, f32[12,3,48,128]{3,2,1,0:T(8,128)S(1)}, u32[]{:S(2)}) copy-start(f32[12,3,48,128]{3,2,1,0:T(8,128)S(1)} %collective-permute-done.16.refs_1_) | copy-start | bytes 2654212
  140.0 13.2 %copy-start.6 = (f32[12,3,48,128]{3,2,1,0:T(8,128)}, f32[12,3,48,128]{3,2,1,0:T(8,128)S(1)}, u32[]{:S(2)}) copy-start(f32[12,3,48,128]{3,2,1,0:T(8,128)S(1)} %collective-permute-done.14.refs_1_) | copy-start | bytes 2654212
  (4 other events, 4.1 us)

commit v11 on v10

--- a/solution.py
+++ b/solution.py
@@ -167,9 +167,9 @@
     arrays = len(conditions)
     places_ref = refs[0]
     source_refs = refs[1 : 1 + arrays]
-    depth_ref, phases_ref = refs[1 + arrays : 3 + arrays]
-    acc_refs = refs[-5 - PARTS : -5]
-    token_ref, codes_ref, even_ref, odd_ref, arrived = refs[-5:]
+    depth_tables_ref, phase_tables_ref = refs[1 + arrays : 3 + arrays]
+    acc_refs = refs[-7 - PARTS : -7]
+    token_ref, codes_ref, depth_ref, phases_ref, even_ref, odd_ref, arrived = refs[-7:]
     token_ref[...] = jnp.zeros_like(token_ref)
     stride = STRIDE
     pairs = source_refs[0].shape[0] - 1
@@ -182,8 +182,14 @@
             source_refs[index].at[pairs, pl.ds(0, TILE)], codes_ref.at[index], arrived.at[index]
         )
 
+    tables = [
+        pltpu.make_async_copy(depth_tables_ref.at[places_ref[2]], depth_ref, arrived.at[arrays]),
+        pltpu.make_async_copy(phase_tables_ref.at[places_ref[2]], phases_ref, arrived.at[arrays + 1]),
+    ]
     for index in range(arrays):
         copies(index).start()
+    for table in tables:
+        table.start()
 
     if first:
 
@@ -197,6 +203,8 @@
 
     for index in range(arrays):
         copies(index).wait()
+    for table in tables:
+        table.wait()
 
     def add_source(index):
         tiles_ref = source_refs[index]
@@ -236,14 +244,15 @@
             accumulate(number + 1, odd_ref)
             return carry
 
-        lax.fori_loop(0, batches // 2, add_pair, 0)
+        lax.fori_loop(0, batches // 2, add_pair, 0, unroll=2)
 
     for index, condition in enumerate(conditions):
         if condition is None:
             add_source(index)
         else:
-            side, depth = condition
-            holds = places_ref[0] >= depth if side == "from" else places_ref[0] < depth
+            holds = places_ref[0] == condition[0]
+            for depth in condition[1:]:
+                holds = jnp.logical_or(holds, places_ref[0] == depth)
             pl.when(holds)(functools.partial(add_source, index))
 
 
@@ -278,7 +287,7 @@
                     )
         return carry
 
-    lax.fori_loop(0, NX // 2 // PARTS, columns, 0, unroll=4)
+    lax.fori_loop(0, NX // 2 // PARTS, columns, 0, unroll=8)
 
 
 def rows_kernel(relative, first, count, chunks, grid_rows, addends, planes_padded, places_ref, *refs):
@@ -320,7 +329,8 @@
                     planes = pl.ds(part * planes_padded, planes_padded)
                     total = value[:planes_padded]
                     for ref in addend_refs:
-                        total = total + ref[first * (CHUNK // 2) + place, number, planes]
+                        shift = first * (CHUNK // 2) if ref.shape[0] > out_ref.shape[0] else 0
+                        total = total + ref[shift + place, number, planes]
                     out_ref[place, number, planes] = total
         return carry
 
@@ -393,17 +403,12 @@
     along = grid_cols // Z_CHIPS
     deep_at = lax.div(lax.axis_index("gy").astype(jnp.int32), jnp.int32(along))
 
-    def shift(value, senders, deep, wide):
-        moves = [
-            (z * along + y, (z + deep) * along + (y + wide) % along) for z in senders for y in range(along)
-        ]
+    def send(value, moves_z, wide):
+        moves = [(a * along + y, b * along + (y + wide) % along) for a, b in moves_z for y in range(along)]
         return lax.ppermute(value, "gy", moves)
 
-    places = jnp.stack((deep_at, lax.axis_index("gx").astype(jnp.int32)))
-    gy = lax.axis_index("gy")
-    matrices, phases = depth_tables(planes)
-    matrix = lax.dynamic_index_in_dim(jnp.asarray(matrices), gy, 0, keepdims=False)
-    phase_rows = lax.dynamic_index_in_dim(jnp.asarray(phases), gy, 0, keepdims=False)
+    places = jnp.stack((deep_at, lax.axis_index("gx").astype(jnp.int32), lax.axis_index("gy").astype(jnp.int32)))
+    matrices, phases = (jnp.asarray(table) for table in depth_tables(planes))
     column = jnp.asarray(column_tables())
     half = NX // 2
     smem = pl.BlockSpec(memory_space=pltpu.SMEM)
@@ -412,59 +417,55 @@
     def in_vmem(arrays):
         return [pltpu.with_memory_space_constraint(array, pltpu.VMEM) for array in arrays]
 
-    def condition(steps):
-        if steps == 0:
-            return None
-        return ("from", steps) if steps > 0 else ("below", Z_CHIPS + steps)
-
     def add_tiles(sources, acc):
-        conditions = [condition(steps) for steps, _ in sources]
+        conditions = [None if len(holders) == Z_CHIPS else tuple(holders) for holders, _ in sources]
         spectra = pltpu.VMEM((16 * TILE * TILE, LANES), F32)
         kept = [jax.ShapeDtypeStruct(acc_shape, F32) if acc else pltpu.VMEM(acc_shape, F32)] * PARTS
         inputs = len(sources) + 3
         *acc, token = pl.pallas_call(
             functools.partial(tiles_kernel, conditions, not acc),
             out_shape=kept + [jax.ShapeDtypeStruct((TILE, LANES), F32)],
-            in_specs=[smem] + [vmem] * (inputs - 1 + len(acc)),
+            in_specs=[smem] + [vmem] * len(sources) + [pl.BlockSpec(memory_space=pl.ANY)] * 2 + [vmem] * len(acc),
             out_specs=[vmem] * (PARTS + 1),
             input_output_aliases={inputs + part: part for part in range(PARTS)} if acc else {},
             scratch_shapes=[
                 pltpu.SMEM((len(sources), TILE, LANES), F32),
+                pltpu.VMEM(matrices.shape[1:], BF16),
+                pltpu.VMEM(phases.shape[1:], F32),
                 spectra,
                 spectra,
-                pltpu.SemaphoreType.DMA((len(sources),)),
+                pltpu.SemaphoreType.DMA((len(sources) + 2,)),
             ],
             compiler_params=params,
             cost_estimate=pl.CostEstimate(flops=0, bytes_accessed=len(sources) << 23, transcendentals=0),
             name="tiles",
-        )(places, *[array for _, array in sources], *in_hbm([matrix, phase_rows]), *in_vmem(acc))
+        )(places, *[array for _, array in sources], *in_hbm([matrices, phases]), *in_vmem(acc))
         return acc, token
 
     def after(value, token):
         return lax.optimization_barrier((value, token))[0]
 
-    held, crossed_y = {0: tiles}, {}
-    acc, waiting = [], [(0, tiles)]
-    token = None
-    for steps in range(1, Z_CHIPS + 1):
-        if steps < Z_CHIPS:
-            for signed in (steps, -steps):
-                value = held[signed - signed // steps]
-                value = value if token is None else after(value, token)
-                senders = range(steps - 1, Z_CHIPS - 1) if signed > 0 else range(1, Z_CHIPS + 1 - steps)
-                held[signed] = shift(value, senders, signed // steps, 0)
-        behind = []
-        for signed in sorted({steps - 1, 1 - steps}):
-            holders = range(signed, Z_CHIPS) if signed >= 0 else range(Z_CHIPS + signed)
-            for wide in range(1, along):
-                value = held[signed] if token is None else after(held[signed], token)
-                crossed_y[signed, wide] = shift(value, holders, 0, wide)
-                behind.append((signed, crossed_y[signed, wide]))
-        acc, token = add_tiles(waiting, acc)
-        waiting = behind
-        if steps < Z_CHIPS:
-            waiting = [(steps, held[steps]), (-steps, held[-steps])] + behind
-    acc, _ = add_tiles(waiting, acc)
+    def across(value, holders):
+        return [(holders, send(value, [(z, z) for z in holders], wide)) for wide in range(1, along)]
+
+    every, ends = range(Z_CHIPS), (0, Z_CHIPS - 1)
+    above, below = range(1, Z_CHIPS), range(Z_CHIPS - 1)
+    upper, lower = range(2, Z_CHIPS), range(Z_CHIPS - 2)
+    from_below = send(tiles, [(z, z + 1) for z in below], 0)
+    from_above = send(tiles, [(z, z - 1) for z in above], 0)
+    from_end = send(tiles, [ends, ends[::-1]], 0)
+    partner = across(tiles, every)
+    acc, token = add_tiles([(every, tiles)], [])
+    near_below, near_above = after(from_below, token), after(from_above, token)
+    from_lower = send(near_below, [(z - 1, z) for z in upper], 0)
+    from_upper = send(near_above, [(z + 1, z) for z in lower], 0)
+    partner_near = across(near_below, above) + across(near_above, below)
+    acc, token = add_tiles([(above, from_below), (below, from_above)] + partner, acc)
+    partner_end = across(after(from_end, token), ends)
+    partner_far = across(after(from_lower, token), upper) + across(after(from_upper, token), lower)
+    acc, token = add_tiles([(ends, from_end)] + partner_near, acc)
+    acc, token = add_tiles([(upper, from_lower), (lower, from_upper)] + partner_end, acc)
+    acc, _ = add_tiles(partner_far, acc)
 
     acc = pl.pallas_call(
         columns_kernel,
@@ -516,16 +517,16 @@
 
     top = grid_rows // 2
     far = arrivals(top, top // 2)
-    parts = []
+    near, crossed = [], []
     for chunk in range(chunks):
         if top == 2:
-            near = [(swap(rows_next(1, chunk, 1, []), 1), 0)]
+            near.append([(swap(rows_next(1, chunk, 1, []), 1), 0)])
         elif chunk == 0:
-            near = [(array, None) for array in arrivals(0, top // 2)]
-        parts.append([(array, chunk if place is None else place) for array, place in near])
-        parts[-1].append((swap(rows_next(top, chunk, 1, far), top), 0))
+            arrived = arrivals(0, top // 2)
+            near += [[(array, place) for array in arrived] for place in range(chunks)]
+        crossed.append(swap(rows_next(top, chunk, 1, far), top))
     kept = rows_next(0, 0, chunks, [])
-    parts = [[(kept, chunk)] + arrays for chunk, arrays in enumerate(parts)]
+    parts = [[(kept, chunk), *near[chunk], (crossed[chunk], 0)] for chunk in range(chunks)]
 
     image = None
     for chunk in range(chunks):

time: 159 us -> 158 us (level)
  the two profiles are of different devices: /device:TPU:0 before, /device:TPU:16 now
where the time goes in v11:
time: 158 us; the launch traced here: 157 us
  Pallas kernels  89.3 us (57%)
  waiting for transfers between devices  36.6 us (23%)
  starting transfers between devices  26.2 us (17%)
  local copies, waits for them, and re-layouts  5.04 us (3%)
    pallas_call x5, Pallas kernels, add_tiles(): pl.pallas_call(functools.partial(tiles_kernel, conditions, not acc), out_...  30.1 us
    pallas_call x6, Pallas kernels, rows_for(): pl.pallas_call(body, in_specs=[smem] + [vmem] * (1 + PARTS + len(addends)...  26.7 us
    ppermute x11, starting transfers between devices, send(): return lax.ppermute(value, 'gy', moves)  23.6 us
    ppermute x5, waiting for transfers between devices, swap(): lax.ppermute(value, 'gx', [(index, index ^ bit) for index in range(grid_r...  20.4 us
    pallas_call x1, Pallas kernels, on_device(): pl.pallas_call(columns_kernel, out_shape=[jax.ShapeDtypeStruct(acc_shape,...  18.6 us
    ppermute x11, waiting for transfers between devices, send(): return lax.ppermute(value, 'gy', moves)  16.2 us
    pallas_call x2, Pallas kernels, on_device(): pl.pallas_call(finish, grid=(1,), out_shape=jax.ShapeDtypeStruct((2, plan...  7.69 us
    pallas_call x1, Pallas kernels, on_device(): pl.pallas_call(functools.partial(spread_kernel, tile_rows, tile_cols, gri...  6.24 us
  transfers between devices with their start and end apart: 16, of which 5 were waited for; matrix products, arithmetic and copies ran while one was open for 0% of the time, Pallas kernels for 32%

profile of v11, /device:TPU:16, one launch (start us, length us, event | category | flops | bytes accessed | tf_op | source)
XLA Modules:
  0.0 157.5 jit_solution(10263996479367580337)
XLA Ops:
  0.0 6.2 %spread.1.refs_1_ = f32[65,16,128]{2,1,0:T(8,128)} custom-call(f32[128,2,128]{2,1,0:T(2,128)} %samples_ref.1, f32[128,3,4,128]{3,2,1,0:T(4,128)} %kernel_ref.1, s32[3,128,128]{2,1,0:T(8,128)} %bitcast.12, s32[1,128]{1,0:T(1,128)} %bitcast.13, s32[1,128]{1,0:T(1,128)} %bitcast.14), custom_call_target="tpu_custom_call" | custom-call | tf_op jit(solution)/shard_map/spread/pallas_call | solution.py:394
  8.6 3.5 %collective-permute-start = (f32[65,16,128]{2,1,0:T(8,128)}, f32[65,16,128]{2,1,0:T(8,128)S(1)}, u32[]{:S(2)}, u32[]{:S(2)}) collective-permute-start(f32[65,16,128]{2,1,0:T(8,128)} %spread.1.refs_1_), channel_id=1, source_target_pairs={{0,2},{1,3},{2,4},{3,5},{4,6},{5,7},{8,10},{9,11},{10,12},{11,13},... | collective-permute-start | bytes 1597448 | tf_op jit(solution)/shard_map/ppermute | solution.py:408
  15.5 5.9 %tiles.5 = (f32[18816,128]{1,0:T(8,128)S(1)}, f32[18816,128]{1,0:T(8,128)S(1)}, f32[18816,128]{1,0:T(8,128)S(1)}, f32[18816,128]{1,0:T(8,128)S(1)}, f32[8,128]{1,0:T(8,128)}) custom-call(s32[3]{0:T(128)S(1)} %pad_add_fusion.refs_0_, f32[65,16,128]{2,1,0:T(8,128)S(1)} %copy-done, bf16[8,48,128]{2,1,0:T(8,128)(2,1)} %constant.23.clone.refs_2_.refs_4_.refs_3_, ...), custom_call_target="tpu_custom_call" | custom-call | bytes 8388608 | tf_op jit(solution)/shard_map/tiles/pallas_call | solution.py:425
  24.7 11.1 %collective-permute-done.refs_1_ = f32[65,16,128]{2,1,0:T(8,128)S(1)} collective-permute-done((f32[65,16,128]{2,1,0:T(8,128)}, f32[65,16,128]{2,1,0:T(8,128)S(1)}, u32[]{:S(2)}, u32[]{:S(2)}) %collective-permute-start) | collective-permute-done | bytes 532512 | tf_op jit(solution)/shard_map/ppermute | solution.py:408
  35.8 3.6 %collective-permute-start.1 = (f32[65,16,128]{2,1,0:T(8,128)S(1)}, f32[65,16,128]{2,1,0:T(8,128)S(1)}, u32[]{:S(2)}, u32[]{:S(2)}) collective-permute-start(f32[65,16,128]{2,1,0:T(8,128)S(1)} %collective-permute-done.refs_1_), channel_id=1, source_target_pairs={{2,4},{3,5},{4,6},{5,7},{10,12},{11,13},{12,14},{13,15},{18,20},{1... | collective-permute-start | bytes 1597448 | tf_op jit(solution)/shard_map/ppermute | solution.py:408
  39.4 3.3 %collective-permute-start.10 = (f32[65,16,128]{2,1,0:T(8,128)S(1)}, f32[65,16,128]{2,1,0:T(8,128)S(1)}, u32[]{:S(2)}, u32[]{:S(2)}) collective-permute-start(f32[65,16,128]{2,1,0:T(8,128)S(1)} %collective-permute-done.2.refs_2_), channel_id=1, source_target_pairs={{0,1},{1,0},{2,3},{3,2},{4,5},{5,4},{8,9},{9,8},{10,11},{11,10},{1... | collective-permute-start | bytes 1597448 | tf_op jit(solution)/shard_map/ppermute | solution.py:408
  42.7 2.6 %collective-permute-start.9 = (f32[65,16,128]{2,1,0:T(8,128)S(1)}, f32[65,16,128]{2,1,0:T(8,128)S(1)}, u32[]{:S(2)}, u32[]{:S(2)}) collective-permute-start(f32[65,16,128]{2,1,0:T(8,128)S(1)} %collective-permute-done.refs_1_), channel_id=1, source_target_pairs={{2,3},{3,2},{4,5},{5,4},{6,7},{7,6},{10,11},{11,10},{12,13},{13,12... | collective-permute-start | bytes 1597448 | tf_op jit(solution)/shard_map/ppermute | solution.py:408
  45.2 8.8 %tiles.6 = (f32[18816,128]{1,0:T(8,128)S(1)}, f32[18816,128]{1,0:T(8,128)S(1)}, f32[18816,128]{1,0:T(8,128)S(1)}, f32[18816,128]{1,0:T(8,128)S(1)}, f32[8,128]{1,0:T(8,128)}) custom-call(s32[3]{0:T(128)S(1)} %pad_add_fusion.refs_0_, ...), custom_call_target="tpu_custom_call", output_to_operand_aliasing={{0}: (6, {}), {1}: (7, {}), {2}: (8, {}), {3}: (9, {})} | custom-call | bytes 25165824 | tf_op jit(solution)/shard_map/tiles/pallas_call | solution.py:425
  55.5 3.3 %collective-permute-start.4 = (f32[65,16,128]{2,1,0:T(8,128)S(1)}, f32[65,16,128]{2,1,0:T(8,128)S(1)}, u32[]{:S(2)}, u32[]{:S(2)}) collective-permute-start(f32[65,16,128]{2,1,0:T(8,128)S(1)} %collective-permute-done.1.refs_1_), channel_id=1, source_target_pairs={{4,5},{5,4},{6,7},{7,6},{12,13},{13,12},{14,15},{15,14},{20,21},{2... | collective-permute-start | bytes 1597448 | tf_op jit(solution)/shard_map/ppermute | solution.py:408
  58.8 3.2 %collective-permute-done.9.refs_2_ = f32[65,16,128]{2,1,0:T(8,128)S(1)} collective-permute-done((f32[65,16,128]{2,1,0:T(8,128)S(1)}, f32[65,16,128]{2,1,0:T(8,128)S(1)}, u32[]{:S(2)}, u32[]{:S(2)}) %collective-permute-start.9) | collective-permute-done | bytes 532512 | tf_op jit(solution)/shard_map/ppermute | solution.py:408
  61.9 6.6 %tiles.7 = (f32[18816,128]{1,0:T(8,128)S(1)}, f32[18816,128]{1,0:T(8,128)S(1)}, f32[18816,128]{1,0:T(8,128)S(1)}, f32[18816,128]{1,0:T(8,128)S(1)}, f32[8,128]{1,0:T(8,128)}) custom-call(s32[3]{0:T(128)S(1)} %pad_add_fusion.refs_0_, ...), custom_call_target="tpu_custom_call", output_to_operand_aliasing={{0}: (6, {}), {1}: (7, {}), {2}: (8, {}), {3}: (9, {})} | custom-call | bytes 25165824 | tf_op jit(solution)/shard_map/tiles/pallas_call | solution.py:425
  68.5 4.5 %tiles.8 = (f32[18816,128]{1,0:T(8,128)S(1)}, f32[18816,128]{1,0:T(8,128)S(1)}, f32[18816,128]{1,0:T(8,128)S(1)}, f32[18816,128]{1,0:T(8,128)S(1)}, f32[8,128]{1,0:T(8,128)}) custom-call(s32[3]{0:T(128)S(1)} %pad_add_fusion.refs_0_, ...), custom_call_target="tpu_custom_call", output_to_operand_aliasing={{0}: (6, {}), {1}: (7, {}), {2}: (8, {}), {3}: (9, {})} | custom-call | bytes 25165824 | tf_op jit(solution)/shard_map/tiles/pallas_call | solution.py:425
  73.1 4.3 %tiles.9 = (f32[18816,128]{1,0:T(8,128)S(1)}, f32[18816,128]{1,0:T(8,128)S(1)}, f32[18816,128]{1,0:T(8,128)S(1)}, f32[18816,128]{1,0:T(8,128)S(1)}, f32[8,128]{1,0:T(8,128)}) custom-call(s32[3]{0:T(128)S(1)} %pad_add_fusion.refs_0_, ...), custom_call_target="tpu_custom_call", output_to_operand_aliasing={{0}: (5, {}), {1}: (6, {}), {2}: (7, {}), {3}: (8, {})} | custom-call | bytes 16777216 | tf_op jit(solution)/shard_map/tiles/pallas_call | solution.py:425
  77.4 18.6 %columns.1 = (f32[18816,128]{1,0:T(8,128)S(1)}, f32[18816,128]{1,0:T(8,128)S(1)}, f32[18816,128]{1,0:T(8,128)S(1)}, f32[18816,128]{1,0:T(8,128)S(1)}) custom-call(f32[18816,128]{1,0:T(8,128)S(1)} %get-tuple-element.59.refs_0_, f32[18816,128]{1,0:T(8,128)S(1)} %get-tuple-element.60.refs_1_, ...), custom_call_target="tpu_custom_call", output_to_operand_aliasing={{0}: (0, {}), {1}: (1, {}), {2}: (2, {}), {3}: (3, {})} | custom-call | tf_op jit(solution)/shard_map/columns/pallas_call | solution.py:470
  96.0 5.5 %rows.6.refs_6_ = f32[24,3,48,128]{3,2,1,0:T(8,128)} custom-call(s32[3]{0:T(128)S(1)} %pad_add_fusion.refs_0_, f32[18816,128]{1,0:T(8,128)S(1)} %get-tuple-element.63.refs_1_, f32[18816,128]{1,0:T(8,128)S(1)} %get-tuple-element.64.refs_2_, f32[18816,128]{1,0:T(8,128)S(1)} %get-tuple-element.65.refs_3_, f32[18816,128]{1,0:T(8,128)S(1)} %get-tuple-element.66.refs_4_, ...), custom_call_target="tpu_custom_call" | custom-call | flops 1 | bytes 1 | tf_op jit(solution)/shard_map/rows/pallas_call | solution.py:490
  101.5 3.6 %rows.7.refs_7_ = f32[12,3,48,128]{3,2,1,0:T(8,128)} custom-call(s32[3]{0:T(128)S(1)} %pad_add_fusion.refs_0_, f32[18816,128]{1,0:T(8,128)S(1)} %get-tuple-element.63.refs_1_, f32[18816,128]{1,0:T(8,128)S(1)} %get-tuple-element.64.refs_2_, f32[18816,128]{1,0:T(8,128)S(1)} %get-tuple-element.65.refs_3_, f32[18816,128]{1,0:T(8,128)S(1)} %get-tuple-element.66.refs_4_, ...), custom_call_target="tpu_custom_call" | custom-call | flops 1 | bytes 1 | tf_op jit(solution)/shard_map/rows/pallas_call | solution.py:490
  106.8 4.2 %rows.8.refs_6_ = f32[12,3,48,128]{3,2,1,0:T(8,128)} custom-call(s32[3]{0:T(128)S(1)} %pad_add_fusion.refs_0_, f32[18816,128]{1,0:T(8,128)S(1)} %get-tuple-element.63.refs_1_, f32[18816,128]{1,0:T(8,128)S(1)} %get-tuple-element.64.refs_2_, f32[18816,128]{1,0:T(8,128)S(1)} %get-tuple-element.65.refs_3_, f32[18816,128]{1,0:T(8,128)S(1)} %get-tuple-element.66.refs_4_, ...), custom_call_target="tpu_custom_call" | custom-call | flops 1 | bytes 1 | tf_op jit(solution)/shard_map/rows/pallas_call | solution.py:490
  112.4 3.6 %rows.9.refs_7_ = f32[12,3,48,128]{3,2,1,0:T(8,128)} custom-call(s32[3]{0:T(128)S(1)} %pad_add_fusion.refs_0_, f32[18816,128]{1,0:T(8,128)S(1)} %get-tuple-element.63.refs_1_, f32[18816,128]{1,0:T(8,128)S(1)} %get-tuple-element.64.refs_2_, f32[18816,128]{1,0:T(8,128)S(1)} %get-tuple-element.65.refs_3_, f32[18816,128]{1,0:T(8,128)S(1)} %get-tuple-element.66.refs_4_, ...), custom_call_target="tpu_custom_call" | custom-call | flops 1 | bytes 1 | tf_op jit(solution)/shard_map/rows/pallas_call | solution.py:490
  116.0 4.3 %rows.10.refs_6_ = f32[12,3,48,128]{3,2,1,0:T(8,128)} custom-call(s32[3]{0:T(128)S(1)} %pad_add_fusion.refs_0_, f32[18816,128]{1,0:T(8,128)S(1)} %get-tuple-element.63.refs_1_, f32[18816,128]{1,0:T(8,128)S(1)} %get-tuple-element.64.refs_2_, f32[18816,128]{1,0:T(8,128)S(1)} %get-tuple-element.65.refs_3_, f32[18816,128]{1,0:T(8,128)S(1)} %get-tuple-element.66.refs_4_, ...), custom_call_target="tpu_custom_call" | custom-call | flops 1 | bytes 1 | tf_op jit(solution)/shard_map/rows/pallas_call | solution.py:490
  121.0 5.6 %rows.11.refs_0_ = f32[24,3,48,128]{3,2,1,0:T(8,128)} custom-call(s32[3]{0:T(128)S(1)} %pad_add_fusion.refs_0_, f32[18816,128]{1,0:T(8,128)S(1)} %get-tuple-element.63.refs_1_, f32[18816,128]{1,0:T(8,128)S(1)} %get-tuple-element.64.refs_2_, f32[18816,128]{1,0:T(8,128)S(1)} %get-tuple-element.65.refs_3_, f32[18816,128]{1,0:T(8,128)S(1)} %get-tuple-element.66.refs_4_, ...), custom_call_target="tpu_custom_call" | custom-call | flops 1 | bytes 1 | tf_op jit(solution)/shard_map/rows/pallas_call | solution.py:490
  126.6 7.2 %collective-permute-done.15.refs_2_ = f32[12,3,48,128]{3,2,1,0:T(8,128)S(1)} collective-permute-done((f32[12,3,48,128]{3,2,1,0:T(8,128)}, f32[12,3,48,128]{3,2,1,0:T(8,128)S(1)}, u32[]{:S(2)}, u32[]{:S(2)}) %collective-permute-start.15) | collective-permute-done | bytes 884768 | tf_op jit(solution)/shard_map/ppermute | solution.py:501
  134.7 3.8 %finish.2.refs_7_ = f32[2,24,48,192]{3,2,1,0:T(8,128)} custom-call(f32[24,3,48,128]{3,2,1,0:T(8,128)} %rows.11.refs_0_, f32[12,3,48,128]{3,2,1,0:T(8,128)} %copy-done.9, f32[12,3,48,128]{3,2,1,0:T(8,128)} %copy-done.10, bf16[512,192]{1,0:T(8,128)(2,1)S(1)} %copy-done.1, f32[1,192]{1,0:T(1,128)S(1)} %bitcast.8, f32[1,48]{1,0:T(1,128)S(1)} %bitcast.10, ...), custom_call_target="tpu_custom_call" | custom-call | tf_op jit(solution)/shard_map/finish/pallas_call | solution.py:538
  138.5 13.2 %collective-permute-done.13.refs_2_ = f32[12,3,48,128]{3,2,1,0:T(8,128)S(1)} collective-permute-done((f32[12,3,48,128]{3,2,1,0:T(8,128)}, f32[12,3,48,128]{3,2,1,0:T(8,128)S(1)}, u32[]{:S(2)}, u32[]{:S(2)}) %collective-permute-start.13) | collective-permute-done | bytes 884768 | tf_op jit(solution)/shard_map/ppermute | solution.py:501
  153.6 3.8 %finish.3 = f32[2,24,48,192]{3,2,1,0:T(8,128)} custom-call(f32[24,3,48,128]{3,2,1,0:T(8,128)} %rows.11.refs_0_, f32[12,3,48,128]{3,2,1,0:T(8,128)} %copy-done.8, f32[12,3,48,128]{3,2,1,0:T(8,128)} %copy-done.7, bf16[512,192]{1,0:T(8,128)(2,1)S(1)} %copy-done.1, f32[1,192]{1,0:T(1,128)S(1)} %bitcast.9, ...), custom_call_target="tpu_custom_call", output_to_operand_aliasing={{}: (7, {})} | custom-call | tf_op jit(solution)/shard_map/finish/pallas_call | solution.py:538
  (46 shorter events, 17.0 us)
Async XLA Ops:
  6.2 17.1 %collective-permute-start.2 = (f32[65,16,128]{2,1,0:T(8,128)}, f32[65,16,128]{2,1,0:T(8,128)S(1)}, u32[]{:S(2)}, u32[]{:S(2)}) collective-permute-start(f32[65,16,128]{2,1,0:T(8,128)} %spread.1.refs_1_), channel_id=1, source_target_pairs={{2,0},{3,1},{4,2},{5,3},{6,4},{7,5},{10,8},{11,9},{12,10},{13,11},... | collective-permute-start | bytes 1597448 | tf_op jit(solution)/shard_map/ppermute | solution.py:408
  8.6 27.2 %collective-permute-start = (f32[65,16,128]{2,1,0:T(8,128)}, f32[65,16,128]{2,1,0:T(8,128)S(1)}, u32[]{:S(2)}, u32[]{:S(2)}) collective-permute-start(f32[65,16,128]{2,1,0:T(8,128)} %spread.1.refs_1_), channel_id=1, source_target_pairs={{0,2},{1,3},{2,4},{3,5},{4,6},{5,7},{8,10},{9,11},{10,12},{11,13},... | collective-permute-start | bytes 1597448 | tf_op jit(solution)/shard_map/ppermute | solution.py:408
  12.1 30.5 %collective-permute-start.3 = (f32[65,16,128]{2,1,0:T(8,128)}, f32[65,16,128]{2,1,0:T(8,128)S(1)}, u32[]{:S(2)}, u32[]{:S(2)}) collective-permute-start(f32[65,16,128]{2,1,0:T(8,128)} %spread.1.refs_1_), channel_id=1, source_target_pairs={{0,1},{1,0},{2,3},{3,2},{4,5},{5,4},{6,7},{7,6},{8,9},{9,8},{10,11... | collective-permute-start | bytes 1597448 | tf_op jit(solution)/shard_map/ppermute | solution.py:408
  13.7 40.3 %collective-permute-start.7 = (f32[65,16,128]{2,1,0:T(8,128)}, f32[65,16,128]{2,1,0:T(8,128)S(1)}, u32[]{:S(2)}, u32[]{:S(2)}) collective-permute-start(f32[65,16,128]{2,1,0:T(8,128)} %spread.1.refs_1_), channel_id=1, source_target_pairs={{0,6},{1,7},{6,0},{7,1},{8,14},{9,15},{14,8},{15,9},{16,22},{17,23... | collective-permute-start | bytes 1597448 | tf_op jit(solution)/shard_map/ppermute | solution.py:408
  14.5 1.0 copy-start
  23.3 31.4 %collective-permute-start.5 = (f32[65,16,128]{2,1,0:T(8,128)S(1)}, f32[65,16,128]{2,1,0:T(8,128)S(1)}, u32[]{:S(2)}, u32[]{:S(2)}) collective-permute-start(f32[65,16,128]{2,1,0:T(8,128)S(1)} %collective-permute-done.2.refs_2_), channel_id=1, source_target_pairs={{2,0},{3,1},{4,2},{5,3},{10,8},{11,9},{12,10},{13,11},{18,16},{19,... | collective-permute-start | bytes 1597448 | tf_op jit(solution)/shard_map/ppermute | solution.py:408
  35.8 19.7 %collective-permute-start.1 = (f32[65,16,128]{2,1,0:T(8,128)S(1)}, f32[65,16,128]{2,1,0:T(8,128)S(1)}, u32[]{:S(2)}, u32[]{:S(2)}) collective-permute-start(f32[65,16,128]{2,1,0:T(8,128)S(1)} %collective-permute-done.refs_1_), channel_id=1, source_target_pairs={{2,4},{3,5},{4,6},{5,7},{10,12},{11,13},{12,14},{13,15},{18,20},{1... | collective-permute-start | bytes 1597448 | tf_op jit(solution)/shard_map/ppermute | solution.py:408
  39.4 19.4 %collective-permute-start.10 = (f32[65,16,128]{2,1,0:T(8,128)S(1)}, f32[65,16,128]{2,1,0:T(8,128)S(1)}, u32[]{:S(2)}, u32[]{:S(2)}) collective-permute-start(f32[65,16,128]{2,1,0:T(8,128)S(1)} %collective-permute-done.2.refs_2_), channel_id=1, source_target_pairs={{0,1},{1,0},{2,3},{3,2},{4,5},{5,4},{8,9},{9,8},{10,11},{11,10},{1... | collective-permute-start | bytes 1597448 | tf_op jit(solution)/shard_map/ppermute | solution.py:408
  42.7 19.3 %collective-permute-start.9 = (f32[65,16,128]{2,1,0:T(8,128)S(1)}, f32[65,16,128]{2,1,0:T(8,128)S(1)}, u32[]{:S(2)}, u32[]{:S(2)}) collective-permute-start(f32[65,16,128]{2,1,0:T(8,128)S(1)} %collective-permute-done.refs_1_), channel_id=1, source_target_pairs={{2,3},{3,2},{4,5},{5,4},{6,7},{7,6},{10,11},{11,10},{12,13},{13,12... | collective-permute-start | bytes 1597448 | tf_op jit(solution)/shard_map/ppermute | solution.py:408
  54.0 14.5 %collective-permute-start.8 = (f32[65,16,128]{2,1,0:T(8,128)S(1)}, f32[65,16,128]{2,1,0:T(8,128)S(1)}, u32[]{:S(2)}, u32[]{:S(2)}) collective-permute-start(f32[65,16,128]{2,1,0:T(8,128)S(1)} %collective-permute-done.7.refs_1_), channel_id=1, source_target_pairs={{0,1},{1,0},{6,7},{7,6},{8,9},{9,8},{14,15},{15,14},{16,17},{17,16... | collective-permute-start | bytes 1597448 | tf_op jit(solution)/shard_map/ppermute | solution.py:408
  54.8 18.3 %collective-permute-start.6 = (f32[65,16,128]{2,1,0:T(8,128)S(1)}, f32[65,16,128]{2,1,0:T(8,128)S(1)}, u32[]{:S(2)}, u32[]{:S(2)}) collective-permute-start(f32[65,16,128]{2,1,0:T(8,128)S(1)} %collective-permute-done.5.refs_2_), channel_id=1, source_target_pairs={{0,1},{1,0},{2,3},{3,2},{8,9},{9,8},{10,11},{11,10},{16,17},{17,16... | collective-permute-start | bytes 1597448 | tf_op jit(solution)/shard_map/ppermute | solution.py:408
  55.5 17.6 %collective-permute-start.4 = (f32[65,16,128]{2,1,0:T(8,128)S(1)}, f32[65,16,128]{2,1,0:T(8,128)S(1)}, u32[]{:S(2)}, u32[]{:S(2)}) collective-permute-start(f32[65,16,128]{2,1,0:T(8,128)S(1)} %collective-permute-done.1.refs_1_), channel_id=1, source_target_pairs={{4,5},{5,4},{6,7},{7,6},{12,13},{13,12},{14,15},{15,14},{20,21},{2... | collective-permute-start | bytes 1597448 | tf_op jit(solution)/shard_map/ppermute | solution.py:408
  101.5 4.1 %collective-permute-start.11 = (f32[24,3,48,128]{3,2,1,0:T(8,128)}, f32[24,3,48,128]{3,2,1,0:T(8,128)S(1)}, u32[]{:S(2)}, u32[]{:S(2)}) collective-permute-start(f32[24,3,48,128]{3,2,1,0:T(8,128)} %rows.6.refs_6_), channel_id=1, source_target_pairs={{0,8},{8,0},{16,24},{24,16},{1,9},{9,1},{17,25},{25,17},{2,10},{10... | collective-permute-start | bytes 5308424 | tf_op jit(solution)/shard_map/ppermute | solution.py:501
  105.1 21.5 %collective-permute-start.14 = (f32[12,3,48,128]{3,2,1,0:T(8,128)}, f32[12,3,48,128]{3,2,1,0:T(8,128)S(1)}, u32[]{:S(2)}, u32[]{:S(2)}) collective-permute-start(f32[12,3,48,128]{3,2,1,0:T(8,128)} %rows.7.refs_7_), channel_id=1, source_target_pairs={{0,8},{8,0},{16,24},{24,16},{1,9},{9,1},{17,25},{25,17},{2,10},{10... | collective-permute-start | bytes 2654216 | tf_op jit(solution)/shard_map/ppermute | solution.py:501
  105.6 1.2 copy-start.5
  111.0 22.7 %collective-permute-start.15 = (f32[12,3,48,128]{3,2,1,0:T(8,128)}, f32[12,3,48,128]{3,2,1,0:T(8,128)S(1)}, u32[]{:S(2)}, u32[]{:S(2)}) collective-permute-start(f32[12,3,48,128]{3,2,1,0:T(8,128)} %rows.8.refs_6_), channel_id=1, source_target_pairs={{0,16},{8,24},{16,0},{24,8},{1,17},{9,25},{17,1},{25,9},{2,18},{10... | collective-permute-start | bytes 2654216 | tf_op jit(solution)/shard_map/ppermute | solution.py:501
  116.0 5.0 %copy-start.6 = (f32[12,3,48,128]{3,2,1,0:T(8,128)S(1)}, f32[12,3,48,128]{3,2,1,0:T(8,128)}, u32[]{:S(2)}) copy-start(f32[12,3,48,128]{3,2,1,0:T(8,128)} %rows.9.refs_7_) | copy-start | bytes 2654212
  120.2 14.4 %copy-start.1 = (bf16[512,192]{1,0:T(8,128)(2,1)S(1)}, bf16[512,192]{1,0:T(8,128)(2,1)}, u32[]{:S(2)}) copy-start(bf16[512,192]{1,0:T(8,128)(2,1)} %constant.27.clone.refs_3_) | copy-start | bytes 589828
  120.2 14.4 %copy-start.2 = (f32[192]{0:T(256)S(1)}, f32[192]{0:T(256)}, u32[]{:S(2)}) copy-start(f32[192]{0:T(256)} %param.19) | copy-start | bytes 2308
  120.2 14.4 %copy-start.3 = (f32[48]{0:T(128)S(1)}, f32[48]{0:T(128)}, u32[]{:S(2)}) copy-start(f32[48]{0:T(128)} %param.20) | copy-start | bytes 580
  120.2 14.4 %copy-start.4 = (f32[24]{0:T(128)S(1)}, f32[24]{0:T(128)}, u32[]{:S(2)}) copy-start(f32[24]{0:T(128)} %refs_6_.3) | copy-start | bytes 292
  120.2 31.5 %collective-permute-start.13 = (f32[12,3,48,128]{3,2,1,0:T(8,128)}, f32[12,3,48,128]{3,2,1,0:T(8,128)S(1)}, u32[]{:S(2)}, u32[]{:S(2)}) collective-permute-start(f32[12,3,48,128]{3,2,1,0:T(8,128)} %rows.10.refs_6_), channel_id=1, source_target_pairs={{0,16},{8,24},{16,0},{24,8},{1,17},{9,25},{17,1},{25,9},{2,18},{10... | collective-permute-start | bytes 2654216 | tf_op jit(solution)/shard_map/ppermute | solution.py:501
  121.0 30.8 %collective-permute-start.12 = (f32[12,3,48,128]{3,2,1,0:T(8,128)S(1)}, f32[12,3,48,128]{3,2,1,0:T(8,128)S(1)}, u32[]{:S(2)}, u32[]{:S(2)}) collective-permute-start(f32[12,3,48,128]{3,2,1,0:T(8,128)S(1)} %copy-done.6), channel_id=1, source_target_pairs={{0,8},{8,0},{16,24},{24,16},{1,9},{9,1},{17,25},{25,17},{2,10},{10... | collective-permute-start | bytes 2654216 | tf_op jit(solution)/shard_map/ppermute | solution.py:501
  126.6 7.2 %copy-start.9 = (f32[12,3,48,128]{3,2,1,0:T(8,128)}, f32[12,3,48,128]{3,2,1,0:T(8,128)S(1)}, u32[]{:S(2)}) copy-start(f32[12,3,48,128]{3,2,1,0:T(8,128)S(1)} %collective-permute-done.14.refs_1_) | copy-start | bytes 2654212
  (3 other events, 2.8 us)

commit v12 on v11

--- a/solution.py
+++ b/solution.py
@@ -71,7 +71,7 @@
     for residue in range(3):
         cos, sin = waves(3 * np.arange(NY // 6) + residue - NY // 4, np.arange(third) - NY // 2, NY)
         high, low = halves(np.concatenate((cos, sin)) / math.sqrt(NY))
-        out.append(np.concatenate((high, high, low), axis=1))
+        out.append(np.block([[high, high], [low, np.zeros_like(low)]]))
     return np.stack(out)
 
 
@@ -159,7 +159,7 @@
         out_ref[pair] = jnp.where(left, piece[: 2 * TILE], piece[2 * TILE :])
         return carry
 
-    lax.fori_loop(0, blocks // 2, pair_body, 0, unroll=4)
+    lax.fori_loop(0, blocks // 2, pair_body, 0, unroll=8)
     out_ref[blocks // 2] = jnp.broadcast_to(codes, (2 * TILE, LANES))
 
 
@@ -260,7 +260,7 @@
     column_ref = refs[PARTS]
     acc_refs = refs[PARTS + 1 :]
     third = NY // 3
-    rows = column_ref.shape[1] // 2
+    rows = column_ref.shape[1] // 4
     turn = jnp.where(lax.broadcasted_iota(jnp.int32, (1, LANES), 1) < LANES // 2, -1.0, 1.0)
 
     def columns(step, carry):
@@ -278,8 +278,9 @@
             for residue in range(3):
                 high, low = split(jnp.concatenate(folded[residue], axis=1))
                 product = jnp.dot(
-                    column_ref[residue], jnp.concatenate((high, low, high), axis=0), preferred_element_type=F32
+                    column_ref[residue], jnp.concatenate((high, low), axis=0), preferred_element_type=F32
                 )
+                product = product[: 2 * rows] + product[2 * rows :]
                 for side, ref in enumerate(acc_refs[pair : pair + 2]):
                     lanes = slice(side * LANES, (side + 1) * LANES)
                     ref[pl.ds(start + residue * rows, rows), :] = (
@@ -448,24 +449,25 @@
     def across(value, holders):
         return [(holders, send(value, [(z, z) for z in holders], wide)) for wide in range(1, along)]
 
-    every, ends = range(Z_CHIPS), (0, Z_CHIPS - 1)
-    above, below = range(1, Z_CHIPS), range(Z_CHIPS - 1)
-    upper, lower = range(2, Z_CHIPS), range(Z_CHIPS - 2)
-    from_below = send(tiles, [(z, z + 1) for z in below], 0)
-    from_above = send(tiles, [(z, z - 1) for z in above], 0)
-    from_end = send(tiles, [ends, ends[::-1]], 0)
-    partner = across(tiles, every)
-    acc, token = add_tiles([(every, tiles)], [])
-    near_below, near_above = after(from_below, token), after(from_above, token)
-    from_lower = send(near_below, [(z - 1, z) for z in upper], 0)
-    from_upper = send(near_above, [(z + 1, z) for z in lower], 0)
-    partner_near = across(near_below, above) + across(near_above, below)
-    acc, token = add_tiles([(above, from_below), (below, from_above)] + partner, acc)
-    partner_end = across(after(from_end, token), ends)
-    partner_far = across(after(from_lower, token), upper) + across(after(from_upper, token), lower)
-    acc, token = add_tiles([(ends, from_end)] + partner_near, acc)
-    acc, token = add_tiles([(upper, from_lower), (lower, from_upper)] + partner_end, acc)
-    acc, _ = add_tiles(partner_far, acc)
+    every = range(Z_CHIPS)
+    passed = {1: tiles, -1: tiles}
+    arrived, token, acc = [(every, tiles)], None, []
+    for steps in range(1, Z_CHIPS + 1):
+        partners = []
+        if steps == 1:
+            partners += across(tiles, every)
+        else:
+            partners += [held for holders, array in arrived[:2] for held in across(after(array, token), holders)]
+        moved = []
+        if steps < Z_CHIPS:
+            for way in (1, -1):
+                moves = [(z, z + way) for z in every if 0 <= z + way < Z_CHIPS and 0 <= z - way * (steps - 1) < Z_CHIPS]
+                value = passed[way] if token is None else after(passed[way], token)
+                passed[way] = send(value, moves, 0)
+                moved.append(([to for _, to in moves], passed[way]))
+        acc, token = add_tiles(arrived, acc)
+        arrived = moved + partners
+    acc, _ = add_tiles(arrived, acc)
 
     acc = pl.pallas_call(
         columns_kernel,
@@ -495,7 +497,7 @@
             compiler_params=params,
             cost_estimate=pl.CostEstimate(flops=1, bytes_accessed=1, transcendentals=0),
             name="rows",
-        )(places, *in_vmem(acc), *in_hbm([row_table] + addends + after))
+        )(places, *in_vmem(acc), *in_hbm([row_table]), *addends, *in_hbm(after))
 
     def swap(value, bit):
         return lax.ppermute(value, "gx", [(index, index ^ bit) for index in range(grid_rows)])
@@ -555,7 +557,7 @@
             compiler_params=params,
             name="finish",
         )(
-            *in_hbm([array for array, _ in parts[chunk]]),
+            *[array for array, _ in parts[chunk]],
             jnp.asarray(order_tables()),
             deapod_first[None, :],
             deapod_second[None, :],

time: 158 us -> 150 us (0.949); the launches traced: 157 us -> 147 us
  waiting for transfers between devices: 36.6 us -> 30.5 us
  Pallas kernels: 89.3 us -> 84.2 us
  starting transfers between devices: 26.2 us -> 29.3 us
  local copies, waits for them, and re-layouts: 5.04 us -> 2.53 us
    ppermute x11 -> x13, waiting for transfers between devices: 16.2 us -> 8.91 us  [send(): return lax.ppermute(value, 'gy', moves)]
    ppermute x11 -> x13, starting transfers between devices: 23.6 us -> 26.7 us  [send(): return lax.ppermute(value, 'gy', moves)]
    unnamed x22 -> x12, local copies, waits for them, and re-layouts: 5.04 us -> 2.53 us
    pallas_call x2, Pallas kernels: 7.69 us -> 5.71 us  [on_device(): pl.pallas_call(finish, grid=(1,), out_shape=jax.ShapeDtypeStruct((2, plan...]
  transfers between devices with their start and end apart: 16 -> 18, of which waited for: 5 -> 4; matrix products, arithmetic and copies ran while one was open for 0% -> 0% of each run, Pallas kernels for 32% -> 35%
where the time goes in v12:
time: 150 us; the launch traced here: 147 us
  Pallas kernels  84.2 us (56%)
  waiting for transfers between devices  30.5 us (20%)
  starting transfers between devices  29.3 us (20%)
  local copies, waits for them, and re-layouts  2.53 us (2%)
    pallas_call x5, Pallas kernels, add_tiles(): pl.pallas_call(functools.partial(tiles_kernel, conditions, not acc), out_...  30.1 us
    ppermute x13, starting transfers between devices, send(): return lax.ppermute(value, 'gy', moves)  26.7 us
    pallas_call x6, Pallas kernels, rows_for(): pl.pallas_call(body, in_specs=[smem] + [vmem] * (1 + PARTS + len(addends)...  25.4 us
    ppermute x5, waiting for transfers between devices, swap(): lax.ppermute(value, 'gx', [(index, index ^ bit) for index in range(grid_r...  21.6 us
    pallas_call x1, Pallas kernels, on_device(): pl.pallas_call(columns_kernel, out_shape=[jax.ShapeDtypeStruct(acc_shape,...  17.7 us
    ppermute x13, waiting for transfers between devices, send(): return lax.ppermute(value, 'gy', moves)  8.91 us
    pallas_call x2, Pallas kernels, on_device(): pl.pallas_call(finish, grid=(1,), out_shape=jax.ShapeDtypeStruct((2, plan...  5.71 us
    pallas_call x1, Pallas kernels, on_device(): pl.pallas_call(functools.partial(spread_kernel, tile_rows, tile_cols, gri...  5.23 us
  transfers between devices with their start and end apart: 18, of which 4 were waited for; matrix products, arithmetic and copies ran while one was open for 0% of the time, Pallas kernels for 35%

profile of v12, /device:TPU:16, one launch (start us, length us, event | category | flops | bytes accessed | tf_op | source)
XLA Modules:
  0.0 146.8 jit_solution(3986016897629837215)
XLA Ops:
  0.0 5.2 %spread.1.refs_1_ = f32[65,16,128]{2,1,0:T(8,128)} custom-call(f32[128,2,128]{2,1,0:T(2,128)} %samples_ref.1, f32[128,3,4,128]{3,2,1,0:T(4,128)} %kernel_ref.1, s32[3,128,128]{2,1,0:T(8,128)} %bitcast.12, s32[1,128]{1,0:T(1,128)} %bitcast.13, s32[1,128]{1,0:T(1,128)} %bitcast.14), custom_call_target="tpu_custom_call" | custom-call | tf_op jit(solution)/shard_map/spread/pallas_call | solution.py:395
  5.2 3.5 %collective-permute-start = (f32[65,16,128]{2,1,0:T(8,128)}, f32[65,16,128]{2,1,0:T(8,128)S(1)}, u32[]{:S(2)}, u32[]{:S(2)}) collective-permute-start(f32[65,16,128]{2,1,0:T(8,128)} %spread.1.refs_1_), channel_id=1, source_target_pairs={{0,2},{1,3},{2,4},{3,5},{4,6},{5,7},{8,10},{9,11},{10,12},{11,13},... | collective-permute-start | bytes 1597448 | tf_op jit(solution)/shard_map/ppermute | solution.py:409
  8.7 2.4 %collective-permute-start.2 = (f32[65,16,128]{2,1,0:T(8,128)}, f32[65,16,128]{2,1,0:T(8,128)S(1)}, u32[]{:S(2)}, u32[]{:S(2)}) collective-permute-start(f32[65,16,128]{2,1,0:T(8,128)} %spread.1.refs_1_), channel_id=1, source_target_pairs={{2,0},{3,1},{4,2},{5,3},{6,4},{7,5},{10,8},{11,9},{12,10},{13,11},... | collective-permute-start | bytes 1597448 | tf_op jit(solution)/shard_map/ppermute | solution.py:409
  13.8 5.9 %tiles.5 = (f32[18816,128]{1,0:T(8,128)S(1)}, f32[18816,128]{1,0:T(8,128)S(1)}, f32[18816,128]{1,0:T(8,128)S(1)}, f32[18816,128]{1,0:T(8,128)S(1)}, f32[8,128]{1,0:T(8,128)}) custom-call(s32[3]{0:T(128)S(1)} %pad_add_fusion.refs_0_, f32[65,16,128]{2,1,0:T(8,128)S(1)} %copy-done.1, bf16[8,48,128]{2,1,0:T(8,128)(2,1)} %constant.23.clone.refs_2_.refs_4_.refs_5_.refs_3_, ...), custom_call_target="tpu_custom_call" | custom-call | bytes 8388608 | tf_op jit(solution)/shard_map/tiles/pallas_call | solution.py:426
  21.2 3.5 %collective-permute-start.1 = (f32[65,16,128]{2,1,0:T(8,128)S(1)}, f32[65,16,128]{2,1,0:T(8,128)S(1)}, u32[]{:S(2)}, u32[]{:S(2)}) collective-permute-start(f32[65,16,128]{2,1,0:T(8,128)S(1)} %collective-permute-done.refs_1_), channel_id=1, source_target_pairs={{2,4},{3,5},{4,6},{5,7},{10,12},{11,13},{12,14},{13,15},{18,20},{1... | collective-permute-start | bytes 1597448 | tf_op jit(solution)/shard_map/ppermute | solution.py:409
  24.7 2.4 %collective-permute-start.5 = (f32[65,16,128]{2,1,0:T(8,128)S(1)}, f32[65,16,128]{2,1,0:T(8,128)S(1)}, u32[]{:S(2)}, u32[]{:S(2)}) collective-permute-start(f32[65,16,128]{2,1,0:T(8,128)S(1)} %collective-permute-done.2.refs_2_), channel_id=1, source_target_pairs={{2,0},{3,1},{4,2},{5,3},{10,8},{11,9},{12,10},{13,11},{18,16},{19,... | collective-permute-start | bytes 1597448 | tf_op jit(solution)/shard_map/ppermute | solution.py:409
  27.1 3.4 %collective-permute-start.6 = (f32[65,16,128]{2,1,0:T(8,128)S(1)}, f32[65,16,128]{2,1,0:T(8,128)S(1)}, u32[]{:S(2)}, u32[]{:S(2)}) collective-permute-start(f32[65,16,128]{2,1,0:T(8,128)S(1)} %collective-permute-done.refs_1_), channel_id=1, source_target_pairs={{2,3},{3,2},{4,5},{5,4},{6,7},{7,6},{10,11},{11,10},{12,13},{13,12... | collective-permute-start | bytes 1597448 | tf_op jit(solution)/shard_map/ppermute | solution.py:409
  30.5 2.4 %collective-permute-start.7 = (f32[65,16,128]{2,1,0:T(8,128)S(1)}, f32[65,16,128]{2,1,0:T(8,128)S(1)}, u32[]{:S(2)}, u32[]{:S(2)}) collective-permute-start(f32[65,16,128]{2,1,0:T(8,128)S(1)} %collective-permute-done.2.refs_2_), channel_id=1, source_target_pairs={{0,1},{1,0},{2,3},{3,2},{4,5},{5,4},{8,9},{9,8},{10,11},{11,10},{1... | collective-permute-start | bytes 1597448 | tf_op jit(solution)/shard_map/ppermute | solution.py:409
  32.9 8.8 %tiles.6 = (f32[18816,128]{1,0:T(8,128)S(1)}, f32[18816,128]{1,0:T(8,128)S(1)}, f32[18816,128]{1,0:T(8,128)S(1)}, f32[18816,128]{1,0:T(8,128)S(1)}, f32[8,128]{1,0:T(8,128)}) custom-call(s32[3]{0:T(128)S(1)} %pad_add_fusion.refs_0_, ...), custom_call_target="tpu_custom_call", output_to_operand_aliasing={{0}: (6, {}), {1}: (7, {}), {2}: (8, {}), {3}: (9, {})} | custom-call | bytes 25165824 | tf_op jit(solution)/shard_map/tiles/pallas_call | solution.py:426
  43.8 3.4 %collective-permute-start.11 = (f32[65,16,128]{2,1,0:T(8,128)S(1)}, f32[65,16,128]{2,1,0:T(8,128)S(1)}, u32[]{:S(2)}, u32[]{:S(2)}) collective-permute-start(f32[65,16,128]{2,1,0:T(8,128)S(1)} %collective-permute-done.1.refs_1_), channel_id=1, source_target_pairs={{4,5},{5,4},{6,7},{7,6},{12,13},{13,12},{14,15},{15,14},{20,21},{2... | collective-permute-start | bytes 1597448 | tf_op jit(solution)/shard_map/ppermute | solution.py:409
  48.0 7.4 %collective-permute-done.7.refs_4_ = f32[65,16,128]{2,1,0:T(8,128)S(1)} collective-permute-done((f32[65,16,128]{2,1,0:T(8,128)S(1)}, f32[65,16,128]{2,1,0:T(8,128)S(1)}, u32[]{:S(2)}, u32[]{:S(2)}) %collective-permute-start.7) | collective-permute-done | bytes 532512 | tf_op jit(solution)/shard_map/ppermute | solution.py:409
  55.4 8.9 %tiles.7 = (f32[18816,128]{1,0:T(8,128)S(1)}, f32[18816,128]{1,0:T(8,128)S(1)}, f32[18816,128]{1,0:T(8,128)S(1)}, f32[18816,128]{1,0:T(8,128)S(1)}, f32[8,128]{1,0:T(8,128)}) custom-call(s32[3]{0:T(128)S(1)} %pad_add_fusion.refs_0_, ...), custom_call_target="tpu_custom_call", output_to_operand_aliasing={{0}: (7, {}), {1}: (8, {}), {2}: (9, {}), {3}: (10, {})} | custom-call | bytes 33554432 | tf_op jit(solution)/shard_map/tiles/pallas_call | solution.py:426
  65.7 4.4 %tiles.8 = (f32[18816,128]{1,0:T(8,128)S(1)}, f32[18816,128]{1,0:T(8,128)S(1)}, f32[18816,128]{1,0:T(8,128)S(1)}, f32[18816,128]{1,0:T(8,128)S(1)}, f32[8,128]{1,0:T(8,128)}) custom-call(s32[3]{0:T(128)S(1)} %pad_add_fusion.refs_0_, ...), custom_call_target="tpu_custom_call", output_to_operand_aliasing={{0}: (7, {}), {1}: (8, {}), {2}: (9, {}), {3}: (10, {})} | custom-call | bytes 33554432 | tf_op jit(solution)/shard_map/tiles/pallas_call | solution.py:426
  72.3 17.7 %columns.1 = (f32[18816,128]{1,0:T(8,128)S(1)}, f32[18816,128]{1,0:T(8,128)S(1)}, f32[18816,128]{1,0:T(8,128)S(1)}, f32[18816,128]{1,0:T(8,128)S(1)}) custom-call(f32[18816,128]{1,0:T(8,128)S(1)} %get-tuple-element.63.refs_0_, f32[18816,128]{1,0:T(8,128)S(1)} %get-tuple-element.64.refs_1_, ...), custom_call_target="tpu_custom_call", output_to_operand_aliasing={{0}: (0, {}), {1}: (1, {}), {2}: (2, {}), {3}: (3, {})} | custom-call | tf_op jit(solution)/shard_map/columns/pallas_call | solution.py:472
  90.0 5.5 %rows.6.refs_6_ = f32[24,3,48,128]{3,2,1,0:T(8,128)} custom-call(s32[3]{0:T(128)S(1)} %pad_add_fusion.refs_0_, f32[18816,128]{1,0:T(8,128)S(1)} %get-tuple-element.67.refs_1_, f32[18816,128]{1,0:T(8,128)S(1)} %get-tuple-element.68.refs_2_, f32[18816,128]{1,0:T(8,128)S(1)} %get-tuple-element.69.refs_3_, f32[18816,128]{1,0:T(8,128)S(1)} %get-tuple-element.70.refs_4_, ...), custom_call_target="tpu_custom_call" | custom-call | flops 1 | bytes 1 | tf_op jit(solution)/shard_map/rows/pallas_call | solution.py:492
  95.5 3.6 %rows.7.refs_7_ = f32[12,3,48,128]{3,2,1,0:T(8,128)} custom-call(s32[3]{0:T(128)S(1)} %pad_add_fusion.refs_0_, f32[18816,128]{1,0:T(8,128)S(1)} %get-tuple-element.67.refs_1_, f32[18816,128]{1,0:T(8,128)S(1)} %get-tuple-element.68.refs_2_, f32[18816,128]{1,0:T(8,128)S(1)} %get-tuple-element.69.refs_3_, f32[18816,128]{1,0:T(8,128)S(1)} %get-tuple-element.70.refs_4_, ...), custom_call_target="tpu_custom_call" | custom-call | flops 1 | bytes 1 | tf_op jit(solution)/shard_map/rows/pallas_call | solution.py:492
  99.6 3.6 %rows.8.refs_6_ = f32[12,3,48,128]{3,2,1,0:T(8,128)} custom-call(s32[3]{0:T(128)S(1)} %pad_add_fusion.refs_0_, f32[18816,128]{1,0:T(8,128)S(1)} %get-tuple-element.67.refs_1_, f32[18816,128]{1,0:T(8,128)S(1)} %get-tuple-element.68.refs_2_, f32[18816,128]{1,0:T(8,128)S(1)} %get-tuple-element.69.refs_3_, f32[18816,128]{1,0:T(8,128)S(1)} %get-tuple-element.70.refs_4_, ...), custom_call_target="tpu_custom_call" | custom-call | flops 1 | bytes 1 | tf_op jit(solution)/shard_map/rows/pallas_call | solution.py:492
  104.7 3.6 %rows.9.refs_7_ = f32[12,3,48,128]{3,2,1,0:T(8,128)} custom-call(s32[3]{0:T(128)S(1)} %pad_add_fusion.refs_0_, f32[18816,128]{1,0:T(8,128)S(1)} %get-tuple-element.67.refs_1_, f32[18816,128]{1,0:T(8,128)S(1)} %get-tuple-element.68.refs_2_, f32[18816,128]{1,0:T(8,128)S(1)} %get-tuple-element.69.refs_3_, f32[18816,128]{1,0:T(8,128)S(1)} %get-tuple-element.70.refs_4_, ...), custom_call_target="tpu_custom_call" | custom-call | flops 1 | bytes 1 | tf_op jit(solution)/shard_map/rows/pallas_call | solution.py:492
  108.3 3.6 %rows.10.refs_6_ = f32[12,3,48,128]{3,2,1,0:T(8,128)} custom-call(s32[3]{0:T(128)S(1)} %pad_add_fusion.refs_0_, f32[18816,128]{1,0:T(8,128)S(1)} %get-tuple-element.67.refs_1_, f32[18816,128]{1,0:T(8,128)S(1)} %get-tuple-element.68.refs_2_, f32[18816,128]{1,0:T(8,128)S(1)} %get-tuple-element.69.refs_3_, f32[18816,128]{1,0:T(8,128)S(1)} %get-tuple-element.70.refs_4_, ...), custom_call_target="tpu_custom_call" | custom-call | flops 1 | bytes 1 | tf_op jit(solution)/shard_map/rows/pallas_call | solution.py:492
  112.5 5.5 %rows.11.refs_0_ = f32[24,3,48,128]{3,2,1,0:T(8,128)} custom-call(s32[3]{0:T(128)S(1)} %pad_add_fusion.refs_0_, f32[18816,128]{1,0:T(8,128)S(1)} %get-tuple-element.67.refs_1_, f32[18816,128]{1,0:T(8,128)S(1)} %get-tuple-element.68.refs_2_, f32[18816,128]{1,0:T(8,128)S(1)} %get-tuple-element.69.refs_3_, f32[18816,128]{1,0:T(8,128)S(1)} %get-tuple-element.70.refs_4_, ...), custom_call_target="tpu_custom_call" | custom-call | flops 1 | bytes 1 | tf_op jit(solution)/shard_map/rows/pallas_call | solution.py:492
  118.0 7.9 %collective-permute-done.17.refs_2_ = f32[12,3,48,128]{3,2,1,0:T(8,128)S(1)} collective-permute-done((f32[12,3,48,128]{3,2,1,0:T(8,128)}, f32[12,3,48,128]{3,2,1,0:T(8,128)S(1)}, u32[]{:S(2)}, u32[]{:S(2)}) %collective-permute-start.17) | collective-permute-done | bytes 884768 | tf_op jit(solution)/shard_map/ppermute | solution.py:503
  127.5 2.9 %finish.2.refs_7_ = f32[2,24,48,192]{3,2,1,0:T(8,128)} custom-call(f32[24,3,48,128]{3,2,1,0:T(8,128)S(1)} %copy-done, f32[12,3,48,128]{3,2,1,0:T(8,128)S(1)} %collective-permute-done.16.refs_1_, f32[12,3,48,128]{3,2,1,0:T(8,128)S(1)} %collective-permute-done.17.refs_2_, bf16[512,192]{1,0:T(8,128)(2,1)S(1)} %copy-done.2, f32[1,192]{1,0:T(1,128)S(1)} %bitcast.8, ...), custom_call_target="tpu_custom_call" | custom-call | tf_op jit(solution)/shard_map/finish/pallas_call | solution.py:540
  130.3 13.6 %collective-permute-done.15.refs_2_ = f32[12,3,48,128]{3,2,1,0:T(8,128)S(1)} collective-permute-done((f32[12,3,48,128]{3,2,1,0:T(8,128)}, f32[12,3,48,128]{3,2,1,0:T(8,128)S(1)}, u32[]{:S(2)}, u32[]{:S(2)}) %collective-permute-start.15) | collective-permute-done | bytes 884768 | tf_op jit(solution)/shard_map/ppermute | solution.py:503
  144.0 2.9 %finish.3 = f32[2,24,48,192]{3,2,1,0:T(8,128)} custom-call(f32[24,3,48,128]{3,2,1,0:T(8,128)S(1)} %copy-done, f32[12,3,48,128]{3,2,1,0:T(8,128)S(1)} %collective-permute-done.14.refs_1_, f32[12,3,48,128]{3,2,1,0:T(8,128)S(1)} %collective-permute-done.15.refs_2_, bf16[512,192]{1,0:T(8,128)(2,1)S(1)} %copy-done.2, ...), custom_call_target="tpu_custom_call", output_to_operand_aliasing={{}: (7, {})} | custom-call | tf_op jit(solution)/shard_map/finish/pallas_call | solution.py:540
  (40 shorter events, 14.5 us)
Async XLA Ops:
  5.2 15.9 %collective-permute-start = (f32[65,16,128]{2,1,0:T(8,128)}, f32[65,16,128]{2,1,0:T(8,128)S(1)}, u32[]{:S(2)}, u32[]{:S(2)}) collective-permute-start(f32[65,16,128]{2,1,0:T(8,128)} %spread.1.refs_1_), channel_id=1, source_target_pairs={{0,2},{1,3},{2,4},{3,5},{4,6},{5,7},{8,10},{9,11},{10,12},{11,13},... | collective-permute-start | bytes 1597448 | tf_op jit(solution)/shard_map/ppermute | solution.py:409
  8.7 15.9 %collective-permute-start.2 = (f32[65,16,128]{2,1,0:T(8,128)}, f32[65,16,128]{2,1,0:T(8,128)S(1)}, u32[]{:S(2)}, u32[]{:S(2)}) collective-permute-start(f32[65,16,128]{2,1,0:T(8,128)} %spread.1.refs_1_), channel_id=1, source_target_pairs={{2,0},{3,1},{4,2},{5,3},{6,4},{7,5},{10,8},{11,9},{12,10},{13,11},... | collective-permute-start | bytes 1597448 | tf_op jit(solution)/shard_map/ppermute | solution.py:409
  11.1 21.9 %collective-permute-start.3 = (f32[65,16,128]{2,1,0:T(8,128)}, f32[65,16,128]{2,1,0:T(8,128)S(1)}, u32[]{:S(2)}, u32[]{:S(2)}) collective-permute-start(f32[65,16,128]{2,1,0:T(8,128)} %spread.1.refs_1_), channel_id=1, source_target_pairs={{0,1},{1,0},{2,3},{3,2},{4,5},{5,4},{6,7},{7,6},{8,9},{9,8},{10,11... | collective-permute-start | bytes 1597448 | tf_op jit(solution)/shard_map/ppermute | solution.py:409
  12.7 1.0 copy-start.1
  21.2 20.6 %collective-permute-start.1 = (f32[65,16,128]{2,1,0:T(8,128)S(1)}, f32[65,16,128]{2,1,0:T(8,128)S(1)}, u32[]{:S(2)}, u32[]{:S(2)}) collective-permute-start(f32[65,16,128]{2,1,0:T(8,128)S(1)} %collective-permute-done.refs_1_), channel_id=1, source_target_pairs={{2,4},{3,5},{4,6},{5,7},{10,12},{11,13},{12,14},{13,15},{18,20},{1... | collective-permute-start | bytes 1597448 | tf_op jit(solution)/shard_map/ppermute | solution.py:409
  24.7 18.5 %collective-permute-start.5 = (f32[65,16,128]{2,1,0:T(8,128)S(1)}, f32[65,16,128]{2,1,0:T(8,128)S(1)}, u32[]{:S(2)}, u32[]{:S(2)}) collective-permute-start(f32[65,16,128]{2,1,0:T(8,128)S(1)} %collective-permute-done.2.refs_2_), channel_id=1, source_target_pairs={{2,0},{3,1},{4,2},{5,3},{10,8},{11,9},{12,10},{13,11},{18,16},{19,... | collective-permute-start | bytes 1597448 | tf_op jit(solution)/shard_map/ppermute | solution.py:409
  27.1 20.2 %collective-permute-start.6 = (f32[65,16,128]{2,1,0:T(8,128)S(1)}, f32[65,16,128]{2,1,0:T(8,128)S(1)}, u32[]{:S(2)}, u32[]{:S(2)}) collective-permute-start(f32[65,16,128]{2,1,0:T(8,128)S(1)} %collective-permute-done.refs_1_), channel_id=1, source_target_pairs={{2,3},{3,2},{4,5},{5,4},{6,7},{7,6},{10,11},{11,10},{12,13},{13,12... | collective-permute-start | bytes 1597448 | tf_op jit(solution)/shard_map/ppermute | solution.py:409
  30.5 24.9 %collective-permute-start.7 = (f32[65,16,128]{2,1,0:T(8,128)S(1)}, f32[65,16,128]{2,1,0:T(8,128)S(1)}, u32[]{:S(2)}, u32[]{:S(2)}) collective-permute-start(f32[65,16,128]{2,1,0:T(8,128)S(1)} %collective-permute-done.2.refs_2_), channel_id=1, source_target_pairs={{0,1},{1,0},{2,3},{3,2},{4,5},{5,4},{8,9},{9,8},{10,11},{11,10},{1... | collective-permute-start | bytes 1597448 | tf_op jit(solution)/shard_map/ppermute | solution.py:409
  41.8 22.5 %collective-permute-start.4 = (f32[65,16,128]{2,1,0:T(8,128)S(1)}, f32[65,16,128]{2,1,0:T(8,128)S(1)}, u32[]{:S(2)}, u32[]{:S(2)}) collective-permute-start(f32[65,16,128]{2,1,0:T(8,128)S(1)} %collective-permute-done.1.refs_1_), channel_id=1, source_target_pairs={{4,6},{5,7},{12,14},{13,15},{20,22},{21,23},{28,30},{29,31}} | collective-permute-start | bytes 1597448 | tf_op jit(solution)/shard_map/ppermute | solution.py:409
  43.1 21.9 %collective-permute-start.9 = (f32[65,16,128]{2,1,0:T(8,128)S(1)}, f32[65,16,128]{2,1,0:T(8,128)S(1)}, u32[]{:S(2)}, u32[]{:S(2)}) collective-permute-start(f32[65,16,128]{2,1,0:T(8,128)S(1)} %collective-permute-done.5.refs_2_), channel_id=1, source_target_pairs={{2,0},{3,1},{10,8},{11,9},{18,16},{19,17},{26,24},{27,25}} | collective-permute-start | bytes 1597448 | tf_op jit(solution)/shard_map/ppermute | solution.py:409
  43.8 21.9 %collective-permute-start.11 = (f32[65,16,128]{2,1,0:T(8,128)S(1)}, f32[65,16,128]{2,1,0:T(8,128)S(1)}, u32[]{:S(2)}, u32[]{:S(2)}) collective-permute-start(f32[65,16,128]{2,1,0:T(8,128)S(1)} %collective-permute-done.1.refs_1_), channel_id=1, source_target_pairs={{4,5},{5,4},{6,7},{7,6},{12,13},{13,12},{14,15},{15,14},{20,21},{2... | collective-permute-start | bytes 1597448 | tf_op jit(solution)/shard_map/ppermute | solution.py:409
  47.3 18.4 %collective-permute-start.12 = (f32[65,16,128]{2,1,0:T(8,128)S(1)}, f32[65,16,128]{2,1,0:T(8,128)S(1)}, u32[]{:S(2)}, u32[]{:S(2)}) collective-permute-start(f32[65,16,128]{2,1,0:T(8,128)S(1)} %collective-permute-done.5.refs_2_), channel_id=1, source_target_pairs={{0,1},{1,0},{2,3},{3,2},{8,9},{9,8},{10,11},{11,10},{16,17},{17,16... | collective-permute-start | bytes 1597448 | tf_op jit(solution)/shard_map/ppermute | solution.py:409
  64.3 5.9 %collective-permute-start.8 = (f32[65,16,128]{2,1,0:T(8,128)S(1)}, f32[65,16,128]{2,1,0:T(8,128)S(1)}, u32[]{:S(2)}, u32[]{:S(2)}) collective-permute-start(f32[65,16,128]{2,1,0:T(8,128)S(1)} %collective-permute-done.4.refs_1_), channel_id=1, source_target_pairs={{6,7},{7,6},{14,15},{15,14},{22,23},{23,22},{30,31},{31,30}} | collective-permute-start | bytes 1597448 | tf_op jit(solution)/shard_map/ppermute | solution.py:409
  65.0 5.2 %collective-permute-start.10 = (f32[65,16,128]{2,1,0:T(8,128)S(1)}, f32[65,16,128]{2,1,0:T(8,128)S(1)}, u32[]{:S(2)}, u32[]{:S(2)}) collective-permute-start(f32[65,16,128]{2,1,0:T(8,128)S(1)} %collective-permute-done.9.refs_2_), channel_id=1, source_target_pairs={{0,1},{1,0},{8,9},{9,8},{16,17},{17,16},{24,25},{25,24}} | collective-permute-start | bytes 1597448 | tf_op jit(solution)/shard_map/ppermute | solution.py:409
  95.5 4.1 %collective-permute-start.13 = (f32[24,3,48,128]{3,2,1,0:T(8,128)}, f32[24,3,48,128]{3,2,1,0:T(8,128)S(1)}, u32[]{:S(2)}, u32[]{:S(2)}) collective-permute-start(f32[24,3,48,128]{3,2,1,0:T(8,128)} %rows.6.refs_6_), channel_id=1, source_target_pairs={{0,8},{8,0},{16,24},{24,16},{1,9},{9,1},{17,25},{25,17},{2,10},{10... | collective-permute-start | bytes 5308424 | tf_op jit(solution)/shard_map/ppermute | solution.py:503
  99.1 18.9 %collective-permute-start.16 = (f32[12,3,48,128]{3,2,1,0:T(8,128)}, f32[12,3,48,128]{3,2,1,0:T(8,128)S(1)}, u32[]{:S(2)}, u32[]{:S(2)}) collective-permute-start(f32[12,3,48,128]{3,2,1,0:T(8,128)} %rows.7.refs_7_), channel_id=1, source_target_pairs={{0,8},{8,0},{16,24},{24,16},{1,9},{9,1},{17,25},{25,17},{2,10},{10... | collective-permute-start | bytes 2654216 | tf_op jit(solution)/shard_map/ppermute | solution.py:503
  103.2 22.7 %collective-permute-start.17 = (f32[12,3,48,128]{3,2,1,0:T(8,128)}, f32[12,3,48,128]{3,2,1,0:T(8,128)S(1)}, u32[]{:S(2)}, u32[]{:S(2)}) collective-permute-start(f32[12,3,48,128]{3,2,1,0:T(8,128)} %rows.8.refs_6_), channel_id=1, source_target_pairs={{0,16},{8,24},{16,0},{24,8},{1,17},{9,25},{17,1},{25,9},{2,18},{10... | collective-permute-start | bytes 2654216 | tf_op jit(solution)/shard_map/ppermute | solution.py:503
  108.3 22.0 %collective-permute-start.14 = (f32[12,3,48,128]{3,2,1,0:T(8,128)}, f32[12,3,48,128]{3,2,1,0:T(8,128)S(1)}, u32[]{:S(2)}, u32[]{:S(2)}) collective-permute-start(f32[12,3,48,128]{3,2,1,0:T(8,128)} %rows.9.refs_7_), channel_id=1, source_target_pairs={{0,8},{8,0},{16,24},{24,16},{1,9},{9,1},{17,25},{25,17},{2,10},{10... | collective-permute-start | bytes 2654216 | tf_op jit(solution)/shard_map/ppermute | solution.py:503
  111.9 14.1 %copy-start.2 = (bf16[512,192]{1,0:T(8,128)(2,1)S(1)}, bf16[512,192]{1,0:T(8,128)(2,1)}, u32[]{:S(2)}) copy-start(bf16[512,192]{1,0:T(8,128)(2,1)} %constant.27.clone.refs_3_) | copy-start | bytes 589828
  111.9 14.1 %copy-start.3 = (f32[192]{0:T(256)S(1)}, f32[192]{0:T(256)}, u32[]{:S(2)}) copy-start(f32[192]{0:T(256)} %param.19) | copy-start | bytes 2308
  111.9 14.1 %copy-start.4 = (f32[48]{0:T(128)S(1)}, f32[48]{0:T(128)}, u32[]{:S(2)}) copy-start(f32[48]{0:T(128)} %param.20) | copy-start | bytes 580
  111.9 14.1 %copy-start.5 = (f32[24]{0:T(128)S(1)}, f32[24]{0:T(128)}, u32[]{:S(2)}) copy-start(f32[24]{0:T(128)} %refs_6_.5) | copy-start | bytes 292
  111.9 32.1 %collective-permute-start.15 = (f32[12,3,48,128]{3,2,1,0:T(8,128)}, f32[12,3,48,128]{3,2,1,0:T(8,128)S(1)}, u32[]{:S(2)}, u32[]{:S(2)}) collective-permute-start(f32[12,3,48,128]{3,2,1,0:T(8,128)} %rows.10.refs_6_), channel_id=1, source_target_pairs={{0,16},{8,24},{16,0},{24,8},{1,17},{9,25},{17,1},{25,9},{2,18},{10... | collective-permute-start | bytes 2654216 | tf_op jit(solution)/shard_map/ppermute | solution.py:503
  126.0 1.5 %copy-start = (f32[24,3,48,128]{3,2,1,0:T(8,128)S(1)}, f32[24,3,48,128]{3,2,1,0:T(8,128)}, u32[]{:S(2)}) copy-start(f32[24,3,48,128]{3,2,1,0:T(8,128)} %rows.11.refs_0_) | copy-start | bytes 5308420

commit v13 on v12

--- a/solution.py
+++ b/solution.py
@@ -163,7 +163,7 @@
     out_ref[blocks // 2] = jnp.broadcast_to(codes, (2 * TILE, LANES))
 
 
-def tiles_kernel(conditions, first, *refs):
+def tiles_kernel(conditions, first, last, *refs):
     arrays = len(conditions)
     places_ref = refs[0]
     source_refs = refs[1 : 1 + arrays]
@@ -255,10 +255,11 @@
                 holds = jnp.logical_or(holds, places_ref[0] == depth)
             pl.when(holds)(functools.partial(add_source, index))
 
-
-def columns_kernel(*refs):
-    column_ref = refs[PARTS]
-    acc_refs = refs[PARTS + 1 :]
+    if last:
+        transform_columns(refs[3 + arrays], acc_refs)
+
+
+def transform_columns(column_ref, acc_refs):
     third = NY // 3
     rows = column_ref.shape[1] // 4
     turn = jnp.where(lax.broadcasted_iota(jnp.int32, (1, LANES), 1) < LANES // 2, -1.0, 1.0)
@@ -288,7 +289,7 @@
                     )
         return carry
 
-    lax.fori_loop(0, NX // 2 // PARTS, columns, 0, unroll=8)
+    lax.fori_loop(0, NX // 2 // PARTS, columns, 0, unroll=16)
 
 
 def rows_kernel(relative, first, count, chunks, grid_rows, addends, planes_padded, places_ref, *refs):
@@ -418,15 +419,15 @@
     def in_vmem(arrays):
         return [pltpu.with_memory_space_constraint(array, pltpu.VMEM) for array in arrays]
 
-    def add_tiles(sources, acc):
+    def add_tiles(sources, acc, columns=()):
         conditions = [None if len(holders) == Z_CHIPS else tuple(holders) for holders, _ in sources]
         spectra = pltpu.VMEM((16 * TILE * TILE, LANES), F32)
         kept = [jax.ShapeDtypeStruct(acc_shape, F32) if acc else pltpu.VMEM(acc_shape, F32)] * PARTS
-        inputs = len(sources) + 3
+        inputs = len(sources) + 3 + len(columns)
         *acc, token = pl.pallas_call(
-            functools.partial(tiles_kernel, conditions, not acc),
+            functools.partial(tiles_kernel, conditions, not acc, bool(columns)),
             out_shape=kept + [jax.ShapeDtypeStruct((TILE, LANES), F32)],
-            in_specs=[smem] + [vmem] * len(sources) + [pl.BlockSpec(memory_space=pl.ANY)] * 2 + [vmem] * len(acc),
+            in_specs=[smem] + [vmem] * len(sources) + [pl.BlockSpec(memory_space=pl.ANY)] * 2 + [vmem] * (len(columns) + len(acc)),
             out_specs=[vmem] * (PARTS + 1),
             input_output_aliases={inputs + part: part for part in range(PARTS)} if acc else {},
             scratch_shapes=[
@@ -440,7 +441,7 @@
             compiler_params=params,
             cost_estimate=pl.CostEstimate(flops=0, bytes_accessed=len(sources) << 23, transcendentals=0),
             name="tiles",
-        )(places, *[array for _, array in sources], *in_hbm([matrices, phases]), *in_vmem(acc))
+        )(places, *[array for _, array in sources], *in_hbm([matrices, phases, *columns]), *in_vmem(acc))
         return acc, token
 
     def after(value, token):
@@ -467,17 +468,7 @@
                 moved.append(([to for _, to in moves], passed[way]))
         acc, token = add_tiles(arrived, acc)
         arrived = moved + partners
-    acc, _ = add_tiles(arrived, acc)
-
-    acc = pl.pallas_call(
-        columns_kernel,
-        out_shape=[jax.ShapeDtypeStruct(acc_shape, F32)] * PARTS,
-        in_specs=[vmem] * (PARTS + 1),
-        out_specs=[vmem] * PARTS,
-        input_output_aliases={part: part for part in range(PARTS)},
-        compiler_params=params,
-        name="columns",
-    )(*in_vmem(acc), *in_hbm([column]))
+    acc, _ = add_tiles(arrived, acc, [column])
 
     row_table = jnp.asarray(row_tables())
     part_shape = (3, 2 * planes_padded, LANES)
@@ -493,11 +484,11 @@
             body,
             in_specs=[smem] + [vmem] * (1 + PARTS + len(addends)) + [pl.BlockSpec(memory_space=pl.ANY)] * len(after),
             out_specs=vmem,
-            out_shape=pltpu.HBM((count * slots,) + part_shape, F32),
+            out_shape=jax.ShapeDtypeStruct((count * slots,) + part_shape, F32),
             compiler_params=params,
             cost_estimate=pl.CostEstimate(flops=1, bytes_accessed=1, transcendentals=0),
             name="rows",
-        )(places, *in_vmem(acc), *in_hbm([row_table]), *addends, *in_hbm(after))
+        )(places, *in_vmem(acc), row_table, *addends, *in_hbm(after))
 
     def swap(value, bit):
         return lax.ppermute(value, "gx", [(index, index ^ bit) for index in range(grid_rows)])

time: 150 us -> 145 us (0.967)
  Pallas kernels: 84.2 us -> 74.1 us
  waiting for transfers between devices: 30.5 us -> 35 us
    pallas_call x6, Pallas kernels: 25.4 us -> 16.8 us  [rows_for(): pl.pallas_call(body, in_specs=[smem] + [vmem] * (1 + PARTS + len(addends)...]
    ppermute x5, waiting for transfers between devices: 21.6 us -> 26 us  [swap(): lax.ppermute(value, 'gx', [(index, index ^ bit) for index in range(grid_r...]
    pallas_call x6 -> x5, Pallas kernels: 47.8 us -> 46.5 us  [add_tiles(): pl.pallas_call(functools.partial(tiles_kernel, conditions, not acc, bool(...]
    unnamed x12 -> x22, local copies, waits for them, and re-layouts: 2.53 us -> 3.6 us
  transfers between devices with their start and end apart: 18 -> 18, of which waited for: 4 -> 5; matrix products, arithmetic and copies ran while one was open for 0% -> 0% of each run, Pallas kernels for 35% -> 30%
where the time goes in v13:
time: 145 us; the launch traced here: 142 us
  Pallas kernels  74.1 us (51%)
  waiting for transfers between devices  35 us (24%)
  starting transfers between devices  29.4 us (20%)
  local copies, waits for them, and re-layouts  3.6 us (2%)
    pallas_call x5, Pallas kernels, add_tiles(): pl.pallas_call(functools.partial(tiles_kernel, conditions, not acc, bool(...  46.5 us
    ppermute x13, starting transfers between devices, send(): return lax.ppermute(value, 'gy', moves)  26.7 us
    ppermute x5, waiting for transfers between devices, swap(): lax.ppermute(value, 'gx', [(index, index ^ bit) for index in range(grid_r...  26 us
    pallas_call x6, Pallas kernels, rows_for(): pl.pallas_call(body, in_specs=[smem] + [vmem] * (1 + PARTS + len(addends)...  16.8 us
    ppermute x13, waiting for transfers between devices, send(): return lax.ppermute(value, 'gy', moves)  8.96 us
    pallas_call x2, Pallas kernels, on_device(): pl.pallas_call(finish, grid=(1,), out_shape=jax.ShapeDtypeStruct((2, plan...  5.54 us
    pallas_call x1, Pallas kernels, on_device(): pl.pallas_call(functools.partial(spread_kernel, tile_rows, tile_cols, gri...  5.23 us
    unnamed x22, local copies, waits for them, and re-layouts  3.6 us
  transfers between devices with their start and end apart: 18, of which 5 were waited for; matrix products, arithmetic and copies ran while one was open for 0% of the time, Pallas kernels for 30%

profile of v13, /device:TPU:16, one launch (start us, length us, event | category | flops | bytes accessed | tf_op | source)
XLA Modules:
  0.0 142.4 jit_solution(16548968379601431861)
XLA Ops:
  0.0 5.2 %spread.1.refs_1_ = f32[65,16,128]{2,1,0:T(8,128)} custom-call(f32[128,2,128]{2,1,0:T(2,128)} %samples_ref.1, f32[128,3,4,128]{3,2,1,0:T(4,128)} %kernel_ref.1, s32[3,128,128]{2,1,0:T(8,128)} %bitcast.12, s32[1,128]{1,0:T(1,128)} %bitcast.13, s32[1,128]{1,0:T(1,128)} %bitcast.14), custom_call_target="tpu_custom_call" | custom-call | tf_op jit(solution)/shard_map/spread/pallas_call | solution.py:396
  5.2 3.5 %collective-permute-start = (f32[65,16,128]{2,1,0:T(8,128)}, f32[65,16,128]{2,1,0:T(8,128)S(1)}, u32[]{:S(2)}, u32[]{:S(2)}) collective-permute-start(f32[65,16,128]{2,1,0:T(8,128)} %spread.1.refs_1_), channel_id=1, source_target_pairs={{0,2},{1,3},{2,4},{3,5},{4,6},{5,7},{8,10},{9,11},{10,12},{11,13},... | collective-permute-start | bytes 1597448 | tf_op jit(solution)/shard_map/ppermute | solution.py:410
  8.7 2.4 %collective-permute-start.2 = (f32[65,16,128]{2,1,0:T(8,128)}, f32[65,16,128]{2,1,0:T(8,128)S(1)}, u32[]{:S(2)}, u32[]{:S(2)}) collective-permute-start(f32[65,16,128]{2,1,0:T(8,128)} %spread.1.refs_1_), channel_id=1, source_target_pairs={{2,0},{3,1},{4,2},{5,3},{6,4},{7,5},{10,8},{11,9},{12,10},{13,11},... | collective-permute-start | bytes 1597448 | tf_op jit(solution)/shard_map/ppermute | solution.py:410
  13.8 5.9 %tiles.5 = (f32[18816,128]{1,0:T(8,128)S(1)}, f32[18816,128]{1,0:T(8,128)S(1)}, f32[18816,128]{1,0:T(8,128)S(1)}, f32[18816,128]{1,0:T(8,128)S(1)}, f32[8,128]{1,0:T(8,128)}) custom-call(s32[3]{0:T(128)S(1)} %pad_add_fusion.refs_0_, f32[65,16,128]{2,1,0:T(8,128)S(1)} %copy-done.6, bf16[8,48,128]{2,1,0:T(8,128)(2,1)} %constant.23.clone.refs_2_.refs_4_.refs_5_.refs_3_, ...), custom_call_target="tpu_custom_call" | custom-call | bytes 8388608 | tf_op jit(solution)/shard_map/tiles/pallas_call | solution.py:427
  21.2 3.5 %collective-permute-start.1 = (f32[65,16,128]{2,1,0:T(8,128)S(1)}, f32[65,16,128]{2,1,0:T(8,128)S(1)}, u32[]{:S(2)}, u32[]{:S(2)}) collective-permute-start(f32[65,16,128]{2,1,0:T(8,128)S(1)} %collective-permute-done.refs_1_), channel_id=1, source_target_pairs={{2,4},{3,5},{4,6},{5,7},{10,12},{11,13},{12,14},{13,15},{18,20},{1... | collective-permute-start | bytes 1597448 | tf_op jit(solution)/shard_map/ppermute | solution.py:410
  24.7 2.4 %collective-permute-start.5 = (f32[65,16,128]{2,1,0:T(8,128)S(1)}, f32[65,16,128]{2,1,0:T(8,128)S(1)}, u32[]{:S(2)}, u32[]{:S(2)}) collective-permute-start(f32[65,16,128]{2,1,0:T(8,128)S(1)} %collective-permute-done.2.refs_2_), channel_id=1, source_target_pairs={{2,0},{3,1},{4,2},{5,3},{10,8},{11,9},{12,10},{13,11},{18,16},{19,... | collective-permute-start | bytes 1597448 | tf_op jit(solution)/shard_map/ppermute | solution.py:410
  27.1 3.4 %collective-permute-start.6 = (f32[65,16,128]{2,1,0:T(8,128)S(1)}, f32[65,16,128]{2,1,0:T(8,128)S(1)}, u32[]{:S(2)}, u32[]{:S(2)}) collective-permute-start(f32[65,16,128]{2,1,0:T(8,128)S(1)} %collective-permute-done.refs_1_), channel_id=1, source_target_pairs={{2,3},{3,2},{4,5},{5,4},{6,7},{7,6},{10,11},{11,10},{12,13},{13,12... | collective-permute-start | bytes 1597448 | tf_op jit(solution)/shard_map/ppermute | solution.py:410
  30.5 2.4 %collective-permute-start.7 = (f32[65,16,128]{2,1,0:T(8,128)S(1)}, f32[65,16,128]{2,1,0:T(8,128)S(1)}, u32[]{:S(2)}, u32[]{:S(2)}) collective-permute-start(f32[65,16,128]{2,1,0:T(8,128)S(1)} %collective-permute-done.2.refs_2_), channel_id=1, source_target_pairs={{0,1},{1,0},{2,3},{3,2},{4,5},{5,4},{8,9},{9,8},{10,11},{11,10},{1... | collective-permute-start | bytes 1597448 | tf_op jit(solution)/shard_map/ppermute | solution.py:410
  32.9 8.8 %tiles.6 = (f32[18816,128]{1,0:T(8,128)S(1)}, f32[18816,128]{1,0:T(8,128)S(1)}, f32[18816,128]{1,0:T(8,128)S(1)}, f32[18816,128]{1,0:T(8,128)S(1)}, f32[8,128]{1,0:T(8,128)}) custom-call(s32[3]{0:T(128)S(1)} %pad_add_fusion.refs_0_, ...), custom_call_target="tpu_custom_call", output_to_operand_aliasing={{0}: (6, {}), {1}: (7, {}), {2}: (8, {}), {3}: (9, {})} | custom-call | bytes 25165824 | tf_op jit(solution)/shard_map/tiles/pallas_call | solution.py:427
  43.8 3.4 %collective-permute-start.11 = (f32[65,16,128]{2,1,0:T(8,128)S(1)}, f32[65,16,128]{2,1,0:T(8,128)S(1)}, u32[]{:S(2)}, u32[]{:S(2)}) collective-permute-start(f32[65,16,128]{2,1,0:T(8,128)S(1)} %collective-permute-done.1.refs_1_), channel_id=1, source_target_pairs={{4,5},{5,4},{6,7},{7,6},{12,13},{13,12},{14,15},{15,14},{20,21},{2... | collective-permute-start | bytes 1597448 | tf_op jit(solution)/shard_map/ppermute | solution.py:410
  48.0 7.5 %collective-permute-done.7.refs_4_ = f32[65,16,128]{2,1,0:T(8,128)S(1)} collective-permute-done((f32[65,16,128]{2,1,0:T(8,128)S(1)}, f32[65,16,128]{2,1,0:T(8,128)S(1)}, u32[]{:S(2)}, u32[]{:S(2)}) %collective-permute-start.7) | collective-permute-done | bytes 532512 | tf_op jit(solution)/shard_map/ppermute | solution.py:410
  55.4 8.8 %tiles.7 = (f32[18816,128]{1,0:T(8,128)S(1)}, f32[18816,128]{1,0:T(8,128)S(1)}, f32[18816,128]{1,0:T(8,128)S(1)}, f32[18816,128]{1,0:T(8,128)S(1)}, f32[8,128]{1,0:T(8,128)}) custom-call(s32[3]{0:T(128)S(1)} %pad_add_fusion.refs_0_, ...), custom_call_target="tpu_custom_call", output_to_operand_aliasing={{0}: (7, {}), {1}: (8, {}), {2}: (9, {}), {3}: (10, {})} | custom-call | bytes 33554432 | tf_op jit(solution)/shard_map/tiles/pallas_call | solution.py:427
  65.7 4.4 %tiles.8 = (f32[18816,128]{1,0:T(8,128)S(1)}, f32[18816,128]{1,0:T(8,128)S(1)}, f32[18816,128]{1,0:T(8,128)S(1)}, f32[18816,128]{1,0:T(8,128)S(1)}, f32[8,128]{1,0:T(8,128)}) custom-call(s32[3]{0:T(128)S(1)} %pad_add_fusion.refs_0_, ...), custom_call_target="tpu_custom_call", output_to_operand_aliasing={{0}: (7, {}), {1}: (8, {}), {2}: (9, {}), {3}: (10, {})} | custom-call | bytes 33554432 | tf_op jit(solution)/shard_map/tiles/pallas_call | solution.py:427
  70.2 18.6 %tiles.9 = (f32[18816,128]{1,0:T(8,128)S(1)}, f32[18816,128]{1,0:T(8,128)S(1)}, f32[18816,128]{1,0:T(8,128)S(1)}, f32[18816,128]{1,0:T(8,128)S(1)}, f32[8,128]{1,0:T(8,128)}) custom-call(s32[3]{0:T(128)S(1)} %pad_add_fusion.refs_0_, ...), custom_call_target="tpu_custom_call", output_to_operand_aliasing={{0}: (6, {}), {1}: (7, {}), {2}: (8, {}), {3}: (9, {})} | custom-call | bytes 16777216 | tf_op jit(solution)/shard_map/tiles/pallas_call | solution.py:427
  88.8 4.1 %rows.6.refs_6_ = f32[24,3,48,128]{3,2,1,0:T(8,128)S(1)} custom-call(s32[3]{0:T(128)S(1)} %pad_add_fusion.refs_0_, f32[18816,128]{1,0:T(8,128)S(1)} %get-tuple-element.59.refs_1_, f32[18816,128]{1,0:T(8,128)S(1)} %get-tuple-element.60.refs_2_, f32[18816,128]{1,0:T(8,128)S(1)} %get-tuple-element.61.refs_3_, f32[18816,128]{1,0:T(8,128)S(1)} %get-tuple-element.62.refs_4_, ...), custom_call_target="tpu_custom_call" | custom-call | flops 1 | bytes 1 | tf_op jit(solution)/shard_map/rows/pallas_call | solution.py:483
  94.1 2.2 %rows.7.refs_7_ = f32[12,3,48,128]{3,2,1,0:T(8,128)S(1)} custom-call(s32[3]{0:T(128)S(1)} %pad_add_fusion.refs_0_, f32[18816,128]{1,0:T(8,128)S(1)} %get-tuple-element.59.refs_1_, f32[18816,128]{1,0:T(8,128)S(1)} %get-tuple-element.60.refs_2_, f32[18816,128]{1,0:T(8,128)S(1)} %get-tuple-element.61.refs_3_, f32[18816,128]{1,0:T(8,128)S(1)} %get-tuple-element.62.refs_4_, ...), custom_call_target="tpu_custom_call" | custom-call | flops 1 | bytes 1 | tf_op jit(solution)/shard_map/rows/pallas_call | solution.py:483
  97.2 2.2 %rows.8.refs_6_ = f32[12,3,48,128]{3,2,1,0:T(8,128)S(1)} custom-call(s32[3]{0:T(128)S(1)} %pad_add_fusion.refs_0_, f32[18816,128]{1,0:T(8,128)S(1)} %get-tuple-element.59.refs_1_, f32[18816,128]{1,0:T(8,128)S(1)} %get-tuple-element.60.refs_2_, f32[18816,128]{1,0:T(8,128)S(1)} %get-tuple-element.61.refs_3_, f32[18816,128]{1,0:T(8,128)S(1)} %get-tuple-element.62.refs_4_, ...), custom_call_target="tpu_custom_call" | custom-call | flops 1 | bytes 1 | tf_op jit(solution)/shard_map/rows/pallas_call | solution.py:483
  101.0 2.2 %rows.9.refs_7_ = f32[12,3,48,128]{3,2,1,0:T(8,128)S(1)} custom-call(s32[3]{0:T(128)S(1)} %pad_add_fusion.refs_0_, f32[18816,128]{1,0:T(8,128)S(1)} %get-tuple-element.59.refs_1_, f32[18816,128]{1,0:T(8,128)S(1)} %get-tuple-element.60.refs_2_, f32[18816,128]{1,0:T(8,128)S(1)} %get-tuple-element.61.refs_3_, f32[18816,128]{1,0:T(8,128)S(1)} %get-tuple-element.62.refs_4_, ...), custom_call_target="tpu_custom_call" | custom-call | flops 1 | bytes 1 | tf_op jit(solution)/shard_map/rows/pallas_call | solution.py:483
  104.1 2.2 %rows.10.refs_6_ = f32[12,3,48,128]{3,2,1,0:T(8,128)S(1)} custom-call(s32[3]{0:T(128)S(1)} %pad_add_fusion.refs_0_, f32[18816,128]{1,0:T(8,128)S(1)} %get-tuple-element.59.refs_1_, f32[18816,128]{1,0:T(8,128)S(1)} %get-tuple-element.60.refs_2_, f32[18816,128]{1,0:T(8,128)S(1)} %get-tuple-element.61.refs_3_, f32[18816,128]{1,0:T(8,128)S(1)} %get-tuple-element.62.refs_4_, ...), custom_call_target="tpu_custom_call" | custom-call | flops 1 | bytes 1 | tf_op jit(solution)/shard_map/rows/pallas_call | solution.py:483
  107.3 3.9 %rows.11.refs_0_ = f32[24,3,48,128]{3,2,1,0:T(8,128)S(1)} custom-call(s32[3]{0:T(128)S(1)} %pad_add_fusion.refs_0_, f32[18816,128]{1,0:T(8,128)S(1)} %get-tuple-element.59.refs_1_, f32[18816,128]{1,0:T(8,128)S(1)} %get-tuple-element.60.refs_2_, f32[18816,128]{1,0:T(8,128)S(1)} %get-tuple-element.61.refs_3_, f32[18816,128]{1,0:T(8,128)S(1)} %get-tuple-element.62.refs_4_, ...), custom_call_target="tpu_custom_call" | custom-call | flops 1 | bytes 1 | tf_op jit(solution)/shard_map/rows/pallas_call | solution.py:483
  111.2 10.9 %collective-permute-done.17.refs_2_ = f32[12,3,48,128]{3,2,1,0:T(8,128)S(1)} collective-permute-done((f32[12,3,48,128]{3,2,1,0:T(8,128)S(1)}, f32[12,3,48,128]{3,2,1,0:T(8,128)S(1)}, u32[]{:S(2)}, u32[]{:S(2)}) %collective-permute-start.17) | collective-permute-done | bytes 884768 | tf_op jit(solution)/shard_map/ppermute | solution.py:494
  122.1 2.8 %finish.2.refs_7_ = f32[2,24,48,192]{3,2,1,0:T(8,128)} custom-call(f32[24,3,48,128]{3,2,1,0:T(8,128)S(1)} %rows.11.refs_0_, f32[12,3,48,128]{3,2,1,0:T(8,128)S(1)} %collective-permute-done.16.refs_1_, f32[12,3,48,128]{3,2,1,0:T(8,128)S(1)} %collective-permute-done.17.refs_2_, bf16[512,192]{1,0:T(8,128)(2,1)S(1)} %copy-done.7, f32[1,192]{1,0:T(1,128)S(1)} %bitcast.8, ...), custom_call_target="tpu_custom_call" | custom-call | tf_op jit(solution)/shard_map/finish/pallas_call | solution.py:531
  124.8 14.8 %collective-permute-done.15.refs_2_ = f32[12,3,48,128]{3,2,1,0:T(8,128)S(1)} collective-permute-done((f32[12,3,48,128]{3,2,1,0:T(8,128)S(1)}, f32[12,3,48,128]{3,2,1,0:T(8,128)S(1)}, u32[]{:S(2)}, u32[]{:S(2)}) %collective-permute-start.15) | collective-permute-done | bytes 884768 | tf_op jit(solution)/shard_map/ppermute | solution.py:494
  139.7 2.8 %finish.3 = f32[2,24,48,192]{3,2,1,0:T(8,128)} custom-call(f32[24,3,48,128]{3,2,1,0:T(8,128)S(1)} %rows.11.refs_0_, f32[12,3,48,128]{3,2,1,0:T(8,128)S(1)} %collective-permute-done.14.refs_1_, f32[12,3,48,128]{3,2,1,0:T(8,128)S(1)} %collective-permute-done.15.refs_2_, bf16[512,192]{1,0:T(8,128)(2,1)S(1)} %copy-done.7, ...), custom_call_target="tpu_custom_call", output_to_operand_aliasing={{}: (7, {})} | custom-call | tf_op jit(solution)/shard_map/finish/pallas_call | solution.py:531
  (49 shorter events, 13.8 us)
Async XLA Ops:
  5.2 15.9 %collective-permute-start = (f32[65,16,128]{2,1,0:T(8,128)}, f32[65,16,128]{2,1,0:T(8,128)S(1)}, u32[]{:S(2)}, u32[]{:S(2)}) collective-permute-start(f32[65,16,128]{2,1,0:T(8,128)} %spread.1.refs_1_), channel_id=1, source_target_pairs={{0,2},{1,3},{2,4},{3,5},{4,6},{5,7},{8,10},{9,11},{10,12},{11,13},... | collective-permute-start | bytes 1597448 | tf_op jit(solution)/shard_map/ppermute | solution.py:410
  8.7 15.9 %collective-permute-start.2 = (f32[65,16,128]{2,1,0:T(8,128)}, f32[65,16,128]{2,1,0:T(8,128)S(1)}, u32[]{:S(2)}, u32[]{:S(2)}) collective-permute-start(f32[65,16,128]{2,1,0:T(8,128)} %spread.1.refs_1_), channel_id=1, source_target_pairs={{2,0},{3,1},{4,2},{5,3},{6,4},{7,5},{10,8},{11,9},{12,10},{13,11},... | collective-permute-start | bytes 1597448 | tf_op jit(solution)/shard_map/ppermute | solution.py:410
  11.1 21.9 %collective-permute-start.3 = (f32[65,16,128]{2,1,0:T(8,128)}, f32[65,16,128]{2,1,0:T(8,128)S(1)}, u32[]{:S(2)}, u32[]{:S(2)}) collective-permute-start(f32[65,16,128]{2,1,0:T(8,128)} %spread.1.refs_1_), channel_id=1, source_target_pairs={{0,1},{1,0},{2,3},{3,2},{4,5},{5,4},{6,7},{7,6},{8,9},{9,8},{10,11... | collective-permute-start | bytes 1597448 | tf_op jit(solution)/shard_map/ppermute | solution.py:410
  21.2 20.6 %collective-permute-start.1 = (f32[65,16,128]{2,1,0:T(8,128)S(1)}, f32[65,16,128]{2,1,0:T(8,128)S(1)}, u32[]{:S(2)}, u32[]{:S(2)}) collective-permute-start(f32[65,16,128]{2,1,0:T(8,128)S(1)} %collective-permute-done.refs_1_), channel_id=1, source_target_pairs={{2,4},{3,5},{4,6},{5,7},{10,12},{11,13},{12,14},{13,15},{18,20},{1... | collective-permute-start | bytes 1597448 | tf_op jit(solution)/shard_map/ppermute | solution.py:410
  24.7 18.4 %collective-permute-start.5 = (f32[65,16,128]{2,1,0:T(8,128)S(1)}, f32[65,16,128]{2,1,0:T(8,128)S(1)}, u32[]{:S(2)}, u32[]{:S(2)}) collective-permute-start(f32[65,16,128]{2,1,0:T(8,128)S(1)} %collective-permute-done.2.refs_2_), channel_id=1, source_target_pairs={{2,0},{3,1},{4,2},{5,3},{10,8},{11,9},{12,10},{13,11},{18,16},{19,... | collective-permute-start | bytes 1597448 | tf_op jit(solution)/shard_map/ppermute | solution.py:410
  27.1 20.2 %collective-permute-start.6 = (f32[65,16,128]{2,1,0:T(8,128)S(1)}, f32[65,16,128]{2,1,0:T(8,128)S(1)}, u32[]{:S(2)}, u32[]{:S(2)}) collective-permute-start(f32[65,16,128]{2,1,0:T(8,128)S(1)} %collective-permute-done.refs_1_), channel_id=1, source_target_pairs={{2,3},{3,2},{4,5},{5,4},{6,7},{7,6},{10,11},{11,10},{12,13},{13,12... | collective-permute-start | bytes 1597448 | tf_op jit(solution)/shard_map/ppermute | solution.py:410
  30.5 24.9 %collective-permute-start.7 = (f32[65,16,128]{2,1,0:T(8,128)S(1)}, f32[65,16,128]{2,1,0:T(8,128)S(1)}, u32[]{:S(2)}, u32[]{:S(2)}) collective-permute-start(f32[65,16,128]{2,1,0:T(8,128)S(1)} %collective-permute-done.2.refs_2_), channel_id=1, source_target_pairs={{0,1},{1,0},{2,3},{3,2},{4,5},{5,4},{8,9},{9,8},{10,11},{11,10},{1... | collective-permute-start | bytes 1597448 | tf_op jit(solution)/shard_map/ppermute | solution.py:410
  41.8 22.5 %collective-permute-start.4 = (f32[65,16,128]{2,1,0:T(8,128)S(1)}, f32[65,16,128]{2,1,0:T(8,128)S(1)}, u32[]{:S(2)}, u32[]{:S(2)}) collective-permute-start(f32[65,16,128]{2,1,0:T(8,128)S(1)} %collective-permute-done.1.refs_1_), channel_id=1, source_target_pairs={{4,6},{5,7},{12,14},{13,15},{20,22},{21,23},{28,30},{29,31}} | collective-permute-start | bytes 1597448 | tf_op jit(solution)/shard_map/ppermute | solution.py:410
  43.1 21.9 %collective-permute-start.9 = (f32[65,16,128]{2,1,0:T(8,128)S(1)}, f32[65,16,128]{2,1,0:T(8,128)S(1)}, u32[]{:S(2)}, u32[]{:S(2)}) collective-permute-start(f32[65,16,128]{2,1,0:T(8,128)S(1)} %collective-permute-done.5.refs_2_), channel_id=1, source_target_pairs={{2,0},{3,1},{10,8},{11,9},{18,16},{19,17},{26,24},{27,25}} | collective-permute-start | bytes 1597448 | tf_op jit(solution)/shard_map/ppermute | solution.py:410
  43.8 21.9 %collective-permute-start.11 = (f32[65,16,128]{2,1,0:T(8,128)S(1)}, f32[65,16,128]{2,1,0:T(8,128)S(1)}, u32[]{:S(2)}, u32[]{:S(2)}) collective-permute-start(f32[65,16,128]{2,1,0:T(8,128)S(1)} %collective-permute-done.1.refs_1_), channel_id=1, source_target_pairs={{4,5},{5,4},{6,7},{7,6},{12,13},{13,12},{14,15},{15,14},{20,21},{2... | collective-permute-start | bytes 1597448 | tf_op jit(solution)/shard_map/ppermute | solution.py:410
  47.3 18.4 %collective-permute-start.12 = (f32[65,16,128]{2,1,0:T(8,128)S(1)}, f32[65,16,128]{2,1,0:T(8,128)S(1)}, u32[]{:S(2)}, u32[]{:S(2)}) collective-permute-start(f32[65,16,128]{2,1,0:T(8,128)S(1)} %collective-permute-done.5.refs_2_), channel_id=1, source_target_pairs={{0,1},{1,0},{2,3},{3,2},{8,9},{9,8},{10,11},{11,10},{16,17},{17,16... | collective-permute-start | bytes 1597448 | tf_op jit(solution)/shard_map/ppermute | solution.py:410
  64.3 5.9 %collective-permute-start.8 = (f32[65,16,128]{2,1,0:T(8,128)S(1)}, f32[65,16,128]{2,1,0:T(8,128)S(1)}, u32[]{:S(2)}, u32[]{:S(2)}) collective-permute-start(f32[65,16,128]{2,1,0:T(8,128)S(1)} %collective-permute-done.4.refs_1_), channel_id=1, source_target_pairs={{6,7},{7,6},{14,15},{15,14},{22,23},{23,22},{30,31},{31,30}} | collective-permute-start | bytes 1597448 | tf_op jit(solution)/shard_map/ppermute | solution.py:410
  65.0 5.2 %collective-permute-start.10 = (f32[65,16,128]{2,1,0:T(8,128)S(1)}, f32[65,16,128]{2,1,0:T(8,128)S(1)}, u32[]{:S(2)}, u32[]{:S(2)}) collective-permute-start(f32[65,16,128]{2,1,0:T(8,128)S(1)} %collective-permute-done.9.refs_2_), channel_id=1, source_target_pairs={{0,1},{1,0},{8,9},{9,8},{16,17},{17,16},{24,25},{25,24}} | collective-permute-start | bytes 1597448 | tf_op jit(solution)/shard_map/ppermute | solution.py:410
  70.2 18.6 %copy-start = (bf16[2,2,192,256]{3,2,1,0:T(8,128)(2,1)S(1)}, bf16[2,2,192,256]{3,2,1,0:T(8,128)(2,1)}, u32[]{:S(2)}) copy-start(bf16[2,2,192,256]{3,2,1,0:T(8,128)(2,1)} %constant.26.clone.refs_5_) | copy-start | bytes 1179652
  92.9 3.8 %collective-permute-start.13 = (f32[24,3,48,128]{3,2,1,0:T(8,128)S(1)}, f32[24,3,48,128]{3,2,1,0:T(8,128)S(1)}, u32[]{:S(2)}, u32[]{:S(2)}) collective-permute-start(f32[24,3,48,128]{3,2,1,0:T(8,128)S(1)} %rows.6.refs_6_), channel_id=1, source_target_pairs={{0,8},{8,0},{16,24},{24,16},{1,9},{9,1},{17,25},{25,17},{2,10},{10... | collective-permute-start | bytes 5308424 | tf_op jit(solution)/shard_map/ppermute | solution.py:494
  96.3 14.9 %collective-permute-start.16 = (f32[12,3,48,128]{3,2,1,0:T(8,128)S(1)}, f32[12,3,48,128]{3,2,1,0:T(8,128)S(1)}, u32[]{:S(2)}, u32[]{:S(2)}) collective-permute-start(f32[12,3,48,128]{3,2,1,0:T(8,128)S(1)} %rows.7.refs_7_), channel_id=1, source_target_pairs={{0,8},{8,0},{16,24},{24,16},{1,9},{9,1},{17,25},{25,17},{2,10},{10... | collective-permute-start | bytes 2654216 | tf_op jit(solution)/shard_map/ppermute | solution.py:494
  99.4 1.6 %copy-start.5 = (f32[12,3,48,128]{3,2,1,0:T(8,128)}, f32[12,3,48,128]{3,2,1,0:T(8,128)S(1)}, u32[]{:S(2)}) copy-start(f32[12,3,48,128]{3,2,1,0:T(8,128)S(1)} %rows.8.refs_6_) | copy-start | bytes 2654212
  99.4 22.6 %collective-permute-start.17 = (f32[12,3,48,128]{3,2,1,0:T(8,128)S(1)}, f32[12,3,48,128]{3,2,1,0:T(8,128)S(1)}, u32[]{:S(2)}, u32[]{:S(2)}) collective-permute-start(f32[12,3,48,128]{3,2,1,0:T(8,128)S(1)} %rows.8.refs_6_), channel_id=1, source_target_pairs={{0,16},{8,24},{16,0},{24,8},{1,17},{9,25},{17,1},{25,9},{2,18},{10... | collective-permute-start | bytes 2654216 | tf_op jit(solution)/shard_map/ppermute | solution.py:494
  103.2 21.6 %collective-permute-start.14 = (f32[12,3,48,128]{3,2,1,0:T(8,128)S(1)}, f32[12,3,48,128]{3,2,1,0:T(8,128)S(1)}, u32[]{:S(2)}, u32[]{:S(2)}) collective-permute-start(f32[12,3,48,128]{3,2,1,0:T(8,128)S(1)} %rows.9.refs_7_), channel_id=1, source_target_pairs={{0,8},{8,0},{16,24},{24,16},{1,9},{9,1},{17,25},{25,17},{2,10},{10... | collective-permute-start | bytes 2654216 | tf_op jit(solution)/shard_map/ppermute | solution.py:494
  106.3 15.7 %copy-start.7 = (bf16[512,192]{1,0:T(8,128)(2,1)S(1)}, bf16[512,192]{1,0:T(8,128)(2,1)}, u32[]{:S(2)}) copy-start(bf16[512,192]{1,0:T(8,128)(2,1)} %constant.27.clone.refs_3_) | copy-start | bytes 589828
  106.3 15.7 %copy-start.8 = (f32[192]{0:T(256)S(1)}, f32[192]{0:T(256)}, u32[]{:S(2)}) copy-start(f32[192]{0:T(256)} %param.19) | copy-start | bytes 2308
  106.4 15.7 %copy-start.9 = (f32[48]{0:T(128)S(1)}, f32[48]{0:T(128)}, u32[]{:S(2)}) copy-start(f32[48]{0:T(128)} %param.20) | copy-start | bytes 580
  106.4 15.7 %copy-start.10 = (f32[24]{0:T(128)S(1)}, f32[24]{0:T(128)}, u32[]{:S(2)}) copy-start(f32[24]{0:T(128)} %refs_6_.5) | copy-start | bytes 292
  106.4 33.3 %collective-permute-start.15 = (f32[12,3,48,128]{3,2,1,0:T(8,128)S(1)}, f32[12,3,48,128]{3,2,1,0:T(8,128)S(1)}, u32[]{:S(2)}, u32[]{:S(2)}) collective-permute-start(f32[12,3,48,128]{3,2,1,0:T(8,128)S(1)} %rows.10.refs_6_), channel_id=1, source_target_pairs={{0,16},{8,24},{16,0},{24,8},{1,17},{9,25},{17,1},{25,9},{2,18},{10... | collective-permute-start | bytes 2654216 | tf_op jit(solution)/shard_map/ppermute | solution.py:494
  (5 other events, 5.1 us)

commit v14 on v13

--- a/solution.py
+++ b/solution.py
@@ -168,14 +168,11 @@
     places_ref = refs[0]
     source_refs = refs[1 : 1 + arrays]
     depth_tables_ref, phase_tables_ref = refs[1 + arrays : 3 + arrays]
-    acc_refs = refs[-7 - PARTS : -7]
-    token_ref, codes_ref, depth_ref, phases_ref, even_ref, odd_ref, arrived = refs[-7:]
+    acc_refs = refs[-5 - PARTS : -5]
+    token_ref, codes_ref, depth_ref, phases_ref, arrived = refs[-5:]
     token_ref[...] = jnp.zeros_like(token_ref)
     stride = STRIDE
     pairs = source_refs[0].shape[0] - 1
-    batch = 8
-    batches = pairs // batch
-    assert batches % 2 == 0
 
     def copies(index):
         return pltpu.make_async_copy(
@@ -209,42 +206,30 @@
     def add_source(index):
         tiles_ref = source_refs[index]
 
-        def spectrum(number, to_ref):
-            tiles = jnp.concatenate([tiles_ref[number * batch + place] for place in range(batch)], axis=1)
-            high, low = split(tiles)
-            to_ref[...] = lax.dot_general(
+        def add_pair(pair, carry):
+            high, low = split(tiles_ref[pair])
+            spectrum = lax.dot_general(
                 jnp.concatenate((high, low, high), axis=0),
                 depth_ref[...],
                 (((0,), (0,)), ((), ())),
                 preferred_element_type=F32,
             )
-
-        def accumulate(number, from_ref):
-            for tile in range(2 * batch):
-                code = codes_ref[index, 0, number * 2 * batch + tile].astype(jnp.int32)
+            for side in range(2):
+                code = codes_ref[index, 0, 2 * pair + side].astype(jnp.int32)
                 base = lax.shift_right_logical(code, 7)
                 phase = jnp.bitwise_and(code, PHASES - 1)
                 cos = phases_ref[0, pl.ds(phase, 1), :]
                 sin = phases_ref[1, pl.ds(phase, 1), :]
                 for i in range(TILE):
-                    row = tile * TILE * TILE + i * TILE
-                    value = from_ref[row : row + TILE, :]
+                    row = side * TILE * TILE + i * TILE
+                    value = spectrum[row : row + TILE]
                     value = value * cos + pltpu.roll(value, LANES // 2, 1) * sin
                     acc_ref = acc_refs[i // CELLS]
                     at = pl.ds(pl.multiple_of(base * TILE + i % CELLS * stride, TILE), TILE)
                     acc_ref[at, :] = acc_ref[at, :] + value
-
-        spectrum(0, even_ref)
-
-        def add_pair(step, carry):
-            number = 2 * step
-            spectrum(number + 1, odd_ref)
-            accumulate(number, even_ref)
-            spectrum(jnp.minimum(number + 2, batches - 2), even_ref)
-            accumulate(number + 1, odd_ref)
             return carry
 
-        lax.fori_loop(0, batches // 2, add_pair, 0, unroll=2)
+        lax.fori_loop(0, pairs, add_pair, 0, unroll=16)
 
     for index, condition in enumerate(conditions):
         if condition is None:
@@ -421,7 +406,6 @@
 
     def add_tiles(sources, acc, columns=()):
         conditions = [None if len(holders) == Z_CHIPS else tuple(holders) for holders, _ in sources]
-        spectra = pltpu.VMEM((16 * TILE * TILE, LANES), F32)
         kept = [jax.ShapeDtypeStruct(acc_shape, F32) if acc else pltpu.VMEM(acc_shape, F32)] * PARTS
         inputs = len(sources) + 3 + len(columns)
         *acc, token = pl.pallas_call(
@@ -434,8 +418,6 @@
                 pltpu.SMEM((len(sources), TILE, LANES), F32),
                 pltpu.VMEM(matrices.shape[1:], BF16),
                 pltpu.VMEM(phases.shape[1:], F32),
-                spectra,
-                spectra,
                 pltpu.SemaphoreType.DMA((len(sources) + 2,)),
             ],
             compiler_params=params,
@@ -488,7 +470,7 @@
             compiler_params=params,
             cost_estimate=pl.CostEstimate(flops=1, bytes_accessed=1, transcendentals=0),
             name="rows",
-        )(places, *in_vmem(acc), row_table, *addends, *in_hbm(after))
+        )(places, *in_vmem(acc), row_table, *addends, *after)
 
     def swap(value, bit):
         return lax.ppermute(value, "gx", [(index, index ^ bit) for index in range(grid_rows)])

time: 145 us -> 146 us (level)
  local copies, waits for them, and re-layouts: 3.6 us -> 1.08 us
  waiting for transfers between devices: 35 us -> 36.7 us
    unnamed x22 -> x12, local copies, waits for them, and re-layouts: 3.6 us -> 1.08 us
    ppermute x5, waiting for transfers between devices: 26 us -> 28.3 us  [swap(): lax.ppermute(value, 'gx', [(index, index ^ bit) for index in range(grid_r...]
  transfers between devices with their start and end apart: 18 -> 18, of which waited for: 5 -> 5; matrix products, arithmetic and copies ran while one was open for 0% -> 0% of each run, Pallas kernels for 30% -> 31%
where the time goes in v14:
time: 146 us; the launch traced here: 143 us
  Pallas kernels  75.1 us (51%)
  waiting for transfers between devices  36.7 us (25%)
  starting transfers between devices  29.5 us (20%)
    pallas_call x5, Pallas kernels, add_tiles(): pl.pallas_call(functools.partial(tiles_kernel, conditions, not acc, bool(...  47.5 us
    ppermute x5, waiting for transfers between devices, swap(): lax.ppermute(value, 'gx', [(index, index ^ bit) for index in range(grid_r...  28.3 us
    ppermute x13, starting transfers between devices, send(): return lax.ppermute(value, 'gy', moves)  26.7 us
    pallas_call x6, Pallas kernels, rows_for(): pl.pallas_call(body, in_specs=[smem] + [vmem] * (1 + PARTS + len(addends)...  16.8 us
    ppermute x13, waiting for transfers between devices, send(): return lax.ppermute(value, 'gy', moves)  8.39 us
    pallas_call x2, Pallas kernels, on_device(): pl.pallas_call(finish, grid=(1,), out_shape=jax.ShapeDtypeStruct((2, plan...  5.54 us
    pallas_call x1, Pallas kernels, on_device(): pl.pallas_call(functools.partial(spread_kernel, tile_rows, tile_cols, gri...  5.23 us
  transfers between devices with their start and end apart: 18, of which 5 were waited for; matrix products, arithmetic and copies ran while one was open for 0% of the time, Pallas kernels for 31%

profile of v14, /device:TPU:16, one launch (start us, length us, event | category | flops | bytes accessed | tf_op | source)
XLA Modules:
  0.0 142.7 jit_solution(12608727792720587005)
XLA Ops:
  0.0 5.2 %spread.1.refs_1_ = f32[65,16,128]{2,1,0:T(8,128)} custom-call(f32[128,2,128]{2,1,0:T(2,128)} %samples_ref.1, f32[128,3,4,128]{3,2,1,0:T(4,128)} %kernel_ref.1, s32[3,128,128]{2,1,0:T(8,128)} %bitcast.12, s32[1,128]{1,0:T(1,128)} %bitcast.13, s32[1,128]{1,0:T(1,128)} %bitcast.14), custom_call_target="tpu_custom_call" | custom-call | tf_op jit(solution)/shard_map/spread/pallas_call | solution.py:381
  5.2 3.5 %collective-permute-start = (f32[65,16,128]{2,1,0:T(8,128)}, f32[65,16,128]{2,1,0:T(8,128)S(1)}, u32[]{:S(2)}, u32[]{:S(2)}) collective-permute-start(f32[65,16,128]{2,1,0:T(8,128)} %spread.1.refs_1_), channel_id=1, source_target_pairs={{0,2},{1,3},{2,4},{3,5},{4,6},{5,7},{8,10},{9,11},{10,12},{11,13},... | collective-permute-start | bytes 1597448 | tf_op jit(solution)/shard_map/ppermute | solution.py:395
  8.7 2.4 %collective-permute-start.2 = (f32[65,16,128]{2,1,0:T(8,128)}, f32[65,16,128]{2,1,0:T(8,128)S(1)}, u32[]{:S(2)}, u32[]{:S(2)}) collective-permute-start(f32[65,16,128]{2,1,0:T(8,128)} %spread.1.refs_1_), channel_id=1, source_target_pairs={{2,0},{3,1},{4,2},{5,3},{6,4},{7,5},{10,8},{11,9},{12,10},{13,11},... | collective-permute-start | bytes 1597448 | tf_op jit(solution)/shard_map/ppermute | solution.py:395
  13.8 6.1 %tiles.5 = (f32[18816,128]{1,0:T(8,128)S(1)}, f32[18816,128]{1,0:T(8,128)S(1)}, f32[18816,128]{1,0:T(8,128)S(1)}, f32[18816,128]{1,0:T(8,128)S(1)}, f32[8,128]{1,0:T(8,128)}) custom-call(s32[3]{0:T(128)S(1)} %pad_add_fusion.refs_0_, f32[65,16,128]{2,1,0:T(8,128)S(1)} %copy-done.1, bf16[8,48,128]{2,1,0:T(8,128)(2,1)} %constant.23.clone.refs_2_.refs_4_.refs_5_.refs_3_, ...), custom_call_target="tpu_custom_call" | custom-call | bytes 8388608 | tf_op jit(solution)/shard_map/tiles/pallas_call | solution.py:411
  21.2 3.5 %collective-permute-start.1 = (f32[65,16,128]{2,1,0:T(8,128)S(1)}, f32[65,16,128]{2,1,0:T(8,128)S(1)}, u32[]{:S(2)}, u32[]{:S(2)}) collective-permute-start(f32[65,16,128]{2,1,0:T(8,128)S(1)} %collective-permute-done.refs_1_), channel_id=1, source_target_pairs={{2,4},{3,5},{4,6},{5,7},{10,12},{11,13},{12,14},{13,15},{18,20},{1... | collective-permute-start | bytes 1597448 | tf_op jit(solution)/shard_map/ppermute | solution.py:395
  24.7 2.4 %collective-permute-start.5 = (f32[65,16,128]{2,1,0:T(8,128)S(1)}, f32[65,16,128]{2,1,0:T(8,128)S(1)}, u32[]{:S(2)}, u32[]{:S(2)}) collective-permute-start(f32[65,16,128]{2,1,0:T(8,128)S(1)} %collective-permute-done.2.refs_2_), channel_id=1, source_target_pairs={{2,0},{3,1},{4,2},{5,3},{10,8},{11,9},{12,10},{13,11},{18,16},{19,... | collective-permute-start | bytes 1597448 | tf_op jit(solution)/shard_map/ppermute | solution.py:395
  27.1 3.4 %collective-permute-start.6 = (f32[65,16,128]{2,1,0:T(8,128)S(1)}, f32[65,16,128]{2,1,0:T(8,128)S(1)}, u32[]{:S(2)}, u32[]{:S(2)}) collective-permute-start(f32[65,16,128]{2,1,0:T(8,128)S(1)} %collective-permute-done.refs_1_), channel_id=1, source_target_pairs={{2,3},{3,2},{4,5},{5,4},{6,7},{7,6},{10,11},{11,10},{12,13},{13,12... | collective-permute-start | bytes 1597448 | tf_op jit(solution)/shard_map/ppermute | solution.py:395
  30.5 2.4 %collective-permute-start.7 = (f32[65,16,128]{2,1,0:T(8,128)S(1)}, f32[65,16,128]{2,1,0:T(8,128)S(1)}, u32[]{:S(2)}, u32[]{:S(2)}) collective-permute-start(f32[65,16,128]{2,1,0:T(8,128)S(1)} %collective-permute-done.2.refs_2_), channel_id=1, source_target_pairs={{0,1},{1,0},{2,3},{3,2},{4,5},{5,4},{8,9},{9,8},{10,11},{11,10},{1... | collective-permute-start | bytes 1597448 | tf_op jit(solution)/shard_map/ppermute | solution.py:395
  32.9 9.2 %tiles.6 = (f32[18816,128]{1,0:T(8,128)S(1)}, f32[18816,128]{1,0:T(8,128)S(1)}, f32[18816,128]{1,0:T(8,128)S(1)}, f32[18816,128]{1,0:T(8,128)S(1)}, f32[8,128]{1,0:T(8,128)}) custom-call(s32[3]{0:T(128)S(1)} %pad_add_fusion.refs_0_, ...), custom_call_target="tpu_custom_call", output_to_operand_aliasing={{0}: (6, {}), {1}: (7, {}), {2}: (8, {}), {3}: (9, {})} | custom-call | bytes 25165824 | tf_op jit(solution)/shard_map/tiles/pallas_call | solution.py:411
  44.2 3.4 %collective-permute-start.11 = (f32[65,16,128]{2,1,0:T(8,128)S(1)}, f32[65,16,128]{2,1,0:T(8,128)S(1)}, u32[]{:S(2)}, u32[]{:S(2)}) collective-permute-start(f32[65,16,128]{2,1,0:T(8,128)S(1)} %collective-permute-done.1.refs_1_), channel_id=1, source_target_pairs={{4,5},{5,4},{6,7},{7,6},{12,13},{13,12},{14,15},{15,14},{20,21},{2... | collective-permute-start | bytes 1597448 | tf_op jit(solution)/shard_map/ppermute | solution.py:395
  48.4 7.1 %collective-permute-done.7.refs_4_ = f32[65,16,128]{2,1,0:T(8,128)S(1)} collective-permute-done((f32[65,16,128]{2,1,0:T(8,128)S(1)}, f32[65,16,128]{2,1,0:T(8,128)S(1)}, u32[]{:S(2)}, u32[]{:S(2)}) %collective-permute-start.7) | collective-permute-done | bytes 532512 | tf_op jit(solution)/shard_map/ppermute | solution.py:395
  55.4 9.2 %tiles.7 = (f32[18816,128]{1,0:T(8,128)S(1)}, f32[18816,128]{1,0:T(8,128)S(1)}, f32[18816,128]{1,0:T(8,128)S(1)}, f32[18816,128]{1,0:T(8,128)S(1)}, f32[8,128]{1,0:T(8,128)}) custom-call(s32[3]{0:T(128)S(1)} %pad_add_fusion.refs_0_, ...), custom_call_target="tpu_custom_call", output_to_operand_aliasing={{0}: (7, {}), {1}: (8, {}), {2}: (9, {}), {3}: (10, {})} | custom-call | bytes 33554432 | tf_op jit(solution)/shard_map/tiles/pallas_call | solution.py:411
  66.1 4.5 %tiles.8 = (f32[18816,128]{1,0:T(8,128)S(1)}, f32[18816,128]{1,0:T(8,128)S(1)}, f32[18816,128]{1,0:T(8,128)S(1)}, f32[18816,128]{1,0:T(8,128)S(1)}, f32[8,128]{1,0:T(8,128)}) custom-call(s32[3]{0:T(128)S(1)} %pad_add_fusion.refs_0_, ...), custom_call_target="tpu_custom_call", output_to_operand_aliasing={{0}: (7, {}), {1}: (8, {}), {2}: (9, {}), {3}: (10, {})} | custom-call | bytes 33554432 | tf_op jit(solution)/shard_map/tiles/pallas_call | solution.py:411
  70.6 18.6 %tiles.9 = (f32[18816,128]{1,0:T(8,128)S(1)}, f32[18816,128]{1,0:T(8,128)S(1)}, f32[18816,128]{1,0:T(8,128)S(1)}, f32[18816,128]{1,0:T(8,128)S(1)}, f32[8,128]{1,0:T(8,128)}) custom-call(s32[3]{0:T(128)S(1)} %pad_add_fusion.refs_0_, ...), custom_call_target="tpu_custom_call", output_to_operand_aliasing={{0}: (6, {}), {1}: (7, {}), {2}: (8, {}), {3}: (9, {})} | custom-call | bytes 16777216 | tf_op jit(solution)/shard_map/tiles/pallas_call | solution.py:411
  89.2 4.1 %rows.6.refs_6_ = f32[24,3,48,128]{3,2,1,0:T(8,128)S(1)} custom-call(s32[3]{0:T(128)S(1)} %pad_add_fusion.refs_0_, f32[18816,128]{1,0:T(8,128)S(1)} %get-tuple-element.59.refs_1_, f32[18816,128]{1,0:T(8,128)S(1)} %get-tuple-element.60.refs_2_, f32[18816,128]{1,0:T(8,128)S(1)} %get-tuple-element.61.refs_3_, f32[18816,128]{1,0:T(8,128)S(1)} %get-tuple-element.62.refs_4_, ...), custom_call_target="tpu_custom_call" | custom-call | flops 1 | bytes 1 | tf_op jit(solution)/shard_map/rows/pallas_call | solution.py:465
  93.4 2.2 %rows.7.refs_7_ = f32[12,3,48,128]{3,2,1,0:T(8,128)S(1)} custom-call(s32[3]{0:T(128)S(1)} %pad_add_fusion.refs_0_, f32[18816,128]{1,0:T(8,128)S(1)} %get-tuple-element.59.refs_1_, f32[18816,128]{1,0:T(8,128)S(1)} %get-tuple-element.60.refs_2_, f32[18816,128]{1,0:T(8,128)S(1)} %get-tuple-element.61.refs_3_, f32[18816,128]{1,0:T(8,128)S(1)} %get-tuple-element.62.refs_4_, ...), custom_call_target="tpu_custom_call" | custom-call | flops 1 | bytes 1 | tf_op jit(solution)/shard_map/rows/pallas_call | solution.py:465
  97.0 2.2 %rows.8.refs_6_ = f32[12,3,48,128]{3,2,1,0:T(8,128)S(1)} custom-call(s32[3]{0:T(128)S(1)} %pad_add_fusion.refs_0_, f32[18816,128]{1,0:T(8,128)S(1)} %get-tuple-element.59.refs_1_, f32[18816,128]{1,0:T(8,128)S(1)} %get-tuple-element.60.refs_2_, f32[18816,128]{1,0:T(8,128)S(1)} %get-tuple-element.61.refs_3_, f32[18816,128]{1,0:T(8,128)S(1)} %get-tuple-element.62.refs_4_, ...), custom_call_target="tpu_custom_call" | custom-call | flops 1 | bytes 1 | tf_op jit(solution)/shard_map/rows/pallas_call | solution.py:465
  100.8 2.2 %rows.9.refs_7_ = f32[12,3,48,128]{3,2,1,0:T(8,128)S(1)} custom-call(s32[3]{0:T(128)S(1)} %pad_add_fusion.refs_0_, f32[18816,128]{1,0:T(8,128)S(1)} %get-tuple-element.59.refs_1_, f32[18816,128]{1,0:T(8,128)S(1)} %get-tuple-element.60.refs_2_, f32[18816,128]{1,0:T(8,128)S(1)} %get-tuple-element.61.refs_3_, f32[18816,128]{1,0:T(8,128)S(1)} %get-tuple-element.62.refs_4_, ...), custom_call_target="tpu_custom_call" | custom-call | flops 1 | bytes 1 | tf_op jit(solution)/shard_map/rows/pallas_call | solution.py:465
  103.1 2.2 %rows.10.refs_6_ = f32[12,3,48,128]{3,2,1,0:T(8,128)S(1)} custom-call(s32[3]{0:T(128)S(1)} %pad_add_fusion.refs_0_, f32[18816,128]{1,0:T(8,128)S(1)} %get-tuple-element.59.refs_1_, f32[18816,128]{1,0:T(8,128)S(1)} %get-tuple-element.60.refs_2_, f32[18816,128]{1,0:T(8,128)S(1)} %get-tuple-element.61.refs_3_, f32[18816,128]{1,0:T(8,128)S(1)} %get-tuple-element.62.refs_4_, ...), custom_call_target="tpu_custom_call" | custom-call | flops 1 | bytes 1 | tf_op jit(solution)/shard_map/rows/pallas_call | solution.py:465
  105.9 3.9 %rows.11.refs_0_ = f32[24,3,48,128]{3,2,1,0:T(8,128)S(1)} custom-call(s32[3]{0:T(128)S(1)} %pad_add_fusion.refs_0_, f32[18816,128]{1,0:T(8,128)S(1)} %get-tuple-element.59.refs_1_, f32[18816,128]{1,0:T(8,128)S(1)} %get-tuple-element.60.refs_2_, f32[18816,128]{1,0:T(8,128)S(1)} %get-tuple-element.61.refs_3_, f32[18816,128]{1,0:T(8,128)S(1)} %get-tuple-element.62.refs_4_, ...), custom_call_target="tpu_custom_call" | custom-call | flops 1 | bytes 1 | tf_op jit(solution)/shard_map/rows/pallas_call | solution.py:465
  109.8 12.0 %collective-permute-done.17.refs_2_ = f32[12,3,48,128]{3,2,1,0:T(8,128)S(1)} collective-permute-done((f32[12,3,48,128]{3,2,1,0:T(8,128)S(1)}, f32[12,3,48,128]{3,2,1,0:T(8,128)S(1)}, u32[]{:S(2)}, u32[]{:S(2)}) %collective-permute-start.17) | collective-permute-done | bytes 884768 | tf_op jit(solution)/shard_map/ppermute | solution.py:476
  121.8 2.8 %finish.2.refs_7_ = f32[2,24,48,192]{3,2,1,0:T(8,128)} custom-call(f32[24,3,48,128]{3,2,1,0:T(8,128)S(1)} %rows.11.refs_0_, f32[12,3,48,128]{3,2,1,0:T(8,128)S(1)} %collective-permute-done.16.refs_1_, f32[12,3,48,128]{3,2,1,0:T(8,128)S(1)} %collective-permute-done.17.refs_2_, bf16[512,192]{1,0:T(8,128)(2,1)S(1)} %copy-done.2, f32[1,192]{1,0:T(1,128)S(1)} %bitcast.8, ...), custom_call_target="tpu_custom_call" | custom-call | tf_op jit(solution)/shard_map/finish/pallas_call | solution.py:513
  124.6 15.4 %collective-permute-done.15.refs_2_ = f32[12,3,48,128]{3,2,1,0:T(8,128)S(1)} collective-permute-done((f32[12,3,48,128]{3,2,1,0:T(8,128)S(1)}, f32[12,3,48,128]{3,2,1,0:T(8,128)S(1)}, u32[]{:S(2)}, u32[]{:S(2)}) %collective-permute-start.15) | collective-permute-done | bytes 884768 | tf_op jit(solution)/shard_map/ppermute | solution.py:476
  140.0 2.8 %finish.3 = f32[2,24,48,192]{3,2,1,0:T(8,128)} custom-call(f32[24,3,48,128]{3,2,1,0:T(8,128)S(1)} %rows.11.refs_0_, f32[12,3,48,128]{3,2,1,0:T(8,128)S(1)} %collective-permute-done.14.refs_1_, f32[12,3,48,128]{3,2,1,0:T(8,128)S(1)} %collective-permute-done.15.refs_2_, bf16[512,192]{1,0:T(8,128)(2,1)S(1)} %copy-done.2, ...), custom_call_target="tpu_custom_call", output_to_operand_aliasing={{}: (7, {})} | custom-call | tf_op jit(solution)/shard_map/finish/pallas_call | solution.py:513
  (39 shorter events, 12.0 us)
Async XLA Ops:
  5.2 15.9 %collective-permute-start = (f32[65,16,128]{2,1,0:T(8,128)}, f32[65,16,128]{2,1,0:T(8,128)S(1)}, u32[]{:S(2)}, u32[]{:S(2)}) collective-permute-start(f32[65,16,128]{2,1,0:T(8,128)} %spread.1.refs_1_), channel_id=1, source_target_pairs={{0,2},{1,3},{2,4},{3,5},{4,6},{5,7},{8,10},{9,11},{10,12},{11,13},... | collective-permute-start | bytes 1597448 | tf_op jit(solution)/shard_map/ppermute | solution.py:395
  8.7 15.9 %collective-permute-start.2 = (f32[65,16,128]{2,1,0:T(8,128)}, f32[65,16,128]{2,1,0:T(8,128)S(1)}, u32[]{:S(2)}, u32[]{:S(2)}) collective-permute-start(f32[65,16,128]{2,1,0:T(8,128)} %spread.1.refs_1_), channel_id=1, source_target_pairs={{2,0},{3,1},{4,2},{5,3},{6,4},{7,5},{10,8},{11,9},{12,10},{13,11},... | collective-permute-start | bytes 1597448 | tf_op jit(solution)/shard_map/ppermute | solution.py:395
  11.1 21.9 %collective-permute-start.3 = (f32[65,16,128]{2,1,0:T(8,128)}, f32[65,16,128]{2,1,0:T(8,128)S(1)}, u32[]{:S(2)}, u32[]{:S(2)}) collective-permute-start(f32[65,16,128]{2,1,0:T(8,128)} %spread.1.refs_1_), channel_id=1, source_target_pairs={{0,1},{1,0},{2,3},{3,2},{4,5},{5,4},{6,7},{7,6},{8,9},{9,8},{10,11... | collective-permute-start | bytes 1597448 | tf_op jit(solution)/shard_map/ppermute | solution.py:395
  12.7 1.0 copy-start.1
  21.2 21.0 %collective-permute-start.1 = (f32[65,16,128]{2,1,0:T(8,128)S(1)}, f32[65,16,128]{2,1,0:T(8,128)S(1)}, u32[]{:S(2)}, u32[]{:S(2)}) collective-permute-start(f32[65,16,128]{2,1,0:T(8,128)S(1)} %collective-permute-done.refs_1_), channel_id=1, source_target_pairs={{2,4},{3,5},{4,6},{5,7},{10,12},{11,13},{12,14},{13,15},{18,20},{1... | collective-permute-start | bytes 1597448 | tf_op jit(solution)/shard_map/ppermute | solution.py:395
  24.7 18.8 %collective-permute-start.5 = (f32[65,16,128]{2,1,0:T(8,128)S(1)}, f32[65,16,128]{2,1,0:T(8,128)S(1)}, u32[]{:S(2)}, u32[]{:S(2)}) collective-permute-start(f32[65,16,128]{2,1,0:T(8,128)S(1)} %collective-permute-done.2.refs_2_), channel_id=1, source_target_pairs={{2,0},{3,1},{4,2},{5,3},{10,8},{11,9},{12,10},{13,11},{18,16},{19,... | collective-permute-start | bytes 1597448 | tf_op jit(solution)/shard_map/ppermute | solution.py:395
  27.1 20.6 %collective-permute-start.6 = (f32[65,16,128]{2,1,0:T(8,128)S(1)}, f32[65,16,128]{2,1,0:T(8,128)S(1)}, u32[]{:S(2)}, u32[]{:S(2)}) collective-permute-start(f32[65,16,128]{2,1,0:T(8,128)S(1)} %collective-permute-done.refs_1_), channel_id=1, source_target_pairs={{2,3},{3,2},{4,5},{5,4},{6,7},{7,6},{10,11},{11,10},{12,13},{13,12... | collective-permute-start | bytes 1597448 | tf_op jit(solution)/shard_map/ppermute | solution.py:395
  30.5 24.9 %collective-permute-start.7 = (f32[65,16,128]{2,1,0:T(8,128)S(1)}, f32[65,16,128]{2,1,0:T(8,128)S(1)}, u32[]{:S(2)}, u32[]{:S(2)}) collective-permute-start(f32[65,16,128]{2,1,0:T(8,128)S(1)} %collective-permute-done.2.refs_2_), channel_id=1, source_target_pairs={{0,1},{1,0},{2,3},{3,2},{4,5},{5,4},{8,9},{9,8},{10,11},{11,10},{1... | collective-permute-start | bytes 1597448 | tf_op jit(solution)/shard_map/ppermute | solution.py:395
  42.2 22.5 %collective-permute-start.4 = (f32[65,16,128]{2,1,0:T(8,128)S(1)}, f32[65,16,128]{2,1,0:T(8,128)S(1)}, u32[]{:S(2)}, u32[]{:S(2)}) collective-permute-start(f32[65,16,128]{2,1,0:T(8,128)S(1)} %collective-permute-done.1.refs_1_), channel_id=1, source_target_pairs={{4,6},{5,7},{12,14},{13,15},{20,22},{21,23},{28,30},{29,31}} | collective-permute-start | bytes 1597448 | tf_op jit(solution)/shard_map/ppermute | solution.py:395
  43.5 21.8 %collective-permute-start.9 = (f32[65,16,128]{2,1,0:T(8,128)S(1)}, f32[65,16,128]{2,1,0:T(8,128)S(1)}, u32[]{:S(2)}, u32[]{:S(2)}) collective-permute-start(f32[65,16,128]{2,1,0:T(8,128)S(1)} %collective-permute-done.5.refs_2_), channel_id=1, source_target_pairs={{2,0},{3,1},{10,8},{11,9},{18,16},{19,17},{26,24},{27,25}} | collective-permute-start | bytes 1597448 | tf_op jit(solution)/shard_map/ppermute | solution.py:395
  44.2 21.9 %collective-permute-start.11 = (f32[65,16,128]{2,1,0:T(8,128)S(1)}, f32[65,16,128]{2,1,0:T(8,128)S(1)}, u32[]{:S(2)}, u32[]{:S(2)}) collective-permute-start(f32[65,16,128]{2,1,0:T(8,128)S(1)} %collective-permute-done.1.refs_1_), channel_id=1, source_target_pairs={{4,5},{5,4},{6,7},{7,6},{12,13},{13,12},{14,15},{15,14},{20,21},{2... | collective-permute-start | bytes 1597448 | tf_op jit(solution)/shard_map/ppermute | solution.py:395
  47.6 18.4 %collective-permute-start.12 = (f32[65,16,128]{2,1,0:T(8,128)S(1)}, f32[65,16,128]{2,1,0:T(8,128)S(1)}, u32[]{:S(2)}, u32[]{:S(2)}) collective-permute-start(f32[65,16,128]{2,1,0:T(8,128)S(1)} %collective-permute-done.5.refs_2_), channel_id=1, source_target_pairs={{0,1},{1,0},{2,3},{3,2},{8,9},{9,8},{10,11},{11,10},{16,17},{17,16... | collective-permute-start | bytes 1597448 | tf_op jit(solution)/shard_map/ppermute | solution.py:395
  64.6 5.9 %collective-permute-start.8 = (f32[65,16,128]{2,1,0:T(8,128)S(1)}, f32[65,16,128]{2,1,0:T(8,128)S(1)}, u32[]{:S(2)}, u32[]{:S(2)}) collective-permute-start(f32[65,16,128]{2,1,0:T(8,128)S(1)} %collective-permute-done.4.refs_1_), channel_id=1, source_target_pairs={{6,7},{7,6},{14,15},{15,14},{22,23},{23,22},{30,31},{31,30}} | collective-permute-start | bytes 1597448 | tf_op jit(solution)/shard_map/ppermute | solution.py:395
  65.4 5.2 %collective-permute-start.10 = (f32[65,16,128]{2,1,0:T(8,128)S(1)}, f32[65,16,128]{2,1,0:T(8,128)S(1)}, u32[]{:S(2)}, u32[]{:S(2)}) collective-permute-start(f32[65,16,128]{2,1,0:T(8,128)S(1)} %collective-permute-done.9.refs_2_), channel_id=1, source_target_pairs={{0,1},{1,0},{8,9},{9,8},{16,17},{17,16},{24,25},{25,24}} | collective-permute-start | bytes 1597448 | tf_op jit(solution)/shard_map/ppermute | solution.py:395
  70.6 18.6 %copy-start = (bf16[2,2,192,256]{3,2,1,0:T(8,128)(2,1)S(1)}, bf16[2,2,192,256]{3,2,1,0:T(8,128)(2,1)}, u32[]{:S(2)}) copy-start(bf16[2,2,192,256]{3,2,1,0:T(8,128)(2,1)} %constant.26.clone.refs_5_) | copy-start | bytes 1179652
  93.3 3.8 %collective-permute-start.13 = (f32[24,3,48,128]{3,2,1,0:T(8,128)S(1)}, f32[24,3,48,128]{3,2,1,0:T(8,128)S(1)}, u32[]{:S(2)}, u32[]{:S(2)}) collective-permute-start(f32[24,3,48,128]{3,2,1,0:T(8,128)S(1)} %rows.6.refs_6_), channel_id=1, source_target_pairs={{0,8},{8,0},{16,24},{24,16},{1,9},{9,1},{17,25},{25,17},{2,10},{10... | collective-permute-start | bytes 5308424 | tf_op jit(solution)/shard_map/ppermute | solution.py:476
  95.6 14.3 %collective-permute-start.16 = (f32[12,3,48,128]{3,2,1,0:T(8,128)S(1)}, f32[12,3,48,128]{3,2,1,0:T(8,128)S(1)}, u32[]{:S(2)}, u32[]{:S(2)}) collective-permute-start(f32[12,3,48,128]{3,2,1,0:T(8,128)S(1)} %rows.7.refs_7_), channel_id=1, source_target_pairs={{0,8},{8,0},{16,24},{24,16},{1,9},{9,1},{17,25},{25,17},{2,10},{10... | collective-permute-start | bytes 2654216 | tf_op jit(solution)/shard_map/ppermute | solution.py:476
  99.3 22.6 %collective-permute-start.17 = (f32[12,3,48,128]{3,2,1,0:T(8,128)S(1)}, f32[12,3,48,128]{3,2,1,0:T(8,128)S(1)}, u32[]{:S(2)}, u32[]{:S(2)}) collective-permute-start(f32[12,3,48,128]{3,2,1,0:T(8,128)S(1)} %rows.8.refs_6_), channel_id=1, source_target_pairs={{0,16},{8,24},{16,0},{24,8},{1,17},{9,25},{17,1},{25,9},{2,18},{10... | collective-permute-start | bytes 2654216 | tf_op jit(solution)/shard_map/ppermute | solution.py:476
  103.0 21.6 %collective-permute-start.14 = (f32[12,3,48,128]{3,2,1,0:T(8,128)S(1)}, f32[12,3,48,128]{3,2,1,0:T(8,128)S(1)}, u32[]{:S(2)}, u32[]{:S(2)}) collective-permute-start(f32[12,3,48,128]{3,2,1,0:T(8,128)S(1)} %rows.9.refs_7_), channel_id=1, source_target_pairs={{0,8},{8,0},{16,24},{24,16},{1,9},{9,1},{17,25},{25,17},{2,10},{10... | collective-permute-start | bytes 2654216 | tf_op jit(solution)/shard_map/ppermute | solution.py:476
  105.3 16.5 %copy-start.2 = (bf16[512,192]{1,0:T(8,128)(2,1)S(1)}, bf16[512,192]{1,0:T(8,128)(2,1)}, u32[]{:S(2)}) copy-start(bf16[512,192]{1,0:T(8,128)(2,1)} %constant.27.clone.refs_3_) | copy-start | bytes 589828
  105.3 16.5 %copy-start.3 = (f32[192]{0:T(256)S(1)}, f32[192]{0:T(256)}, u32[]{:S(2)}) copy-start(f32[192]{0:T(256)} %param.19) | copy-start | bytes 2308
  105.3 16.5 %copy-start.4 = (f32[48]{0:T(128)S(1)}, f32[48]{0:T(128)}, u32[]{:S(2)}) copy-start(f32[48]{0:T(128)} %param.20) | copy-start | bytes 580
  105.3 16.5 %copy-start.5 = (f32[24]{0:T(128)S(1)}, f32[24]{0:T(128)}, u32[]{:S(2)}) copy-start(f32[24]{0:T(128)} %refs_6_.5) | copy-start | bytes 292
  105.3 34.6 %collective-permute-start.15 = (f32[12,3,48,128]{3,2,1,0:T(8,128)S(1)}, f32[12,3,48,128]{3,2,1,0:T(8,128)S(1)}, u32[]{:S(2)}, u32[]{:S(2)}) collective-permute-start(f32[12,3,48,128]{3,2,1,0:T(8,128)S(1)} %rows.10.refs_6_), channel_id=1, source_target_pairs={{0,16},{8,24},{16,0},{24,8},{1,17},{9,25},{17,1},{25,9},{2,18},{10... | collective-permute-start | bytes 2654216 | tf_op jit(solution)/shard_map/ppermute | solution.py:476

commit v15 on v13

--- a/solution.py
+++ b/solution.py
@@ -159,7 +159,7 @@
         out_ref[pair] = jnp.where(left, piece[: 2 * TILE], piece[2 * TILE :])
         return carry
 
-    lax.fori_loop(0, blocks // 2, pair_body, 0, unroll=8)
+    lax.fori_loop(0, blocks // 2, pair_body, 0, unroll=16)
     out_ref[blocks // 2] = jnp.broadcast_to(codes, (2 * TILE, LANES))
 
 
@@ -452,13 +452,12 @@
 
     every = range(Z_CHIPS)
     passed = {1: tiles, -1: tiles}
-    arrived, token, acc = [(every, tiles)], None, []
+    arrived, waiting, token, acc = [(every, tiles)], [], None, []
     for steps in range(1, Z_CHIPS + 1):
+        ready, waiting = (waiting, []) if steps == Z_CHIPS else (waiting[:-1], waiting[-1:])
         partners = []
-        if steps == 1:
-            partners += across(tiles, every)
-        else:
-            partners += [held for holders, array in arrived[:2] for held in across(after(array, token), holders)]
+        for holders, array in arrived:
+            partners += across(array if token is None else after(array, token), holders)
         moved = []
         if steps < Z_CHIPS:
             for way in (1, -1):
@@ -466,9 +465,10 @@
                 value = passed[way] if token is None else after(passed[way], token)
                 passed[way] = send(value, moves, 0)
                 moved.append(([to for _, to in moves], passed[way]))
-        acc, token = add_tiles(arrived, acc)
-        arrived = moved + partners
-    acc, _ = add_tiles(arrived, acc, [column])
+        acc, token = add_tiles(arrived + [pair for pairs in ready for pair in pairs], acc)
+        arrived = moved
+        waiting.append(partners)
+    acc, _ = add_tiles(waiting[-1], acc, [column])
 
     row_table = jnp.asarray(row_tables())
     part_shape = (3, 2 * planes_padded, LANES)
@@ -488,7 +488,7 @@
             compiler_params=params,
             cost_estimate=pl.CostEstimate(flops=1, bytes_accessed=1, transcendentals=0),
             name="rows",
-        )(places, *in_vmem(acc), row_table, *addends, *in_hbm(after))
+        )(places, *in_vmem(acc), row_table, *addends, *after)
 
     def swap(value, bit):
         return lax.ppermute(value, "gx", [(index, index ^ bit) for index in range(grid_rows)])

time: 145 us -> 159 us (1.097)
  waiting for transfers between devices: 35 us -> 51.2 us
  local copies, waits for them, and re-layouts: 3.6 us -> 0.03 us
  starting transfers between devices: 29.4 us -> 31.6 us
    ppermute x13, waiting for transfers between devices: 8.96 us -> 22.9 us  [send(): return lax.ppermute(value, 'gy', moves)]
    unnamed x22 -> x10, local copies, waits for them, and re-layouts: 3.6 us -> 0.03 us
    ppermute x5, waiting for transfers between devices: 26 us -> 28.3 us  [swap(): lax.ppermute(value, 'gx', [(index, index ^ bit) for index in range(grid_r...]
    ppermute x13, starting transfers between devices: 26.7 us -> 28.9 us  [send(): return lax.ppermute(value, 'gy', moves)]
  transfers between devices with their start and end apart: 18 -> 18, of which waited for: 5 -> 7; matrix products, arithmetic and copies ran while one was open for 0% -> 0% of each run, Pallas kernels for 30% -> 28%
where the time goes in v15:
time: 159 us; the launch traced here: 157 us
  Pallas kernels  74.2 us (47%)
  waiting for transfers between devices  51.2 us (32%)
  starting transfers between devices  31.6 us (20%)
    pallas_call x5, Pallas kernels, add_tiles(): pl.pallas_call(functools.partial(tiles_kernel, conditions, not acc, bool(...  47.2 us
    ppermute x13, starting transfers between devices, send(): return lax.ppermute(value, 'gy', moves)  28.9 us
    ppermute x5, waiting for transfers between devices, swap(): lax.ppermute(value, 'gx', [(index, index ^ bit) for index in range(grid_r...  28.3 us
    ppermute x13, waiting for transfers between devices, send(): return lax.ppermute(value, 'gy', moves)  22.9 us
    pallas_call x6, Pallas kernels, rows_for(): pl.pallas_call(body, in_specs=[smem] + [vmem] * (1 + PARTS + len(addends)...  16.8 us
    pallas_call x2, Pallas kernels, on_device(): pl.pallas_call(finish, grid=(1,), out_shape=jax.ShapeDtypeStruct((2, plan...  5.54 us
    pallas_call x1, Pallas kernels, on_device(): pl.pallas_call(functools.partial(spread_kernel, tile_rows, tile_cols, gri...  4.72 us
  transfers between devices with their start and end apart: 18, of which 7 were waited for; matrix products, arithmetic and copies ran while one was open for 0% of the time, Pallas kernels for 28%

profile of v15, /device:TPU:16, one launch (start us, length us, event | category | flops | bytes accessed | tf_op | source)
XLA Modules:
  0.0 157.5 jit_solution(10839801595907298050)
XLA Ops:
  0.0 4.7 %spread.1.refs_1_ = f32[65,16,128]{2,1,0:T(8,128)} custom-call(f32[128,2,128]{2,1,0:T(2,128)} %samples_ref.1, f32[128,3,4,128]{3,2,1,0:T(4,128)} %kernel_ref.1, s32[3,128,128]{2,1,0:T(8,128)} %bitcast.12, s32[1,128]{1,0:T(1,128)} %bitcast.13, s32[1,128]{1,0:T(1,128)} %bitcast.14), custom_call_target="tpu_custom_call" | custom-call | tf_op jit(solution)/shard_map/spread/pallas_call | solution.py:396
  4.7 3.5 %collective-permute-start = (f32[65,16,128]{2,1,0:T(8,128)}, f32[65,16,128]{2,1,0:T(8,128)S(1)}, u32[]{:S(2)}, u32[]{:S(2)}) collective-permute-start(f32[65,16,128]{2,1,0:T(8,128)} %spread.1.refs_1_), channel_id=1, source_target_pairs={{0,2},{1,3},{2,4},{3,5},{4,6},{5,7},{8,10},{9,11},{10,12},{11,13},... | collective-permute-start | bytes 1597448 | tf_op jit(solution)/shard_map/ppermute | solution.py:410
  8.2 2.4 %collective-permute-start.2 = (f32[65,16,128]{2,1,0:T(8,128)}, f32[65,16,128]{2,1,0:T(8,128)S(1)}, u32[]{:S(2)}, u32[]{:S(2)}) collective-permute-start(f32[65,16,128]{2,1,0:T(8,128)} %spread.1.refs_1_), channel_id=1, source_target_pairs={{2,0},{3,1},{4,2},{5,3},{6,4},{7,5},{10,8},{11,9},{12,10},{13,11},... | collective-permute-start | bytes 1597448 | tf_op jit(solution)/shard_map/ppermute | solution.py:410
  10.6 6.4 %tiles.5 = (f32[18816,128]{1,0:T(8,128)S(1)}, f32[18816,128]{1,0:T(8,128)S(1)}, f32[18816,128]{1,0:T(8,128)S(1)}, f32[18816,128]{1,0:T(8,128)S(1)}, f32[8,128]{1,0:T(8,128)}) custom-call(s32[3]{0:T(128)S(1)} %pad_add_fusion.refs_0_, f32[65,16,128]{2,1,0:T(8,128)} %spread.1.refs_1_, bf16[8,48,128]{2,1,0:T(8,128)(2,1)} %constant.23.clone.refs_2_.refs_3_.refs_4_.refs_7_, ...), custom_call_target="tpu_custom_call" | custom-call | bytes 8388608 | tf_op jit(solution)/shard_map/tiles/pallas_call | solution.py:427
  17.1 3.6 %collective-permute-done.refs_1_ = f32[65,16,128]{2,1,0:T(8,128)S(1)} collective-permute-done((f32[65,16,128]{2,1,0:T(8,128)}, f32[65,16,128]{2,1,0:T(8,128)S(1)}, u32[]{:S(2)}, u32[]{:S(2)}) %collective-permute-start) | collective-permute-done | bytes 532512 | tf_op jit(solution)/shard_map/ppermute | solution.py:410
  20.6 3.5 %collective-permute-start.1 = (f32[65,16,128]{2,1,0:T(8,128)S(1)}, f32[65,16,128]{2,1,0:T(8,128)S(1)}, u32[]{:S(2)}, u32[]{:S(2)}) collective-permute-start(f32[65,16,128]{2,1,0:T(8,128)S(1)} %collective-permute-done.refs_1_), channel_id=1, source_target_pairs={{2,4},{3,5},{4,6},{5,7},{10,12},{11,13},{12,14},{13,15},{18,20},{1... | collective-permute-start | bytes 1597448 | tf_op jit(solution)/shard_map/ppermute | solution.py:410
  24.1 2.4 %collective-permute-start.4 = (f32[65,16,128]{2,1,0:T(8,128)S(1)}, f32[65,16,128]{2,1,0:T(8,128)S(1)}, u32[]{:S(2)}, u32[]{:S(2)}) collective-permute-start(f32[65,16,128]{2,1,0:T(8,128)S(1)} %collective-permute-done.2.refs_2_), channel_id=1, source_target_pairs={{2,0},{3,1},{4,2},{5,3},{10,8},{11,9},{12,10},{13,11},{18,16},{19,... | collective-permute-start | bytes 1597448 | tf_op jit(solution)/shard_map/ppermute | solution.py:410
  28.1 6.6 %tiles.6 = (f32[18816,128]{1,0:T(8,128)S(1)}, f32[18816,128]{1,0:T(8,128)S(1)}, f32[18816,128]{1,0:T(8,128)S(1)}, f32[18816,128]{1,0:T(8,128)S(1)}, f32[8,128]{1,0:T(8,128)}) custom-call(s32[3]{0:T(128)S(1)} %pad_add_fusion.refs_0_, ...), custom_call_target="tpu_custom_call", output_to_operand_aliasing={{0}: (5, {}), {1}: (6, {}), {2}: (7, {}), {3}: (8, {})} | custom-call | bytes 16777216 | tf_op jit(solution)/shard_map/tiles/pallas_call | solution.py:427
  35.5 3.5 %collective-permute-start.3 = (f32[65,16,128]{2,1,0:T(8,128)S(1)}, f32[65,16,128]{2,1,0:T(8,128)S(1)}, u32[]{:S(2)}, u32[]{:S(2)}) collective-permute-start(f32[65,16,128]{2,1,0:T(8,128)S(1)} %collective-permute-done.1.refs_1_), channel_id=1, source_target_pairs={{4,6},{5,7},{12,14},{13,15},{20,22},{21,23},{28,30},{29,31}} | collective-permute-start | bytes 1597448 | tf_op jit(solution)/shard_map/ppermute | solution.py:410
  39.7 3.4 %collective-permute-start.9 = (f32[65,16,128]{2,1,0:T(8,128)S(1)}, f32[65,16,128]{2,1,0:T(8,128)S(1)}, u32[]{:S(2)}, u32[]{:S(2)}) collective-permute-start(f32[65,16,128]{2,1,0:T(8,128)S(1)} %collective-permute-done.refs_1_), channel_id=1, source_target_pairs={{2,3},{3,2},{4,5},{5,4},{6,7},{7,6},{10,11},{11,10},{12,13},{13,12... | collective-permute-start | bytes 1597448 | tf_op jit(solution)/shard_map/ppermute | solution.py:410
  43.2 2.4 %collective-permute-start.10 = (f32[65,16,128]{2,1,0:T(8,128)S(1)}, f32[65,16,128]{2,1,0:T(8,128)S(1)}, u32[]{:S(2)}, u32[]{:S(2)}) collective-permute-start(f32[65,16,128]{2,1,0:T(8,128)S(1)} %collective-permute-done.2.refs_2_), channel_id=1, source_target_pairs={{0,1},{1,0},{2,3},{3,2},{4,5},{5,4},{8,9},{9,8},{10,11},{11,10},{1... | collective-permute-start | bytes 1597448 | tf_op jit(solution)/shard_map/ppermute | solution.py:410
  45.6 3.4 %collective-permute-start.11 = (f32[65,16,128]{2,1,0:T(8,128)S(1)}, f32[65,16,128]{2,1,0:T(8,128)S(1)}, u32[]{:S(2)}, u32[]{:S(2)}) collective-permute-start(f32[65,16,128]{2,1,0:T(8,128)S(1)} %collective-permute-done.1.refs_1_), channel_id=1, source_target_pairs={{4,5},{5,4},{6,7},{7,6},{12,13},{13,12},{14,15},{15,14},{20,21},{2... | collective-permute-start | bytes 1597448 | tf_op jit(solution)/shard_map/ppermute | solution.py:410
  49.0 6.6 %tiles.7 = (f32[18816,128]{1,0:T(8,128)S(1)}, f32[18816,128]{1,0:T(8,128)S(1)}, f32[18816,128]{1,0:T(8,128)S(1)}, f32[18816,128]{1,0:T(8,128)S(1)}, f32[8,128]{1,0:T(8,128)}) custom-call(s32[3]{0:T(128)S(1)} %pad_add_fusion.refs_0_, ...), custom_call_target="tpu_custom_call", output_to_operand_aliasing={{0}: (6, {}), {1}: (7, {}), {2}: (8, {}), {3}: (9, {})} | custom-call | bytes 25165824 | tf_op jit(solution)/shard_map/tiles/pallas_call | solution.py:427
  57.7 10.3 %collective-permute-done.10.refs_4_ = f32[65,16,128]{2,1,0:T(8,128)S(1)} collective-permute-done((f32[65,16,128]{2,1,0:T(8,128)S(1)}, f32[65,16,128]{2,1,0:T(8,128)S(1)}, u32[]{:S(2)}, u32[]{:S(2)}) %collective-permute-start.10) | collective-permute-done | bytes 532512 | tf_op jit(solution)/shard_map/ppermute | solution.py:410
  68.1 8.1 %collective-permute-done.11.refs_5_ = f32[65,16,128]{2,1,0:T(8,128)S(1)} collective-permute-done((f32[65,16,128]{2,1,0:T(8,128)S(1)}, f32[65,16,128]{2,1,0:T(8,128)S(1)}, u32[]{:S(2)}, u32[]{:S(2)}) %collective-permute-start.11) | collective-permute-done | bytes 532512 | tf_op jit(solution)/shard_map/ppermute | solution.py:410
  76.2 9.1 %tiles.8 = (f32[18816,128]{1,0:T(8,128)S(1)}, f32[18816,128]{1,0:T(8,128)S(1)}, f32[18816,128]{1,0:T(8,128)S(1)}, f32[18816,128]{1,0:T(8,128)S(1)}, f32[8,128]{1,0:T(8,128)}) custom-call(s32[3]{0:T(128)S(1)} %pad_add_fusion.refs_0_, ...), custom_call_target="tpu_custom_call", output_to_operand_aliasing={{0}: (9, {}), {1}: (10, {}), {2}: (11, {}), {3}: (12, {})} | custom-call | bytes 50331648 | tf_op jit(solution)/shard_map/tiles/pallas_call | solution.py:427
  85.3 18.6 %tiles.9 = (f32[18816,128]{1,0:T(8,128)S(1)}, f32[18816,128]{1,0:T(8,128)S(1)}, f32[18816,128]{1,0:T(8,128)S(1)}, f32[18816,128]{1,0:T(8,128)S(1)}, f32[8,128]{1,0:T(8,128)}) custom-call(s32[3]{0:T(128)S(1)} %pad_add_fusion.refs_0_, ...), custom_call_target="tpu_custom_call", output_to_operand_aliasing={{0}: (6, {}), {1}: (7, {}), {2}: (8, {}), {3}: (9, {})} | custom-call | bytes 16777216 | tf_op jit(solution)/shard_map/tiles/pallas_call | solution.py:427
  103.9 4.1 %rows.6.refs_6_ = f32[24,3,48,128]{3,2,1,0:T(8,128)S(1)} custom-call(s32[3]{0:T(128)S(1)} %pad_add_fusion.refs_0_, f32[18816,128]{1,0:T(8,128)S(1)} %get-tuple-element.59.refs_1_, f32[18816,128]{1,0:T(8,128)S(1)} %get-tuple-element.60.refs_2_, f32[18816,128]{1,0:T(8,128)S(1)} %get-tuple-element.61.refs_3_, f32[18816,128]{1,0:T(8,128)S(1)} %get-tuple-element.62.refs_4_, ...), custom_call_target="tpu_custom_call" | custom-call | flops 1 | bytes 1 | tf_op jit(solution)/shard_map/rows/pallas_call | solution.py:483
  117.7 2.2 %rows.10.refs_6_ = f32[12,3,48,128]{3,2,1,0:T(8,128)S(1)} custom-call(s32[3]{0:T(128)S(1)} %pad_add_fusion.refs_0_, f32[18816,128]{1,0:T(8,128)S(1)} %get-tuple-element.59.refs_1_, f32[18816,128]{1,0:T(8,128)S(1)} %get-tuple-element.60.refs_2_, f32[18816,128]{1,0:T(8,128)S(1)} %get-tuple-element.61.refs_3_, f32[18816,128]{1,0:T(8,128)S(1)} %get-tuple-element.62.refs_4_, ...), custom_call_target="tpu_custom_call" | custom-call | flops 1 | bytes 1 | tf_op jit(solution)/shard_map/rows/pallas_call | solution.py:483
  120.6 3.9 %rows.11.refs_0_ = f32[24,3,48,128]{3,2,1,0:T(8,128)S(1)} custom-call(s32[3]{0:T(128)S(1)} %pad_add_fusion.refs_0_, f32[18816,128]{1,0:T(8,128)S(1)} %get-tuple-element.59.refs_1_, f32[18816,128]{1,0:T(8,128)S(1)} %get-tuple-element.60.refs_2_, f32[18816,128]{1,0:T(8,128)S(1)} %get-tuple-element.61.refs_3_, f32[18816,128]{1,0:T(8,128)S(1)} %get-tuple-element.62.refs_4_, ...), custom_call_target="tpu_custom_call" | custom-call | flops 1 | bytes 1 | tf_op jit(solution)/shard_map/rows/pallas_call | solution.py:483
  124.5 12.0 %collective-permute-done.17.refs_2_ = f32[12,3,48,128]{3,2,1,0:T(8,128)S(1)} collective-permute-done((f32[12,3,48,128]{3,2,1,0:T(8,128)S(1)}, f32[12,3,48,128]{3,2,1,0:T(8,128)S(1)}, u32[]{:S(2)}, u32[]{:S(2)}) %collective-permute-start.17) | collective-permute-done | bytes 884768 | tf_op jit(solution)/shard_map/ppermute | solution.py:494
  136.6 2.8 %finish.2.refs_7_ = f32[2,24,48,192]{3,2,1,0:T(8,128)} custom-call(f32[24,3,48,128]{3,2,1,0:T(8,128)S(1)} %rows.11.refs_0_, f32[12,3,48,128]{3,2,1,0:T(8,128)S(1)} %collective-permute-done.16.refs_1_, f32[12,3,48,128]{3,2,1,0:T(8,128)S(1)} %collective-permute-done.17.refs_2_, bf16[512,192]{1,0:T(8,128)(2,1)S(1)} %copy-done.1, f32[1,192]{1,0:T(1,128)S(1)} %bitcast.8, ...), custom_call_target="tpu_custom_call" | custom-call | tf_op jit(solution)/shard_map/finish/pallas_call | solution.py:531
  139.3 15.4 %collective-permute-done.15.refs_2_ = f32[12,3,48,128]{3,2,1,0:T(8,128)S(1)} collective-permute-done((f32[12,3,48,128]{3,2,1,0:T(8,128)S(1)}, f32[12,3,48,128]{3,2,1,0:T(8,128)S(1)}, u32[]{:S(2)}, u32[]{:S(2)}) %collective-permute-start.15) | collective-permute-done | bytes 884768 | tf_op jit(solution)/shard_map/ppermute | solution.py:494
  154.7 2.8 %finish.3 = f32[2,24,48,192]{3,2,1,0:T(8,128)} custom-call(f32[24,3,48,128]{3,2,1,0:T(8,128)S(1)} %rows.11.refs_0_, f32[12,3,48,128]{3,2,1,0:T(8,128)S(1)} %collective-permute-done.14.refs_1_, f32[12,3,48,128]{3,2,1,0:T(8,128)S(1)} %collective-permute-done.15.refs_2_, bf16[512,192]{1,0:T(8,128)(2,1)S(1)} %copy-done.1, ...), custom_call_target="tpu_custom_call", output_to_operand_aliasing={{}: (7, {})} | custom-call | tf_op jit(solution)/shard_map/finish/pallas_call | solution.py:531
  (37 shorter events, 15.6 us)
Async XLA Ops:
  4.7 15.9 %collective-permute-start = (f32[65,16,128]{2,1,0:T(8,128)}, f32[65,16,128]{2,1,0:T(8,128)S(1)}, u32[]{:S(2)}, u32[]{:S(2)}) collective-permute-start(f32[65,16,128]{2,1,0:T(8,128)} %spread.1.refs_1_), channel_id=1, source_target_pairs={{0,2},{1,3},{2,4},{3,5},{4,6},{5,7},{8,10},{9,11},{10,12},{11,13},... | collective-permute-start | bytes 1597448 | tf_op jit(solution)/shard_map/ppermute | solution.py:410
  8.2 15.9 %collective-permute-start.2 = (f32[65,16,128]{2,1,0:T(8,128)}, f32[65,16,128]{2,1,0:T(8,128)S(1)}, u32[]{:S(2)}, u32[]{:S(2)}) collective-permute-start(f32[65,16,128]{2,1,0:T(8,128)} %spread.1.refs_1_), channel_id=1, source_target_pairs={{2,0},{3,1},{4,2},{5,3},{6,4},{7,5},{10,8},{11,9},{12,10},{13,11},... | collective-permute-start | bytes 1597448 | tf_op jit(solution)/shard_map/ppermute | solution.py:410
  20.6 14.8 %collective-permute-start.1 = (f32[65,16,128]{2,1,0:T(8,128)S(1)}, f32[65,16,128]{2,1,0:T(8,128)S(1)}, u32[]{:S(2)}, u32[]{:S(2)}) collective-permute-start(f32[65,16,128]{2,1,0:T(8,128)S(1)} %collective-permute-done.refs_1_), channel_id=1, source_target_pairs={{2,4},{3,5},{4,6},{5,7},{10,12},{11,13},{12,14},{13,15},{18,20},{1... | collective-permute-start | bytes 1597448 | tf_op jit(solution)/shard_map/ppermute | solution.py:410
  24.1 14.9 %collective-permute-start.4 = (f32[65,16,128]{2,1,0:T(8,128)S(1)}, f32[65,16,128]{2,1,0:T(8,128)S(1)}, u32[]{:S(2)}, u32[]{:S(2)}) collective-permute-start(f32[65,16,128]{2,1,0:T(8,128)S(1)} %collective-permute-done.2.refs_2_), channel_id=1, source_target_pairs={{2,0},{3,1},{4,2},{5,3},{10,8},{11,9},{12,10},{13,11},{18,16},{19,... | collective-permute-start | bytes 1597448 | tf_op jit(solution)/shard_map/ppermute | solution.py:410
  26.6 19.0 %collective-permute-start.5 = (f32[65,16,128]{2,1,0:T(8,128)}, f32[65,16,128]{2,1,0:T(8,128)S(1)}, u32[]{:S(2)}, u32[]{:S(2)}) collective-permute-start(f32[65,16,128]{2,1,0:T(8,128)} %spread.1.refs_1_), channel_id=1, source_target_pairs={{0,1},{1,0},{2,3},{3,2},{4,5},{5,4},{6,7},{7,6},{8,9},{9,8},{10,11... | collective-permute-start | bytes 1597448 | tf_op jit(solution)/shard_map/ppermute | solution.py:410
  35.5 20.1 %collective-permute-start.3 = (f32[65,16,128]{2,1,0:T(8,128)S(1)}, f32[65,16,128]{2,1,0:T(8,128)S(1)}, u32[]{:S(2)}, u32[]{:S(2)}) collective-permute-start(f32[65,16,128]{2,1,0:T(8,128)S(1)} %collective-permute-done.1.refs_1_), channel_id=1, source_target_pairs={{4,6},{5,7},{12,14},{13,15},{20,22},{21,23},{28,30},{29,31}} | collective-permute-start | bytes 1597448 | tf_op jit(solution)/shard_map/ppermute | solution.py:410
  39.0 17.3 %collective-permute-start.7 = (f32[65,16,128]{2,1,0:T(8,128)S(1)}, f32[65,16,128]{2,1,0:T(8,128)S(1)}, u32[]{:S(2)}, u32[]{:S(2)}) collective-permute-start(f32[65,16,128]{2,1,0:T(8,128)S(1)} %collective-permute-done.4.refs_2_), channel_id=1, source_target_pairs={{2,0},{3,1},{10,8},{11,9},{18,16},{19,17},{26,24},{27,25}} | collective-permute-start | bytes 1597448 | tf_op jit(solution)/shard_map/ppermute | solution.py:410
  39.7 17.3 %collective-permute-start.9 = (f32[65,16,128]{2,1,0:T(8,128)S(1)}, f32[65,16,128]{2,1,0:T(8,128)S(1)}, u32[]{:S(2)}, u32[]{:S(2)}) collective-permute-start(f32[65,16,128]{2,1,0:T(8,128)S(1)} %collective-permute-done.refs_1_), channel_id=1, source_target_pairs={{2,3},{3,2},{4,5},{5,4},{6,7},{7,6},{10,11},{11,10},{12,13},{13,12... | collective-permute-start | bytes 1597448 | tf_op jit(solution)/shard_map/ppermute | solution.py:410
  43.2 24.9 %collective-permute-start.10 = (f32[65,16,128]{2,1,0:T(8,128)S(1)}, f32[65,16,128]{2,1,0:T(8,128)S(1)}, u32[]{:S(2)}, u32[]{:S(2)}) collective-permute-start(f32[65,16,128]{2,1,0:T(8,128)S(1)} %collective-permute-done.2.refs_2_), channel_id=1, source_target_pairs={{0,1},{1,0},{2,3},{3,2},{4,5},{5,4},{8,9},{9,8},{10,11},{11,10},{1... | collective-permute-start | bytes 1597448 | tf_op jit(solution)/shard_map/ppermute | solution.py:410
  45.6 30.6 %collective-permute-start.11 = (f32[65,16,128]{2,1,0:T(8,128)S(1)}, f32[65,16,128]{2,1,0:T(8,128)S(1)}, u32[]{:S(2)}, u32[]{:S(2)}) collective-permute-start(f32[65,16,128]{2,1,0:T(8,128)S(1)} %collective-permute-done.1.refs_1_), channel_id=1, source_target_pairs={{4,5},{5,4},{6,7},{7,6},{12,13},{13,12},{14,15},{15,14},{20,21},{2... | collective-permute-start | bytes 1597448 | tf_op jit(solution)/shard_map/ppermute | solution.py:410
  55.6 20.6 %collective-permute-start.12 = (f32[65,16,128]{2,1,0:T(8,128)S(1)}, f32[65,16,128]{2,1,0:T(8,128)S(1)}, u32[]{:S(2)}, u32[]{:S(2)}) collective-permute-start(f32[65,16,128]{2,1,0:T(8,128)S(1)} %collective-permute-done.4.refs_2_), channel_id=1, source_target_pairs={{0,1},{1,0},{2,3},{3,2},{8,9},{9,8},{10,11},{11,10},{16,17},{17,16... | collective-permute-start | bytes 1597448 | tf_op jit(solution)/shard_map/ppermute | solution.py:410
  56.3 29.0 %collective-permute-start.8 = (f32[65,16,128]{2,1,0:T(8,128)S(1)}, f32[65,16,128]{2,1,0:T(8,128)S(1)}, u32[]{:S(2)}, u32[]{:S(2)}) collective-permute-start(f32[65,16,128]{2,1,0:T(8,128)S(1)} %collective-permute-done.7.refs_2_), channel_id=1, source_target_pairs={{0,1},{1,0},{8,9},{9,8},{16,17},{17,16},{24,25},{25,24}} | collective-permute-start | bytes 1597448 | tf_op jit(solution)/shard_map/ppermute | solution.py:410
  57.0 28.3 %collective-permute-start.6 = (f32[65,16,128]{2,1,0:T(8,128)S(1)}, f32[65,16,128]{2,1,0:T(8,128)S(1)}, u32[]{:S(2)}, u32[]{:S(2)}) collective-permute-start(f32[65,16,128]{2,1,0:T(8,128)S(1)} %collective-permute-done.3.refs_1_), channel_id=1, source_target_pairs={{6,7},{7,6},{14,15},{15,14},{22,23},{23,22},{30,31},{31,30}} | collective-permute-start | bytes 1597448 | tf_op jit(solution)/shard_map/ppermute | solution.py:410
  85.3 18.6 %copy-start = (bf16[2,2,192,256]{3,2,1,0:T(8,128)(2,1)S(1)}, bf16[2,2,192,256]{3,2,1,0:T(8,128)(2,1)}, u32[]{:S(2)}) copy-start(bf16[2,2,192,256]{3,2,1,0:T(8,128)(2,1)} %constant.26.clone.refs_5_) | copy-start | bytes 1179652
  108.0 3.8 %collective-permute-start.13 = (f32[24,3,48,128]{3,2,1,0:T(8,128)S(1)}, f32[24,3,48,128]{3,2,1,0:T(8,128)S(1)}, u32[]{:S(2)}, u32[]{:S(2)}) collective-permute-start(f32[24,3,48,128]{3,2,1,0:T(8,128)S(1)} %rows.6.refs_6_), channel_id=1, source_target_pairs={{0,8},{8,0},{16,24},{24,16},{1,9},{9,1},{17,25},{25,17},{2,10},{10... | collective-permute-start | bytes 5308424 | tf_op jit(solution)/shard_map/ppermute | solution.py:494
  110.3 14.2 %collective-permute-start.16 = (f32[12,3,48,128]{3,2,1,0:T(8,128)S(1)}, f32[12,3,48,128]{3,2,1,0:T(8,128)S(1)}, u32[]{:S(2)}, u32[]{:S(2)}) collective-permute-start(f32[12,3,48,128]{3,2,1,0:T(8,128)S(1)} %rows.7.refs_7_), channel_id=1, source_target_pairs={{0,8},{8,0},{16,24},{24,16},{1,9},{9,1},{17,25},{25,17},{2,10},{10... | collective-permute-start | bytes 2654216 | tf_op jit(solution)/shard_map/ppermute | solution.py:494
  114.0 22.6 %collective-permute-start.17 = (f32[12,3,48,128]{3,2,1,0:T(8,128)S(1)}, f32[12,3,48,128]{3,2,1,0:T(8,128)S(1)}, u32[]{:S(2)}, u32[]{:S(2)}) collective-permute-start(f32[12,3,48,128]{3,2,1,0:T(8,128)S(1)} %rows.8.refs_6_), channel_id=1, source_target_pairs={{0,16},{8,24},{16,0},{24,8},{1,17},{9,25},{17,1},{25,9},{2,18},{10... | collective-permute-start | bytes 2654216 | tf_op jit(solution)/shard_map/ppermute | solution.py:494
  120.0 16.6 %copy-start.1 = (bf16[512,192]{1,0:T(8,128)(2,1)S(1)}, bf16[512,192]{1,0:T(8,128)(2,1)}, u32[]{:S(2)}) copy-start(bf16[512,192]{1,0:T(8,128)(2,1)} %constant.27.clone.refs_3_) | copy-start | bytes 589828
  120.0 16.6 %copy-start.2 = (f32[192]{0:T(256)S(1)}, f32[192]{0:T(256)}, u32[]{:S(2)}) copy-start(f32[192]{0:T(256)} %param.19) | copy-start | bytes 2308
  120.0 16.6 %copy-start.3 = (f32[48]{0:T(128)S(1)}, f32[48]{0:T(128)}, u32[]{:S(2)}) copy-start(f32[48]{0:T(128)} %param.20) | copy-start | bytes 580
  120.0 16.6 %copy-start.4 = (f32[24]{0:T(128)S(1)}, f32[24]{0:T(128)}, u32[]{:S(2)}) copy-start(f32[24]{0:T(128)} %refs_6_.3) | copy-start | bytes 292
  120.0 34.7 %collective-permute-start.15 = (f32[12,3,48,128]{3,2,1,0:T(8,128)S(1)}, f32[12,3,48,128]{3,2,1,0:T(8,128)S(1)}, u32[]{:S(2)}, u32[]{:S(2)}) collective-permute-start(f32[12,3,48,128]{3,2,1,0:T(8,128)S(1)} %rows.10.refs_6_), channel_id=1, source_target_pairs={{0,16},{8,24},{16,0},{24,8},{1,17},{9,25},{17,1},{25,9},{2,18},{10... | collective-permute-start | bytes 2654216 | tf_op jit(solution)/shard_map/ppermute | solution.py:494
  120.6 34.1 %collective-permute-start.14 = (f32[12,3,48,128]{3,2,1,0:T(8,128)S(1)}, f32[12,3,48,128]{3,2,1,0:T(8,128)S(1)}, u32[]{:S(2)}, u32[]{:S(2)}) collective-permute-start(f32[12,3,48,128]{3,2,1,0:T(8,128)S(1)} %rows.9.refs_7_), channel_id=1, source_target_pairs={{0,8},{8,0},{16,24},{24,16},{1,9},{9,1},{17,25},{25,17},{2,10},{10... | collective-permute-start | bytes 2654216 | tf_op jit(solution)/shard_map/ppermute | solution.py:494

commit v16 on v13

--- a/solution.py
+++ b/solution.py
@@ -159,7 +159,7 @@
         out_ref[pair] = jnp.where(left, piece[: 2 * TILE], piece[2 * TILE :])
         return carry
 
-    lax.fori_loop(0, blocks // 2, pair_body, 0, unroll=8)
+    lax.fori_loop(0, blocks // 2, pair_body, 0, unroll=16)
     out_ref[blocks // 2] = jnp.broadcast_to(codes, (2 * TILE, LANES))
 
 
@@ -488,7 +488,7 @@
             compiler_params=params,
             cost_estimate=pl.CostEstimate(flops=1, bytes_accessed=1, transcendentals=0),
             name="rows",
-        )(places, *in_vmem(acc), row_table, *addends, *in_hbm(after))
+        )(places, *in_vmem(acc), row_table, *addends, *after)
 
     def swap(value, bit):
         return lax.ppermute(value, "gx", [(index, index ^ bit) for index in range(grid_rows)])

time: 145 us -> 144 us (level)
  local copies, waits for them, and re-layouts: 3.6 us -> 1.08 us
  waiting for transfers between devices: 35 us -> 37.2 us
    unnamed x22 -> x12, local copies, waits for them, and re-layouts: 3.6 us -> 1.08 us
    ppermute x5, waiting for transfers between devices: 26 us -> 28.3 us  [swap(): lax.ppermute(value, 'gx', [(index, index ^ bit) for index in range(grid_r...]
  transfers between devices with their start and end apart: 18 -> 18, of which waited for: 5 -> 5; matrix products, arithmetic and copies ran while one was open for 0% -> 0% of each run, Pallas kernels for 30% -> 31%
where the time goes in v16:
time: 144 us; the launch traced here: 142 us
  Pallas kernels  73.6 us (51%)
  waiting for transfers between devices  37.2 us (26%)
  starting transfers between devices  29.5 us (20%)
    pallas_call x5, Pallas kernels, add_tiles(): pl.pallas_call(functools.partial(tiles_kernel, conditions, not acc, bool(...  46.5 us
    ppermute x5, waiting for transfers between devices, swap(): lax.ppermute(value, 'gx', [(index, index ^ bit) for index in range(grid_r...  28.3 us
    ppermute x13, starting transfers between devices, send(): return lax.ppermute(value, 'gy', moves)  26.7 us
    pallas_call x6, Pallas kernels, rows_for(): pl.pallas_call(body, in_specs=[smem] + [vmem] * (1 + PARTS + len(addends)...  16.8 us
    ppermute x13, waiting for transfers between devices, send(): return lax.ppermute(value, 'gy', moves)  8.96 us
    pallas_call x2, Pallas kernels, on_device(): pl.pallas_call(finish, grid=(1,), out_shape=jax.ShapeDtypeStruct((2, plan...  5.54 us
    pallas_call x1, Pallas kernels, on_device(): pl.pallas_call(functools.partial(spread_kernel, tile_rows, tile_cols, gri...  4.72 us
  transfers between devices with their start and end apart: 18, of which 5 were waited for; matrix products, arithmetic and copies ran while one was open for 0% of the time, Pallas kernels for 31%

profile of v16, /device:TPU:16, one launch (start us, length us, event | category | flops | bytes accessed | tf_op | source)
XLA Modules:
  0.0 141.8 jit_solution(924428791462427593)
XLA Ops:
  0.0 4.7 %spread.1.refs_1_ = f32[65,16,128]{2,1,0:T(8,128)} custom-call(f32[128,2,128]{2,1,0:T(2,128)} %samples_ref.1, f32[128,3,4,128]{3,2,1,0:T(4,128)} %kernel_ref.1, s32[3,128,128]{2,1,0:T(8,128)} %bitcast.12, s32[1,128]{1,0:T(1,128)} %bitcast.13, s32[1,128]{1,0:T(1,128)} %bitcast.14), custom_call_target="tpu_custom_call" | custom-call | tf_op jit(solution)/shard_map/spread/pallas_call | solution.py:396
  4.7 3.5 %collective-permute-start = (f32[65,16,128]{2,1,0:T(8,128)}, f32[65,16,128]{2,1,0:T(8,128)S(1)}, u32[]{:S(2)}, u32[]{:S(2)}) collective-permute-start(f32[65,16,128]{2,1,0:T(8,128)} %spread.1.refs_1_), channel_id=1, source_target_pairs={{0,2},{1,3},{2,4},{3,5},{4,6},{5,7},{8,10},{9,11},{10,12},{11,13},... | collective-permute-start | bytes 1597448 | tf_op jit(solution)/shard_map/ppermute | solution.py:410
  8.2 2.4 %collective-permute-start.2 = (f32[65,16,128]{2,1,0:T(8,128)}, f32[65,16,128]{2,1,0:T(8,128)S(1)}, u32[]{:S(2)}, u32[]{:S(2)}) collective-permute-start(f32[65,16,128]{2,1,0:T(8,128)} %spread.1.refs_1_), channel_id=1, source_target_pairs={{2,0},{3,1},{4,2},{5,3},{6,4},{7,5},{10,8},{11,9},{12,10},{13,11},... | collective-permute-start | bytes 1597448 | tf_op jit(solution)/shard_map/ppermute | solution.py:410
  13.3 5.9 %tiles.5 = (f32[18816,128]{1,0:T(8,128)S(1)}, f32[18816,128]{1,0:T(8,128)S(1)}, f32[18816,128]{1,0:T(8,128)S(1)}, f32[18816,128]{1,0:T(8,128)S(1)}, f32[8,128]{1,0:T(8,128)}) custom-call(s32[3]{0:T(128)S(1)} %pad_add_fusion.refs_0_, f32[65,16,128]{2,1,0:T(8,128)S(1)} %copy-done.1, bf16[8,48,128]{2,1,0:T(8,128)(2,1)} %constant.23.clone.refs_2_.refs_4_.refs_5_.refs_3_, ...), custom_call_target="tpu_custom_call" | custom-call | bytes 8388608 | tf_op jit(solution)/shard_map/tiles/pallas_call | solution.py:427
  20.6 3.5 %collective-permute-start.1 = (f32[65,16,128]{2,1,0:T(8,128)S(1)}, f32[65,16,128]{2,1,0:T(8,128)S(1)}, u32[]{:S(2)}, u32[]{:S(2)}) collective-permute-start(f32[65,16,128]{2,1,0:T(8,128)S(1)} %collective-permute-done.refs_1_), channel_id=1, source_target_pairs={{2,4},{3,5},{4,6},{5,7},{10,12},{11,13},{12,14},{13,15},{18,20},{1... | collective-permute-start | bytes 1597448 | tf_op jit(solution)/shard_map/ppermute | solution.py:410
  24.1 2.4 %collective-permute-start.5 = (f32[65,16,128]{2,1,0:T(8,128)S(1)}, f32[65,16,128]{2,1,0:T(8,128)S(1)}, u32[]{:S(2)}, u32[]{:S(2)}) collective-permute-start(f32[65,16,128]{2,1,0:T(8,128)S(1)} %collective-permute-done.2.refs_2_), channel_id=1, source_target_pairs={{2,0},{3,1},{4,2},{5,3},{10,8},{11,9},{12,10},{13,11},{18,16},{19,... | collective-permute-start | bytes 1597448 | tf_op jit(solution)/shard_map/ppermute | solution.py:410
  26.6 3.4 %collective-permute-start.6 = (f32[65,16,128]{2,1,0:T(8,128)S(1)}, f32[65,16,128]{2,1,0:T(8,128)S(1)}, u32[]{:S(2)}, u32[]{:S(2)}) collective-permute-start(f32[65,16,128]{2,1,0:T(8,128)S(1)} %collective-permute-done.refs_1_), channel_id=1, source_target_pairs={{2,3},{3,2},{4,5},{5,4},{6,7},{7,6},{10,11},{11,10},{12,13},{13,12... | collective-permute-start | bytes 1597448 | tf_op jit(solution)/shard_map/ppermute | solution.py:410
  30.0 2.4 %collective-permute-start.7 = (f32[65,16,128]{2,1,0:T(8,128)S(1)}, f32[65,16,128]{2,1,0:T(8,128)S(1)}, u32[]{:S(2)}, u32[]{:S(2)}) collective-permute-start(f32[65,16,128]{2,1,0:T(8,128)S(1)} %collective-permute-done.2.refs_2_), channel_id=1, source_target_pairs={{0,1},{1,0},{2,3},{3,2},{4,5},{5,4},{8,9},{9,8},{10,11},{11,10},{1... | collective-permute-start | bytes 1597448 | tf_op jit(solution)/shard_map/ppermute | solution.py:410
  32.4 8.8 %tiles.6 = (f32[18816,128]{1,0:T(8,128)S(1)}, f32[18816,128]{1,0:T(8,128)S(1)}, f32[18816,128]{1,0:T(8,128)S(1)}, f32[18816,128]{1,0:T(8,128)S(1)}, f32[8,128]{1,0:T(8,128)}) custom-call(s32[3]{0:T(128)S(1)} %pad_add_fusion.refs_0_, ...), custom_call_target="tpu_custom_call", output_to_operand_aliasing={{0}: (6, {}), {1}: (7, {}), {2}: (8, {}), {3}: (9, {})} | custom-call | bytes 25165824 | tf_op jit(solution)/shard_map/tiles/pallas_call | solution.py:427
  43.3 3.4 %collective-permute-start.11 = (f32[65,16,128]{2,1,0:T(8,128)S(1)}, f32[65,16,128]{2,1,0:T(8,128)S(1)}, u32[]{:S(2)}, u32[]{:S(2)}) collective-permute-start(f32[65,16,128]{2,1,0:T(8,128)S(1)} %collective-permute-done.1.refs_1_), channel_id=1, source_target_pairs={{4,5},{5,4},{6,7},{7,6},{12,13},{13,12},{14,15},{15,14},{20,21},{2... | collective-permute-start | bytes 1597448 | tf_op jit(solution)/shard_map/ppermute | solution.py:410
  47.4 7.5 %collective-permute-done.7.refs_4_ = f32[65,16,128]{2,1,0:T(8,128)S(1)} collective-permute-done((f32[65,16,128]{2,1,0:T(8,128)S(1)}, f32[65,16,128]{2,1,0:T(8,128)S(1)}, u32[]{:S(2)}, u32[]{:S(2)}) %collective-permute-start.7) | collective-permute-done | bytes 532512 | tf_op jit(solution)/shard_map/ppermute | solution.py:410
  54.9 8.8 %tiles.7 = (f32[18816,128]{1,0:T(8,128)S(1)}, f32[18816,128]{1,0:T(8,128)S(1)}, f32[18816,128]{1,0:T(8,128)S(1)}, f32[18816,128]{1,0:T(8,128)S(1)}, f32[8,128]{1,0:T(8,128)}) custom-call(s32[3]{0:T(128)S(1)} %pad_add_fusion.refs_0_, ...), custom_call_target="tpu_custom_call", output_to_operand_aliasing={{0}: (7, {}), {1}: (8, {}), {2}: (9, {}), {3}: (10, {})} | custom-call | bytes 33554432 | tf_op jit(solution)/shard_map/tiles/pallas_call | solution.py:427
  65.2 4.4 %tiles.8 = (f32[18816,128]{1,0:T(8,128)S(1)}, f32[18816,128]{1,0:T(8,128)S(1)}, f32[18816,128]{1,0:T(8,128)S(1)}, f32[18816,128]{1,0:T(8,128)S(1)}, f32[8,128]{1,0:T(8,128)}) custom-call(s32[3]{0:T(128)S(1)} %pad_add_fusion.refs_0_, ...), custom_call_target="tpu_custom_call", output_to_operand_aliasing={{0}: (7, {}), {1}: (8, {}), {2}: (9, {}), {3}: (10, {})} | custom-call | bytes 33554432 | tf_op jit(solution)/shard_map/tiles/pallas_call | solution.py:427
  69.7 18.6 %tiles.9 = (f32[18816,128]{1,0:T(8,128)S(1)}, f32[18816,128]{1,0:T(8,128)S(1)}, f32[18816,128]{1,0:T(8,128)S(1)}, f32[18816,128]{1,0:T(8,128)S(1)}, f32[8,128]{1,0:T(8,128)}) custom-call(s32[3]{0:T(128)S(1)} %pad_add_fusion.refs_0_, ...), custom_call_target="tpu_custom_call", output_to_operand_aliasing={{0}: (6, {}), {1}: (7, {}), {2}: (8, {}), {3}: (9, {})} | custom-call | bytes 16777216 | tf_op jit(solution)/shard_map/tiles/pallas_call | solution.py:427
  88.3 4.1 %rows.6.refs_6_ = f32[24,3,48,128]{3,2,1,0:T(8,128)S(1)} custom-call(s32[3]{0:T(128)S(1)} %pad_add_fusion.refs_0_, f32[18816,128]{1,0:T(8,128)S(1)} %get-tuple-element.59.refs_1_, f32[18816,128]{1,0:T(8,128)S(1)} %get-tuple-element.60.refs_2_, f32[18816,128]{1,0:T(8,128)S(1)} %get-tuple-element.61.refs_3_, f32[18816,128]{1,0:T(8,128)S(1)} %get-tuple-element.62.refs_4_, ...), custom_call_target="tpu_custom_call" | custom-call | flops 1 | bytes 1 | tf_op jit(solution)/shard_map/rows/pallas_call | solution.py:483
  92.4 2.2 %rows.7.refs_7_ = f32[12,3,48,128]{3,2,1,0:T(8,128)S(1)} custom-call(s32[3]{0:T(128)S(1)} %pad_add_fusion.refs_0_, f32[18816,128]{1,0:T(8,128)S(1)} %get-tuple-element.59.refs_1_, f32[18816,128]{1,0:T(8,128)S(1)} %get-tuple-element.60.refs_2_, f32[18816,128]{1,0:T(8,128)S(1)} %get-tuple-element.61.refs_3_, f32[18816,128]{1,0:T(8,128)S(1)} %get-tuple-element.62.refs_4_, ...), custom_call_target="tpu_custom_call" | custom-call | flops 1 | bytes 1 | tf_op jit(solution)/shard_map/rows/pallas_call | solution.py:483
  96.1 2.2 %rows.8.refs_6_ = f32[12,3,48,128]{3,2,1,0:T(8,128)S(1)} custom-call(s32[3]{0:T(128)S(1)} %pad_add_fusion.refs_0_, f32[18816,128]{1,0:T(8,128)S(1)} %get-tuple-element.59.refs_1_, f32[18816,128]{1,0:T(8,128)S(1)} %get-tuple-element.60.refs_2_, f32[18816,128]{1,0:T(8,128)S(1)} %get-tuple-element.61.refs_3_, f32[18816,128]{1,0:T(8,128)S(1)} %get-tuple-element.62.refs_4_, ...), custom_call_target="tpu_custom_call" | custom-call | flops 1 | bytes 1 | tf_op jit(solution)/shard_map/rows/pallas_call | solution.py:483
  99.9 2.2 %rows.9.refs_7_ = f32[12,3,48,128]{3,2,1,0:T(8,128)S(1)} custom-call(s32[3]{0:T(128)S(1)} %pad_add_fusion.refs_0_, f32[18816,128]{1,0:T(8,128)S(1)} %get-tuple-element.59.refs_1_, f32[18816,128]{1,0:T(8,128)S(1)} %get-tuple-element.60.refs_2_, f32[18816,128]{1,0:T(8,128)S(1)} %get-tuple-element.61.refs_3_, f32[18816,128]{1,0:T(8,128)S(1)} %get-tuple-element.62.refs_4_, ...), custom_call_target="tpu_custom_call" | custom-call | flops 1 | bytes 1 | tf_op jit(solution)/shard_map/rows/pallas_call | solution.py:483
  102.1 2.2 %rows.10.refs_6_ = f32[12,3,48,128]{3,2,1,0:T(8,128)S(1)} custom-call(s32[3]{0:T(128)S(1)} %pad_add_fusion.refs_0_, f32[18816,128]{1,0:T(8,128)S(1)} %get-tuple-element.59.refs_1_, f32[18816,128]{1,0:T(8,128)S(1)} %get-tuple-element.60.refs_2_, f32[18816,128]{1,0:T(8,128)S(1)} %get-tuple-element.61.refs_3_, f32[18816,128]{1,0:T(8,128)S(1)} %get-tuple-element.62.refs_4_, ...), custom_call_target="tpu_custom_call" | custom-call | flops 1 | bytes 1 | tf_op jit(solution)/shard_map/rows/pallas_call | solution.py:483
  105.0 3.9 %rows.11.refs_0_ = f32[24,3,48,128]{3,2,1,0:T(8,128)S(1)} custom-call(s32[3]{0:T(128)S(1)} %pad_add_fusion.refs_0_, f32[18816,128]{1,0:T(8,128)S(1)} %get-tuple-element.59.refs_1_, f32[18816,128]{1,0:T(8,128)S(1)} %get-tuple-element.60.refs_2_, f32[18816,128]{1,0:T(8,128)S(1)} %get-tuple-element.61.refs_3_, f32[18816,128]{1,0:T(8,128)S(1)} %get-tuple-element.62.refs_4_, ...), custom_call_target="tpu_custom_call" | custom-call | flops 1 | bytes 1 | tf_op jit(solution)/shard_map/rows/pallas_call | solution.py:483
  108.9 12.0 %collective-permute-done.17.refs_2_ = f32[12,3,48,128]{3,2,1,0:T(8,128)S(1)} collective-permute-done((f32[12,3,48,128]{3,2,1,0:T(8,128)S(1)}, f32[12,3,48,128]{3,2,1,0:T(8,128)S(1)}, u32[]{:S(2)}, u32[]{:S(2)}) %collective-permute-start.17) | collective-permute-done | bytes 884768 | tf_op jit(solution)/shard_map/ppermute | solution.py:494
  120.9 2.8 %finish.2.refs_7_ = f32[2,24,48,192]{3,2,1,0:T(8,128)} custom-call(f32[24,3,48,128]{3,2,1,0:T(8,128)S(1)} %rows.11.refs_0_, f32[12,3,48,128]{3,2,1,0:T(8,128)S(1)} %collective-permute-done.16.refs_1_, f32[12,3,48,128]{3,2,1,0:T(8,128)S(1)} %collective-permute-done.17.refs_2_, bf16[512,192]{1,0:T(8,128)(2,1)S(1)} %copy-done.2, f32[1,192]{1,0:T(1,128)S(1)} %bitcast.8, ...), custom_call_target="tpu_custom_call" | custom-call | tf_op jit(solution)/shard_map/finish/pallas_call | solution.py:531
  123.7 15.4 %collective-permute-done.15.refs_2_ = f32[12,3,48,128]{3,2,1,0:T(8,128)S(1)} collective-permute-done((f32[12,3,48,128]{3,2,1,0:T(8,128)S(1)}, f32[12,3,48,128]{3,2,1,0:T(8,128)S(1)}, u32[]{:S(2)}, u32[]{:S(2)}) %collective-permute-start.15) | collective-permute-done | bytes 884768 | tf_op jit(solution)/shard_map/ppermute | solution.py:494
  139.1 2.8 %finish.3 = f32[2,24,48,192]{3,2,1,0:T(8,128)} custom-call(f32[24,3,48,128]{3,2,1,0:T(8,128)S(1)} %rows.11.refs_0_, f32[12,3,48,128]{3,2,1,0:T(8,128)S(1)} %collective-permute-done.14.refs_1_, f32[12,3,48,128]{3,2,1,0:T(8,128)S(1)} %collective-permute-done.15.refs_2_, bf16[512,192]{1,0:T(8,128)(2,1)S(1)} %copy-done.2, ...), custom_call_target="tpu_custom_call", output_to_operand_aliasing={{}: (7, {})} | custom-call | tf_op jit(solution)/shard_map/finish/pallas_call | solution.py:531
  (39 shorter events, 12.1 us)
Async XLA Ops:
  4.7 15.9 %collective-permute-start = (f32[65,16,128]{2,1,0:T(8,128)}, f32[65,16,128]{2,1,0:T(8,128)S(1)}, u32[]{:S(2)}, u32[]{:S(2)}) collective-permute-start(f32[65,16,128]{2,1,0:T(8,128)} %spread.1.refs_1_), channel_id=1, source_target_pairs={{0,2},{1,3},{2,4},{3,5},{4,6},{5,7},{8,10},{9,11},{10,12},{11,13},... | collective-permute-start | bytes 1597448 | tf_op jit(solution)/shard_map/ppermute | solution.py:410
  8.2 15.9 %collective-permute-start.2 = (f32[65,16,128]{2,1,0:T(8,128)}, f32[65,16,128]{2,1,0:T(8,128)S(1)}, u32[]{:S(2)}, u32[]{:S(2)}) collective-permute-start(f32[65,16,128]{2,1,0:T(8,128)} %spread.1.refs_1_), channel_id=1, source_target_pairs={{2,0},{3,1},{4,2},{5,3},{6,4},{7,5},{10,8},{11,9},{12,10},{13,11},... | collective-permute-start | bytes 1597448 | tf_op jit(solution)/shard_map/ppermute | solution.py:410
  10.6 21.9 %collective-permute-start.3 = (f32[65,16,128]{2,1,0:T(8,128)}, f32[65,16,128]{2,1,0:T(8,128)S(1)}, u32[]{:S(2)}, u32[]{:S(2)}) collective-permute-start(f32[65,16,128]{2,1,0:T(8,128)} %spread.1.refs_1_), channel_id=1, source_target_pairs={{0,1},{1,0},{2,3},{3,2},{4,5},{5,4},{6,7},{7,6},{8,9},{9,8},{10,11... | collective-permute-start | bytes 1597448 | tf_op jit(solution)/shard_map/ppermute | solution.py:410
  12.2 1.0 copy-start.1
  20.6 20.6 %collective-permute-start.1 = (f32[65,16,128]{2,1,0:T(8,128)S(1)}, f32[65,16,128]{2,1,0:T(8,128)S(1)}, u32[]{:S(2)}, u32[]{:S(2)}) collective-permute-start(f32[65,16,128]{2,1,0:T(8,128)S(1)} %collective-permute-done.refs_1_), channel_id=1, source_target_pairs={{2,4},{3,5},{4,6},{5,7},{10,12},{11,13},{12,14},{13,15},{18,20},{1... | collective-permute-start | bytes 1597448 | tf_op jit(solution)/shard_map/ppermute | solution.py:410
  24.1 18.4 %collective-permute-start.5 = (f32[65,16,128]{2,1,0:T(8,128)S(1)}, f32[65,16,128]{2,1,0:T(8,128)S(1)}, u32[]{:S(2)}, u32[]{:S(2)}) collective-permute-start(f32[65,16,128]{2,1,0:T(8,128)S(1)} %collective-permute-done.2.refs_2_), channel_id=1, source_target_pairs={{2,0},{3,1},{4,2},{5,3},{10,8},{11,9},{12,10},{13,11},{18,16},{19,... | collective-permute-start | bytes 1597448 | tf_op jit(solution)/shard_map/ppermute | solution.py:410
  26.6 20.2 %collective-permute-start.6 = (f32[65,16,128]{2,1,0:T(8,128)S(1)}, f32[65,16,128]{2,1,0:T(8,128)S(1)}, u32[]{:S(2)}, u32[]{:S(2)}) collective-permute-start(f32[65,16,128]{2,1,0:T(8,128)S(1)} %collective-permute-done.refs_1_), channel_id=1, source_target_pairs={{2,3},{3,2},{4,5},{5,4},{6,7},{7,6},{10,11},{11,10},{12,13},{13,12... | collective-permute-start | bytes 1597448 | tf_op jit(solution)/shard_map/ppermute | solution.py:410
  30.0 24.9 %collective-permute-start.7 = (f32[65,16,128]{2,1,0:T(8,128)S(1)}, f32[65,16,128]{2,1,0:T(8,128)S(1)}, u32[]{:S(2)}, u32[]{:S(2)}) collective-permute-start(f32[65,16,128]{2,1,0:T(8,128)S(1)} %collective-permute-done.2.refs_2_), channel_id=1, source_target_pairs={{0,1},{1,0},{2,3},{3,2},{4,5},{5,4},{8,9},{9,8},{10,11},{11,10},{1... | collective-permute-start | bytes 1597448 | tf_op jit(solution)/shard_map/ppermute | solution.py:410
  41.3 22.5 %collective-permute-start.4 = (f32[65,16,128]{2,1,0:T(8,128)S(1)}, f32[65,16,128]{2,1,0:T(8,128)S(1)}, u32[]{:S(2)}, u32[]{:S(2)}) collective-permute-start(f32[65,16,128]{2,1,0:T(8,128)S(1)} %collective-permute-done.1.refs_1_), channel_id=1, source_target_pairs={{4,6},{5,7},{12,14},{13,15},{20,22},{21,23},{28,30},{29,31}} | collective-permute-start | bytes 1597448 | tf_op jit(solution)/shard_map/ppermute | solution.py:410
  42.6 21.9 %collective-permute-start.9 = (f32[65,16,128]{2,1,0:T(8,128)S(1)}, f32[65,16,128]{2,1,0:T(8,128)S(1)}, u32[]{:S(2)}, u32[]{:S(2)}) collective-permute-start(f32[65,16,128]{2,1,0:T(8,128)S(1)} %collective-permute-done.5.refs_2_), channel_id=1, source_target_pairs={{2,0},{3,1},{10,8},{11,9},{18,16},{19,17},{26,24},{27,25}} | collective-permute-start | bytes 1597448 | tf_op jit(solution)/shard_map/ppermute | solution.py:410
  43.3 21.9 %collective-permute-start.11 = (f32[65,16,128]{2,1,0:T(8,128)S(1)}, f32[65,16,128]{2,1,0:T(8,128)S(1)}, u32[]{:S(2)}, u32[]{:S(2)}) collective-permute-start(f32[65,16,128]{2,1,0:T(8,128)S(1)} %collective-permute-done.1.refs_1_), channel_id=1, source_target_pairs={{4,5},{5,4},{6,7},{7,6},{12,13},{13,12},{14,15},{15,14},{20,21},{2... | collective-permute-start | bytes 1597448 | tf_op jit(solution)/shard_map/ppermute | solution.py:410
  46.7 18.4 %collective-permute-start.12 = (f32[65,16,128]{2,1,0:T(8,128)S(1)}, f32[65,16,128]{2,1,0:T(8,128)S(1)}, u32[]{:S(2)}, u32[]{:S(2)}) collective-permute-start(f32[65,16,128]{2,1,0:T(8,128)S(1)} %collective-permute-done.5.refs_2_), channel_id=1, source_target_pairs={{0,1},{1,0},{2,3},{3,2},{8,9},{9,8},{10,11},{11,10},{16,17},{17,16... | collective-permute-start | bytes 1597448 | tf_op jit(solution)/shard_map/ppermute | solution.py:410
  63.8 5.9 %collective-permute-start.8 = (f32[65,16,128]{2,1,0:T(8,128)S(1)}, f32[65,16,128]{2,1,0:T(8,128)S(1)}, u32[]{:S(2)}, u32[]{:S(2)}) collective-permute-start(f32[65,16,128]{2,1,0:T(8,128)S(1)} %collective-permute-done.4.refs_1_), channel_id=1, source_target_pairs={{6,7},{7,6},{14,15},{15,14},{22,23},{23,22},{30,31},{31,30}} | collective-permute-start | bytes 1597448 | tf_op jit(solution)/shard_map/ppermute | solution.py:410
  64.5 5.2 %collective-permute-start.10 = (f32[65,16,128]{2,1,0:T(8,128)S(1)}, f32[65,16,128]{2,1,0:T(8,128)S(1)}, u32[]{:S(2)}, u32[]{:S(2)}) collective-permute-start(f32[65,16,128]{2,1,0:T(8,128)S(1)} %collective-permute-done.9.refs_2_), channel_id=1, source_target_pairs={{0,1},{1,0},{8,9},{9,8},{16,17},{17,16},{24,25},{25,24}} | collective-permute-start | bytes 1597448 | tf_op jit(solution)/shard_map/ppermute | solution.py:410
  69.7 18.6 %copy-start = (bf16[2,2,192,256]{3,2,1,0:T(8,128)(2,1)S(1)}, bf16[2,2,192,256]{3,2,1,0:T(8,128)(2,1)}, u32[]{:S(2)}) copy-start(bf16[2,2,192,256]{3,2,1,0:T(8,128)(2,1)} %constant.26.clone.refs_5_) | copy-start | bytes 1179652
  92.4 3.8 %collective-permute-start.13 = (f32[24,3,48,128]{3,2,1,0:T(8,128)S(1)}, f32[24,3,48,128]{3,2,1,0:T(8,128)S(1)}, u32[]{:S(2)}, u32[]{:S(2)}) collective-permute-start(f32[24,3,48,128]{3,2,1,0:T(8,128)S(1)} %rows.6.refs_6_), channel_id=1, source_target_pairs={{0,8},{8,0},{16,24},{24,16},{1,9},{9,1},{17,25},{25,17},{2,10},{10... | collective-permute-start | bytes 5308424 | tf_op jit(solution)/shard_map/ppermute | solution.py:494
  94.6 14.3 %collective-permute-start.16 = (f32[12,3,48,128]{3,2,1,0:T(8,128)S(1)}, f32[12,3,48,128]{3,2,1,0:T(8,128)S(1)}, u32[]{:S(2)}, u32[]{:S(2)}) collective-permute-start(f32[12,3,48,128]{3,2,1,0:T(8,128)S(1)} %rows.7.refs_7_), channel_id=1, source_target_pairs={{0,8},{8,0},{16,24},{24,16},{1,9},{9,1},{17,25},{25,17},{2,10},{10... | collective-permute-start | bytes 2654216 | tf_op jit(solution)/shard_map/ppermute | solution.py:494
  98.3 22.6 %collective-permute-start.17 = (f32[12,3,48,128]{3,2,1,0:T(8,128)S(1)}, f32[12,3,48,128]{3,2,1,0:T(8,128)S(1)}, u32[]{:S(2)}, u32[]{:S(2)}) collective-permute-start(f32[12,3,48,128]{3,2,1,0:T(8,128)S(1)} %rows.8.refs_6_), channel_id=1, source_target_pairs={{0,16},{8,24},{16,0},{24,8},{1,17},{9,25},{17,1},{25,9},{2,18},{10... | collective-permute-start | bytes 2654216 | tf_op jit(solution)/shard_map/ppermute | solution.py:494
  102.1 21.6 %collective-permute-start.14 = (f32[12,3,48,128]{3,2,1,0:T(8,128)S(1)}, f32[12,3,48,128]{3,2,1,0:T(8,128)S(1)}, u32[]{:S(2)}, u32[]{:S(2)}) collective-permute-start(f32[12,3,48,128]{3,2,1,0:T(8,128)S(1)} %rows.9.refs_7_), channel_id=1, source_target_pairs={{0,8},{8,0},{16,24},{24,16},{1,9},{9,1},{17,25},{25,17},{2,10},{10... | collective-permute-start | bytes 2654216 | tf_op jit(solution)/shard_map/ppermute | solution.py:494
  104.4 16.5 %copy-start.2 = (bf16[512,192]{1,0:T(8,128)(2,1)S(1)}, bf16[512,192]{1,0:T(8,128)(2,1)}, u32[]{:S(2)}) copy-start(bf16[512,192]{1,0:T(8,128)(2,1)} %constant.27.clone.refs_3_) | copy-start | bytes 589828
  104.4 16.5 %copy-start.3 = (f32[192]{0:T(256)S(1)}, f32[192]{0:T(256)}, u32[]{:S(2)}) copy-start(f32[192]{0:T(256)} %param.19) | copy-start | bytes 2308
  104.4 16.5 %copy-start.4 = (f32[48]{0:T(128)S(1)}, f32[48]{0:T(128)}, u32[]{:S(2)}) copy-start(f32[48]{0:T(128)} %param.20) | copy-start | bytes 580
  104.4 16.5 %copy-start.5 = (f32[24]{0:T(128)S(1)}, f32[24]{0:T(128)}, u32[]{:S(2)}) copy-start(f32[24]{0:T(128)} %refs_6_.5) | copy-start | bytes 292
  104.4 34.6 %collective-permute-start.15 = (f32[12,3,48,128]{3,2,1,0:T(8,128)S(1)}, f32[12,3,48,128]{3,2,1,0:T(8,128)S(1)}, u32[]{:S(2)}, u32[]{:S(2)}) collective-permute-start(f32[12,3,48,128]{3,2,1,0:T(8,128)S(1)} %rows.10.refs_6_), channel_id=1, source_target_pairs={{0,16},{8,24},{16,0},{24,8},{1,17},{9,25},{17,1},{25,9},{2,18},{10... | collective-permute-start | bytes 2654216 | tf_op jit(solution)/shard_map/ppermute | solution.py:494
